TPU v7x, 256 devices: a whole 4x4x8 slice. The times are simulated.
256 devices in a mesh: wide: 8 (over y_lo, x), narrow: 32 (over z, y_hi, core).
Axes of the slice: x: 4, y: 4 (y_hi: 2, y_lo: 2; y = y_hi * 2 + y_lo), z: 8, core: 2. Of those that a mesh axis runs over, the one named last changes fastest.
Arguments:
- iterate: bfloat16 [3584, 18432], P('wide', 'narrow'), may hold values from -0.078125 to 0.078125
Outputs:
- update: bfloat16 [3584, 18432], P('wide', 'narrow')
All inputs are finite; a program needn't handle non-finite values.
Results may differ from a plain program's by a relative error of at most 0.0065.
Values may be sent and summed in bfloat16 or wider, within the bound.
No kernel may reach another device: no remote copies, remote signals or barrier semaphores. Data moves between devices by JAX's collectives and lax.ppermute only.
A program may use at most 64 MiB of HBM per device.

v0:
```python
import functools

import jax
import jax.numpy as jnp
from jax import lax
from jax.experimental import pallas as pl
from jax.experimental.pallas import tpu as pltpu
from jax.sharding import PartitionSpec as P

COLS = 18432

coef_a = 3.4445
coef_b = -4.775
coef_c = 2.0315

Z_SIZE = 8
f32, bf16 = jnp.float32, jnp.bfloat16


def from_x(value, step):
    pairs = [(y * 4 + (x + step) % 4, y * 4 + x) for y in range(2) for x in range(4)]
    return lax.ppermute(value, "wide", pairs)


def from_y(value):
    return lax.ppermute(value, "wide", [(w, (w + 4) % 8) for w in range(8)])


def from_z(value, step):
    pairs = [(((z + step) % 8) * 4 + r, z * 4 + r) for z in range(8) for r in range(4)]
    return lax.ppermute(value, "narrow", pairs)


def from_y_hi(value):
    return lax.ppermute(value, "narrow", [(n, n ^ 2) for n in range(32)])


def from_y_both(value):
    pairs = [((w, n), ((w + 4) % 8, n ^ 2)) for w in range(8) for n in range(32)]
    return lax.ppermute(value, ("wide", "narrow"), [(a * 32 + b, c * 32 + d) for (a, b), (c, d) in pairs])


def from_core(value):
    return lax.ppermute(value, "narrow", [(n, n ^ 1) for n in range(32)])


def rows_of(left, right):
    return lax.dot_general(left, right, (((1,), (1,)), ((), ())), preferred_element_type=f32)


def dot(left, right):
    return jnp.dot(left, right, preferred_element_type=f32)


def cat(*parts, axis=0):
    return jnp.concatenate(parts, axis=axis)


def gather_first(own):
    return from_x(own, 1), from_x(own, -1), from_y(own)


def gather_second(right, left, across):
    half = right.shape[0] // 16 * 8
    via_y = from_y(cat(right[:half], left[:half]))
    via_right = from_x(cat(across[half:], right[:half]), 1)
    via_left = from_x(cat(across[half:], left[half:]), -1)
    rest = right.shape[0] - half
    far = cat(via_right[rest:], via_left[rest:])
    return far, cat(via_y[:half], via_right[:rest]), cat(via_y[half:], via_left[:rest])


def gather_third(far, across_right, across_left):
    third = far.shape[0] // 24 * 8
    part_y = from_y(far[:third])
    part_right = from_x(across_right[third : 2 * third], 1)
    part_left = from_x(across_left[2 * third :], -1)
    return cat(part_y, part_right, part_left)


def along_z(value, hops):
    pairs = [(z * 4 + r, (z + hops * (1 - 2 * (r % 2))) % 8 * 4 + r) for z in range(8) for r in range(4)]
    return lax.ppermute(value, "narrow", pairs)


def found_kernel(mine, *refs):
    block_ref, *x_refs = refs[:9]
    if mine:
        found_ref, lhs, rhs, sems = refs[9:]
    else:
        before_ref, found_ref, sent_ref, lhs, rhs, sems = refs[9:]
    rows, cols = x_refs[0].shape
    core = lax.rem(lax.axis_index("narrow"), 2)

    def run(picks):
        copies = [pltpu.make_async_copy(block_ref, lhs, sems.at[4])]
        for at, pick in enumerate(picks):
            copies.append(pltpu.make_async_copy(x_refs[pick], rhs.at[pl.ds(at * rows, rows)], sems.at[at]))
        for copy in copies:
            copy.start()
        for copy in copies:
            copy.wait()

    @pl.when(core == (0 if mine else 1))
    def _():
        run((0, 1, 4, 5))

    @pl.when(core == (1 if mine else 0))
    def _():
        run((2, 3, 6, 7))

    for start in range(0, cols, 256):
        part = pl.ds(start, min(256, cols - start))
        value = dot(lhs[0], rhs[: 2 * rows, part]) + dot(lhs[1], rhs[2 * rows :, part])
        if not mine:
            value = before_ref[:, part] + value
            sent_ref[:, part] = value.astype(bf16)
        found_ref[:, part] = value


def found_part(block, x_blocks, before=None):
    rows, cols = x_blocks[0].shape
    mine = before is None
    found = jax.ShapeDtypeStruct((rows, cols), f32)
    vmem = pl.BlockSpec(memory_space=pltpu.VMEM)
    return pl.pallas_call(
        functools.partial(found_kernel, mine),
        out_shape=found if mine else (found, jax.ShapeDtypeStruct((rows, cols), bf16)),
        in_specs=[pl.BlockSpec(memory_space=pl.ANY)] * 9 + ([] if mine else [vmem]),
        out_specs=vmem if mine else (vmem, vmem),
        scratch_shapes=[
            pltpu.VMEM(block.shape, bf16),
            pltpu.VMEM((4 * rows, cols), bf16),
            pltpu.SemaphoreType.DMA((5,)),
        ],
        compiler_params=pltpu.CompilerParams(vmem_limit_bytes=16 * 2**20),
        cost_estimate=pl.CostEstimate(flops=8 * rows * rows * cols, bytes_accessed=6 * 2**20, transcendentals=0),
    )(block, *x_blocks, *([] if mine else [before]))


def local(own):
    rows = own.shape[0]
    narrow_pos = lax.axis_index("narrow")
    core = narrow_pos % 2
    z_pos = narrow_pos // 4
    unit = rows // Z_SIZE

    right, left, across = gather_first(own)
    half_rows = rows // 2
    far = cat(from_x(right[:half_rows], 1), from_x(left[half_rows:], -1))
    same = cat(own, right, left, far)
    x_right, x_left, x_far = right, left, far

    both = cat(own, across)
    order = ((0, 4), (0, 3), (1, 3), (0, 2), (1, 2), (0, 1), (1, 1), (1, 0))

    def units_of(core):
        def place(which, step):
            owner = jnp.where(core == 0, which, 1 - which)
            return owner * rows + ((z_pos + step * (1 - 2 * core)) % 8) * unit

        return cat(*[lax.dynamic_slice_in_dim(both, place(*at), unit, 0) for at in order])

    given = rows_of(units_of(1 - core), same).astype(bf16)
    kept = lax.optimization_barrier(rows_of(units_of(core), same))
    summed = kept + from_core(given).astype(f32)

    def units(start, stop):
        return summed[start * unit : stop * unit]

    three, left = lax.optimization_barrier((units(1, 3).astype(bf16), left))
    passed = along_z(three, 1).astype(f32) + jnp.pad(along_z(units(0, 1).astype(bf16), 2).astype(f32), ((0, unit), (0, 0)))
    two, one, far = lax.optimization_barrier(((units(3, 5) + passed).astype(bf16), units(5, 7).astype(bf16), far))
    passed = along_z(two, 2).astype(f32) + along_z(one, 1).astype(f32)
    total = passed + jnp.pad(units(7, 8), ((unit, 0), (0, 0)))
    total, other_left, other_far = lax.optimization_barrier((total, from_y(left), from_y(far)))

    width = 2 * rows
    total = jnp.where(core == 0, total, cat(total[unit:], total[:unit])).reshape(2, unit, 2 * width)
    given = lax.dynamic_slice_in_dim(total, (1 - core) * width, width, 2).astype(bf16)
    total = (lax.dynamic_slice_in_dim(total, core * width, width, 2) + from_core(given).astype(f32)).astype(bf16)

    gram_same = total[0].astype(f32) + from_y_hi(total[0]).astype(f32)
    gram_other = from_y(total[1]).astype(f32) + from_y_both(total[1]).astype(f32)
    gram = jnp.stack([gram_same, gram_other]).astype(bf16)

    gram, right = lax.optimization_barrier((gram, right))
    up1, down1 = from_z(gram, 1), from_z(gram, -1)
    up2, down2 = from_z(gram, 2), from_z(gram, -2)
    up1, down1, up2, down2, other_right = lax.optimization_barrier((up1, down1, up2, down2, from_y(right)))
    up3, down3 = from_z(up2, 1), from_z(down2, -1)
    up4, down4 = from_z(up2[:1], 2), from_z(down2[1:], -2)
    block = jnp.zeros((2, rows, width), bf16)
    pieces = ((0, gram), (1, up1), (-1, down1), (2, up2), (-2, down2), (3, up3), (-3, down3), (4, cat(up4, down4)))
    for step, piece in pieces:
        block = lax.dynamic_update_slice_in_dim(block, piece, ((z_pos + step) % 8) * unit, 1)
    got = from_core(block)
    low = jnp.where(core == 0, block, got)
    high = jnp.where(core == 0, got, block)
    gram_rows = cat(low[0], high[0], low[1], high[1], axis=1)

    x_blocks = (own, x_right, x_left, x_far, across, other_right, other_left, other_far)
    found, sent = found_part(got, x_blocks, found_part(block, x_blocks))
    right, left, across = gather_first(sent)
    far, across_right, across_left = gather_second(right, left, across)
    across_far = gather_third(far, across_right, across_left)
    three, seven = 3 * rows, 7 * rows
    product = dot(gram_rows[:, :three], cat(sent, right, left))
    product = product + dot(gram_rows[:, three:seven], cat(far, across, across_right, across_left))
    start = coef_a * own.astype(f32) + coef_b * found + coef_c * product
    scale = float(COLS) ** 0.5
    return (scale * (start + coef_c * dot(gram_rows[:, seven:], across_far))).astype(bf16)


def solution(mesh):
    return jax.shard_map(
        local,
        mesh=mesh,
        in_specs=(P("wide", "narrow"),),
        out_specs=P("wide", "narrow"),
        check_vma=False,
    )
```

profile of v0, /device:TPU:24, one launch (start us, length us, event | category | flops | bytes accessed | tf_op | source)
XLA Modules:
  0.0 178.5 jit_solution(13556603430733376446)
XLA Ops:
  0.0 2.8 %collective-permute-start.1 = (bf16[448,576]{1,0:T(8,128)(2,1)}, bf16[448,576]{1,0:T(8,128)(2,1)S(1)}, u32[]{:S(2)}, u32[]{:S(2)}) collective-permute-start(bf16[448,576]{1,0:T(8,128)(2,1)} %refs_1_.3), channel_id=1, source_target_pairs={{32,0},{64,32},{96,64},{0,96},{160,128},{192,160},{224,192},{128,2... | collective-permute-start | bytes 1548296 | tf_op jit(solution)/shard_map/ppermute | solution.py:22
  3.5 1.2 constant_dynamic-update-slice_fusion.6
  4.7 10.6 %collective-permute-done.1.refs_2_ = bf16[448,576]{1,0:T(8,128)(2,1)S(1)} collective-permute-done((bf16[448,576]{1,0:T(8,128)(2,1)}, bf16[448,576]{1,0:T(8,128)(2,1)S(1)}, u32[]{:S(2)}, u32[]{:S(2)}) %collective-permute-start.1) | collective-permute-done | bytes 516128 | tf_op jit(solution)/shard_map/ppermute | solution.py:22
  15.3 3.7 %collective-permute-start.3 = (bf16[224,576]{1,0:T(8,128)(2,1)S(1)}, bf16[224,576]{1,0:T(8,128)(2,1)S(1)}, u32[]{:S(2)}, u32[]{:S(2)}) collective-permute-start(bf16[224,576]{1,0:T(8,128)(2,1)S(1)} %slice.143), channel_id=1, source_target_pairs={{32,0},{64,32},{96,64},{0,96},{160,128},{192,160},{224,192},{128,2... | collective-permute-start | bytes 774152 | tf_op jit(solution)/shard_map/ppermute | solution.py:22
  19.7 4.5 %collective-permute-done.3 = bf16[224,576]{1,0:T(8,128)(2,1)S(1)} collective-permute-done((bf16[224,576]{1,0:T(8,128)(2,1)S(1)}, bf16[224,576]{1,0:T(8,128)(2,1)S(1)}, u32[]{:S(2)}, u32[]{:S(2)}) %collective-permute-start.3) | collective-permute-done | bytes 258080 | tf_op jit(solution)/shard_map/ppermute | solution.py:22
  24.3 3.5 %collective-permute-done.4 = bf16[224,576]{1,0:T(8,128)(2,1)S(1)} collective-permute-done((bf16[224,576]{1,0:T(8,128)(2,1)S(1)}, bf16[224,576]{1,0:T(8,128)(2,1)S(1)}, u32[]{:S(2)}, u32[]{:S(2)}) %collective-permute-start.4) | collective-permute-done | bytes 258080 | tf_op jit(solution)/shard_map/ppermute | solution.py:22
  27.8 1.5 convolution_convert_fusion
  29.4 1.5 fusion.35
  30.9 1.9 %collective-permute-done.5 = bf16[448,1792]{1,0:T(8,128)(2,1)S(1)} collective-permute-done((bf16[448,1792]{1,0:T(8,128)(2,1)S(1)}, bf16[448,1792]{1,0:T(8,128)(2,1)S(1)}, u32[]{:S(2)}, u32[]{:S(2)}) %collective-permute-start.5) | collective-permute-done | bytes 1605664 | tf_op jit(solution)/shard_map/ppermute | solution.py:44
  34.1 1.9 %collective-permute-start.6 = (bf16[112,1792]{1,0:T(8,128)(2,1)S(1)}, bf16[112,1792]{1,0:T(8,128)(2,1)S(1)}, u32[]{:S(2)}, u32[]{:S(2)}) collective-permute-start(bf16[112,1792]{1,0:T(8,128)(2,1)S(1)} %get-tuple-element.22), channel_id=1, source_target_pairs={{0,4},{1,29},{2,6},{3,31},{4,8},{5,1},{6,10},{7,3},{8,12},{9,5},{1... | collective-permute-start | bytes 1204232 | tf_op jit(solution)/shard_map/ppermute | solution.py:83
  36.1 3.3 %collective-permute-start.7 = (bf16[56,1792]{1,0:T(8,128)(2,1)S(1)}, bf16[56,1792]{1,0:T(8,128)(2,1)S(1)}, u32[]{:S(2)}, u32[]{:S(2)}) collective-permute-start(bf16[56,1792]{1,0:T(8,128)(2,1)S(1)} %slice.147), channel_id=1, source_target_pairs={{0,8},{1,25},{2,10},{3,27},{4,12},{5,29},{6,14},{7,31},{8,16},{9,1... | collective-permute-start | bytes 602120 | tf_op jit(solution)/shard_map/ppermute | solution.py:83
  39.4 10.6 %collective-permute-done.7 = bf16[56,1792]{1,0:T(8,128)(2,1)S(1)} collective-permute-done((bf16[56,1792]{1,0:T(8,128)(2,1)S(1)}, bf16[56,1792]{1,0:T(8,128)(2,1)S(1)}, u32[]{:S(2)}, u32[]{:S(2)}) %collective-permute-start.7) | collective-permute-done | bytes 200736 | tf_op jit(solution)/shard_map/ppermute | solution.py:83
  50.9 2.1 %collective-permute-start.9 = (bf16[112,1792]{1,0:T(8,128)(2,1)}, bf16[112,1792]{1,0:T(8,128)(2,1)}, u32[]{:S(2)}, u32[]{:S(2)}) collective-permute-start(bf16[112,1792]{1,0:T(8,128)(2,1)} %get-tuple-element.24), channel_id=1, source_target_pairs={{0,4},{1,29},{2,6},{3,31},{4,8},{5,1},{6,10},{7,3},{8,12},{9,5},{1... | collective-permute-start | bytes 1204232 | tf_op jit(solution)/shard_map/ppermute | solution.py:83
  53.7 1.3 collective-permute-start.11
  55.0 1.0 slice.149
  56.1 9.5 %collective-permute-done.8 = bf16[112,1792]{1,0:T(8,128)(2,1)} collective-permute-done((bf16[112,1792]{1,0:T(8,128)(2,1)}, bf16[112,1792]{1,0:T(8,128)(2,1)}, u32[]{:S(2)}, u32[]{:S(2)}) %collective-permute-start.8) | collective-permute-done | bytes 401440 | tf_op jit(solution)/shard_map/ppermute | solution.py:83
  65.5 4.2 %collective-permute-done.9 = bf16[112,1792]{1,0:T(8,128)(2,1)} collective-permute-done((bf16[112,1792]{1,0:T(8,128)(2,1)}, bf16[112,1792]{1,0:T(8,128)(2,1)}, u32[]{:S(2)}, u32[]{:S(2)}) %collective-permute-start.9) | collective-permute-done | bytes 401440 | tf_op jit(solution)/shard_map/ppermute | solution.py:83
  69.7 1.2 pad_add_fusion
  71.0 10.0 %collective-permute-done.11.refs_8_ = bf16[448,576]{1,0:T(8,128)(2,1)S(1)} collective-permute-done((bf16[448,576]{1,0:T(8,128)(2,1)S(1)}, bf16[448,576]{1,0:T(8,128)(2,1)S(1)}, u32[]{:S(2)}, u32[]{:S(2)}) %collective-permute-start.11) | collective-permute-done | bytes 516128 | tf_op jit(solution)/shard_map/ppermute | solution.py:26
  82.8 1.8 %collective-permute-done.12 = bf16[2,56,896]{2,1,0:T(8,128)(2,1)} collective-permute-done((bf16[2,56,896]{2,1,0:T(8,128)(2,1)}, bf16[2,56,896]{2,1,0:T(8,128)(2,1)}, u32[]{:S(2)}, u32[]{:S(2)}) %collective-permute-start.12) | collective-permute-done | bytes 200736 | tf_op jit(solution)/shard_map/ppermute | solution.py:44
  84.6 1.1 add_convert_fusion
  85.8 1.3 collective-permute-start.13
  87.1 2.9 %collective-permute-start.15 = (bf16[56,896]{1,0:T(8,128)(2,1)S(1)}, bf16[56,896]{1,0:T(8,128)(2,1)S(1)}, u32[]{:S(2)}, u32[]{:S(2)}) collective-permute-start(bf16[56,896]{1,0:T(8,128)(2,1)S(1)} %get-tuple-element.83), channel_id=1, source_target_pairs={{0,130},{1,131},{2,128},{3,129},{4,134},{5,135},{6,132},{7,133},{8... | collective-permute-start | bytes 301064 | tf_op jit(solution)/shard_map/ppermute | solution.py:40
  89.9 3.1 %collective-permute-done.13 = bf16[56,896]{1,0:T(8,128)(2,1)S(1)} collective-permute-done((bf16[56,896]{1,0:T(8,128)(2,1)S(1)}, bf16[56,896]{1,0:T(8,128)(2,1)S(1)}, u32[]{:S(2)}, u32[]{:S(2)}) %collective-permute-start.13) | collective-permute-done | bytes 100384 | tf_op jit(solution)/shard_map/ppermute | solution.py:35
  93.1 1.3 collective-permute-done.15
  96.6 1.2 collective-permute-start.17
  98.5 2.3 %collective-permute-start.19 = (bf16[2,56,896]{2,1,0:T(8,128)(2,1)}, bf16[2,56,896]{2,1,0:T(8,128)(2,1)}, u32[]{:S(2)}, u32[]{:S(2)}) collective-permute-start(bf16[2,56,896]{2,1,0:T(8,128)(2,1)} %pad_maximum_fusion.9), channel_id=1, source_target_pairs={{24,0},{25,1},{26,2},{27,3},{28,4},{29,5},{30,6},{31,7},{0,8},{1,9... | collective-permute-start | bytes 602120 | tf_op jit(solution)/shard_map/ppermute | solution.py:31
  101.9 3.3 %collective-permute-done.16 = bf16[2,56,896]{2,1,0:T(8,128)(2,1)} collective-permute-done((bf16[2,56,896]{2,1,0:T(8,128)(2,1)}, bf16[2,56,896]{2,1,0:T(8,128)(2,1)}, u32[]{:S(2)}, u32[]{:S(2)}) %collective-permute-start.16) | collective-permute-done | bytes 200736 | tf_op jit(solution)/shard_map/ppermute | solution.py:31
  105.2 4.6 %collective-permute-done.17 = bf16[2,56,896]{2,1,0:T(8,128)(2,1)} collective-permute-done((bf16[2,56,896]{2,1,0:T(8,128)(2,1)}, bf16[2,56,896]{2,1,0:T(8,128)(2,1)}, u32[]{:S(2)}, u32[]{:S(2)}) %collective-permute-start.17) | collective-permute-done | bytes 200736 | tf_op jit(solution)/shard_map/ppermute | solution.py:31
  109.7 2.7 %collective-permute-done.18 = bf16[2,56,896]{2,1,0:T(8,128)(2,1)} collective-permute-done((bf16[2,56,896]{2,1,0:T(8,128)(2,1)}, bf16[2,56,896]{2,1,0:T(8,128)(2,1)}, u32[]{:S(2)}, u32[]{:S(2)}) %collective-permute-start.18) | collective-permute-done | bytes 200736 | tf_op jit(solution)/shard_map/ppermute | solution.py:31
  114.4 1.1 collective-permute-start.22
  116.4 1.8 collective-permute-start.23
  118.2 1.2 collective-permute-start.24
  125.2 3.1 %shard_map.17.refs_9_ = f32[448,576]{1,0:T(8,128)S(1)} custom-call(bf16[2,448,896]{2,1,0:T(8,128)(2,1)S(1)} %maximum_dynamic-update-slice_fusion.refs_0_, bf16[448,576]{1,0:T(8,128)(2,1)S(1)} %copy-done, bf16[448,576]{1,0:T(8,128)(2,1)S(1)} %collective-permute-done.1.refs_2_, bf16[448,576]{1,0:T(8,128)(2,1)S(1)} %collective-permute-done.2.refs_3_, ...), custom_call_target="tpu_custom_call" | custom-call | flops 924844032 | bytes 6291456 | tf_op jit(solution)/shard_map/pallas_call | solution.py:126
  128.6 2.3 %shard_map.18 = (f32[448,576]{1,0:T(8,128)S(1)}, bf16[448,576]{1,0:T(8,128)(2,1)S(1)}) custom-call(bf16[2,448,896]{2,1,0:T(8,128)(2,1)S(1)} %collective-permute-done.25.refs_0_, bf16[448,576]{1,0:T(8,128)(2,1)S(1)} %copy-done, bf16[448,576]{1,0:T(8,128)(2,1)S(1)} %collective-permute-done.1.refs_2_, bf16[448,576]{1,0:T(8,128)(2,1)S(1)} %collective-permute-done.2.refs_3_, ...), custom_call_target="tpu_custom_call" | custom-call | flops 924844032 | bytes 6291456 | tf_op jit(solution)/shard_map/pallas_call | solution.py:126
  130.9 1.4 collective-permute-start.28
  132.3 3.2 %collective-permute-start.26 = (bf16[448,576]{1,0:T(8,128)(2,1)S(1)}, bf16[448,576]{1,0:T(8,128)(2,1)S(1)}, u32[]{:S(2)}, u32[]{:S(2)}) collective-permute-start(bf16[448,576]{1,0:T(8,128)(2,1)S(1)} %get-tuple-element.38), channel_id=1, source_target_pairs={{32,0},{64,32},{96,64},{0,96},{160,128},{192,160},{224,192},{128,2... | collective-permute-start | bytes 1548296 | tf_op jit(solution)/shard_map/ppermute | solution.py:22
  135.9 10.9 %collective-permute-done.28 = bf16[448,576]{1,0:T(8,128)(2,1)S(1)} collective-permute-done((bf16[448,576]{1,0:T(8,128)(2,1)S(1)}, bf16[448,576]{1,0:T(8,128)(2,1)S(1)}, u32[]{:S(2)}, u32[]{:S(2)}) %collective-permute-start.28) | collective-permute-done | bytes 516128 | tf_op jit(solution)/shard_map/ppermute | solution.py:26
  146.8 2.2 %collective-permute-done.27 = bf16[448,576]{1,0:T(8,128)(2,1)S(1)} collective-permute-done((bf16[448,576]{1,0:T(8,128)(2,1)S(1)}, bf16[448,576]{1,0:T(8,128)(2,1)S(1)}, u32[]{:S(2)}, u32[]{:S(2)}) %collective-permute-start.27) | collective-permute-done | bytes 516128 | tf_op jit(solution)/shard_map/ppermute | solution.py:22
  149.3 3.0 %collective-permute-start.29 = (bf16[448,576]{1,0:T(8,128)(2,1)S(1)}, bf16[448,576]{1,0:T(8,128)(2,1)S(1)}, u32[]{:S(2)}, u32[]{:S(2)}) collective-permute-start(bf16[448,576]{1,0:T(8,128)(2,1)S(1)} %get-tuple-element.76), channel_id=1, source_target_pairs={{32,0},{64,32},{96,64},{0,96},{160,128},{192,160},{224,192},{128,2... | collective-permute-start | bytes 1548296 | tf_op jit(solution)/shard_map/ppermute | solution.py:22
  153.4 10.7 %collective-permute-done.29 = bf16[448,576]{1,0:T(8,128)(2,1)S(1)} collective-permute-done((bf16[448,576]{1,0:T(8,128)(2,1)S(1)}, bf16[448,576]{1,0:T(8,128)(2,1)S(1)}, u32[]{:S(2)}, u32[]{:S(2)}) %collective-permute-start.29) | collective-permute-done | bytes 516128 | tf_op jit(solution)/shard_map/ppermute | solution.py:22
  164.2 3.6 %collective-permute-done.30 = bf16[448,576]{1,0:T(8,128)(2,1)S(1)} collective-permute-done((bf16[448,576]{1,0:T(8,128)(2,1)S(1)}, bf16[448,576]{1,0:T(8,128)(2,1)S(1)}, u32[]{:S(2)}, u32[]{:S(2)}) %collective-permute-start.30) | collective-permute-done | bytes 516128 | tf_op jit(solution)/shard_map/ppermute | solution.py:22
  168.1 1.9 %collective-permute-start.33 = (bf16[144,576]{1,0:T(8,128)(2,1)S(1)}, bf16[144,576]{1,0:T(8,128)(2,1)S(1)}, u32[]{:S(2)}, u32[]{:S(2)}) collective-permute-start(bf16[144,576]{1,0:T(8,128)(2,1)S(1)} %pad_maximum_fusion.10), channel_id=1, source_target_pairs={{32,0},{64,32},{96,64},{0,96},{160,128},{192,160},{224,192},{128,2... | collective-permute-start | bytes 497672 | tf_op jit(solution)/shard_map/ppermute | solution.py:22
  171.2 1.6 fusion.6
  172.8 1.2 fusion.11
  174.0 1.9 %collective-permute-done.32 = bf16[144,576]{1,0:T(8,128)(2,1)S(1)} collective-permute-done((bf16[144,576]{1,0:T(8,128)(2,1)S(1)}, bf16[144,576]{1,0:T(8,128)(2,1)S(1)}, u32[]{:S(2)}, u32[]{:S(2)}) %collective-permute-start.32) | collective-permute-done | bytes 165920 | tf_op jit(solution)/shard_map/ppermute | solution.py:26
  175.9 1.1 collective-permute-done.34
  177.1 1.4 multiply_convert_fusion
  (93 shorter events, 22.3 us)
Async XLA Ops:
  0.0 15.3 %collective-permute-start.1 = (bf16[448,576]{1,0:T(8,128)(2,1)}, bf16[448,576]{1,0:T(8,128)(2,1)S(1)}, u32[]{:S(2)}, u32[]{:S(2)}) collective-permute-start(bf16[448,576]{1,0:T(8,128)(2,1)} %refs_1_.3), channel_id=1, source_target_pairs={{32,0},{64,32},{96,64},{0,96},{160,128},{192,160},{224,192},{128,2... | collective-permute-start | bytes 1548296 | tf_op jit(solution)/shard_map/ppermute | solution.py:22
  2.8 16.2 %collective-permute-start.2 = (bf16[448,576]{1,0:T(8,128)(2,1)}, bf16[448,576]{1,0:T(8,128)(2,1)S(1)}, u32[]{:S(2)}, u32[]{:S(2)}) collective-permute-start(bf16[448,576]{1,0:T(8,128)(2,1)} %refs_1_.3), channel_id=1, source_target_pairs={{96,0},{0,32},{32,64},{64,96},{224,128},{128,160},{160,192},{192,2... | collective-permute-start | bytes 1548296 | tf_op jit(solution)/shard_map/ppermute | solution.py:22
  2.8 16.4 %collective-permute-start = (bf16[448,576]{1,0:T(8,128)(2,1)}, bf16[448,576]{1,0:T(8,128)(2,1)S(1)}, u32[]{:S(2)}, u32[]{:S(2)}) collective-permute-start(bf16[448,576]{1,0:T(8,128)(2,1)} %refs_1_.3), channel_id=1, source_target_pairs={{0,128},{32,160},{64,192},{96,224},{128,0},{160,32},{192,64},{224,... | collective-permute-start | bytes 1548296 | tf_op jit(solution)/shard_map/ppermute | solution.py:26
  15.3 8.9 %collective-permute-start.3 = (bf16[224,576]{1,0:T(8,128)(2,1)S(1)}, bf16[224,576]{1,0:T(8,128)(2,1)S(1)}, u32[]{:S(2)}, u32[]{:S(2)}) collective-permute-start(bf16[224,576]{1,0:T(8,128)(2,1)S(1)} %slice.143), channel_id=1, source_target_pairs={{32,0},{64,32},{96,64},{0,96},{160,128},{192,160},{224,192},{128,2... | collective-permute-start | bytes 774152 | tf_op jit(solution)/shard_map/ppermute | solution.py:22
  19.0 8.7 %collective-permute-start.4 = (bf16[224,576]{1,0:T(8,128)(2,1)S(1)}, bf16[224,576]{1,0:T(8,128)(2,1)S(1)}, u32[]{:S(2)}, u32[]{:S(2)}) collective-permute-start(bf16[224,576]{1,0:T(8,128)(2,1)S(1)} %slice.144), channel_id=1, source_target_pairs={{96,0},{0,32},{32,64},{64,96},{224,128},{128,160},{160,192},{192,2... | collective-permute-start | bytes 774152 | tf_op jit(solution)/shard_map/ppermute | solution.py:22
  29.3 3.5 %collective-permute-start.5 = (bf16[448,1792]{1,0:T(8,128)(2,1)S(1)}, bf16[448,1792]{1,0:T(8,128)(2,1)S(1)}, u32[]{:S(2)}, u32[]{:S(2)}) collective-permute-start(bf16[448,1792]{1,0:T(8,128)(2,1)S(1)} %convolution_convert_fusion), channel_id=1, source_target_pairs={{0,1},{1,0},{2,3},{3,2},{4,5},{5,4},{6,7},{7,6},{8,9},{9,8},{10,11... | collective-permute-start | bytes 4816904 | tf_op jit(solution)/shard_map/ppermute | solution.py:44
  33.2 17.6 %copy-start.1 = (f32[448,1792]{1,0:T(8,128)}, f32[448,1792]{1,0:T(8,128)S(1)}, u32[]{:S(2)}) copy-start(f32[448,1792]{1,0:T(8,128)S(1)} %get-tuple-element.40) | copy-start | bytes 9633796
  34.1 15.9 %collective-permute-start.6 = (bf16[112,1792]{1,0:T(8,128)(2,1)S(1)}, bf16[112,1792]{1,0:T(8,128)(2,1)S(1)}, u32[]{:S(2)}, u32[]{:S(2)}) collective-permute-start(bf16[112,1792]{1,0:T(8,128)(2,1)S(1)} %get-tuple-element.22), channel_id=1, source_target_pairs={{0,4},{1,29},{2,6},{3,31},{4,8},{5,1},{6,10},{7,3},{8,12},{9,5},{1... | collective-permute-start | bytes 1204232 | tf_op jit(solution)/shard_map/ppermute | solution.py:83
  36.1 13.9 %collective-permute-start.7 = (bf16[56,1792]{1,0:T(8,128)(2,1)S(1)}, bf16[56,1792]{1,0:T(8,128)(2,1)S(1)}, u32[]{:S(2)}, u32[]{:S(2)}) collective-permute-start(bf16[56,1792]{1,0:T(8,128)(2,1)S(1)} %slice.147), channel_id=1, source_target_pairs={{0,8},{1,25},{2,10},{3,27},{4,12},{5,29},{6,14},{7,31},{8,16},{9,1... | collective-permute-start | bytes 602120 | tf_op jit(solution)/shard_map/ppermute | solution.py:83
  50.9 14.7 %collective-permute-start.8 = (bf16[112,1792]{1,0:T(8,128)(2,1)}, bf16[112,1792]{1,0:T(8,128)(2,1)}, u32[]{:S(2)}, u32[]{:S(2)}) collective-permute-start(bf16[112,1792]{1,0:T(8,128)(2,1)} %fusion.15), channel_id=1, source_target_pairs={{0,8},{1,25},{2,10},{3,27},{4,12},{5,29},{6,14},{7,31},{8,16},{9,1... | collective-permute-start | bytes 1204232 | tf_op jit(solution)/shard_map/ppermute | solution.py:83
  50.9 18.9 %collective-permute-start.9 = (bf16[112,1792]{1,0:T(8,128)(2,1)}, bf16[112,1792]{1,0:T(8,128)(2,1)}, u32[]{:S(2)}, u32[]{:S(2)}) collective-permute-start(bf16[112,1792]{1,0:T(8,128)(2,1)} %get-tuple-element.24), channel_id=1, source_target_pairs={{0,4},{1,29},{2,6},{3,31},{4,8},{5,1},{6,10},{7,3},{8,12},{9,5},{1... | collective-permute-start | bytes 1204232 | tf_op jit(solution)/shard_map/ppermute | solution.py:83
  53.0 18.0 %collective-permute-start.10 = (bf16[448,576]{1,0:T(8,128)(2,1)S(1)}, bf16[448,576]{1,0:T(8,128)(2,1)S(1)}, u32[]{:S(2)}, u32[]{:S(2)}) collective-permute-start(bf16[448,576]{1,0:T(8,128)(2,1)S(1)} %collective-permute-done.2.refs_3_), channel_id=1, source_target_pairs={{0,128},{32,160},{64,192},{96,224},{128,0},{160,32},{192,64},{224,... | collective-permute-start | bytes 1548296 | tf_op jit(solution)/shard_map/ppermute | solution.py:26
  53.7 27.3 %collective-permute-start.11 = (bf16[448,576]{1,0:T(8,128)(2,1)S(1)}, bf16[448,576]{1,0:T(8,128)(2,1)S(1)}, u32[]{:S(2)}, u32[]{:S(2)}) collective-permute-start(bf16[448,576]{1,0:T(8,128)(2,1)S(1)} %get-tuple-element.26.refs_4_), channel_id=1, source_target_pairs={{0,128},{32,160},{64,192},{96,224},{128,0},{160,32},{192,64},{224,... | collective-permute-start | bytes 1548296 | tf_op jit(solution)/shard_map/ppermute | solution.py:26
  81.2 0.9 copy-start.2
  82.8 1.8 %collective-permute-start.12 = (bf16[2,56,896]{2,1,0:T(8,128)(2,1)}, bf16[2,56,896]{2,1,0:T(8,128)(2,1)}, u32[]{:S(2)}, u32[]{:S(2)}) collective-permute-start(bf16[2,56,896]{2,1,0:T(8,128)(2,1)} %dynamic-slice_convert_fusion), channel_id=1, source_target_pairs={{0,1},{1,0},{2,3},{3,2},{4,5},{5,4},{6,7},{7,6},{8,9},{9,8},{10,11... | collective-permute-start | bytes 602120 | tf_op jit(solution)/shard_map/ppermute | solution.py:44
  85.8 7.3 %collective-permute-start.13 = (bf16[56,896]{1,0:T(8,128)(2,1)S(1)}, bf16[56,896]{1,0:T(8,128)(2,1)S(1)}, u32[]{:S(2)}, u32[]{:S(2)}) collective-permute-start(bf16[56,896]{1,0:T(8,128)(2,1)S(1)} %get-tuple-element.82), channel_id=1, source_target_pairs={{0,2},{1,3},{2,0},{3,1},{4,6},{5,7},{6,4},{7,5},{8,10},{9,11},{10,... | collective-permute-start | bytes 301064 | tf_op jit(solution)/shard_map/ppermute | solution.py:35
  87.1 6.0 %collective-permute-start.14 = (bf16[56,896]{1,0:T(8,128)(2,1)S(1)}, bf16[56,896]{1,0:T(8,128)(2,1)S(1)}, u32[]{:S(2)}, u32[]{:S(2)}) collective-permute-start(bf16[56,896]{1,0:T(8,128)(2,1)S(1)} %get-tuple-element.83), channel_id=1, source_target_pairs={{0,128},{32,160},{64,192},{96,224},{128,0},{160,32},{192,64},{224,... | collective-permute-start | bytes 301064 | tf_op jit(solution)/shard_map/ppermute | solution.py:26
  87.1 7.3 %collective-permute-start.15 = (bf16[56,896]{1,0:T(8,128)(2,1)S(1)}, bf16[56,896]{1,0:T(8,128)(2,1)S(1)}, u32[]{:S(2)}, u32[]{:S(2)}) collective-permute-start(bf16[56,896]{1,0:T(8,128)(2,1)S(1)} %get-tuple-element.83), channel_id=1, source_target_pairs={{0,130},{1,131},{2,128},{3,129},{4,134},{5,135},{6,132},{7,133},{8... | collective-permute-start | bytes 301064 | tf_op jit(solution)/shard_map/ppermute | solution.py:40
  95.1 17.3 %collective-permute-start.20 = (bf16[448,576]{1,0:T(8,128)(2,1)S(1)}, bf16[448,576]{1,0:T(8,128)(2,1)}, u32[]{:S(2)}, u32[]{:S(2)}) collective-permute-start(bf16[448,576]{1,0:T(8,128)(2,1)S(1)} %collective-permute-done.1.refs_2_), channel_id=1, source_target_pairs={{0,128},{32,160},{64,192},{96,224},{128,0},{160,32},{192,64},{224,... | collective-permute-start | bytes 1548296 | tf_op jit(solution)/shard_map/ppermute | solution.py:26
  95.9 9.3 %collective-permute-start.16 = (bf16[2,56,896]{2,1,0:T(8,128)(2,1)}, bf16[2,56,896]{2,1,0:T(8,128)(2,1)}, u32[]{:S(2)}, u32[]{:S(2)}) collective-permute-start(bf16[2,56,896]{2,1,0:T(8,128)(2,1)} %pad_maximum_fusion.9), channel_id=1, source_target_pairs={{4,0},{5,1},{6,2},{7,3},{8,4},{9,5},{10,6},{11,7},{12,8},{13,9},{1... | collective-permute-start | bytes 602120 | tf_op jit(solution)/shard_map/ppermute | solution.py:31
  96.6 13.1 %collective-permute-start.17 = (bf16[2,56,896]{2,1,0:T(8,128)(2,1)}, bf16[2,56,896]{2,1,0:T(8,128)(2,1)}, u32[]{:S(2)}, u32[]{:S(2)}) collective-permute-start(bf16[2,56,896]{2,1,0:T(8,128)(2,1)} %pad_maximum_fusion.9), channel_id=1, source_target_pairs={{28,0},{29,1},{30,2},{31,3},{0,4},{1,5},{2,6},{3,7},{4,8},{5,9},{6... | collective-permute-start | bytes 602120 | tf_op jit(solution)/shard_map/ppermute | solution.py:31
  97.9 14.6 %collective-permute-start.18 = (bf16[2,56,896]{2,1,0:T(8,128)(2,1)}, bf16[2,56,896]{2,1,0:T(8,128)(2,1)}, u32[]{:S(2)}, u32[]{:S(2)}) collective-permute-start(bf16[2,56,896]{2,1,0:T(8,128)(2,1)} %pad_maximum_fusion.9), channel_id=1, source_target_pairs={{8,0},{9,1},{10,2},{11,3},{12,4},{13,5},{14,6},{15,7},{16,8},{17,9... | collective-permute-start | bytes 602120 | tf_op jit(solution)/shard_map/ppermute | solution.py:31
  98.5 14.0 %collective-permute-start.19 = (bf16[2,56,896]{2,1,0:T(8,128)(2,1)}, bf16[2,56,896]{2,1,0:T(8,128)(2,1)}, u32[]{:S(2)}, u32[]{:S(2)}) collective-permute-start(bf16[2,56,896]{2,1,0:T(8,128)(2,1)} %pad_maximum_fusion.9), channel_id=1, source_target_pairs={{24,0},{25,1},{26,2},{27,3},{28,4},{29,5},{30,6},{31,7},{0,8},{1,9... | collective-permute-start | bytes 602120 | tf_op jit(solution)/shard_map/ppermute | solution.py:31
  101.9 23.2 %copy-start = (bf16[448,576]{1,0:T(8,128)(2,1)S(1)}, bf16[448,576]{1,0:T(8,128)(2,1)}, u32[]{:S(2)}) copy-start(bf16[448,576]{1,0:T(8,128)(2,1)} %refs_1_.3) | copy-start | bytes 1548292
  112.5 10.8 %collective-permute-start.21 = (bf16[2,56,896]{2,1,0:T(8,128)(2,1)}, bf16[2,56,896]{2,1,0:T(8,128)(2,1)S(1)}, u32[]{:S(2)}, u32[]{:S(2)}) collective-permute-start(bf16[2,56,896]{2,1,0:T(8,128)(2,1)} %collective-permute-done.18), channel_id=1, source_target_pairs={{4,0},{5,1},{6,2},{7,3},{8,4},{9,5},{10,6},{11,7},{12,8},{13,9},{1... | collective-permute-start | bytes 602120 | tf_op jit(solution)/shard_map/ppermute | solution.py:31
  114.4 8.9 %collective-permute-start.22 = (bf16[2,56,896]{2,1,0:T(8,128)(2,1)}, bf16[2,56,896]{2,1,0:T(8,128)(2,1)S(1)}, u32[]{:S(2)}, u32[]{:S(2)}) collective-permute-start(bf16[2,56,896]{2,1,0:T(8,128)(2,1)} %collective-permute-done.19), channel_id=1, source_target_pairs={{28,0},{29,1},{30,2},{31,3},{0,4},{1,5},{2,6},{3,7},{4,8},{5,9},{6... | collective-permute-start | bytes 602120 | tf_op jit(solution)/shard_map/ppermute | solution.py:31
  116.4 7.6 %collective-permute-start.23 = (bf16[1,56,896]{2,1,0:T(8,128)(2,1)S(1)}, bf16[1,56,896]{2,1,0:T(8,128)(2,1)S(1)}, u32[]{:S(2)}, u32[]{:S(2)}) collective-permute-start(bf16[1,56,896]{2,1,0:T(8,128)(2,1)S(1)} %slice.121), channel_id=1, source_target_pairs={{8,0},{9,1},{10,2},{11,3},{12,4},{13,5},{14,6},{15,7},{16,8},{17,9... | collective-permute-start | bytes 301064 | tf_op jit(solution)/shard_map/ppermute | solution.py:31
  118.2 6.8 %collective-permute-start.24 = (bf16[1,56,896]{2,1,0:T(8,128)(2,1)S(1)}, bf16[1,56,896]{2,1,0:T(8,128)(2,1)S(1)}, u32[]{:S(2)}, u32[]{:S(2)}) collective-permute-start(bf16[1,56,896]{2,1,0:T(8,128)(2,1)S(1)} %slice.122), channel_id=1, source_target_pairs={{24,0},{25,1},{26,2},{27,3},{28,4},{29,5},{30,6},{31,7},{0,8},{1,9... | collective-permute-start | bytes 301064 | tf_op jit(solution)/shard_map/ppermute | solution.py:31
  125.0 3.5 %collective-permute-start.25 = (bf16[2,448,896]{2,1,0:T(8,128)(2,1)S(1)}, bf16[2,448,896]{2,1,0:T(8,128)(2,1)S(1)}, u32[]{:S(2)}, u32[]{:S(2)}) collective-permute-start(bf16[2,448,896]{2,1,0:T(8,128)(2,1)S(1)} %maximum_dynamic-update-slice_fusion.refs_0_), channel_id=1, source_target_pairs={{0,1},{1,0},{2,3},{3,2},{4,5},{5,4},{6,7},{7,6},{8,9},{9,8},{10,11... | collective-permute-start | bytes 4816904 | tf_op jit(solution)/shard_map/ppermute | solution.py:44
  130.9 15.8 %collective-permute-start.28 = (bf16[448,576]{1,0:T(8,128)(2,1)S(1)}, bf16[448,576]{1,0:T(8,128)(2,1)S(1)}, u32[]{:S(2)}, u32[]{:S(2)}) collective-permute-start(bf16[448,576]{1,0:T(8,128)(2,1)S(1)} %get-tuple-element.38), channel_id=1, source_target_pairs={{0,128},{32,160},{64,192},{96,224},{128,0},{160,32},{192,64},{224,... | collective-permute-start | bytes 1548296 | tf_op jit(solution)/shard_map/ppermute | solution.py:26
  132.3 16.7 %collective-permute-start.27 = (bf16[448,576]{1,0:T(8,128)(2,1)S(1)}, bf16[448,576]{1,0:T(8,128)(2,1)S(1)}, u32[]{:S(2)}, u32[]{:S(2)}) collective-permute-start(bf16[448,576]{1,0:T(8,128)(2,1)S(1)} %get-tuple-element.38), channel_id=1, source_target_pairs={{96,0},{0,32},{32,64},{64,96},{224,128},{128,160},{160,192},{192,2... | collective-permute-start | bytes 1548296 | tf_op jit(solution)/shard_map/ppermute | solution.py:22
  132.3 16.7 %collective-permute-start.26 = (bf16[448,576]{1,0:T(8,128)(2,1)S(1)}, bf16[448,576]{1,0:T(8,128)(2,1)S(1)}, u32[]{:S(2)}, u32[]{:S(2)}) collective-permute-start(bf16[448,576]{1,0:T(8,128)(2,1)S(1)} %get-tuple-element.38), channel_id=1, source_target_pairs={{32,0},{64,32},{96,64},{0,96},{160,128},{192,160},{224,192},{128,2... | collective-permute-start | bytes 1548296 | tf_op jit(solution)/shard_map/ppermute | solution.py:22
  149.3 14.9 %collective-permute-start.29 = (bf16[448,576]{1,0:T(8,128)(2,1)S(1)}, bf16[448,576]{1,0:T(8,128)(2,1)S(1)}, u32[]{:S(2)}, u32[]{:S(2)}) collective-permute-start(bf16[448,576]{1,0:T(8,128)(2,1)S(1)} %get-tuple-element.76), channel_id=1, source_target_pairs={{32,0},{64,32},{96,64},{0,96},{160,128},{192,160},{224,192},{128,2... | collective-permute-start | bytes 1548296 | tf_op jit(solution)/shard_map/ppermute | solution.py:22
  152.4 15.4 %collective-permute-start.30 = (bf16[448,576]{1,0:T(8,128)(2,1)S(1)}, bf16[448,576]{1,0:T(8,128)(2,1)S(1)}, u32[]{:S(2)}, u32[]{:S(2)}) collective-permute-start(bf16[448,576]{1,0:T(8,128)(2,1)S(1)} %get-tuple-element.77), channel_id=1, source_target_pairs={{96,0},{0,32},{32,64},{64,96},{224,128},{128,160},{160,192},{192,2... | collective-permute-start | bytes 1548296 | tf_op jit(solution)/shard_map/ppermute | solution.py:22
  152.6 15.3 %collective-permute-start.31 = (bf16[448,576]{1,0:T(8,128)(2,1)S(1)}, bf16[448,576]{1,0:T(8,128)(2,1)S(1)}, u32[]{:S(2)}, u32[]{:S(2)}) collective-permute-start(bf16[448,576]{1,0:T(8,128)(2,1)S(1)} %get-tuple-element.75), channel_id=1, source_target_pairs={{0,128},{32,160},{64,192},{96,224},{128,0},{160,32},{192,64},{224,... | collective-permute-start | bytes 1548296 | tf_op jit(solution)/shard_map/ppermute | solution.py:26
  168.1 5.9 %collective-permute-start.33 = (bf16[144,576]{1,0:T(8,128)(2,1)S(1)}, bf16[144,576]{1,0:T(8,128)(2,1)S(1)}, u32[]{:S(2)}, u32[]{:S(2)}) collective-permute-start(bf16[144,576]{1,0:T(8,128)(2,1)S(1)} %pad_maximum_fusion.10), channel_id=1, source_target_pairs={{32,0},{64,32},{96,64},{0,96},{160,128},{192,160},{224,192},{128,2... | collective-permute-start | bytes 497672 | tf_op jit(solution)/shard_map/ppermute | solution.py:22
  170.0 7.0 %collective-permute-start.34 = (bf16[160,576]{1,0:T(8,128)(2,1)S(1)}, bf16[160,576]{1,0:T(8,128)(2,1)S(1)}, u32[]{:S(2)}, u32[]{:S(2)}) collective-permute-start(bf16[160,576]{1,0:T(8,128)(2,1)S(1)} %slice.168), channel_id=1, source_target_pairs={{96,0},{0,32},{32,64},{64,96},{224,128},{128,160},{160,192},{192,2... | collective-permute-start | bytes 552968 | tf_op jit(solution)/shard_map/ppermute | solution.py:22
  170.3 5.6 %collective-permute-start.32 = (bf16[144,576]{1,0:T(8,128)(2,1)S(1)}, bf16[144,576]{1,0:T(8,128)(2,1)S(1)}, u32[]{:S(2)}, u32[]{:S(2)}) collective-permute-start(bf16[144,576]{1,0:T(8,128)(2,1)S(1)} %slice.167), channel_id=1, source_target_pairs={{0,128},{32,160},{64,192},{96,224},{128,0},{160,32},{192,64},{224,... | collective-permute-start | bytes 497672 | tf_op jit(solution)/shard_map/ppermute | solution.py:26
where the time goes:
time: 179 us; the launch traced here: 178 us
  waiting for transfers between devices  104 us (58%)
  starting transfers between devices  43.3 us (24%)
  local copies, waits for them, and re-layouts  13.1 us (7%)
  matrix products  7.25 us (4%)
  Pallas kernels  5.44 us (3%)
  other arithmetic  4.97 us (3%)
    ppermute x10, waiting for transfers between devices, from_x(): return lax.ppermute(value, 'wide', pairs)  36.3 us
    ppermute x4, waiting for transfers between devices, along_z(): return lax.ppermute(value, 'narrow', pairs)  24.3 us
    ppermute x8, waiting for transfers between devices, from_y(): return lax.ppermute(value, 'wide', [(w, (w + 4) % 8) for w in range(8)])  22.8 us
    ppermute x10, starting transfers between devices, from_x(): return lax.ppermute(value, 'wide', pairs)  15 us
    ppermute x8, waiting for transfers between devices, from_z(): return lax.ppermute(value, 'narrow', pairs)  12.2 us
    ppermute x8, starting transfers between devices, from_z(): return lax.ppermute(value, 'narrow', pairs)  10 us
    ppermute x4, starting transfers between devices, along_z(): return lax.ppermute(value, 'narrow', pairs)  7.41 us
    ppermute x8, starting transfers between devices, from_y(): return lax.ppermute(value, 'wide', [(w, (w + 4) % 8) for w in range(8)])  6.51 us
  transfers between devices with their start and end apart: 35, of which 23 were waited for; matrix products, arithmetic and copies ran while one was open for 9% of the time, Pallas kernels for 2%

commit v1 on v0

--- a/solution.py
+++ b/solution.py
@@ -168,12 +168,13 @@
     def units(start, stop):
         return summed[start * unit : stop * unit]
 
-    three, left = lax.optimization_barrier((units(1, 3).astype(bf16), left))
-    passed = along_z(three, 1).astype(f32) + jnp.pad(along_z(units(0, 1).astype(bf16), 2).astype(f32), ((0, unit), (0, 0)))
-    two, one, far = lax.optimization_barrier(((units(3, 5) + passed).astype(bf16), units(5, 7).astype(bf16), far))
+    passed = along_z(units(1, 3).astype(bf16), 1).astype(f32) + jnp.pad(along_z(units(0, 1).astype(bf16), 2).astype(f32), ((0, unit), (0, 0)))
+    two, one, other_left = lax.optimization_barrier(
+        ((units(3, 5) + passed).astype(bf16), units(5, 7).astype(bf16), from_y(left))
+    )
     passed = along_z(two, 2).astype(f32) + along_z(one, 1).astype(f32)
     total = passed + jnp.pad(units(7, 8), ((unit, 0), (0, 0)))
-    total, other_left, other_far = lax.optimization_barrier((total, from_y(left), from_y(far)))
+    total, other_far = lax.optimization_barrier((total, from_y(far)))
 
     width = 2 * rows
     total = jnp.where(core == 0, total, cat(total[unit:], total[:unit])).reshape(2, unit, 2 * width)

time: 179 us -> 174 us (0.972)
  waiting for transfers between devices: 104 us -> 95.8 us
  starting transfers between devices: 43.3 us -> 46.2 us
    ppermute x8, waiting for transfers between devices: 22.8 us -> 16.5 us  [from_y(): return lax.ppermute(value, 'wide', [(w, (w + 4) % 8) for w in range(8)])]
    ppermute x4, waiting for transfers between devices: 24.3 us -> 20.7 us  [along_z(): return lax.ppermute(value, 'narrow', pairs)]
    ppermute x8, starting transfers between devices: 10 us -> 12.8 us  [from_z(): return lax.ppermute(value, 'narrow', pairs)]
  transfers between devices with their start and end apart: 35 -> 35, of which waited for: 23 -> 23; matrix products, arithmetic and copies ran while one was open for 9% -> 10% of each run, Pallas kernels for 2% -> 2%
where the time goes in v1:
time: 174 us; the launch traced here: 173 us
  waiting for transfers between devices  95.8 us (55%)
  starting transfers between devices  46.2 us (27%)
  local copies, waits for them, and re-layouts  13.1 us (8%)
  matrix products  7.25 us (4%)
  Pallas kernels  5.44 us (3%)
  other arithmetic  4.97 us (3%)
    ppermute x10, waiting for transfers between devices, from_x(): return lax.ppermute(value, 'wide', pairs)  36.3 us
    ppermute x4, waiting for transfers between devices, along_z(): return lax.ppermute(value, 'narrow', pairs)  20.7 us
    ppermute x8, waiting for transfers between devices, from_y(): return lax.ppermute(value, 'wide', [(w, (w + 4) % 8) for w in range(8)])  16.5 us
    ppermute x10, starting transfers between devices, from_x(): return lax.ppermute(value, 'wide', pairs)  15 us
    ppermute x8, waiting for transfers between devices, from_z(): return lax.ppermute(value, 'narrow', pairs)  13.9 us
    ppermute x8, starting transfers between devices, from_z(): return lax.ppermute(value, 'narrow', pairs)  12.8 us
    ppermute x4, starting transfers between devices, along_z(): return lax.ppermute(value, 'narrow', pairs)  8.16 us
    ppermute x8, starting transfers between devices, from_y(): return lax.ppermute(value, 'wide', [(w, (w + 4) % 8) for w in range(8)])  5.98 us
  transfers between devices with their start and end apart: 35, of which 23 were waited for; matrix products, arithmetic and copies ran while one was open for 10% of the time, Pallas kernels for 2%

profile of v1, /device:TPU:24, one launch (start us, length us, event | category | flops | bytes accessed | tf_op | source)
XLA Modules:
  0.0 173.2 jit_solution(11962126880072579531)
XLA Ops:
  0.0 2.8 %collective-permute-start.1 = (bf16[448,576]{1,0:T(8,128)(2,1)}, bf16[448,576]{1,0:T(8,128)(2,1)S(1)}, u32[]{:S(2)}, u32[]{:S(2)}) collective-permute-start(bf16[448,576]{1,0:T(8,128)(2,1)} %refs_1_.3), channel_id=1, source_target_pairs={{32,0},{64,32},{96,64},{0,96},{160,128},{192,160},{224,192},{128,2... | collective-permute-start | bytes 1548296 | tf_op jit(solution)/shard_map/ppermute | solution.py:22
  3.5 1.2 constant_dynamic-update-slice_fusion.6
  4.7 10.6 %collective-permute-done.1.refs_2_ = bf16[448,576]{1,0:T(8,128)(2,1)S(1)} collective-permute-done((bf16[448,576]{1,0:T(8,128)(2,1)}, bf16[448,576]{1,0:T(8,128)(2,1)S(1)}, u32[]{:S(2)}, u32[]{:S(2)}) %collective-permute-start.1) | collective-permute-done | bytes 516128 | tf_op jit(solution)/shard_map/ppermute | solution.py:22
  15.3 3.7 %collective-permute-start.3 = (bf16[224,576]{1,0:T(8,128)(2,1)S(1)}, bf16[224,576]{1,0:T(8,128)(2,1)S(1)}, u32[]{:S(2)}, u32[]{:S(2)}) collective-permute-start(bf16[224,576]{1,0:T(8,128)(2,1)S(1)} %slice.143), channel_id=1, source_target_pairs={{32,0},{64,32},{96,64},{0,96},{160,128},{192,160},{224,192},{128,2... | collective-permute-start | bytes 774152 | tf_op jit(solution)/shard_map/ppermute | solution.py:22
  19.7 4.5 %collective-permute-done.3 = bf16[224,576]{1,0:T(8,128)(2,1)S(1)} collective-permute-done((bf16[224,576]{1,0:T(8,128)(2,1)S(1)}, bf16[224,576]{1,0:T(8,128)(2,1)S(1)}, u32[]{:S(2)}, u32[]{:S(2)}) %collective-permute-start.3) | collective-permute-done | bytes 258080 | tf_op jit(solution)/shard_map/ppermute | solution.py:22
  24.3 3.5 %collective-permute-done.4 = bf16[224,576]{1,0:T(8,128)(2,1)S(1)} collective-permute-done((bf16[224,576]{1,0:T(8,128)(2,1)S(1)}, bf16[224,576]{1,0:T(8,128)(2,1)S(1)}, u32[]{:S(2)}, u32[]{:S(2)}) %collective-permute-start.4) | collective-permute-done | bytes 258080 | tf_op jit(solution)/shard_map/ppermute | solution.py:22
  27.8 1.5 convolution_convert_fusion
  29.4 1.5 fusion.35
  30.9 1.9 %collective-permute-done.5 = bf16[448,1792]{1,0:T(8,128)(2,1)S(1)} collective-permute-done((bf16[448,1792]{1,0:T(8,128)(2,1)S(1)}, bf16[448,1792]{1,0:T(8,128)(2,1)S(1)}, u32[]{:S(2)}, u32[]{:S(2)}) %collective-permute-start.5) | collective-permute-done | bytes 1605664 | tf_op jit(solution)/shard_map/ppermute | solution.py:44
  34.1 1.9 %collective-permute-start.6 = (bf16[112,1792]{1,0:T(8,128)(2,1)S(1)}, bf16[112,1792]{1,0:T(8,128)(2,1)S(1)}, u32[]{:S(2)}, u32[]{:S(2)}) collective-permute-start(bf16[112,1792]{1,0:T(8,128)(2,1)S(1)} %get-tuple-element.42), channel_id=1, source_target_pairs={{0,4},{1,29},{2,6},{3,31},{4,8},{5,1},{6,10},{7,3},{8,12},{9,5},{1... | collective-permute-start | bytes 1204232 | tf_op jit(solution)/shard_map/ppermute | solution.py:83
  36.1 3.3 %collective-permute-start.7 = (bf16[56,1792]{1,0:T(8,128)(2,1)S(1)}, bf16[56,1792]{1,0:T(8,128)(2,1)S(1)}, u32[]{:S(2)}, u32[]{:S(2)}) collective-permute-start(bf16[56,1792]{1,0:T(8,128)(2,1)S(1)} %slice.147), channel_id=1, source_target_pairs={{0,8},{1,25},{2,10},{3,27},{4,12},{5,29},{6,14},{7,31},{8,16},{9,1... | collective-permute-start | bytes 602120 | tf_op jit(solution)/shard_map/ppermute | solution.py:83
  40.1 9.8 %collective-permute-done.7 = bf16[56,1792]{1,0:T(8,128)(2,1)S(1)} collective-permute-done((bf16[56,1792]{1,0:T(8,128)(2,1)S(1)}, bf16[56,1792]{1,0:T(8,128)(2,1)S(1)}, u32[]{:S(2)}, u32[]{:S(2)}) %collective-permute-start.7) | collective-permute-done | bytes 200736 | tf_op jit(solution)/shard_map/ppermute | solution.py:83
  50.9 3.7 %collective-permute-done.8.refs_7_ = bf16[448,576]{1,0:T(8,128)(2,1)S(1)} collective-permute-done((bf16[448,576]{1,0:T(8,128)(2,1)S(1)}, bf16[448,576]{1,0:T(8,128)(2,1)S(1)}, u32[]{:S(2)}, u32[]{:S(2)}) %collective-permute-start.8) | collective-permute-done | bytes 516128 | tf_op jit(solution)/shard_map/ppermute | solution.py:26
  54.6 2.4 %collective-permute-start.10 = (bf16[112,1792]{1,0:T(8,128)(2,1)}, bf16[112,1792]{1,0:T(8,128)(2,1)}, u32[]{:S(2)}, u32[]{:S(2)}) collective-permute-start(bf16[112,1792]{1,0:T(8,128)(2,1)} %get-tuple-element.20), channel_id=1, source_target_pairs={{0,4},{1,29},{2,6},{3,31},{4,8},{5,1},{6,10},{7,3},{8,12},{9,5},{1... | collective-permute-start | bytes 1204232 | tf_op jit(solution)/shard_map/ppermute | solution.py:83
  59.2 4.7 %collective-permute-done.10 = bf16[112,1792]{1,0:T(8,128)(2,1)} collective-permute-done((bf16[112,1792]{1,0:T(8,128)(2,1)}, bf16[112,1792]{1,0:T(8,128)(2,1)}, u32[]{:S(2)}, u32[]{:S(2)}) %collective-permute-start.10) | collective-permute-done | bytes 401440 | tf_op jit(solution)/shard_map/ppermute | solution.py:83
  64.0 6.2 %collective-permute-done.9 = bf16[112,1792]{1,0:T(8,128)(2,1)} collective-permute-done((bf16[112,1792]{1,0:T(8,128)(2,1)}, bf16[112,1792]{1,0:T(8,128)(2,1)}, u32[]{:S(2)}, u32[]{:S(2)}) %collective-permute-start.9) | collective-permute-done | bytes 401440 | tf_op jit(solution)/shard_map/ppermute | solution.py:83
  70.1 1.2 pad_add_fusion
  73.2 1.8 %collective-permute-done.12 = bf16[2,56,896]{2,1,0:T(8,128)(2,1)} collective-permute-done((bf16[2,56,896]{2,1,0:T(8,128)(2,1)}, bf16[2,56,896]{2,1,0:T(8,128)(2,1)}, u32[]{:S(2)}, u32[]{:S(2)}) %collective-permute-start.12) | collective-permute-done | bytes 200736 | tf_op jit(solution)/shard_map/ppermute | solution.py:44
  75.0 1.1 add_convert_fusion
  76.1 1.3 collective-permute-start.13
  77.5 2.9 %collective-permute-start.15 = (bf16[56,896]{1,0:T(8,128)(2,1)S(1)}, bf16[56,896]{1,0:T(8,128)(2,1)S(1)}, u32[]{:S(2)}, u32[]{:S(2)}) collective-permute-start(bf16[56,896]{1,0:T(8,128)(2,1)S(1)} %get-tuple-element.77), channel_id=1, source_target_pairs={{0,130},{1,131},{2,128},{3,129},{4,134},{5,135},{6,132},{7,133},{8... | collective-permute-start | bytes 301064 | tf_op jit(solution)/shard_map/ppermute | solution.py:40
  80.3 3.1 %collective-permute-done.13 = bf16[56,896]{1,0:T(8,128)(2,1)S(1)} collective-permute-done((bf16[56,896]{1,0:T(8,128)(2,1)S(1)}, bf16[56,896]{1,0:T(8,128)(2,1)S(1)}, u32[]{:S(2)}, u32[]{:S(2)}) %collective-permute-start.13) | collective-permute-done | bytes 100384 | tf_op jit(solution)/shard_map/ppermute | solution.py:35
  83.4 1.3 collective-permute-done.15
  86.2 3.4 %collective-permute-start.16 = (bf16[2,56,896]{2,1,0:T(8,128)(2,1)}, bf16[2,56,896]{2,1,0:T(8,128)(2,1)}, u32[]{:S(2)}, u32[]{:S(2)}) collective-permute-start(bf16[2,56,896]{2,1,0:T(8,128)(2,1)} %pad_maximum_fusion.9), channel_id=1, source_target_pairs={{4,0},{5,1},{6,2},{7,3},{8,4},{9,5},{10,6},{11,7},{12,8},{13,9},{1... | collective-permute-start | bytes 602120 | tf_op jit(solution)/shard_map/ppermute | solution.py:31
  90.1 1.1 collective-permute-start.18
  91.2 1.9 %collective-permute-start.19 = (bf16[2,56,896]{2,1,0:T(8,128)(2,1)}, bf16[2,56,896]{2,1,0:T(8,128)(2,1)}, u32[]{:S(2)}, u32[]{:S(2)}) collective-permute-start(bf16[2,56,896]{2,1,0:T(8,128)(2,1)} %pad_maximum_fusion.9), channel_id=1, source_target_pairs={{24,0},{25,1},{26,2},{27,3},{28,4},{29,5},{30,6},{31,7},{0,8},{1,9... | collective-permute-start | bytes 602120 | tf_op jit(solution)/shard_map/ppermute | solution.py:31
  94.1 3.0 %collective-permute-done.16 = bf16[2,56,896]{2,1,0:T(8,128)(2,1)} collective-permute-done((bf16[2,56,896]{2,1,0:T(8,128)(2,1)}, bf16[2,56,896]{2,1,0:T(8,128)(2,1)}, u32[]{:S(2)}, u32[]{:S(2)}) %collective-permute-start.16) | collective-permute-done | bytes 200736 | tf_op jit(solution)/shard_map/ppermute | solution.py:31
  97.2 5.8 %collective-permute-done.17 = bf16[2,56,896]{2,1,0:T(8,128)(2,1)} collective-permute-done((bf16[2,56,896]{2,1,0:T(8,128)(2,1)}, bf16[2,56,896]{2,1,0:T(8,128)(2,1)}, u32[]{:S(2)}, u32[]{:S(2)}) %collective-permute-start.17) | collective-permute-done | bytes 200736 | tf_op jit(solution)/shard_map/ppermute | solution.py:31
  103.0 1.9 %collective-permute-done.18 = bf16[2,56,896]{2,1,0:T(8,128)(2,1)} collective-permute-done((bf16[2,56,896]{2,1,0:T(8,128)(2,1)}, bf16[2,56,896]{2,1,0:T(8,128)(2,1)}, u32[]{:S(2)}, u32[]{:S(2)}) %collective-permute-start.18) | collective-permute-done | bytes 200736 | tf_op jit(solution)/shard_map/ppermute | solution.py:31
  104.9 1.4 collective-permute-start.21
  107.2 1.2 collective-permute-start.22
  109.4 3.4 %collective-permute-start.23 = (bf16[1,56,896]{2,1,0:T(8,128)(2,1)S(1)}, bf16[1,56,896]{2,1,0:T(8,128)(2,1)S(1)}, u32[]{:S(2)}, u32[]{:S(2)}) collective-permute-start(bf16[1,56,896]{2,1,0:T(8,128)(2,1)S(1)} %slice.121), channel_id=1, source_target_pairs={{8,0},{9,1},{10,2},{11,3},{12,4},{13,5},{14,6},{15,7},{16,8},{17,9... | collective-permute-start | bytes 301064 | tf_op jit(solution)/shard_map/ppermute | solution.py:31
  117.1 2.7 %collective-permute-done.24 = bf16[1,56,896]{2,1,0:T(8,128)(2,1)S(1)} collective-permute-done((bf16[1,56,896]{2,1,0:T(8,128)(2,1)S(1)}, bf16[1,56,896]{2,1,0:T(8,128)(2,1)S(1)}, u32[]{:S(2)}, u32[]{:S(2)}) %collective-permute-start.24) | collective-permute-done | bytes 100384 | tf_op jit(solution)/shard_map/ppermute | solution.py:31
  119.9 3.1 %shard_map.17.refs_9_ = f32[448,576]{1,0:T(8,128)S(1)} custom-call(bf16[2,448,896]{2,1,0:T(8,128)(2,1)S(1)} %maximum_dynamic-update-slice_fusion.refs_0_, bf16[448,576]{1,0:T(8,128)(2,1)S(1)} %copy-done, bf16[448,576]{1,0:T(8,128)(2,1)S(1)} %collective-permute-done.1.refs_2_, bf16[448,576]{1,0:T(8,128)(2,1)S(1)} %collective-permute-done.2.refs_3_, ...), custom_call_target="tpu_custom_call" | custom-call | flops 924844032 | bytes 6291456 | tf_op jit(solution)/shard_map/pallas_call | solution.py:126
  123.3 2.3 %shard_map.18 = (f32[448,576]{1,0:T(8,128)S(1)}, bf16[448,576]{1,0:T(8,128)(2,1)S(1)}) custom-call(bf16[2,448,896]{2,1,0:T(8,128)(2,1)S(1)} %collective-permute-done.25.refs_0_, bf16[448,576]{1,0:T(8,128)(2,1)S(1)} %copy-done, bf16[448,576]{1,0:T(8,128)(2,1)S(1)} %collective-permute-done.1.refs_2_, bf16[448,576]{1,0:T(8,128)(2,1)S(1)} %collective-permute-done.2.refs_3_, ...), custom_call_target="tpu_custom_call" | custom-call | flops 924844032 | bytes 6291456 | tf_op jit(solution)/shard_map/pallas_call | solution.py:126
  125.7 1.4 collective-permute-start.28
  127.1 3.2 %collective-permute-start.26 = (bf16[448,576]{1,0:T(8,128)(2,1)S(1)}, bf16[448,576]{1,0:T(8,128)(2,1)S(1)}, u32[]{:S(2)}, u32[]{:S(2)}) collective-permute-start(bf16[448,576]{1,0:T(8,128)(2,1)S(1)} %get-tuple-element.32), channel_id=1, source_target_pairs={{32,0},{64,32},{96,64},{0,96},{160,128},{192,160},{224,192},{128,2... | collective-permute-start | bytes 1548296 | tf_op jit(solution)/shard_map/ppermute | solution.py:22
  130.6 10.9 %collective-permute-done.28 = bf16[448,576]{1,0:T(8,128)(2,1)S(1)} collective-permute-done((bf16[448,576]{1,0:T(8,128)(2,1)S(1)}, bf16[448,576]{1,0:T(8,128)(2,1)S(1)}, u32[]{:S(2)}, u32[]{:S(2)}) %collective-permute-start.28) | collective-permute-done | bytes 516128 | tf_op jit(solution)/shard_map/ppermute | solution.py:26
  141.6 2.2 %collective-permute-done.27 = bf16[448,576]{1,0:T(8,128)(2,1)S(1)} collective-permute-done((bf16[448,576]{1,0:T(8,128)(2,1)S(1)}, bf16[448,576]{1,0:T(8,128)(2,1)S(1)}, u32[]{:S(2)}, u32[]{:S(2)}) %collective-permute-start.27) | collective-permute-done | bytes 516128 | tf_op jit(solution)/shard_map/ppermute | solution.py:22
  144.1 3.0 %collective-permute-start.29 = (bf16[448,576]{1,0:T(8,128)(2,1)S(1)}, bf16[448,576]{1,0:T(8,128)(2,1)S(1)}, u32[]{:S(2)}, u32[]{:S(2)}) collective-permute-start(bf16[448,576]{1,0:T(8,128)(2,1)S(1)} %get-tuple-element.70), channel_id=1, source_target_pairs={{32,0},{64,32},{96,64},{0,96},{160,128},{192,160},{224,192},{128,2... | collective-permute-start | bytes 1548296 | tf_op jit(solution)/shard_map/ppermute | solution.py:22
  148.2 10.7 %collective-permute-done.29 = bf16[448,576]{1,0:T(8,128)(2,1)S(1)} collective-permute-done((bf16[448,576]{1,0:T(8,128)(2,1)S(1)}, bf16[448,576]{1,0:T(8,128)(2,1)S(1)}, u32[]{:S(2)}, u32[]{:S(2)}) %collective-permute-start.29) | collective-permute-done | bytes 516128 | tf_op jit(solution)/shard_map/ppermute | solution.py:22
  159.0 3.6 %collective-permute-done.30 = bf16[448,576]{1,0:T(8,128)(2,1)S(1)} collective-permute-done((bf16[448,576]{1,0:T(8,128)(2,1)S(1)}, bf16[448,576]{1,0:T(8,128)(2,1)S(1)}, u32[]{:S(2)}, u32[]{:S(2)}) %collective-permute-start.30) | collective-permute-done | bytes 516128 | tf_op jit(solution)/shard_map/ppermute | solution.py:22
  162.8 1.9 %collective-permute-start.33 = (bf16[144,576]{1,0:T(8,128)(2,1)S(1)}, bf16[144,576]{1,0:T(8,128)(2,1)S(1)}, u32[]{:S(2)}, u32[]{:S(2)}) collective-permute-start(bf16[144,576]{1,0:T(8,128)(2,1)S(1)} %pad_maximum_fusion.10), channel_id=1, source_target_pairs={{32,0},{64,32},{96,64},{0,96},{160,128},{192,160},{224,192},{128,2... | collective-permute-start | bytes 497672 | tf_op jit(solution)/shard_map/ppermute | solution.py:22
  166.0 1.6 fusion.6
  167.6 1.2 fusion.11
  168.8 1.9 %collective-permute-done.32 = bf16[144,576]{1,0:T(8,128)(2,1)S(1)} collective-permute-done((bf16[144,576]{1,0:T(8,128)(2,1)S(1)}, bf16[144,576]{1,0:T(8,128)(2,1)S(1)}, u32[]{:S(2)}, u32[]{:S(2)}) %collective-permute-start.32) | collective-permute-done | bytes 165920 | tf_op jit(solution)/shard_map/ppermute | solution.py:26
  170.7 1.1 collective-permute-done.34
  171.8 1.4 multiply_convert_fusion
  (93 shorter events, 21.4 us)
Async XLA Ops:
  0.0 15.3 %collective-permute-start.1 = (bf16[448,576]{1,0:T(8,128)(2,1)}, bf16[448,576]{1,0:T(8,128)(2,1)S(1)}, u32[]{:S(2)}, u32[]{:S(2)}) collective-permute-start(bf16[448,576]{1,0:T(8,128)(2,1)} %refs_1_.3), channel_id=1, source_target_pairs={{32,0},{64,32},{96,64},{0,96},{160,128},{192,160},{224,192},{128,2... | collective-permute-start | bytes 1548296 | tf_op jit(solution)/shard_map/ppermute | solution.py:22
  2.8 16.2 %collective-permute-start.2 = (bf16[448,576]{1,0:T(8,128)(2,1)}, bf16[448,576]{1,0:T(8,128)(2,1)S(1)}, u32[]{:S(2)}, u32[]{:S(2)}) collective-permute-start(bf16[448,576]{1,0:T(8,128)(2,1)} %refs_1_.3), channel_id=1, source_target_pairs={{96,0},{0,32},{32,64},{64,96},{224,128},{128,160},{160,192},{192,2... | collective-permute-start | bytes 1548296 | tf_op jit(solution)/shard_map/ppermute | solution.py:22
  2.8 16.4 %collective-permute-start = (bf16[448,576]{1,0:T(8,128)(2,1)}, bf16[448,576]{1,0:T(8,128)(2,1)S(1)}, u32[]{:S(2)}, u32[]{:S(2)}) collective-permute-start(bf16[448,576]{1,0:T(8,128)(2,1)} %refs_1_.3), channel_id=1, source_target_pairs={{0,128},{32,160},{64,192},{96,224},{128,0},{160,32},{192,64},{224,... | collective-permute-start | bytes 1548296 | tf_op jit(solution)/shard_map/ppermute | solution.py:26
  15.3 8.9 %collective-permute-start.3 = (bf16[224,576]{1,0:T(8,128)(2,1)S(1)}, bf16[224,576]{1,0:T(8,128)(2,1)S(1)}, u32[]{:S(2)}, u32[]{:S(2)}) collective-permute-start(bf16[224,576]{1,0:T(8,128)(2,1)S(1)} %slice.143), channel_id=1, source_target_pairs={{32,0},{64,32},{96,64},{0,96},{160,128},{192,160},{224,192},{128,2... | collective-permute-start | bytes 774152 | tf_op jit(solution)/shard_map/ppermute | solution.py:22
  19.0 8.7 %collective-permute-start.4 = (bf16[224,576]{1,0:T(8,128)(2,1)S(1)}, bf16[224,576]{1,0:T(8,128)(2,1)S(1)}, u32[]{:S(2)}, u32[]{:S(2)}) collective-permute-start(bf16[224,576]{1,0:T(8,128)(2,1)S(1)} %slice.144), channel_id=1, source_target_pairs={{96,0},{0,32},{32,64},{64,96},{224,128},{128,160},{160,192},{192,2... | collective-permute-start | bytes 774152 | tf_op jit(solution)/shard_map/ppermute | solution.py:22
  29.3 3.5 %collective-permute-start.5 = (bf16[448,1792]{1,0:T(8,128)(2,1)S(1)}, bf16[448,1792]{1,0:T(8,128)(2,1)S(1)}, u32[]{:S(2)}, u32[]{:S(2)}) collective-permute-start(bf16[448,1792]{1,0:T(8,128)(2,1)S(1)} %convolution_convert_fusion), channel_id=1, source_target_pairs={{0,1},{1,0},{2,3},{3,2},{4,5},{5,4},{6,7},{7,6},{8,9},{9,8},{10,11... | collective-permute-start | bytes 4816904 | tf_op jit(solution)/shard_map/ppermute | solution.py:44
  33.2 17.6 %copy-start.1 = (f32[448,1792]{1,0:T(8,128)}, f32[448,1792]{1,0:T(8,128)S(1)}, u32[]{:S(2)}) copy-start(f32[448,1792]{1,0:T(8,128)S(1)} %get-tuple-element.34) | copy-start | bytes 9633796
  34.1 15.9 %collective-permute-start.6 = (bf16[112,1792]{1,0:T(8,128)(2,1)S(1)}, bf16[112,1792]{1,0:T(8,128)(2,1)S(1)}, u32[]{:S(2)}, u32[]{:S(2)}) collective-permute-start(bf16[112,1792]{1,0:T(8,128)(2,1)S(1)} %get-tuple-element.42), channel_id=1, source_target_pairs={{0,4},{1,29},{2,6},{3,31},{4,8},{5,1},{6,10},{7,3},{8,12},{9,5},{1... | collective-permute-start | bytes 1204232 | tf_op jit(solution)/shard_map/ppermute | solution.py:83
  36.1 13.9 %collective-permute-start.7 = (bf16[56,1792]{1,0:T(8,128)(2,1)S(1)}, bf16[56,1792]{1,0:T(8,128)(2,1)S(1)}, u32[]{:S(2)}, u32[]{:S(2)}) collective-permute-start(bf16[56,1792]{1,0:T(8,128)(2,1)S(1)} %slice.147), channel_id=1, source_target_pairs={{0,8},{1,25},{2,10},{3,27},{4,12},{5,29},{6,14},{7,31},{8,16},{9,1... | collective-permute-start | bytes 602120 | tf_op jit(solution)/shard_map/ppermute | solution.py:83
  39.4 15.2 %collective-permute-start.8 = (bf16[448,576]{1,0:T(8,128)(2,1)S(1)}, bf16[448,576]{1,0:T(8,128)(2,1)S(1)}, u32[]{:S(2)}, u32[]{:S(2)}) collective-permute-start(bf16[448,576]{1,0:T(8,128)(2,1)S(1)} %collective-permute-done.2.refs_3_), channel_id=1, source_target_pairs={{0,128},{32,160},{64,192},{96,224},{128,0},{160,32},{192,64},{224,... | collective-permute-start | bytes 1548296 | tf_op jit(solution)/shard_map/ppermute | solution.py:26
  54.6 9.4 %collective-permute-start.10 = (bf16[112,1792]{1,0:T(8,128)(2,1)}, bf16[112,1792]{1,0:T(8,128)(2,1)}, u32[]{:S(2)}, u32[]{:S(2)}) collective-permute-start(bf16[112,1792]{1,0:T(8,128)(2,1)} %get-tuple-element.20), channel_id=1, source_target_pairs={{0,4},{1,29},{2,6},{3,31},{4,8},{5,1},{6,10},{7,3},{8,12},{9,5},{1... | collective-permute-start | bytes 1204232 | tf_op jit(solution)/shard_map/ppermute | solution.py:83
  57.0 13.1 %collective-permute-start.9 = (bf16[112,1792]{1,0:T(8,128)(2,1)}, bf16[112,1792]{1,0:T(8,128)(2,1)}, u32[]{:S(2)}, u32[]{:S(2)}) collective-permute-start(bf16[112,1792]{1,0:T(8,128)(2,1)} %fusion.15), channel_id=1, source_target_pairs={{0,8},{1,25},{2,10},{3,27},{4,12},{5,29},{6,14},{7,31},{8,16},{9,1... | collective-permute-start | bytes 1204232 | tf_op jit(solution)/shard_map/ppermute | solution.py:83
  57.5 13.9 %collective-permute-start.11 = (bf16[448,576]{1,0:T(8,128)(2,1)S(1)}, bf16[448,576]{1,0:T(8,128)(2,1)S(1)}, u32[]{:S(2)}, u32[]{:S(2)}) collective-permute-start(bf16[448,576]{1,0:T(8,128)(2,1)S(1)} %get-tuple-element.72.refs_4_), channel_id=1, source_target_pairs={{0,128},{32,160},{64,192},{96,224},{128,0},{160,32},{192,64},{224,... | collective-permute-start | bytes 1548296 | tf_op jit(solution)/shard_map/ppermute | solution.py:26
  71.5 0.9 copy-start.2
  73.2 1.8 %collective-permute-start.12 = (bf16[2,56,896]{2,1,0:T(8,128)(2,1)}, bf16[2,56,896]{2,1,0:T(8,128)(2,1)}, u32[]{:S(2)}, u32[]{:S(2)}) collective-permute-start(bf16[2,56,896]{2,1,0:T(8,128)(2,1)} %dynamic-slice_convert_fusion), channel_id=1, source_target_pairs={{0,1},{1,0},{2,3},{3,2},{4,5},{5,4},{6,7},{7,6},{8,9},{9,8},{10,11... | collective-permute-start | bytes 602120 | tf_op jit(solution)/shard_map/ppermute | solution.py:44
  76.1 7.3 %collective-permute-start.13 = (bf16[56,896]{1,0:T(8,128)(2,1)S(1)}, bf16[56,896]{1,0:T(8,128)(2,1)S(1)}, u32[]{:S(2)}, u32[]{:S(2)}) collective-permute-start(bf16[56,896]{1,0:T(8,128)(2,1)S(1)} %get-tuple-element.76), channel_id=1, source_target_pairs={{0,2},{1,3},{2,0},{3,1},{4,6},{5,7},{6,4},{7,5},{8,10},{9,11},{10,... | collective-permute-start | bytes 301064 | tf_op jit(solution)/shard_map/ppermute | solution.py:35
  77.4 6.0 %collective-permute-start.14 = (bf16[56,896]{1,0:T(8,128)(2,1)S(1)}, bf16[56,896]{1,0:T(8,128)(2,1)S(1)}, u32[]{:S(2)}, u32[]{:S(2)}) collective-permute-start(bf16[56,896]{1,0:T(8,128)(2,1)S(1)} %get-tuple-element.77), channel_id=1, source_target_pairs={{0,128},{32,160},{64,192},{96,224},{128,0},{160,32},{192,64},{224,... | collective-permute-start | bytes 301064 | tf_op jit(solution)/shard_map/ppermute | solution.py:26
  77.5 7.3 %collective-permute-start.15 = (bf16[56,896]{1,0:T(8,128)(2,1)S(1)}, bf16[56,896]{1,0:T(8,128)(2,1)S(1)}, u32[]{:S(2)}, u32[]{:S(2)}) collective-permute-start(bf16[56,896]{1,0:T(8,128)(2,1)S(1)} %get-tuple-element.77), channel_id=1, source_target_pairs={{0,130},{1,131},{2,128},{3,129},{4,134},{5,135},{6,132},{7,133},{8... | collective-permute-start | bytes 301064 | tf_op jit(solution)/shard_map/ppermute | solution.py:40
  85.5 19.5 %collective-permute-start.20 = (bf16[448,576]{1,0:T(8,128)(2,1)S(1)}, bf16[448,576]{1,0:T(8,128)(2,1)}, u32[]{:S(2)}, u32[]{:S(2)}) collective-permute-start(bf16[448,576]{1,0:T(8,128)(2,1)S(1)} %collective-permute-done.1.refs_2_), channel_id=1, source_target_pairs={{0,128},{32,160},{64,192},{96,224},{128,0},{160,32},{192,64},{224,... | collective-permute-start | bytes 1548296 | tf_op jit(solution)/shard_map/ppermute | solution.py:26
  86.2 10.9 %collective-permute-start.16 = (bf16[2,56,896]{2,1,0:T(8,128)(2,1)}, bf16[2,56,896]{2,1,0:T(8,128)(2,1)}, u32[]{:S(2)}, u32[]{:S(2)}) collective-permute-start(bf16[2,56,896]{2,1,0:T(8,128)(2,1)} %pad_maximum_fusion.9), channel_id=1, source_target_pairs={{4,0},{5,1},{6,2},{7,3},{8,4},{9,5},{10,6},{11,7},{12,8},{13,9},{1... | collective-permute-start | bytes 602120 | tf_op jit(solution)/shard_map/ppermute | solution.py:31
  89.6 13.4 %collective-permute-start.17 = (bf16[2,56,896]{2,1,0:T(8,128)(2,1)}, bf16[2,56,896]{2,1,0:T(8,128)(2,1)}, u32[]{:S(2)}, u32[]{:S(2)}) collective-permute-start(bf16[2,56,896]{2,1,0:T(8,128)(2,1)} %pad_maximum_fusion.9), channel_id=1, source_target_pairs={{28,0},{29,1},{30,2},{31,3},{0,4},{1,5},{2,6},{3,7},{4,8},{5,9},{6... | collective-permute-start | bytes 602120 | tf_op jit(solution)/shard_map/ppermute | solution.py:31
  90.1 14.8 %collective-permute-start.18 = (bf16[2,56,896]{2,1,0:T(8,128)(2,1)}, bf16[2,56,896]{2,1,0:T(8,128)(2,1)}, u32[]{:S(2)}, u32[]{:S(2)}) collective-permute-start(bf16[2,56,896]{2,1,0:T(8,128)(2,1)} %pad_maximum_fusion.9), channel_id=1, source_target_pairs={{8,0},{9,1},{10,2},{11,3},{12,4},{13,5},{14,6},{15,7},{16,8},{17,9... | collective-permute-start | bytes 602120 | tf_op jit(solution)/shard_map/ppermute | solution.py:31
  91.2 13.8 %collective-permute-start.19 = (bf16[2,56,896]{2,1,0:T(8,128)(2,1)}, bf16[2,56,896]{2,1,0:T(8,128)(2,1)}, u32[]{:S(2)}, u32[]{:S(2)}) collective-permute-start(bf16[2,56,896]{2,1,0:T(8,128)(2,1)} %pad_maximum_fusion.9), channel_id=1, source_target_pairs={{24,0},{25,1},{26,2},{27,3},{28,4},{29,5},{30,6},{31,7},{0,8},{1,9... | collective-permute-start | bytes 602120 | tf_op jit(solution)/shard_map/ppermute | solution.py:31
  94.1 25.8 %copy-start = (bf16[448,576]{1,0:T(8,128)(2,1)S(1)}, bf16[448,576]{1,0:T(8,128)(2,1)}, u32[]{:S(2)}) copy-start(bf16[448,576]{1,0:T(8,128)(2,1)} %refs_1_.3) | copy-start | bytes 1548292
  104.9 11.7 %collective-permute-start.21 = (bf16[2,56,896]{2,1,0:T(8,128)(2,1)}, bf16[2,56,896]{2,1,0:T(8,128)(2,1)S(1)}, u32[]{:S(2)}, u32[]{:S(2)}) collective-permute-start(bf16[2,56,896]{2,1,0:T(8,128)(2,1)} %collective-permute-done.18), channel_id=1, source_target_pairs={{4,0},{5,1},{6,2},{7,3},{8,4},{9,5},{10,6},{11,7},{12,8},{13,9},{1... | collective-permute-start | bytes 602120 | tf_op jit(solution)/shard_map/ppermute | solution.py:31
  107.2 9.4 %collective-permute-start.22 = (bf16[2,56,896]{2,1,0:T(8,128)(2,1)}, bf16[2,56,896]{2,1,0:T(8,128)(2,1)S(1)}, u32[]{:S(2)}, u32[]{:S(2)}) collective-permute-start(bf16[2,56,896]{2,1,0:T(8,128)(2,1)} %collective-permute-done.19), channel_id=1, source_target_pairs={{28,0},{29,1},{30,2},{31,3},{0,4},{1,5},{2,6},{3,7},{4,8},{5,9},{6... | collective-permute-start | bytes 602120 | tf_op jit(solution)/shard_map/ppermute | solution.py:31
  109.4 7.7 %collective-permute-start.23 = (bf16[1,56,896]{2,1,0:T(8,128)(2,1)S(1)}, bf16[1,56,896]{2,1,0:T(8,128)(2,1)S(1)}, u32[]{:S(2)}, u32[]{:S(2)}) collective-permute-start(bf16[1,56,896]{2,1,0:T(8,128)(2,1)S(1)} %slice.121), channel_id=1, source_target_pairs={{8,0},{9,1},{10,2},{11,3},{12,4},{13,5},{14,6},{15,7},{16,8},{17,9... | collective-permute-start | bytes 301064 | tf_op jit(solution)/shard_map/ppermute | solution.py:31
  112.8 7.0 %collective-permute-start.24 = (bf16[1,56,896]{2,1,0:T(8,128)(2,1)S(1)}, bf16[1,56,896]{2,1,0:T(8,128)(2,1)S(1)}, u32[]{:S(2)}, u32[]{:S(2)}) collective-permute-start(bf16[1,56,896]{2,1,0:T(8,128)(2,1)S(1)} %slice.122), channel_id=1, source_target_pairs={{24,0},{25,1},{26,2},{27,3},{28,4},{29,5},{30,6},{31,7},{0,8},{1,9... | collective-permute-start | bytes 301064 | tf_op jit(solution)/shard_map/ppermute | solution.py:31
  119.8 3.5 %collective-permute-start.25 = (bf16[2,448,896]{2,1,0:T(8,128)(2,1)S(1)}, bf16[2,448,896]{2,1,0:T(8,128)(2,1)S(1)}, u32[]{:S(2)}, u32[]{:S(2)}) collective-permute-start(bf16[2,448,896]{2,1,0:T(8,128)(2,1)S(1)} %maximum_dynamic-update-slice_fusion.refs_0_), channel_id=1, source_target_pairs={{0,1},{1,0},{2,3},{3,2},{4,5},{5,4},{6,7},{7,6},{8,9},{9,8},{10,11... | collective-permute-start | bytes 4816904 | tf_op jit(solution)/shard_map/ppermute | solution.py:44
  125.7 15.8 %collective-permute-start.28 = (bf16[448,576]{1,0:T(8,128)(2,1)S(1)}, bf16[448,576]{1,0:T(8,128)(2,1)S(1)}, u32[]{:S(2)}, u32[]{:S(2)}) collective-permute-start(bf16[448,576]{1,0:T(8,128)(2,1)S(1)} %get-tuple-element.32), channel_id=1, source_target_pairs={{0,128},{32,160},{64,192},{96,224},{128,0},{160,32},{192,64},{224,... | collective-permute-start | bytes 1548296 | tf_op jit(solution)/shard_map/ppermute | solution.py:26
  127.1 16.7 %collective-permute-start.27 = (bf16[448,576]{1,0:T(8,128)(2,1)S(1)}, bf16[448,576]{1,0:T(8,128)(2,1)S(1)}, u32[]{:S(2)}, u32[]{:S(2)}) collective-permute-start(bf16[448,576]{1,0:T(8,128)(2,1)S(1)} %get-tuple-element.32), channel_id=1, source_target_pairs={{96,0},{0,32},{32,64},{64,96},{224,128},{128,160},{160,192},{192,2... | collective-permute-start | bytes 1548296 | tf_op jit(solution)/shard_map/ppermute | solution.py:22
  127.1 16.7 %collective-permute-start.26 = (bf16[448,576]{1,0:T(8,128)(2,1)S(1)}, bf16[448,576]{1,0:T(8,128)(2,1)S(1)}, u32[]{:S(2)}, u32[]{:S(2)}) collective-permute-start(bf16[448,576]{1,0:T(8,128)(2,1)S(1)} %get-tuple-element.32), channel_id=1, source_target_pairs={{32,0},{64,32},{96,64},{0,96},{160,128},{192,160},{224,192},{128,2... | collective-permute-start | bytes 1548296 | tf_op jit(solution)/shard_map/ppermute | solution.py:22
  144.1 14.9 %collective-permute-start.29 = (bf16[448,576]{1,0:T(8,128)(2,1)S(1)}, bf16[448,576]{1,0:T(8,128)(2,1)S(1)}, u32[]{:S(2)}, u32[]{:S(2)}) collective-permute-start(bf16[448,576]{1,0:T(8,128)(2,1)S(1)} %get-tuple-element.70), channel_id=1, source_target_pairs={{32,0},{64,32},{96,64},{0,96},{160,128},{192,160},{224,192},{128,2... | collective-permute-start | bytes 1548296 | tf_op jit(solution)/shard_map/ppermute | solution.py:22
  147.2 15.4 %collective-permute-start.30 = (bf16[448,576]{1,0:T(8,128)(2,1)S(1)}, bf16[448,576]{1,0:T(8,128)(2,1)S(1)}, u32[]{:S(2)}, u32[]{:S(2)}) collective-permute-start(bf16[448,576]{1,0:T(8,128)(2,1)S(1)} %get-tuple-element.71), channel_id=1, source_target_pairs={{96,0},{0,32},{32,64},{64,96},{224,128},{128,160},{160,192},{192,2... | collective-permute-start | bytes 1548296 | tf_op jit(solution)/shard_map/ppermute | solution.py:22
  147.4 15.3 %collective-permute-start.31 = (bf16[448,576]{1,0:T(8,128)(2,1)S(1)}, bf16[448,576]{1,0:T(8,128)(2,1)S(1)}, u32[]{:S(2)}, u32[]{:S(2)}) collective-permute-start(bf16[448,576]{1,0:T(8,128)(2,1)S(1)} %get-tuple-element.69), channel_id=1, source_target_pairs={{0,128},{32,160},{64,192},{96,224},{128,0},{160,32},{192,64},{224,... | collective-permute-start | bytes 1548296 | tf_op jit(solution)/shard_map/ppermute | solution.py:26
  162.8 5.9 %collective-permute-start.33 = (bf16[144,576]{1,0:T(8,128)(2,1)S(1)}, bf16[144,576]{1,0:T(8,128)(2,1)S(1)}, u32[]{:S(2)}, u32[]{:S(2)}) collective-permute-start(bf16[144,576]{1,0:T(8,128)(2,1)S(1)} %pad_maximum_fusion.10), channel_id=1, source_target_pairs={{32,0},{64,32},{96,64},{0,96},{160,128},{192,160},{224,192},{128,2... | collective-permute-start | bytes 497672 | tf_op jit(solution)/shard_map/ppermute | solution.py:22
  164.8 7.0 %collective-permute-start.34 = (bf16[160,576]{1,0:T(8,128)(2,1)S(1)}, bf16[160,576]{1,0:T(8,128)(2,1)S(1)}, u32[]{:S(2)}, u32[]{:S(2)}) collective-permute-start(bf16[160,576]{1,0:T(8,128)(2,1)S(1)} %slice.168), channel_id=1, source_target_pairs={{96,0},{0,32},{32,64},{64,96},{224,128},{128,160},{160,192},{192,2... | collective-permute-start | bytes 552968 | tf_op jit(solution)/shard_map/ppermute | solution.py:22
  165.1 5.6 %collective-permute-start.32 = (bf16[144,576]{1,0:T(8,128)(2,1)S(1)}, bf16[144,576]{1,0:T(8,128)(2,1)S(1)}, u32[]{:S(2)}, u32[]{:S(2)}) collective-permute-start(bf16[144,576]{1,0:T(8,128)(2,1)S(1)} %slice.167), channel_id=1, source_target_pairs={{0,128},{32,160},{64,192},{96,224},{128,0},{160,32},{192,64},{224,... | collective-permute-start | bytes 497672 | tf_op jit(solution)/shard_map/ppermute | solution.py:26

commit v2 on v1

--- a/solution.py
+++ b/solution.py
@@ -58,24 +58,6 @@
 
 def gather_first(own):
     return from_x(own, 1), from_x(own, -1), from_y(own)
-
-
-def gather_second(right, left, across):
-    half = right.shape[0] // 16 * 8
-    via_y = from_y(cat(right[:half], left[:half]))
-    via_right = from_x(cat(across[half:], right[:half]), 1)
-    via_left = from_x(cat(across[half:], left[half:]), -1)
-    rest = right.shape[0] - half
-    far = cat(via_right[rest:], via_left[rest:])
-    return far, cat(via_y[:half], via_right[:rest]), cat(via_y[half:], via_left[:rest])
-
-
-def gather_third(far, across_right, across_left):
-    third = far.shape[0] // 24 * 8
-    part_y = from_y(far[:third])
-    part_right = from_x(across_right[third : 2 * third], 1)
-    part_left = from_x(across_left[2 * third :], -1)
-    return cat(part_y, part_right, part_left)
 
 
 def along_z(value, hops):
@@ -133,7 +115,7 @@
             pltpu.VMEM((4 * rows, cols), bf16),
             pltpu.SemaphoreType.DMA((5,)),
         ],
-        compiler_params=pltpu.CompilerParams(vmem_limit_bytes=16 * 2**20),
+        compiler_params=pltpu.CompilerParams(vmem_limit_bytes=9 * 2**20),
         cost_estimate=pl.CostEstimate(flops=8 * rows * rows * cols, bytes_accessed=6 * 2**20, transcendentals=0),
     )(block, *x_blocks, *([] if mine else [before]))
 
@@ -169,12 +151,13 @@
         return summed[start * unit : stop * unit]
 
     passed = along_z(units(1, 3).astype(bf16), 1).astype(f32) + jnp.pad(along_z(units(0, 1).astype(bf16), 2).astype(f32), ((0, unit), (0, 0)))
-    two, one, other_left = lax.optimization_barrier(
-        ((units(3, 5) + passed).astype(bf16), units(5, 7).astype(bf16), from_y(left))
+    two, one, late_across, late_far = lax.optimization_barrier(
+        ((units(3, 5) + passed).astype(bf16), units(5, 7).astype(bf16), across, far)
     )
     passed = along_z(two, 2).astype(f32) + along_z(one, 1).astype(f32)
     total = passed + jnp.pad(units(7, 8), ((unit, 0), (0, 0)))
-    total, other_far = lax.optimization_barrier((total, from_y(far)))
+    others = (from_x(late_across, 1), from_x(late_across, -1), from_y(late_far))
+    total, other_right, other_left, other_far = lax.optimization_barrier((total, *others))
 
     width = 2 * rows
     total = jnp.where(core == 0, total, cat(total[unit:], total[:unit])).reshape(2, unit, 2 * width)
@@ -185,10 +168,8 @@
     gram_other = from_y(total[1]).astype(f32) + from_y_both(total[1]).astype(f32)
     gram = jnp.stack([gram_same, gram_other]).astype(bf16)
 
-    gram, right = lax.optimization_barrier((gram, right))
     up1, down1 = from_z(gram, 1), from_z(gram, -1)
     up2, down2 = from_z(gram, 2), from_z(gram, -2)
-    up1, down1, up2, down2, other_right = lax.optimization_barrier((up1, down1, up2, down2, from_y(right)))
     up3, down3 = from_z(up2, 1), from_z(down2, -1)
     up4, down4 = from_z(up2[:1], 2), from_z(down2[1:], -2)
     block = jnp.zeros((2, rows, width), bf16)
@@ -203,14 +184,21 @@
     x_blocks = (own, x_right, x_left, x_far, across, other_right, other_left, other_far)
     found, sent = found_part(got, x_blocks, found_part(block, x_blocks))
     right, left, across = gather_first(sent)
-    far, across_right, across_left = gather_second(right, left, across)
-    across_far = gather_third(far, across_right, across_left)
-    three, seven = 3 * rows, 7 * rows
-    product = dot(gram_rows[:, :three], cat(sent, right, left))
-    product = product + dot(gram_rows[:, three:seven], cat(far, across, across_right, across_left))
+    half, few = rows // 2, rows // 48 * 8
+    via_y = from_y(cat(right[few:], left[few:]))
+    via_right = from_x(cat(right[:half], across[:few]), 1)
+    via_left = from_x(cat(left[half:], across[:few]), -1)
+    across_far = from_x(across, 2)
+    far = cat(via_right[:half], via_left[:half])
+    across_right = cat(via_right[half:], via_y[: rows - few])
+    across_left = cat(via_left[half:], via_y[rows - few :])
+
+    three, four, five = 3 * rows, 4 * rows, 5 * rows
+    product = dot(gram_rows[:, :three], cat(sent, right, left)) + dot(gram_rows[:, four:five], across)
     start = coef_a * own.astype(f32) + coef_b * found + coef_c * product
     scale = float(COLS) ** 0.5
-    return (scale * (start + coef_c * dot(gram_rows[:, seven:], across_far))).astype(bf16)
+    last = dot(gram_rows[:, three:four], far) + dot(gram_rows[:, five:], cat(across_right, across_left, across_far))
+    return (scale * (start + coef_c * last)).astype(bf16)
 
 
 def solution(mesh):

time: 174 us -> 176 us (1.011)
  local copies, waits for them, and re-layouts: 13.1 us -> 23.6 us
  waiting for transfers between devices: 95.8 us -> 86.7 us
  starting transfers between devices: 46.2 us -> 40.3 us
  matrix products: 7.25 us -> 12.5 us
    unnamed x21 -> x61, local copies, waits for them, and re-layouts: 2.74 us -> 9.9 us
    ppermute x8 -> x5, waiting for transfers between devices: 16.5 us -> 10.6 us  [from_y(): return lax.ppermute(value, 'wide', [(w, (w + 4) % 8) for w in range(8)])]
    dot_general x3 -> x4, matrix products: 4.25 us -> 9.49 us  [dot(): return jnp.dot(left, right, preferred_element_type=f32)]
    ppermute x10 -> x11, waiting for transfers between devices: 36.3 us -> 32.3 us  [from_x(): return lax.ppermute(value, 'wide', pairs)]
    concatenate x4 -> x5, local copies, waits for them, and re-layouts: 0.22 us -> 3.82 us  [cat(): return jnp.concatenate(parts, axis=axis)]
    ppermute x8, waiting for transfers between devices: 13.9 us -> 10.7 us  [from_z(): return lax.ppermute(value, 'narrow', pairs)]
    ppermute x4, waiting for transfers between devices: 20.7 us -> 23.5 us  [along_z(): return lax.ppermute(value, 'narrow', pairs)]
    ppermute x8 -> x5, starting transfers between devices: 5.98 us -> 3.3 us  [from_y(): return lax.ppermute(value, 'wide', [(w, (w + 4) % 8) for w in range(8)])]
  transfers between devices with their start and end apart: 35 -> 33, of which waited for: 23 -> 17; matrix products, arithmetic and copies ran while one was open for 10% -> 15% of each run, Pallas kernels for 2% -> 1%
where the time goes in v2:
time: 176 us; the launch traced here: 175 us
  waiting for transfers between devices  86.7 us (49%)
  starting transfers between devices  40.3 us (23%)
  local copies, waits for them, and re-layouts  23.6 us (13%)
  matrix products  12.5 us (7%)
  other arithmetic  5.84 us (3%)
  Pallas kernels  5.22 us (3%)
    ppermute x11, waiting for transfers between devices, from_x(): return lax.ppermute(value, 'wide', pairs)  32.3 us
    ppermute x4, waiting for transfers between devices, along_z(): return lax.ppermute(value, 'narrow', pairs)  23.5 us
    ppermute x11, starting transfers between devices, from_x(): return lax.ppermute(value, 'wide', pairs)  13.8 us
    ppermute x8, starting transfers between devices, from_z(): return lax.ppermute(value, 'narrow', pairs)  12 us
    ppermute x8, waiting for transfers between devices, from_z(): return lax.ppermute(value, 'narrow', pairs)  10.7 us
    ppermute x5, waiting for transfers between devices, from_y(): return lax.ppermute(value, 'wide', [(w, (w + 4) % 8) for w in range(8)])  10.6 us
    unnamed x61, local copies, waits for them, and re-layouts  9.9 us
    dot_general x4, matrix products, dot(): return jnp.dot(left, right, preferred_element_type=f32)  9.49 us
  transfers between devices with their start and end apart: 33, of which 17 were waited for; matrix products, arithmetic and copies ran while one was open for 15% of the time, Pallas kernels for 1%

profile of v2, /device:TPU:24, one launch (start us, length us, event | category | flops | bytes accessed | tf_op | source)
XLA Modules:
  0.0 174.7 jit_solution(896475917018483867)
XLA Ops:
  0.0 2.8 %collective-permute-start.1 = (bf16[448,576]{1,0:T(8,128)(2,1)}, bf16[448,576]{1,0:T(8,128)(2,1)S(1)}, u32[]{:S(2)}, u32[]{:S(2)}) collective-permute-start(bf16[448,576]{1,0:T(8,128)(2,1)} %refs_1_.3), channel_id=1, source_target_pairs={{32,0},{64,32},{96,64},{0,96},{160,128},{192,160},{224,192},{128,2... | collective-permute-start | bytes 1548296 | tf_op jit(solution)/shard_map/ppermute | solution.py:22
  3.5 1.2 constant_dynamic-update-slice_fusion.6
  4.7 10.6 %collective-permute-done.1.refs_2_ = bf16[448,576]{1,0:T(8,128)(2,1)S(1)} collective-permute-done((bf16[448,576]{1,0:T(8,128)(2,1)}, bf16[448,576]{1,0:T(8,128)(2,1)S(1)}, u32[]{:S(2)}, u32[]{:S(2)}) %collective-permute-start.1) | collective-permute-done | bytes 516128 | tf_op jit(solution)/shard_map/ppermute | solution.py:22
  15.3 3.7 %collective-permute-start.3 = (bf16[224,576]{1,0:T(8,128)(2,1)S(1)}, bf16[224,576]{1,0:T(8,128)(2,1)S(1)}, u32[]{:S(2)}, u32[]{:S(2)}) collective-permute-start(bf16[224,576]{1,0:T(8,128)(2,1)S(1)} %slice.136), channel_id=1, source_target_pairs={{32,0},{64,32},{96,64},{0,96},{160,128},{192,160},{224,192},{128,2... | collective-permute-start | bytes 774152 | tf_op jit(solution)/shard_map/ppermute | solution.py:22
  19.7 4.5 %collective-permute-done.3 = bf16[224,576]{1,0:T(8,128)(2,1)S(1)} collective-permute-done((bf16[224,576]{1,0:T(8,128)(2,1)S(1)}, bf16[224,576]{1,0:T(8,128)(2,1)S(1)}, u32[]{:S(2)}, u32[]{:S(2)}) %collective-permute-start.3) | collective-permute-done | bytes 258080 | tf_op jit(solution)/shard_map/ppermute | solution.py:22
  24.3 3.5 %collective-permute-done.4 = bf16[224,576]{1,0:T(8,128)(2,1)S(1)} collective-permute-done((bf16[224,576]{1,0:T(8,128)(2,1)S(1)}, bf16[224,576]{1,0:T(8,128)(2,1)S(1)}, u32[]{:S(2)}, u32[]{:S(2)}) %collective-permute-start.4) | collective-permute-done | bytes 258080 | tf_op jit(solution)/shard_map/ppermute | solution.py:22
  27.8 1.5 convolution_convert_fusion
  29.4 1.5 fusion.35
  30.9 1.9 %collective-permute-done.5 = bf16[448,1792]{1,0:T(8,128)(2,1)S(1)} collective-permute-done((bf16[448,1792]{1,0:T(8,128)(2,1)S(1)}, bf16[448,1792]{1,0:T(8,128)(2,1)S(1)}, u32[]{:S(2)}, u32[]{:S(2)}) %collective-permute-start.5) | collective-permute-done | bytes 1605664 | tf_op jit(solution)/shard_map/ppermute | solution.py:44
  34.1 1.9 %collective-permute-start.6 = (bf16[112,1792]{1,0:T(8,128)(2,1)S(1)}, bf16[112,1792]{1,0:T(8,128)(2,1)S(1)}, u32[]{:S(2)}, u32[]{:S(2)}) collective-permute-start(bf16[112,1792]{1,0:T(8,128)(2,1)S(1)} %get-tuple-element.34), channel_id=1, source_target_pairs={{0,4},{1,29},{2,6},{3,31},{4,8},{5,1},{6,10},{7,3},{8,12},{9,5},{1... | collective-permute-start | bytes 1204232 | tf_op jit(solution)/shard_map/ppermute | solution.py:65
  36.1 3.3 %collective-permute-start.7 = (bf16[56,1792]{1,0:T(8,128)(2,1)S(1)}, bf16[56,1792]{1,0:T(8,128)(2,1)S(1)}, u32[]{:S(2)}, u32[]{:S(2)}) collective-permute-start(bf16[56,1792]{1,0:T(8,128)(2,1)S(1)} %slice.140), channel_id=1, source_target_pairs={{0,8},{1,25},{2,10},{3,27},{4,12},{5,29},{6,14},{7,31},{8,16},{9,1... | collective-permute-start | bytes 602120 | tf_op jit(solution)/shard_map/ppermute | solution.py:65
  39.4 10.6 %collective-permute-done.7 = bf16[56,1792]{1,0:T(8,128)(2,1)S(1)} collective-permute-done((bf16[56,1792]{1,0:T(8,128)(2,1)S(1)}, bf16[56,1792]{1,0:T(8,128)(2,1)S(1)}, u32[]{:S(2)}, u32[]{:S(2)}) %collective-permute-start.7) | collective-permute-done | bytes 200736 | tf_op jit(solution)/shard_map/ppermute | solution.py:65
  50.9 1.6 collective-permute-start.9
  53.3 1.8 %collective-permute-start.11 = (bf16[448,576]{1,0:T(8,128)(2,1)S(1)}, bf16[448,576]{1,0:T(8,128)(2,1)S(1)}, u32[]{:S(2)}, u32[]{:S(2)}) collective-permute-start(bf16[448,576]{1,0:T(8,128)(2,1)S(1)} %collective-permute-done.refs_5_), channel_id=1, source_target_pairs={{96,0},{0,32},{32,64},{64,96},{224,128},{128,160},{160,192},{192,2... | collective-permute-start | bytes 1548296 | tf_op jit(solution)/shard_map/ppermute | solution.py:22
  56.8 3.4 %collective-permute-done.9 = bf16[112,1792]{1,0:T(8,128)(2,1)} collective-permute-done((bf16[112,1792]{1,0:T(8,128)(2,1)}, bf16[112,1792]{1,0:T(8,128)(2,1)}, u32[]{:S(2)}, u32[]{:S(2)}) %collective-permute-start.9) | collective-permute-done | bytes 401440 | tf_op jit(solution)/shard_map/ppermute | solution.py:65
  60.3 9.5 %collective-permute-done.8 = bf16[112,1792]{1,0:T(8,128)(2,1)} collective-permute-done((bf16[112,1792]{1,0:T(8,128)(2,1)}, bf16[112,1792]{1,0:T(8,128)(2,1)}, u32[]{:S(2)}, u32[]{:S(2)}) %collective-permute-start.8) | collective-permute-done | bytes 401440 | tf_op jit(solution)/shard_map/ppermute | solution.py:65
  69.7 1.2 pad_add_fusion
  73.1 1.4 collective-permute-done.13
  74.5 1.0 add_convert_fusion
  75.6 1.3 collective-permute-start.14
  76.9 2.2 %collective-permute-start.16 = (bf16[56,896]{1,0:T(8,128)(2,1)S(1)}, bf16[56,896]{1,0:T(8,128)(2,1)S(1)}, u32[]{:S(2)}, u32[]{:S(2)}) collective-permute-start(bf16[56,896]{1,0:T(8,128)(2,1)S(1)} %get-tuple-element.64), channel_id=1, source_target_pairs={{0,130},{1,131},{2,128},{3,129},{4,134},{5,135},{6,132},{7,133},{8... | collective-permute-start | bytes 301064 | tf_op jit(solution)/shard_map/ppermute | solution.py:40
  79.1 3.2 %collective-permute-done.14 = bf16[56,896]{1,0:T(8,128)(2,1)S(1)} collective-permute-done((bf16[56,896]{1,0:T(8,128)(2,1)S(1)}, bf16[56,896]{1,0:T(8,128)(2,1)S(1)}, u32[]{:S(2)}, u32[]{:S(2)}) %collective-permute-start.14) | collective-permute-done | bytes 100384 | tf_op jit(solution)/shard_map/ppermute | solution.py:35
  82.4 1.8 %collective-permute-done.16 = bf16[56,896]{1,0:T(8,128)(2,1)S(1)} collective-permute-done((bf16[56,896]{1,0:T(8,128)(2,1)S(1)}, bf16[56,896]{1,0:T(8,128)(2,1)S(1)}, u32[]{:S(2)}, u32[]{:S(2)}) %collective-permute-start.16) | collective-permute-done | bytes 100384 | tf_op jit(solution)/shard_map/ppermute | solution.py:40
  85.5 3.7 %collective-permute-start.19 = (bf16[2,56,896]{2,1,0:T(8,128)(2,1)}, bf16[2,56,896]{2,1,0:T(8,128)(2,1)}, u32[]{:S(2)}, u32[]{:S(2)}) collective-permute-start(bf16[2,56,896]{2,1,0:T(8,128)(2,1)} %get-tuple-element.61), channel_id=1, source_target_pairs={{8,0},{9,1},{10,2},{11,3},{12,4},{13,5},{14,6},{15,7},{16,8},{17,9... | collective-permute-start | bytes 602120 | tf_op jit(solution)/shard_map/ppermute | solution.py:31
  89.2 2.0 %collective-permute-start.18 = (bf16[2,56,896]{2,1,0:T(8,128)(2,1)}, bf16[2,56,896]{2,1,0:T(8,128)(2,1)}, u32[]{:S(2)}, u32[]{:S(2)}) collective-permute-start(bf16[2,56,896]{2,1,0:T(8,128)(2,1)} %get-tuple-element.61), channel_id=1, source_target_pairs={{28,0},{29,1},{30,2},{31,3},{0,4},{1,5},{2,6},{3,7},{4,8},{5,9},{6... | collective-permute-start | bytes 602120 | tf_op jit(solution)/shard_map/ppermute | solution.py:31
  91.3 6.0 %collective-permute-done.20 = bf16[2,56,896]{2,1,0:T(8,128)(2,1)S(1)} collective-permute-done((bf16[2,56,896]{2,1,0:T(8,128)(2,1)}, bf16[2,56,896]{2,1,0:T(8,128)(2,1)S(1)}, u32[]{:S(2)}, u32[]{:S(2)}) %collective-permute-start.20) | collective-permute-done | bytes 200736 | tf_op jit(solution)/shard_map/ppermute | solution.py:31
  97.4 1.3 collective-permute-done.19
  99.6 3.7 %collective-permute-start.23 = (bf16[1,56,896]{2,1,0:T(8,128)(2,1)S(1)}, bf16[1,56,896]{2,1,0:T(8,128)(2,1)S(1)}, u32[]{:S(2)}, u32[]{:S(2)}) collective-permute-start(bf16[1,56,896]{2,1,0:T(8,128)(2,1)S(1)} %slice.145), channel_id=1, source_target_pairs={{8,0},{9,1},{10,2},{11,3},{12,4},{13,5},{14,6},{15,7},{16,8},{17,9... | collective-permute-start | bytes 301064 | tf_op jit(solution)/shard_map/ppermute | solution.py:31
  103.9 1.4 collective-permute-start.22
  108.2 3.4 %collective-permute-done.21 = bf16[2,56,896]{2,1,0:T(8,128)(2,1)S(1)} collective-permute-done((bf16[2,56,896]{2,1,0:T(8,128)(2,1)}, bf16[2,56,896]{2,1,0:T(8,128)(2,1)S(1)}, u32[]{:S(2)}, u32[]{:S(2)}) %collective-permute-start.21) | collective-permute-done | bytes 200736 | tf_op jit(solution)/shard_map/ppermute | solution.py:31
  111.9 2.1 %shard_map.17.refs_9_ = f32[448,576]{1,0:T(8,128)S(1)} custom-call(bf16[2,448,896]{2,1,0:T(8,128)(2,1)S(1)} %maximum_dynamic-update-slice_fusion.refs_0_, bf16[448,576]{1,0:T(8,128)(2,1)S(1)} %copy-done, bf16[448,576]{1,0:T(8,128)(2,1)S(1)} %collective-permute-done.1.refs_2_, bf16[448,576]{1,0:T(8,128)(2,1)S(1)} %collective-permute-done.2.refs_3_, ...), custom_call_target="tpu_custom_call" | custom-call | flops 924844032 | bytes 6291456 | tf_op jit(solution)/shard_map/pallas_call | solution.py:108
  114.1 1.2 collective-permute-done.25.refs_0_
  115.3 3.1 %shard_map.18 = (f32[448,576]{1,0:T(8,128)S(1)}, bf16[448,576]{1,0:T(8,128)(2,1)S(1)}) custom-call(bf16[2,448,896]{2,1,0:T(8,128)(2,1)S(1)} %collective-permute-done.25.refs_0_, bf16[448,576]{1,0:T(8,128)(2,1)S(1)} %copy-done, bf16[448,576]{1,0:T(8,128)(2,1)S(1)} %collective-permute-done.1.refs_2_, bf16[448,576]{1,0:T(8,128)(2,1)S(1)} %collective-permute-done.2.refs_3_, ...), custom_call_target="tpu_custom_call" | custom-call | flops 924844032 | bytes 6291456 | tf_op jit(solution)/shard_map/pallas_call | solution.py:108
  120.3 1.2 collective-permute-start.27
  121.7 1.5 slice_bitcast_fusion
  123.2 10.5 %collective-permute-done.28 = bf16[448,576]{1,0:T(8,128)(2,1)S(1)} collective-permute-done((bf16[448,576]{1,0:T(8,128)(2,1)S(1)}, bf16[448,576]{1,0:T(8,128)(2,1)S(1)}, u32[]{:S(2)}, u32[]{:S(2)}) %collective-permute-start.28) | collective-permute-done | bytes 516128 | tf_op jit(solution)/shard_map/ppermute | solution.py:26
  133.8 1.7 collective-permute-done.27
  136.6 3.2 %collective-permute-start.29 = (bf16[296,576]{1,0:T(8,128)(2,1)}, bf16[296,576]{1,0:T(8,128)(2,1)}, u32[]{:S(2)}, u32[]{:S(2)}) collective-permute-start(bf16[296,576]{1,0:T(8,128)(2,1)} %get-tuple-element.65), channel_id=1, source_target_pairs={{32,0},{64,32},{96,64},{0,96},{160,128},{192,160},{224,192},{128,2... | collective-permute-start | bytes 1022984 | tf_op jit(solution)/shard_map/ppermute | solution.py:22
  140.1 1.7 copy.2
  141.8 1.7 collective-permute-start.31
  143.6 1.6 fusion.24
  145.2 2.2 %fusion.9 = f32[448,576]{1,0:T(8,128)} fusion(f32[448,576]{1,0:T(8,128)S(1)} %fusion.24, bf16[448,576]{1,0:T(8,128)(2,1)S(1)} %copy-done.18, bf16[448,576]{1,0:T(8,128)(2,1)S(1)} %copy-done.16, bf16[448,576]{1,0:T(8,128)(2,1)S(1)} %copy-done.11, bf16[448,896]{1,0:T(8,128)(2,1)S(1)} %get-tuple-element.32, bf16[448,896]{1,0:T(8,128)(2,1)S(1)} %copy-done.20), kind=kOutput, calls=%fused_computation.11 | convolution fusion | flops 701202432 | bytes 5218304 | tf_op jit(solution)/shard_map/dot_general | solution.py:52
  147.5 12.0 %collective-permute-done.30 = bf16[296,576]{1,0:T(8,128)(2,1)} collective-permute-done((bf16[296,576]{1,0:T(8,128)(2,1)}, bf16[296,576]{1,0:T(8,128)(2,1)}, u32[]{:S(2)}, u32[]{:S(2)}) %collective-permute-start.30) | collective-permute-done | bytes 341024 | tf_op jit(solution)/shard_map/ppermute | solution.py:22
  161.4 1.5 slice_dynamic-update-slice_fusion.1
  162.9 1.6 fusion.19
  166.2 1.7 slice_dynamic-update-slice_fusion
  168.8 1.9 %constant_dynamic-update-slice_fusion.9 = bf16[1344,576]{1,0:T(8,128)(2,1)} fusion(bf16[1344,576]{1,0:T(8,128)(2,1)} %constant_dynamic-update-slice_fusion.10, bf16[448,576]{1,0:T(8,128)(2,1)} %collective-permute-done.32), kind=kLoop, calls=%fused_computation.76 | loop fusion | bytes 1146880 | tf_op jit(solution)/shard_map/concatenate | solution.py:56
  170.7 4.0 %fusion.15 = bf16[448,576]{1,0:T(8,128)(2,1)} fusion(f32[448,576]{1,0:T(8,128)S(1)} %copy-done.14, bf16[1344,576]{1,0:T(8,128)(2,1)} %constant_dynamic-update-slice_fusion.9, bf16[448,896]{1,0:T(8,128)(2,1)S(1)} %copy-done.19, bf16[448,896]{1,0:T(8,128)(2,1)S(1)} %get-tuple-element.67, f32[448,576]{1,0:T(8,128)} %fusion.9, f32[448,576]{1,0:T(8,128)S(1)} %copy-done.9, ...), kind=kOutput, calls=%fused_computation.16 | convolution fusion | flops 698621952 | bytes 7282688 | tf_op jit(solution)/shard_map/dot_general | solution.py:52
  (130 shorter events, 22.5 us)
Async XLA Ops:
  0.0 15.3 %collective-permute-start.1 = (bf16[448,576]{1,0:T(8,128)(2,1)}, bf16[448,576]{1,0:T(8,128)(2,1)S(1)}, u32[]{:S(2)}, u32[]{:S(2)}) collective-permute-start(bf16[448,576]{1,0:T(8,128)(2,1)} %refs_1_.3), channel_id=1, source_target_pairs={{32,0},{64,32},{96,64},{0,96},{160,128},{192,160},{224,192},{128,2... | collective-permute-start | bytes 1548296 | tf_op jit(solution)/shard_map/ppermute | solution.py:22
  2.8 16.2 %collective-permute-start.2 = (bf16[448,576]{1,0:T(8,128)(2,1)}, bf16[448,576]{1,0:T(8,128)(2,1)S(1)}, u32[]{:S(2)}, u32[]{:S(2)}) collective-permute-start(bf16[448,576]{1,0:T(8,128)(2,1)} %refs_1_.3), channel_id=1, source_target_pairs={{96,0},{0,32},{32,64},{64,96},{224,128},{128,160},{160,192},{192,2... | collective-permute-start | bytes 1548296 | tf_op jit(solution)/shard_map/ppermute | solution.py:22
  2.8 16.4 %collective-permute-start = (bf16[448,576]{1,0:T(8,128)(2,1)}, bf16[448,576]{1,0:T(8,128)(2,1)S(1)}, u32[]{:S(2)}, u32[]{:S(2)}) collective-permute-start(bf16[448,576]{1,0:T(8,128)(2,1)} %refs_1_.3), channel_id=1, source_target_pairs={{0,128},{32,160},{64,192},{96,224},{128,0},{160,32},{192,64},{224,... | collective-permute-start | bytes 1548296 | tf_op jit(solution)/shard_map/ppermute | solution.py:26
  15.3 8.9 %collective-permute-start.3 = (bf16[224,576]{1,0:T(8,128)(2,1)S(1)}, bf16[224,576]{1,0:T(8,128)(2,1)S(1)}, u32[]{:S(2)}, u32[]{:S(2)}) collective-permute-start(bf16[224,576]{1,0:T(8,128)(2,1)S(1)} %slice.136), channel_id=1, source_target_pairs={{32,0},{64,32},{96,64},{0,96},{160,128},{192,160},{224,192},{128,2... | collective-permute-start | bytes 774152 | tf_op jit(solution)/shard_map/ppermute | solution.py:22
  19.0 8.7 %collective-permute-start.4 = (bf16[224,576]{1,0:T(8,128)(2,1)S(1)}, bf16[224,576]{1,0:T(8,128)(2,1)S(1)}, u32[]{:S(2)}, u32[]{:S(2)}) collective-permute-start(bf16[224,576]{1,0:T(8,128)(2,1)S(1)} %slice.137), channel_id=1, source_target_pairs={{96,0},{0,32},{32,64},{64,96},{224,128},{128,160},{160,192},{192,2... | collective-permute-start | bytes 774152 | tf_op jit(solution)/shard_map/ppermute | solution.py:22
  27.8 27.2 %copy-start.2 = (bf16[448,576]{1,0:T(8,128)(2,1)}, bf16[448,576]{1,0:T(8,128)(2,1)S(1)}, u32[]{:S(2)}) copy-start(bf16[448,576]{1,0:T(8,128)(2,1)S(1)} %get-tuple-element.18.refs_4_) | copy-start | bytes 1548292
  29.3 3.5 %collective-permute-start.5 = (bf16[448,1792]{1,0:T(8,128)(2,1)S(1)}, bf16[448,1792]{1,0:T(8,128)(2,1)S(1)}, u32[]{:S(2)}, u32[]{:S(2)}) collective-permute-start(bf16[448,1792]{1,0:T(8,128)(2,1)S(1)} %convolution_convert_fusion), channel_id=1, source_target_pairs={{0,1},{1,0},{2,3},{3,2},{4,5},{5,4},{6,7},{7,6},{8,9},{9,8},{10,11... | collective-permute-start | bytes 4816904 | tf_op jit(solution)/shard_map/ppermute | solution.py:44
  33.2 17.6 %copy-start.12 = (f32[448,1792]{1,0:T(8,128)}, f32[448,1792]{1,0:T(8,128)S(1)}, u32[]{:S(2)}) copy-start(f32[448,1792]{1,0:T(8,128)S(1)} %get-tuple-element.26) | copy-start | bytes 9633796
  34.1 15.9 %collective-permute-start.6 = (bf16[112,1792]{1,0:T(8,128)(2,1)S(1)}, bf16[112,1792]{1,0:T(8,128)(2,1)S(1)}, u32[]{:S(2)}, u32[]{:S(2)}) collective-permute-start(bf16[112,1792]{1,0:T(8,128)(2,1)S(1)} %get-tuple-element.34), channel_id=1, source_target_pairs={{0,4},{1,29},{2,6},{3,31},{4,8},{5,1},{6,10},{7,3},{8,12},{9,5},{1... | collective-permute-start | bytes 1204232 | tf_op jit(solution)/shard_map/ppermute | solution.py:65
  36.1 13.9 %collective-permute-start.7 = (bf16[56,1792]{1,0:T(8,128)(2,1)S(1)}, bf16[56,1792]{1,0:T(8,128)(2,1)S(1)}, u32[]{:S(2)}, u32[]{:S(2)}) collective-permute-start(bf16[56,1792]{1,0:T(8,128)(2,1)S(1)} %slice.140), channel_id=1, source_target_pairs={{0,8},{1,25},{2,10},{3,27},{4,12},{5,29},{6,14},{7,31},{8,16},{9,1... | collective-permute-start | bytes 602120 | tf_op jit(solution)/shard_map/ppermute | solution.py:65
  50.9 9.4 %collective-permute-start.9 = (bf16[112,1792]{1,0:T(8,128)(2,1)}, bf16[112,1792]{1,0:T(8,128)(2,1)}, u32[]{:S(2)}, u32[]{:S(2)}) collective-permute-start(bf16[112,1792]{1,0:T(8,128)(2,1)} %get-tuple-element.16), channel_id=1, source_target_pairs={{0,4},{1,29},{2,6},{3,31},{4,8},{5,1},{6,10},{7,3},{8,12},{9,5},{1... | collective-permute-start | bytes 1204232 | tf_op jit(solution)/shard_map/ppermute | solution.py:65
  52.5 17.3 %collective-permute-start.8 = (bf16[112,1792]{1,0:T(8,128)(2,1)}, bf16[112,1792]{1,0:T(8,128)(2,1)}, u32[]{:S(2)}, u32[]{:S(2)}) collective-permute-start(bf16[112,1792]{1,0:T(8,128)(2,1)} %fusion.18), channel_id=1, source_target_pairs={{0,8},{1,25},{2,10},{3,27},{4,12},{5,29},{6,14},{7,31},{8,16},{9,1... | collective-permute-start | bytes 1204232 | tf_op jit(solution)/shard_map/ppermute | solution.py:65
  53.0 17.9 %collective-permute-start.10 = (bf16[448,576]{1,0:T(8,128)(2,1)S(1)}, bf16[448,576]{1,0:T(8,128)(2,1)S(1)}, u32[]{:S(2)}, u32[]{:S(2)}) collective-permute-start(bf16[448,576]{1,0:T(8,128)(2,1)S(1)} %collective-permute-done.refs_5_), channel_id=1, source_target_pairs={{32,0},{64,32},{96,64},{0,96},{160,128},{192,160},{224,192},{128,2... | collective-permute-start | bytes 1548296 | tf_op jit(solution)/shard_map/ppermute | solution.py:22
  53.3 17.7 %collective-permute-start.11 = (bf16[448,576]{1,0:T(8,128)(2,1)S(1)}, bf16[448,576]{1,0:T(8,128)(2,1)S(1)}, u32[]{:S(2)}, u32[]{:S(2)}) collective-permute-start(bf16[448,576]{1,0:T(8,128)(2,1)S(1)} %collective-permute-done.refs_5_), channel_id=1, source_target_pairs={{96,0},{0,32},{32,64},{64,96},{224,128},{128,160},{160,192},{192,2... | collective-permute-start | bytes 1548296 | tf_op jit(solution)/shard_map/ppermute | solution.py:22
  55.0 16.0 %collective-permute-start.12 = (bf16[448,576]{1,0:T(8,128)(2,1)S(1)}, bf16[448,576]{1,0:T(8,128)(2,1)}, u32[]{:S(2)}, u32[]{:S(2)}) collective-permute-start(bf16[448,576]{1,0:T(8,128)(2,1)S(1)} %get-tuple-element.18.refs_4_), channel_id=1, source_target_pairs={{0,128},{32,160},{64,192},{96,224},{128,0},{160,32},{192,64},{224,... | collective-permute-start | bytes 1548296 | tf_op jit(solution)/shard_map/ppermute | solution.py:26
  73.0 1.5 collective-permute-start.13
  75.6 6.8 %collective-permute-start.14 = (bf16[56,896]{1,0:T(8,128)(2,1)S(1)}, bf16[56,896]{1,0:T(8,128)(2,1)S(1)}, u32[]{:S(2)}, u32[]{:S(2)}) collective-permute-start(bf16[56,896]{1,0:T(8,128)(2,1)S(1)} %get-tuple-element.63), channel_id=1, source_target_pairs={{0,2},{1,3},{2,0},{3,1},{4,6},{5,7},{6,4},{7,5},{8,10},{9,11},{10,... | collective-permute-start | bytes 301064 | tf_op jit(solution)/shard_map/ppermute | solution.py:35
  76.9 7.3 %collective-permute-start.16 = (bf16[56,896]{1,0:T(8,128)(2,1)S(1)}, bf16[56,896]{1,0:T(8,128)(2,1)S(1)}, u32[]{:S(2)}, u32[]{:S(2)}) collective-permute-start(bf16[56,896]{1,0:T(8,128)(2,1)S(1)} %get-tuple-element.64), channel_id=1, source_target_pairs={{0,130},{1,131},{2,128},{3,129},{4,134},{5,135},{6,132},{7,133},{8... | collective-permute-start | bytes 301064 | tf_op jit(solution)/shard_map/ppermute | solution.py:40
  79.1 5.1 %collective-permute-start.15 = (bf16[56,896]{1,0:T(8,128)(2,1)S(1)}, bf16[56,896]{1,0:T(8,128)(2,1)S(1)}, u32[]{:S(2)}, u32[]{:S(2)}) collective-permute-start(bf16[56,896]{1,0:T(8,128)(2,1)S(1)} %get-tuple-element.64), channel_id=1, source_target_pairs={{0,128},{32,160},{64,192},{96,224},{128,0},{160,32},{192,64},{224,... | collective-permute-start | bytes 301064 | tf_op jit(solution)/shard_map/ppermute | solution.py:26
  85.1 12.2 %collective-permute-start.20 = (bf16[2,56,896]{2,1,0:T(8,128)(2,1)}, bf16[2,56,896]{2,1,0:T(8,128)(2,1)S(1)}, u32[]{:S(2)}, u32[]{:S(2)}) collective-permute-start(bf16[2,56,896]{2,1,0:T(8,128)(2,1)} %get-tuple-element.61), channel_id=1, source_target_pairs={{24,0},{25,1},{26,2},{27,3},{28,4},{29,5},{30,6},{31,7},{0,8},{1,9... | collective-permute-start | bytes 602120 | tf_op jit(solution)/shard_map/ppermute | solution.py:31
  85.5 13.1 %collective-permute-start.19 = (bf16[2,56,896]{2,1,0:T(8,128)(2,1)}, bf16[2,56,896]{2,1,0:T(8,128)(2,1)}, u32[]{:S(2)}, u32[]{:S(2)}) collective-permute-start(bf16[2,56,896]{2,1,0:T(8,128)(2,1)} %get-tuple-element.61), channel_id=1, source_target_pairs={{8,0},{9,1},{10,2},{11,3},{12,4},{13,5},{14,6},{15,7},{16,8},{17,9... | collective-permute-start | bytes 602120 | tf_op jit(solution)/shard_map/ppermute | solution.py:31
  89.2 14.7 %collective-permute-start.17 = (bf16[2,56,896]{2,1,0:T(8,128)(2,1)}, bf16[2,56,896]{2,1,0:T(8,128)(2,1)}, u32[]{:S(2)}, u32[]{:S(2)}) collective-permute-start(bf16[2,56,896]{2,1,0:T(8,128)(2,1)} %get-tuple-element.61), channel_id=1, source_target_pairs={{4,0},{5,1},{6,2},{7,3},{8,4},{9,5},{10,6},{11,7},{12,8},{13,9},{1... | collective-permute-start | bytes 602120 | tf_op jit(solution)/shard_map/ppermute | solution.py:31
  89.2 17.0 %collective-permute-start.18 = (bf16[2,56,896]{2,1,0:T(8,128)(2,1)}, bf16[2,56,896]{2,1,0:T(8,128)(2,1)}, u32[]{:S(2)}, u32[]{:S(2)}) collective-permute-start(bf16[2,56,896]{2,1,0:T(8,128)(2,1)} %get-tuple-element.61), channel_id=1, source_target_pairs={{28,0},{29,1},{30,2},{31,3},{0,4},{1,5},{2,6},{3,7},{4,8},{5,9},{6... | collective-permute-start | bytes 602120 | tf_op jit(solution)/shard_map/ppermute | solution.py:31
  91.3 20.6 %copy-start = (bf16[448,576]{1,0:T(8,128)(2,1)S(1)}, bf16[448,576]{1,0:T(8,128)(2,1)}, u32[]{:S(2)}) copy-start(bf16[448,576]{1,0:T(8,128)(2,1)} %refs_1_.3) | copy-start | bytes 1548292
  91.3 20.6 %copy-start.3 = (bf16[448,576]{1,0:T(8,128)(2,1)S(1)}, bf16[448,576]{1,0:T(8,128)(2,1)}, u32[]{:S(2)}) copy-start(bf16[448,576]{1,0:T(8,128)(2,1)} %copy-done.2) | copy-start | bytes 1548292
  91.3 20.6 %copy-start.5 = (bf16[448,576]{1,0:T(8,128)(2,1)S(1)}, bf16[448,576]{1,0:T(8,128)(2,1)}, u32[]{:S(2)}) copy-start(bf16[448,576]{1,0:T(8,128)(2,1)} %copy-done.4) | copy-start | bytes 1548292
  91.3 20.6 %copy-start.7 = (bf16[448,576]{1,0:T(8,128)(2,1)S(1)}, bf16[448,576]{1,0:T(8,128)(2,1)}, u32[]{:S(2)}) copy-start(bf16[448,576]{1,0:T(8,128)(2,1)} %copy-done.6) | copy-start | bytes 1548292
  97.3 14.4 %collective-permute-start.24 = (bf16[1,56,896]{2,1,0:T(8,128)(2,1)S(1)}, bf16[1,56,896]{2,1,0:T(8,128)(2,1)S(1)}, u32[]{:S(2)}, u32[]{:S(2)}) collective-permute-start(bf16[1,56,896]{2,1,0:T(8,128)(2,1)S(1)} %slice.146), channel_id=1, source_target_pairs={{24,0},{25,1},{26,2},{27,3},{28,4},{29,5},{30,6},{31,7},{0,8},{1,9... | collective-permute-start | bytes 301064 | tf_op jit(solution)/shard_map/ppermute | solution.py:31
  99.6 12.1 %collective-permute-start.23 = (bf16[1,56,896]{2,1,0:T(8,128)(2,1)S(1)}, bf16[1,56,896]{2,1,0:T(8,128)(2,1)S(1)}, u32[]{:S(2)}, u32[]{:S(2)}) collective-permute-start(bf16[1,56,896]{2,1,0:T(8,128)(2,1)S(1)} %slice.145), channel_id=1, source_target_pairs={{8,0},{9,1},{10,2},{11,3},{12,4},{13,5},{14,6},{15,7},{16,8},{17,9... | collective-permute-start | bytes 301064 | tf_op jit(solution)/shard_map/ppermute | solution.py:31
  103.3 8.4 %collective-permute-start.21 = (bf16[2,56,896]{2,1,0:T(8,128)(2,1)}, bf16[2,56,896]{2,1,0:T(8,128)(2,1)S(1)}, u32[]{:S(2)}, u32[]{:S(2)}) collective-permute-start(bf16[2,56,896]{2,1,0:T(8,128)(2,1)} %collective-permute-done.19), channel_id=1, source_target_pairs={{4,0},{5,1},{6,2},{7,3},{8,4},{9,5},{10,6},{11,7},{12,8},{13,9},{1... | collective-permute-start | bytes 602120 | tf_op jit(solution)/shard_map/ppermute | solution.py:31
  103.9 7.8 %collective-permute-start.22 = (bf16[2,56,896]{2,1,0:T(8,128)(2,1)S(1)}, bf16[2,56,896]{2,1,0:T(8,128)(2,1)S(1)}, u32[]{:S(2)}, u32[]{:S(2)}) collective-permute-start(bf16[2,56,896]{2,1,0:T(8,128)(2,1)S(1)} %collective-permute-done.20), channel_id=1, source_target_pairs={{28,0},{29,1},{30,2},{31,3},{0,4},{1,5},{2,6},{3,7},{4,8},{5,9},{6... | collective-permute-start | bytes 602120 | tf_op jit(solution)/shard_map/ppermute | solution.py:31
  111.8 3.5 %collective-permute-start.25 = (bf16[2,448,896]{2,1,0:T(8,128)(2,1)S(1)}, bf16[2,448,896]{2,1,0:T(8,128)(2,1)S(1)}, u32[]{:S(2)}, u32[]{:S(2)}) collective-permute-start(bf16[2,448,896]{2,1,0:T(8,128)(2,1)S(1)} %maximum_dynamic-update-slice_fusion.refs_0_), channel_id=1, source_target_pairs={{0,1},{1,0},{2,3},{3,2},{4,5},{5,4},{6,7},{7,6},{8,9},{9,8},{10,11... | collective-permute-start | bytes 4816904 | tf_op jit(solution)/shard_map/ppermute | solution.py:44
  119.4 14.4 %collective-permute-start.28 = (bf16[448,576]{1,0:T(8,128)(2,1)S(1)}, bf16[448,576]{1,0:T(8,128)(2,1)S(1)}, u32[]{:S(2)}, u32[]{:S(2)}) collective-permute-start(bf16[448,576]{1,0:T(8,128)(2,1)S(1)} %get-tuple-element.24), channel_id=1, source_target_pairs={{0,128},{32,160},{64,192},{96,224},{128,0},{160,32},{192,64},{224,... | collective-permute-start | bytes 1548296 | tf_op jit(solution)/shard_map/ppermute | solution.py:26
  119.4 14.4 %collective-permute-start.26 = (bf16[448,576]{1,0:T(8,128)(2,1)S(1)}, bf16[448,576]{1,0:T(8,128)(2,1)S(1)}, u32[]{:S(2)}, u32[]{:S(2)}) collective-permute-start(bf16[448,576]{1,0:T(8,128)(2,1)S(1)} %get-tuple-element.24), channel_id=1, source_target_pairs={{32,0},{64,32},{96,64},{0,96},{160,128},{192,160},{224,192},{128,2... | collective-permute-start | bytes 1548296 | tf_op jit(solution)/shard_map/ppermute | solution.py:22
  120.3 15.3 %collective-permute-start.27 = (bf16[448,576]{1,0:T(8,128)(2,1)S(1)}, bf16[448,576]{1,0:T(8,128)(2,1)S(1)}, u32[]{:S(2)}, u32[]{:S(2)}) collective-permute-start(bf16[448,576]{1,0:T(8,128)(2,1)S(1)} %get-tuple-element.24), channel_id=1, source_target_pairs={{96,0},{0,32},{32,64},{64,96},{224,128},{128,160},{160,192},{192,2... | collective-permute-start | bytes 1548296 | tf_op jit(solution)/shard_map/ppermute | solution.py:22
  133.8 6.1 %copy-start.21 = (bf16[448,576]{1,0:T(8,128)(2,1)}, bf16[448,576]{1,0:T(8,128)(2,1)S(1)}, u32[]{:S(2)}) copy-start(bf16[448,576]{1,0:T(8,128)(2,1)S(1)} %collective-permute-done.28) | copy-start | bytes 1548292
  133.8 6.1 %copy-start.15 = (bf16[448,576]{1,0:T(8,128)(2,1)}, bf16[448,576]{1,0:T(8,128)(2,1)S(1)}, u32[]{:S(2)}) copy-start(bf16[448,576]{1,0:T(8,128)(2,1)S(1)} %collective-permute-done.26) | copy-start | bytes 1548292
  135.5 4.4 %copy-start.17 = (bf16[448,576]{1,0:T(8,128)(2,1)}, bf16[448,576]{1,0:T(8,128)(2,1)S(1)}, u32[]{:S(2)}) copy-start(bf16[448,576]{1,0:T(8,128)(2,1)S(1)} %collective-permute-done.27) | copy-start | bytes 1548292
  136.6 22.8 %collective-permute-start.30 = (bf16[296,576]{1,0:T(8,128)(2,1)}, bf16[296,576]{1,0:T(8,128)(2,1)}, u32[]{:S(2)}, u32[]{:S(2)}) collective-permute-start(bf16[296,576]{1,0:T(8,128)(2,1)} %get-tuple-element.66), channel_id=1, source_target_pairs={{96,0},{0,32},{32,64},{64,96},{224,128},{128,160},{160,192},{192,2... | collective-permute-start | bytes 1022984 | tf_op jit(solution)/shard_map/ppermute | solution.py:22
  136.6 23.8 %collective-permute-start.29 = (bf16[296,576]{1,0:T(8,128)(2,1)}, bf16[296,576]{1,0:T(8,128)(2,1)}, u32[]{:S(2)}, u32[]{:S(2)}) collective-permute-start(bf16[296,576]{1,0:T(8,128)(2,1)} %get-tuple-element.65), channel_id=1, source_target_pairs={{32,0},{64,32},{96,64},{0,96},{160,128},{192,160},{224,192},{128,2... | collective-permute-start | bytes 1022984 | tf_op jit(solution)/shard_map/ppermute | solution.py:22
  140.1 5.1 %copy-start.11 = (bf16[448,576]{1,0:T(8,128)(2,1)S(1)}, bf16[448,576]{1,0:T(8,128)(2,1)}, u32[]{:S(2)}) copy-start(bf16[448,576]{1,0:T(8,128)(2,1)} %copy-done.10) | copy-start | bytes 1548292
  141.8 3.4 %copy-start.20 = (bf16[448,896]{1,0:T(8,128)(2,1)S(1)}, bf16[448,896]{1,0:T(8,128)(2,1)}, u32[]{:S(2)}) copy-start(bf16[448,896]{1,0:T(8,128)(2,1)} %get-tuple-element.68) | copy-start | bytes 2408452
  141.8 22.7 %collective-permute-start.31 = (bf16[752,576]{0,1:T(8,128)(2,1)}, bf16[752,576]{0,1:T(8,128)(2,1)S(1)}, u32[]{:S(2)}, u32[]{:S(2)}) collective-permute-start(bf16[752,576]{0,1:T(8,128)(2,1)} %copy.2), channel_id=1, source_target_pairs={{0,128},{32,160},{64,192},{96,224},{128,0},{160,32},{192,64},{224,... | collective-permute-start | bytes 2598920 | tf_op jit(solution)/shard_map/ppermute | solution.py:26
  143.6 25.2 %collective-permute-start.32 = (bf16[448,576]{1,0:T(8,128)(2,1)}, bf16[448,576]{1,0:T(8,128)(2,1)}, u32[]{:S(2)}, u32[]{:S(2)}) collective-permute-start(bf16[448,576]{1,0:T(8,128)(2,1)} %copy-done.21), channel_id=1, source_target_pairs={{64,0},{96,32},{0,64},{32,96},{192,128},{224,160},{128,192},{160,2... | collective-permute-start | bytes 1548296 | tf_op jit(solution)/shard_map/ppermute | solution.py:22
  165.1 5.6 %copy-start.19 = (bf16[448,896]{1,0:T(8,128)(2,1)S(1)}, bf16[448,896]{1,0:T(8,128)(2,1)}, u32[]{:S(2)}) copy-start(bf16[448,896]{1,0:T(8,128)(2,1)} %get-tuple-element.31) | copy-start | bytes 2408452
  165.3 5.3 %copy-start.1 = (bf16[448,576]{1,0:T(8,128)(2,1)S(1)}, bf16[448,576]{1,0:T(8,128)(2,1)}, u32[]{:S(2)}) copy-start(bf16[448,576]{1,0:T(8,128)(2,1)} %refs_1_.3) | copy-start | bytes 1548292
  165.3 5.3 %copy-start.9 = (f32[448,576]{1,0:T(8,128)S(1)}, f32[448,576]{1,0:T(8,128)}, u32[]{:S(2)}) copy-start(f32[448,576]{1,0:T(8,128)} %copy-done.8) | copy-start | bytes 3096580
  165.4 5.3 %copy-start.14 = (f32[448,576]{1,0:T(8,128)S(1)}, f32[448,576]{1,0:T(8,128)}, u32[]{:S(2)}) copy-start(f32[448,576]{1,0:T(8,128)} %fusion.19) | copy-start | bytes 3096580
  (7 other events, 12.9 us)

commit v3 on v2

--- a/solution.py
+++ b/solution.py
@@ -120,6 +120,68 @@
     )(block, *x_blocks, *([] if mine else [before]))
 
 
+def close_kernel(few, block_ref, got_ref, *refs):
+    own_y, right, left, across, via_y, via_right, via_left, across_far = refs[:8]
+    found_ref, own_ref, out_ref, lhs, rhs, total, sems = refs[8:]
+    rows, cols = own_ref.shape
+    half, more = rows // 2, rows - few
+    core = lax.rem(lax.axis_index("narrow"), 2)
+
+    pieces = [
+        (block_ref, lhs.at[core]),
+        (got_ref, lhs.at[1 - core]),
+        (own_y, 0),
+        (right, rows),
+        (left, 2 * rows),
+        (via_right.at[pl.ds(0, half)], 3 * rows),
+        (via_left.at[pl.ds(0, half)], 3 * rows + half),
+        (across, 4 * rows),
+        (via_right.at[pl.ds(half, few)], 5 * rows),
+        (via_y.at[pl.ds(0, more)], 5 * rows + few),
+        (via_left.at[pl.ds(half, few)], 6 * rows),
+        (via_y.at[pl.ds(more, more)], 6 * rows + few),
+        (across_far, 7 * rows),
+    ]
+    copies = []
+    for at, (source, place) in enumerate(pieces):
+        target = rhs.at[pl.ds(place, source.shape[0])] if isinstance(place, int) else place
+        copies.append(pltpu.make_async_copy(source, target, sems.at[at]))
+    for copy in copies:
+        copy.start()
+    parts = [pl.ds(start, min(256, cols - start)) for start in range(0, cols, 256)]
+    width = 2 * rows
+    for copy in copies[:7]:
+        copy.wait()
+    for part in parts:
+        total[:, part] = dot(lhs[0, 0], rhs[:width, part]) + dot(lhs[1, 0], rhs[width : 2 * width, part])
+    for copy in copies[7:]:
+        copy.wait()
+    scale = float(COLS) ** 0.5
+    for part in parts:
+        value = dot(lhs[0, 1], rhs[2 * width : 3 * width, part]) + dot(lhs[1, 1], rhs[3 * width :, part])
+        value = coef_b * found_ref[:, part] + coef_c * (total[:, part] + value)
+        out_ref[:, part] = (scale * (coef_a * own_ref[:, part].astype(f32) + value)).astype(bf16)
+
+
+def close(few, block, got, blocks, found, own):
+    rows, cols = own.shape
+    vmem = pl.BlockSpec(memory_space=pltpu.VMEM)
+    return pl.pallas_call(
+        functools.partial(close_kernel, few),
+        out_shape=jax.ShapeDtypeStruct((rows, cols), bf16),
+        in_specs=[pl.BlockSpec(memory_space=pl.ANY)] * 10 + [vmem, vmem],
+        out_specs=vmem,
+        scratch_shapes=[
+            pltpu.VMEM((2, *block.shape), bf16),
+            pltpu.VMEM((8 * rows, cols), bf16),
+            pltpu.VMEM((rows, cols), f32),
+            pltpu.SemaphoreType.DMA((13,)),
+        ],
+        compiler_params=pltpu.CompilerParams(vmem_limit_bytes=16 * 2**20),
+        cost_estimate=pl.CostEstimate(flops=16 * rows * rows * cols, bytes_accessed=10 * 2**20, transcendentals=0),
+    )(block, got, *blocks, found, own)
+
+
 def local(own):
     rows = own.shape[0]
     narrow_pos = lax.axis_index("narrow")
@@ -177,28 +239,15 @@
     for step, piece in pieces:
         block = lax.dynamic_update_slice_in_dim(block, piece, ((z_pos + step) % 8) * unit, 1)
     got = from_core(block)
-    low = jnp.where(core == 0, block, got)
-    high = jnp.where(core == 0, got, block)
-    gram_rows = cat(low[0], high[0], low[1], high[1], axis=1)
-
     x_blocks = (own, x_right, x_left, x_far, across, other_right, other_left, other_far)
     found, sent = found_part(got, x_blocks, found_part(block, x_blocks))
     right, left, across = gather_first(sent)
-    half, few = rows // 2, rows // 48 * 8
+    half, few = rows // 2, 80
     via_y = from_y(cat(right[few:], left[few:]))
     via_right = from_x(cat(right[:half], across[:few]), 1)
     via_left = from_x(cat(left[half:], across[:few]), -1)
     across_far = from_x(across, 2)
-    far = cat(via_right[:half], via_left[:half])
-    across_right = cat(via_right[half:], via_y[: rows - few])
-    across_left = cat(via_left[half:], via_y[rows - few :])
-
-    three, four, five = 3 * rows, 4 * rows, 5 * rows
-    product = dot(gram_rows[:, :three], cat(sent, right, left)) + dot(gram_rows[:, four:five], across)
-    start = coef_a * own.astype(f32) + coef_b * found + coef_c * product
-    scale = float(COLS) ** 0.5
-    last = dot(gram_rows[:, three:four], far) + dot(gram_rows[:, five:], cat(across_right, across_left, across_far))
-    return (scale * (start + coef_c * last)).astype(bf16)
+    return close(few, block, got, (sent, right, left, across, via_y, via_right, via_left, across_far), found, own)
 
 
 def solution(mesh):

time: 176 us -> 175 us (level)
  matrix products: 12.5 us -> 3 us
  Pallas kernels: 5.22 us -> 12 us
  waiting for transfers between devices: 86.7 us -> 91.1 us
  local copies, waits for them, and re-layouts: 23.6 us -> 19.6 us
    dot_general x4 -> x0, matrix products: 9.49 us -> none  [dot(): return jnp.dot(left, right, preferred_element_type=f32)]
    pallas_call x0 -> x1, Pallas kernels: none -> 5.64 us  [close(): pl.pallas_call(functools.partial(close_kernel, few), out_shape=jax.ShapeD...]
    ppermute x5, waiting for transfers between devices: 10.6 us -> 14.2 us  [from_y(): return lax.ppermute(value, 'wide', [(w, (w + 4) % 8) for w in range(8)])]
    slice x3 -> x0, local copies, waits for them, and re-layouts: 2.21 us -> none  [the longest x2 1.97 us: local(): far = cat(via_right[:half], via_left[:half])]
    ppermute x0 -> x1, local copies, waits for them, and re-layouts: none -> 1.93 us  [from_y(): return lax.ppermute(value, 'wide', [(w, (w + 4) % 8) for w in range(8)])]
    unnamed x61 -> x43, local copies, waits for them, and re-layouts: 9.9 us -> 8.1 us
    concatenate x5 -> x4, local copies, waits for them, and re-layouts: 3.82 us -> 2.41 us  [cat(): return jnp.concatenate(parts, axis=axis)]
  transfers between devices with their start and end apart: 33 -> 33, of which waited for: 17 -> 18; matrix products, arithmetic and copies ran while one was open for 15% -> 10% of each run, Pallas kernels for 1% -> 1%
where the time goes in v3:
time: 175 us; the launch traced here: 172 us
  waiting for transfers between devices  91.1 us (52%)
  starting transfers between devices  40.7 us (23%)
  local copies, waits for them, and re-layouts  19.6 us (11%)
  Pallas kernels  12 us (7%)
  other arithmetic  5.48 us (3%)
  matrix products  3 us (2%)
    ppermute x11, waiting for transfers between devices, from_x(): return lax.ppermute(value, 'wide', pairs)  33 us
    ppermute x4, waiting for transfers between devices, along_z(): return lax.ppermute(value, 'narrow', pairs)  23.5 us
    ppermute x5, waiting for transfers between devices, from_y(): return lax.ppermute(value, 'wide', [(w, (w + 4) % 8) for w in range(8)])  14.2 us
    ppermute x11, starting transfers between devices, from_x(): return lax.ppermute(value, 'wide', pairs)  13.8 us
    ppermute x8, starting transfers between devices, from_z(): return lax.ppermute(value, 'narrow', pairs)  12.1 us
    ppermute x8, waiting for transfers between devices, from_z(): return lax.ppermute(value, 'narrow', pairs)  11.3 us
    unnamed x43, local copies, waits for them, and re-layouts  8.1 us
    ppermute x4, starting transfers between devices, along_z(): return lax.ppermute(value, 'narrow', pairs)  7.41 us
  transfers between devices with their start and end apart: 33, of which 18 were waited for; matrix products, arithmetic and copies ran while one was open for 10% of the time, Pallas kernels for 1%

profile of v3, /device:TPU:24, one launch (start us, length us, event | category | flops | bytes accessed | tf_op | source)
XLA Modules:
  0.0 172.5 jit_solution(16087578574421884869)
XLA Ops:
  0.0 2.8 %collective-permute-start.1 = (bf16[448,576]{1,0:T(8,128)(2,1)}, bf16[448,576]{1,0:T(8,128)(2,1)S(1)}, u32[]{:S(2)}, u32[]{:S(2)}) collective-permute-start(bf16[448,576]{1,0:T(8,128)(2,1)} %refs_9_.1), channel_id=1, source_target_pairs={{32,0},{64,32},{96,64},{0,96},{160,128},{192,160},{224,192},{128,2... | collective-permute-start | bytes 1548296 | tf_op jit(solution)/shard_map/ppermute | solution.py:22
  3.5 1.2 constant_dynamic-update-slice_fusion.6
  4.7 10.6 %collective-permute-done.1.refs_2_ = bf16[448,576]{1,0:T(8,128)(2,1)S(1)} collective-permute-done((bf16[448,576]{1,0:T(8,128)(2,1)}, bf16[448,576]{1,0:T(8,128)(2,1)S(1)}, u32[]{:S(2)}, u32[]{:S(2)}) %collective-permute-start.1) | collective-permute-done | bytes 516128 | tf_op jit(solution)/shard_map/ppermute | solution.py:22
  15.3 3.7 %collective-permute-start.3 = (bf16[224,576]{1,0:T(8,128)(2,1)S(1)}, bf16[224,576]{1,0:T(8,128)(2,1)S(1)}, u32[]{:S(2)}, u32[]{:S(2)}) collective-permute-start(bf16[224,576]{1,0:T(8,128)(2,1)S(1)} %slice.78), channel_id=1, source_target_pairs={{32,0},{64,32},{96,64},{0,96},{160,128},{192,160},{224,192},{128,2... | collective-permute-start | bytes 774152 | tf_op jit(solution)/shard_map/ppermute | solution.py:22
  19.7 4.5 %collective-permute-done.3 = bf16[224,576]{1,0:T(8,128)(2,1)S(1)} collective-permute-done((bf16[224,576]{1,0:T(8,128)(2,1)S(1)}, bf16[224,576]{1,0:T(8,128)(2,1)S(1)}, u32[]{:S(2)}, u32[]{:S(2)}) %collective-permute-start.3) | collective-permute-done | bytes 258080 | tf_op jit(solution)/shard_map/ppermute | solution.py:22
  24.3 3.5 %collective-permute-done.4 = bf16[224,576]{1,0:T(8,128)(2,1)S(1)} collective-permute-done((bf16[224,576]{1,0:T(8,128)(2,1)S(1)}, bf16[224,576]{1,0:T(8,128)(2,1)S(1)}, u32[]{:S(2)}, u32[]{:S(2)}) %collective-permute-start.4) | collective-permute-done | bytes 258080 | tf_op jit(solution)/shard_map/ppermute | solution.py:22
  27.8 1.5 convolution_convert_fusion
  29.4 1.5 fusion.6
  30.9 1.9 %collective-permute-done.5 = bf16[448,1792]{1,0:T(8,128)(2,1)S(1)} collective-permute-done((bf16[448,1792]{1,0:T(8,128)(2,1)S(1)}, bf16[448,1792]{1,0:T(8,128)(2,1)S(1)}, u32[]{:S(2)}, u32[]{:S(2)}) %collective-permute-start.5) | collective-permute-done | bytes 1605664 | tf_op jit(solution)/shard_map/ppermute | solution.py:44
  34.2 1.9 %collective-permute-start.6 = (bf16[112,1792]{1,0:T(8,128)(2,1)S(1)}, bf16[112,1792]{1,0:T(8,128)(2,1)S(1)}, u32[]{:S(2)}, u32[]{:S(2)}) collective-permute-start(bf16[112,1792]{1,0:T(8,128)(2,1)S(1)} %get-tuple-element.28), channel_id=1, source_target_pairs={{0,4},{1,29},{2,6},{3,31},{4,8},{5,1},{6,10},{7,3},{8,12},{9,5},{1... | collective-permute-start | bytes 1204232 | tf_op jit(solution)/shard_map/ppermute | solution.py:65
  36.1 3.3 %collective-permute-start.7 = (bf16[56,1792]{1,0:T(8,128)(2,1)S(1)}, bf16[56,1792]{1,0:T(8,128)(2,1)S(1)}, u32[]{:S(2)}, u32[]{:S(2)}) collective-permute-start(bf16[56,1792]{1,0:T(8,128)(2,1)S(1)} %slice.82), channel_id=1, source_target_pairs={{0,8},{1,25},{2,10},{3,27},{4,12},{5,29},{6,14},{7,31},{8,16},{9,1... | collective-permute-start | bytes 602120 | tf_op jit(solution)/shard_map/ppermute | solution.py:65
  39.4 10.6 %collective-permute-done.7 = bf16[56,1792]{1,0:T(8,128)(2,1)S(1)} collective-permute-done((bf16[56,1792]{1,0:T(8,128)(2,1)S(1)}, bf16[56,1792]{1,0:T(8,128)(2,1)S(1)}, u32[]{:S(2)}, u32[]{:S(2)}) %collective-permute-start.7) | collective-permute-done | bytes 200736 | tf_op jit(solution)/shard_map/ppermute | solution.py:65
  50.9 2.1 %collective-permute-start.9 = (bf16[112,1792]{1,0:T(8,128)(2,1)}, bf16[112,1792]{1,0:T(8,128)(2,1)}, u32[]{:S(2)}, u32[]{:S(2)}) collective-permute-start(bf16[112,1792]{1,0:T(8,128)(2,1)} %get-tuple-element.16), channel_id=1, source_target_pairs={{0,4},{1,29},{2,6},{3,31},{4,8},{5,1},{6,10},{7,3},{8,12},{9,5},{1... | collective-permute-start | bytes 1204232 | tf_op jit(solution)/shard_map/ppermute | solution.py:65
  53.3 1.8 %collective-permute-start.11 = (bf16[448,576]{1,0:T(8,128)(2,1)S(1)}, bf16[448,576]{1,0:T(8,128)(2,1)}, u32[]{:S(2)}, u32[]{:S(2)}) collective-permute-start(bf16[448,576]{1,0:T(8,128)(2,1)S(1)} %collective-permute-done.refs_5_), channel_id=1, source_target_pairs={{96,0},{0,32},{32,64},{64,96},{224,128},{128,160},{160,192},{192,2... | collective-permute-start | bytes 1548296 | tf_op jit(solution)/shard_map/ppermute | solution.py:22
  56.8 8.7 %collective-permute-done.8 = bf16[112,1792]{1,0:T(8,128)(2,1)} collective-permute-done((bf16[112,1792]{1,0:T(8,128)(2,1)}, bf16[112,1792]{1,0:T(8,128)(2,1)}, u32[]{:S(2)}, u32[]{:S(2)}) %collective-permute-start.8) | collective-permute-done | bytes 401440 | tf_op jit(solution)/shard_map/ppermute | solution.py:65
  65.6 4.2 %collective-permute-done.9 = bf16[112,1792]{1,0:T(8,128)(2,1)} collective-permute-done((bf16[112,1792]{1,0:T(8,128)(2,1)}, bf16[112,1792]{1,0:T(8,128)(2,1)}, u32[]{:S(2)}, u32[]{:S(2)}) %collective-permute-start.9) | collective-permute-done | bytes 401440 | tf_op jit(solution)/shard_map/ppermute | solution.py:65
  69.8 1.2 pad_add_fusion
  71.9 1.4 collective-permute-done.13
  73.4 1.3 collective-permute-start.14
  74.8 2.9 %collective-permute-start.16 = (bf16[56,896]{1,0:T(8,128)(2,1)S(1)}, bf16[56,896]{1,0:T(8,128)(2,1)S(1)}, u32[]{:S(2)}, u32[]{:S(2)}) collective-permute-start(bf16[56,896]{1,0:T(8,128)(2,1)S(1)} %get-tuple-element.56), channel_id=1, source_target_pairs={{0,130},{1,131},{2,128},{3,129},{4,134},{5,135},{6,132},{7,133},{8... | collective-permute-start | bytes 301064 | tf_op jit(solution)/shard_map/ppermute | solution.py:40
  77.6 3.1 %collective-permute-done.14 = bf16[56,896]{1,0:T(8,128)(2,1)S(1)} collective-permute-done((bf16[56,896]{1,0:T(8,128)(2,1)S(1)}, bf16[56,896]{1,0:T(8,128)(2,1)S(1)}, u32[]{:S(2)}, u32[]{:S(2)}) %collective-permute-start.14) | collective-permute-done | bytes 100384 | tf_op jit(solution)/shard_map/ppermute | solution.py:35
  80.8 1.3 collective-permute-done.16
  82.9 2.9 %collective-permute-start.20 = (bf16[2,56,896]{2,1,0:T(8,128)(2,1)}, bf16[2,56,896]{2,1,0:T(8,128)(2,1)S(1)}, u32[]{:S(2)}, u32[]{:S(2)}) collective-permute-start(bf16[2,56,896]{2,1,0:T(8,128)(2,1)} %get-tuple-element.53), channel_id=1, source_target_pairs={{24,0},{25,1},{26,2},{27,3},{28,4},{29,5},{30,6},{31,7},{0,8},{1,9... | collective-permute-start | bytes 602120 | tf_op jit(solution)/shard_map/ppermute | solution.py:31
  85.9 1.8 %collective-permute-start.17 = (bf16[2,56,896]{2,1,0:T(8,128)(2,1)}, bf16[2,56,896]{2,1,0:T(8,128)(2,1)}, u32[]{:S(2)}, u32[]{:S(2)}) collective-permute-start(bf16[2,56,896]{2,1,0:T(8,128)(2,1)} %get-tuple-element.53), channel_id=1, source_target_pairs={{4,0},{5,1},{6,2},{7,3},{8,4},{9,5},{10,6},{11,7},{12,8},{13,9},{1... | collective-permute-start | bytes 602120 | tf_op jit(solution)/shard_map/ppermute | solution.py:31
  87.9 7.4 %collective-permute-done.19 = bf16[2,56,896]{2,1,0:T(8,128)(2,1)} collective-permute-done((bf16[2,56,896]{2,1,0:T(8,128)(2,1)}, bf16[2,56,896]{2,1,0:T(8,128)(2,1)}, u32[]{:S(2)}, u32[]{:S(2)}) %collective-permute-start.19) | collective-permute-done | bytes 200736 | tf_op jit(solution)/shard_map/ppermute | solution.py:31
  96.2 1.7 collective-permute-start.23
  97.9 1.4 collective-permute-start.24
  99.3 4.0 %collective-permute-start.21 = (bf16[2,56,896]{2,1,0:T(8,128)(2,1)}, bf16[2,56,896]{2,1,0:T(8,128)(2,1)S(1)}, u32[]{:S(2)}, u32[]{:S(2)}) collective-permute-start(bf16[2,56,896]{2,1,0:T(8,128)(2,1)} %collective-permute-done.19), channel_id=1, source_target_pairs={{4,0},{5,1},{6,2},{7,3},{8,4},{9,5},{10,6},{11,7},{12,8},{13,9},{1... | collective-permute-start | bytes 602120 | tf_op jit(solution)/shard_map/ppermute | solution.py:31
  106.2 1.4 collective-permute-done.21
  107.6 2.6 %collective-permute-done.22 = bf16[2,56,896]{2,1,0:T(8,128)(2,1)S(1)} collective-permute-done((bf16[2,56,896]{2,1,0:T(8,128)(2,1)S(1)}, bf16[2,56,896]{2,1,0:T(8,128)(2,1)S(1)}, u32[]{:S(2)}, u32[]{:S(2)}) %collective-permute-start.22) | collective-permute-done | bytes 200736 | tf_op jit(solution)/shard_map/ppermute | solution.py:31
  110.4 2.1 %shard_map.17.refs_9_ = f32[448,576]{1,0:T(8,128)S(1)} custom-call(bf16[2,448,896]{2,1,0:T(8,128)(2,1)S(1)} %maximum_dynamic-update-slice_fusion.refs_0_.block_ref, bf16[448,576]{1,0:T(8,128)(2,1)S(1)} %copy-done, bf16[448,576]{1,0:T(8,128)(2,1)S(1)} %collective-permute-done.1.refs_2_, bf16[448,576]{1,0:T(8,128)(2,1)S(1)} %collective-permute-done.2.refs_3_, ...), custom_call_target="tpu_custom_call" | custom-call | flops 924844032 | bytes 6291456 | tf_op jit(solution)/shard_map/pallas_call | solution.py:108
  112.6 1.2 collective-permute-done.25.refs_0_.got_ref
  113.8 4.2 %shard_map.18 = (f32[448,576]{1,0:T(8,128)S(1)}, bf16[448,576]{1,0:T(8,128)(2,1)}) custom-call(bf16[2,448,896]{2,1,0:T(8,128)(2,1)S(1)} %collective-permute-done.25.refs_0_.got_ref, bf16[448,576]{1,0:T(8,128)(2,1)S(1)} %copy-done, bf16[448,576]{1,0:T(8,128)(2,1)S(1)} %collective-permute-done.1.refs_2_, bf16[448,576]{1,0:T(8,128)(2,1)S(1)} %collective-permute-done.2.refs_3_, ...), custom_call_target="tpu_custom_call" | custom-call | flops 924844032 | bytes 6291456 | tf_op jit(solution)/shard_map/pallas_call | solution.py:108
  119.1 2.0 %collective-permute-start.27 = (bf16[448,576]{1,0:T(8,128)(2,1)}, bf16[448,576]{1,0:T(8,128)(2,1)S(1)}, u32[]{:S(2)}, u32[]{:S(2)}) collective-permute-start(bf16[448,576]{1,0:T(8,128)(2,1)} %get-tuple-element.23.refs_0_), channel_id=1, source_target_pairs={{96,0},{0,32},{32,64},{64,96},{224,128},{128,160},{160,192},{192,2... | collective-permute-start | bytes 1548296 | tf_op jit(solution)/shard_map/ppermute | solution.py:22
  121.8 11.6 %collective-permute-done.26.refs_1_ = bf16[448,576]{1,0:T(8,128)(2,1)S(1)} collective-permute-done((bf16[448,576]{1,0:T(8,128)(2,1)}, bf16[448,576]{1,0:T(8,128)(2,1)S(1)}, u32[]{:S(2)}, u32[]{:S(2)}) %collective-permute-start.26) | collective-permute-done | bytes 516128 | tf_op jit(solution)/shard_map/ppermute | solution.py:22
  133.5 1.2 collective-permute-done.27.refs_2_
  134.7 1.1 pad_maximum_fusion
  135.8 2.2 %copy.2 = bf16[736,576]{0,1:T(8,128)(2,1)} copy(bf16[736,576]{1,0:T(8,128)(2,1)} %pad_maximum_fusion) | data formatting | bytes 1695744 | tf_op jit(solution)/shard_map/concatenate | solution.py:56
  140.6 1.0 pad_maximum_fusion.1
  141.7 2.3 %collective-permute-start.30 = (bf16[304,576]{1,0:T(8,128)(2,1)}, bf16[304,576]{1,0:T(8,128)(2,1)S(1)}, u32[]{:S(2)}, u32[]{:S(2)}) collective-permute-start(bf16[304,576]{1,0:T(8,128)(2,1)} %get-tuple-element.58), channel_id=1, source_target_pairs={{32,0},{64,32},{96,64},{0,96},{160,128},{192,160},{224,192},{128,2... | collective-permute-start | bytes 1050632 | tf_op jit(solution)/shard_map/ppermute | solution.py:22
  144.0 14.2 %collective-permute-done.29 = bf16[736,576]{0,1:T(8,128)(2,1)} collective-permute-done((bf16[736,576]{0,1:T(8,128)(2,1)}, bf16[736,576]{0,1:T(8,128)(2,1)}, u32[]{:S(2)}, u32[]{:S(2)}) %collective-permute-start.29) | collective-permute-done | bytes 847904 | tf_op jit(solution)/shard_map/ppermute | solution.py:26
  158.2 1.9 %copy.3.refs_4_ = bf16[736,576]{1,0:T(8,128)(2,1)S(1)} copy(bf16[736,576]{0,1:T(8,128)(2,1)} %collective-permute-done.29) | data formatting | bytes 1695744 | tf_op jit(solution)/shard_map/ppermute | solution.py:26
  160.2 1.7 collective-permute-done.31.refs_6_
  161.9 1.4 copy-done.2
  163.3 1.1 copy-done.8
  164.3 1.1 copy-done.10
  165.4 1.3 copy-done.14
  166.7 5.6 %shard_map.19 = bf16[448,576]{1,0:T(8,128)(2,1)} custom-call(bf16[2,448,896]{2,1,0:T(8,128)(2,1)S(1)} %maximum_dynamic-update-slice_fusion.refs_0_.block_ref, bf16[2,448,896]{2,1,0:T(8,128)(2,1)S(1)} %copy-done.2, bf16[448,576]{1,0:T(8,128)(2,1)} %get-tuple-element.23.refs_0_, bf16[448,576]{1,0:T(8,128)(2,1)S(1)} %copy-done.8, ...), custom_call_target="tpu_custom_call" | custom-call | flops 1849688064 | bytes 10485760 | tf_op jit(solution)/shard_map/pallas_call | solution.py:169
  (104 shorter events, 16.4 us)
Async XLA Ops:
  0.0 15.3 %collective-permute-start.1 = (bf16[448,576]{1,0:T(8,128)(2,1)}, bf16[448,576]{1,0:T(8,128)(2,1)S(1)}, u32[]{:S(2)}, u32[]{:S(2)}) collective-permute-start(bf16[448,576]{1,0:T(8,128)(2,1)} %refs_9_.1), channel_id=1, source_target_pairs={{32,0},{64,32},{96,64},{0,96},{160,128},{192,160},{224,192},{128,2... | collective-permute-start | bytes 1548296 | tf_op jit(solution)/shard_map/ppermute | solution.py:22
  2.8 16.2 %collective-permute-start.2 = (bf16[448,576]{1,0:T(8,128)(2,1)}, bf16[448,576]{1,0:T(8,128)(2,1)S(1)}, u32[]{:S(2)}, u32[]{:S(2)}) collective-permute-start(bf16[448,576]{1,0:T(8,128)(2,1)} %refs_9_.1), channel_id=1, source_target_pairs={{96,0},{0,32},{32,64},{64,96},{224,128},{128,160},{160,192},{192,2... | collective-permute-start | bytes 1548296 | tf_op jit(solution)/shard_map/ppermute | solution.py:22
  2.8 16.4 %collective-permute-start = (bf16[448,576]{1,0:T(8,128)(2,1)}, bf16[448,576]{1,0:T(8,128)(2,1)S(1)}, u32[]{:S(2)}, u32[]{:S(2)}) collective-permute-start(bf16[448,576]{1,0:T(8,128)(2,1)} %refs_9_.1), channel_id=1, source_target_pairs={{0,128},{32,160},{64,192},{96,224},{128,0},{160,32},{192,64},{224,... | collective-permute-start | bytes 1548296 | tf_op jit(solution)/shard_map/ppermute | solution.py:26
  15.3 8.9 %collective-permute-start.3 = (bf16[224,576]{1,0:T(8,128)(2,1)S(1)}, bf16[224,576]{1,0:T(8,128)(2,1)S(1)}, u32[]{:S(2)}, u32[]{:S(2)}) collective-permute-start(bf16[224,576]{1,0:T(8,128)(2,1)S(1)} %slice.78), channel_id=1, source_target_pairs={{32,0},{64,32},{96,64},{0,96},{160,128},{192,160},{224,192},{128,2... | collective-permute-start | bytes 774152 | tf_op jit(solution)/shard_map/ppermute | solution.py:22
  19.0 8.7 %collective-permute-start.4 = (bf16[224,576]{1,0:T(8,128)(2,1)S(1)}, bf16[224,576]{1,0:T(8,128)(2,1)S(1)}, u32[]{:S(2)}, u32[]{:S(2)}) collective-permute-start(bf16[224,576]{1,0:T(8,128)(2,1)S(1)} %slice.79), channel_id=1, source_target_pairs={{96,0},{0,32},{32,64},{64,96},{224,128},{128,160},{160,192},{192,2... | collective-permute-start | bytes 774152 | tf_op jit(solution)/shard_map/ppermute | solution.py:22
  19.1 34.1 %copy-start.3 = (bf16[448,576]{1,0:T(8,128)(2,1)}, bf16[448,576]{1,0:T(8,128)(2,1)S(1)}, u32[]{:S(2)}) copy-start(bf16[448,576]{1,0:T(8,128)(2,1)S(1)} %collective-permute-done.refs_5_) | copy-start | bytes 1548292
  27.8 27.2 %copy-start.5 = (bf16[448,576]{1,0:T(8,128)(2,1)}, bf16[448,576]{1,0:T(8,128)(2,1)S(1)}, u32[]{:S(2)}) copy-start(bf16[448,576]{1,0:T(8,128)(2,1)S(1)} %get-tuple-element.18.refs_4_) | copy-start | bytes 1548292
  29.3 3.5 %collective-permute-start.5 = (bf16[448,1792]{1,0:T(8,128)(2,1)S(1)}, bf16[448,1792]{1,0:T(8,128)(2,1)S(1)}, u32[]{:S(2)}, u32[]{:S(2)}) collective-permute-start(bf16[448,1792]{1,0:T(8,128)(2,1)S(1)} %convolution_convert_fusion), channel_id=1, source_target_pairs={{0,1},{1,0},{2,3},{3,2},{4,5},{5,4},{6,7},{7,6},{8,9},{9,8},{10,11... | collective-permute-start | bytes 4816904 | tf_op jit(solution)/shard_map/ppermute | solution.py:44
  33.2 21.8 %copy-start.15 = (f32[448,1792]{1,0:T(8,128)}, f32[448,1792]{1,0:T(8,128)S(1)}, u32[]{:S(2)}) copy-start(f32[448,1792]{1,0:T(8,128)S(1)} %get-tuple-element.26) | copy-start | bytes 9633796
  34.2 15.9 %collective-permute-start.6 = (bf16[112,1792]{1,0:T(8,128)(2,1)S(1)}, bf16[112,1792]{1,0:T(8,128)(2,1)S(1)}, u32[]{:S(2)}, u32[]{:S(2)}) collective-permute-start(bf16[112,1792]{1,0:T(8,128)(2,1)S(1)} %get-tuple-element.28), channel_id=1, source_target_pairs={{0,4},{1,29},{2,6},{3,31},{4,8},{5,1},{6,10},{7,3},{8,12},{9,5},{1... | collective-permute-start | bytes 1204232 | tf_op jit(solution)/shard_map/ppermute | solution.py:65
  36.1 13.9 %collective-permute-start.7 = (bf16[56,1792]{1,0:T(8,128)(2,1)S(1)}, bf16[56,1792]{1,0:T(8,128)(2,1)S(1)}, u32[]{:S(2)}, u32[]{:S(2)}) collective-permute-start(bf16[56,1792]{1,0:T(8,128)(2,1)S(1)} %slice.82), channel_id=1, source_target_pairs={{0,8},{1,25},{2,10},{3,27},{4,12},{5,29},{6,14},{7,31},{8,16},{9,1... | collective-permute-start | bytes 602120 | tf_op jit(solution)/shard_map/ppermute | solution.py:65
  50.9 14.7 %collective-permute-start.8 = (bf16[112,1792]{1,0:T(8,128)(2,1)}, bf16[112,1792]{1,0:T(8,128)(2,1)}, u32[]{:S(2)}, u32[]{:S(2)}) collective-permute-start(bf16[112,1792]{1,0:T(8,128)(2,1)} %fusion), channel_id=1, source_target_pairs={{0,8},{1,25},{2,10},{3,27},{4,12},{5,29},{6,14},{7,31},{8,16},{9,1... | collective-permute-start | bytes 1204232 | tf_op jit(solution)/shard_map/ppermute | solution.py:65
  50.9 18.9 %collective-permute-start.9 = (bf16[112,1792]{1,0:T(8,128)(2,1)}, bf16[112,1792]{1,0:T(8,128)(2,1)}, u32[]{:S(2)}, u32[]{:S(2)}) collective-permute-start(bf16[112,1792]{1,0:T(8,128)(2,1)} %get-tuple-element.16), channel_id=1, source_target_pairs={{0,4},{1,29},{2,6},{3,31},{4,8},{5,1},{6,10},{7,3},{8,12},{9,5},{1... | collective-permute-start | bytes 1204232 | tf_op jit(solution)/shard_map/ppermute | solution.py:65
  53.0 18.0 %collective-permute-start.10 = (bf16[448,576]{1,0:T(8,128)(2,1)S(1)}, bf16[448,576]{1,0:T(8,128)(2,1)S(1)}, u32[]{:S(2)}, u32[]{:S(2)}) collective-permute-start(bf16[448,576]{1,0:T(8,128)(2,1)S(1)} %collective-permute-done.refs_5_), channel_id=1, source_target_pairs={{32,0},{64,32},{96,64},{0,96},{160,128},{192,160},{224,192},{128,2... | collective-permute-start | bytes 1548296 | tf_op jit(solution)/shard_map/ppermute | solution.py:22
  53.3 17.7 %collective-permute-start.11 = (bf16[448,576]{1,0:T(8,128)(2,1)S(1)}, bf16[448,576]{1,0:T(8,128)(2,1)}, u32[]{:S(2)}, u32[]{:S(2)}) collective-permute-start(bf16[448,576]{1,0:T(8,128)(2,1)S(1)} %collective-permute-done.refs_5_), channel_id=1, source_target_pairs={{96,0},{0,32},{32,64},{64,96},{224,128},{128,160},{160,192},{192,2... | collective-permute-start | bytes 1548296 | tf_op jit(solution)/shard_map/ppermute | solution.py:22
  55.1 16.0 %collective-permute-start.12 = (bf16[448,576]{1,0:T(8,128)(2,1)S(1)}, bf16[448,576]{1,0:T(8,128)(2,1)}, u32[]{:S(2)}, u32[]{:S(2)}) collective-permute-start(bf16[448,576]{1,0:T(8,128)(2,1)S(1)} %get-tuple-element.18.refs_4_), channel_id=1, source_target_pairs={{0,128},{32,160},{64,192},{96,224},{128,0},{160,32},{192,64},{224,... | collective-permute-start | bytes 1548296 | tf_op jit(solution)/shard_map/ppermute | solution.py:26
  71.8 1.5 collective-permute-start.13
  73.4 7.3 %collective-permute-start.14 = (bf16[56,896]{1,0:T(8,128)(2,1)S(1)}, bf16[56,896]{1,0:T(8,128)(2,1)S(1)}, u32[]{:S(2)}, u32[]{:S(2)}) collective-permute-start(bf16[56,896]{1,0:T(8,128)(2,1)S(1)} %get-tuple-element.55), channel_id=1, source_target_pairs={{0,2},{1,3},{2,0},{3,1},{4,6},{5,7},{6,4},{7,5},{8,10},{9,11},{10,... | collective-permute-start | bytes 301064 | tf_op jit(solution)/shard_map/ppermute | solution.py:35
  74.8 6.0 %collective-permute-start.15 = (bf16[56,896]{1,0:T(8,128)(2,1)S(1)}, bf16[56,896]{1,0:T(8,128)(2,1)S(1)}, u32[]{:S(2)}, u32[]{:S(2)}) collective-permute-start(bf16[56,896]{1,0:T(8,128)(2,1)S(1)} %get-tuple-element.56), channel_id=1, source_target_pairs={{0,128},{32,160},{64,192},{96,224},{128,0},{160,32},{192,64},{224,... | collective-permute-start | bytes 301064 | tf_op jit(solution)/shard_map/ppermute | solution.py:26
  74.8 7.3 %collective-permute-start.16 = (bf16[56,896]{1,0:T(8,128)(2,1)S(1)}, bf16[56,896]{1,0:T(8,128)(2,1)S(1)}, u32[]{:S(2)}, u32[]{:S(2)}) collective-permute-start(bf16[56,896]{1,0:T(8,128)(2,1)S(1)} %get-tuple-element.56), channel_id=1, source_target_pairs={{0,130},{1,131},{2,128},{3,129},{4,134},{5,135},{6,132},{7,133},{8... | collective-permute-start | bytes 301064 | tf_op jit(solution)/shard_map/ppermute | solution.py:40
  82.9 12.3 %collective-permute-start.19 = (bf16[2,56,896]{2,1,0:T(8,128)(2,1)}, bf16[2,56,896]{2,1,0:T(8,128)(2,1)}, u32[]{:S(2)}, u32[]{:S(2)}) collective-permute-start(bf16[2,56,896]{2,1,0:T(8,128)(2,1)} %get-tuple-element.53), channel_id=1, source_target_pairs={{8,0},{9,1},{10,2},{11,3},{12,4},{13,5},{14,6},{15,7},{16,8},{17,9... | collective-permute-start | bytes 602120 | tf_op jit(solution)/shard_map/ppermute | solution.py:31
  82.9 14.9 %collective-permute-start.20 = (bf16[2,56,896]{2,1,0:T(8,128)(2,1)}, bf16[2,56,896]{2,1,0:T(8,128)(2,1)S(1)}, u32[]{:S(2)}, u32[]{:S(2)}) collective-permute-start(bf16[2,56,896]{2,1,0:T(8,128)(2,1)} %get-tuple-element.53), channel_id=1, source_target_pairs={{24,0},{25,1},{26,2},{27,3},{28,4},{29,5},{30,6},{31,7},{0,8},{1,9... | collective-permute-start | bytes 602120 | tf_op jit(solution)/shard_map/ppermute | solution.py:31
  85.9 17.4 %collective-permute-start.17 = (bf16[2,56,896]{2,1,0:T(8,128)(2,1)}, bf16[2,56,896]{2,1,0:T(8,128)(2,1)}, u32[]{:S(2)}, u32[]{:S(2)}) collective-permute-start(bf16[2,56,896]{2,1,0:T(8,128)(2,1)} %get-tuple-element.53), channel_id=1, source_target_pairs={{4,0},{5,1},{6,2},{7,3},{8,4},{9,5},{10,6},{11,7},{12,8},{13,9},{1... | collective-permute-start | bytes 602120 | tf_op jit(solution)/shard_map/ppermute | solution.py:31
  87.6 16.6 %collective-permute-start.18 = (bf16[2,56,896]{2,1,0:T(8,128)(2,1)}, bf16[2,56,896]{2,1,0:T(8,128)(2,1)}, u32[]{:S(2)}, u32[]{:S(2)}) collective-permute-start(bf16[2,56,896]{2,1,0:T(8,128)(2,1)} %get-tuple-element.53), channel_id=1, source_target_pairs={{28,0},{29,1},{30,2},{31,3},{0,4},{1,5},{2,6},{3,7},{4,8},{5,9},{6... | collective-permute-start | bytes 602120 | tf_op jit(solution)/shard_map/ppermute | solution.py:31
  87.9 22.5 %copy-start = (bf16[448,576]{1,0:T(8,128)(2,1)S(1)}, bf16[448,576]{1,0:T(8,128)(2,1)}, u32[]{:S(2)}) copy-start(bf16[448,576]{1,0:T(8,128)(2,1)} %refs_9_.1) | copy-start | bytes 1548292
  87.9 22.5 %copy-start.4 = (bf16[448,576]{1,0:T(8,128)(2,1)S(1)}, bf16[448,576]{1,0:T(8,128)(2,1)}, u32[]{:S(2)}) copy-start(bf16[448,576]{1,0:T(8,128)(2,1)} %copy-done.3) | copy-start | bytes 1548292
  87.9 22.5 %copy-start.6 = (bf16[448,576]{1,0:T(8,128)(2,1)S(1)}, bf16[448,576]{1,0:T(8,128)(2,1)}, u32[]{:S(2)}) copy-start(bf16[448,576]{1,0:T(8,128)(2,1)} %copy-done.5) | copy-start | bytes 1548292
  87.9 22.5 %copy-start.12 = (bf16[448,576]{1,0:T(8,128)(2,1)S(1)}, bf16[448,576]{1,0:T(8,128)(2,1)}, u32[]{:S(2)}) copy-start(bf16[448,576]{1,0:T(8,128)(2,1)} %copy-done.11) | copy-start | bytes 1548292
  96.2 14.1 %collective-permute-start.23 = (bf16[1,56,896]{2,1,0:T(8,128)(2,1)S(1)}, bf16[1,56,896]{2,1,0:T(8,128)(2,1)S(1)}, u32[]{:S(2)}, u32[]{:S(2)}) collective-permute-start(bf16[1,56,896]{2,1,0:T(8,128)(2,1)S(1)} %slice.87), channel_id=1, source_target_pairs={{8,0},{9,1},{10,2},{11,3},{12,4},{13,5},{14,6},{15,7},{16,8},{17,9... | collective-permute-start | bytes 301064 | tf_op jit(solution)/shard_map/ppermute | solution.py:31
  97.9 12.4 %collective-permute-start.24 = (bf16[1,56,896]{2,1,0:T(8,128)(2,1)S(1)}, bf16[1,56,896]{2,1,0:T(8,128)(2,1)S(1)}, u32[]{:S(2)}, u32[]{:S(2)}) collective-permute-start(bf16[1,56,896]{2,1,0:T(8,128)(2,1)S(1)} %slice.88), channel_id=1, source_target_pairs={{24,0},{25,1},{26,2},{27,3},{28,4},{29,5},{30,6},{31,7},{0,8},{1,9... | collective-permute-start | bytes 301064 | tf_op jit(solution)/shard_map/ppermute | solution.py:31
  99.3 8.4 %collective-permute-start.21 = (bf16[2,56,896]{2,1,0:T(8,128)(2,1)}, bf16[2,56,896]{2,1,0:T(8,128)(2,1)S(1)}, u32[]{:S(2)}, u32[]{:S(2)}) collective-permute-start(bf16[2,56,896]{2,1,0:T(8,128)(2,1)} %collective-permute-done.19), channel_id=1, source_target_pairs={{4,0},{5,1},{6,2},{7,3},{8,4},{9,5},{10,6},{11,7},{12,8},{13,9},{1... | collective-permute-start | bytes 602120 | tf_op jit(solution)/shard_map/ppermute | solution.py:31
  103.3 6.9 %collective-permute-start.22 = (bf16[2,56,896]{2,1,0:T(8,128)(2,1)S(1)}, bf16[2,56,896]{2,1,0:T(8,128)(2,1)S(1)}, u32[]{:S(2)}, u32[]{:S(2)}) collective-permute-start(bf16[2,56,896]{2,1,0:T(8,128)(2,1)S(1)} %collective-permute-done.20), channel_id=1, source_target_pairs={{28,0},{29,1},{30,2},{31,3},{0,4},{1,5},{2,6},{3,7},{4,8},{5,9},{6... | collective-permute-start | bytes 602120 | tf_op jit(solution)/shard_map/ppermute | solution.py:31
  110.3 3.5 %collective-permute-start.25 = (bf16[2,448,896]{2,1,0:T(8,128)(2,1)S(1)}, bf16[2,448,896]{2,1,0:T(8,128)(2,1)S(1)}, u32[]{:S(2)}, u32[]{:S(2)}) collective-permute-start(bf16[2,448,896]{2,1,0:T(8,128)(2,1)S(1)} %maximum_dynamic-update-slice_fusion.refs_0_.block_ref), channel_id=1, source_target_pairs={{0,1},{1,0},{2,3},{3,2},{4,5},{5,4},{6,7},{7,6},{8,9},{9,8},{10,11... | collective-permute-start | bytes 4816904 | tf_op jit(solution)/shard_map/ppermute | solution.py:44
  113.8 4.2 %copy-start.1 = (bf16[2,448,896]{2,1,0:T(8,128)(2,1)}, bf16[2,448,896]{2,1,0:T(8,128)(2,1)S(1)}, u32[]{:S(2)}) copy-start(bf16[2,448,896]{2,1,0:T(8,128)(2,1)S(1)} %collective-permute-done.25.refs_0_.got_ref) | copy-start | bytes 4816900
  118.1 1.0 copy-start.13
  119.1 14.3 %collective-permute-start.26 = (bf16[448,576]{1,0:T(8,128)(2,1)}, bf16[448,576]{1,0:T(8,128)(2,1)S(1)}, u32[]{:S(2)}, u32[]{:S(2)}) collective-permute-start(bf16[448,576]{1,0:T(8,128)(2,1)} %get-tuple-element.23.refs_0_), channel_id=1, source_target_pairs={{32,0},{64,32},{96,64},{0,96},{160,128},{192,160},{224,192},{128,2... | collective-permute-start | bytes 1548296 | tf_op jit(solution)/shard_map/ppermute | solution.py:22
  119.1 15.6 %collective-permute-start.27 = (bf16[448,576]{1,0:T(8,128)(2,1)}, bf16[448,576]{1,0:T(8,128)(2,1)S(1)}, u32[]{:S(2)}, u32[]{:S(2)}) collective-permute-start(bf16[448,576]{1,0:T(8,128)(2,1)} %get-tuple-element.23.refs_0_), channel_id=1, source_target_pairs={{96,0},{0,32},{32,64},{64,96},{224,128},{128,160},{160,192},{192,2... | collective-permute-start | bytes 1548296 | tf_op jit(solution)/shard_map/ppermute | solution.py:22
  121.1 17.7 %collective-permute-start.28 = (bf16[448,576]{1,0:T(8,128)(2,1)}, bf16[448,576]{1,0:T(8,128)(2,1)}, u32[]{:S(2)}, u32[]{:S(2)}) collective-permute-start(bf16[448,576]{1,0:T(8,128)(2,1)} %get-tuple-element.23.refs_0_), channel_id=1, source_target_pairs={{0,128},{32,160},{64,192},{96,224},{128,0},{160,32},{192,64},{224,... | collective-permute-start | bytes 1548296 | tf_op jit(solution)/shard_map/ppermute | solution.py:26
  133.4 6.2 %copy-start.7 = (bf16[448,576]{1,0:T(8,128)(2,1)}, bf16[448,576]{1,0:T(8,128)(2,1)S(1)}, u32[]{:S(2)}) copy-start(bf16[448,576]{1,0:T(8,128)(2,1)S(1)} %collective-permute-done.26.refs_1_) | copy-start | bytes 1548292
  134.6 5.1 %copy-start.9 = (bf16[448,576]{1,0:T(8,128)(2,1)}, bf16[448,576]{1,0:T(8,128)(2,1)S(1)}, u32[]{:S(2)}) copy-start(bf16[448,576]{1,0:T(8,128)(2,1)S(1)} %collective-permute-done.27.refs_2_) | copy-start | bytes 1548292
  138.0 20.2 %collective-permute-start.29 = (bf16[736,576]{0,1:T(8,128)(2,1)}, bf16[736,576]{0,1:T(8,128)(2,1)}, u32[]{:S(2)}, u32[]{:S(2)}) collective-permute-start(bf16[736,576]{0,1:T(8,128)(2,1)} %copy.2), channel_id=1, source_target_pairs={{0,128},{32,160},{64,192},{96,224},{128,0},{160,32},{192,64},{224,... | collective-permute-start | bytes 2543624 | tf_op jit(solution)/shard_map/ppermute | solution.py:26
  138.8 23.1 %collective-permute-start.32 = (bf16[448,576]{1,0:T(8,128)(2,1)}, bf16[448,576]{1,0:T(8,128)(2,1)}, u32[]{:S(2)}, u32[]{:S(2)}) collective-permute-start(bf16[448,576]{1,0:T(8,128)(2,1)} %collective-permute-done.28.refs_3_), channel_id=1, source_target_pairs={{64,0},{96,32},{0,64},{32,96},{192,128},{224,160},{128,192},{160,2... | collective-permute-start | bytes 1548296 | tf_op jit(solution)/shard_map/ppermute | solution.py:22
  141.7 18.5 %collective-permute-start.30 = (bf16[304,576]{1,0:T(8,128)(2,1)}, bf16[304,576]{1,0:T(8,128)(2,1)S(1)}, u32[]{:S(2)}, u32[]{:S(2)}) collective-permute-start(bf16[304,576]{1,0:T(8,128)(2,1)} %get-tuple-element.58), channel_id=1, source_target_pairs={{32,0},{64,32},{96,64},{0,96},{160,128},{192,160},{224,192},{128,2... | collective-permute-start | bytes 1050632 | tf_op jit(solution)/shard_map/ppermute | solution.py:22
  144.0 17.9 %collective-permute-start.31 = (bf16[304,576]{1,0:T(8,128)(2,1)}, bf16[304,576]{1,0:T(8,128)(2,1)}, u32[]{:S(2)}, u32[]{:S(2)}) collective-permute-start(bf16[304,576]{1,0:T(8,128)(2,1)} %get-tuple-element.57), channel_id=1, source_target_pairs={{96,0},{0,32},{32,64},{64,96},{224,128},{128,160},{160,192},{192,2... | collective-permute-start | bytes 1050632 | tf_op jit(solution)/shard_map/ppermute | solution.py:22
  161.9 1.4 copy-start.2
  163.3 1.1 copy-start.8
  164.3 1.1 copy-start.10
  165.4 1.3 copy-start.14
  (1 other events, 0.8 us)

commit v4 on v3

--- a/solution.py
+++ b/solution.py
@@ -80,8 +80,6 @@
             copies.append(pltpu.make_async_copy(x_refs[pick], rhs.at[pl.ds(at * rows, rows)], sems.at[at]))
         for copy in copies:
             copy.start()
-        for copy in copies:
-            copy.wait()
 
     @pl.when(core == (0 if mine else 1))
     def _():
@@ -91,9 +89,19 @@
     def _():
         run((2, 3, 6, 7))
 
-    for start in range(0, cols, 256):
-        part = pl.ds(start, min(256, cols - start))
-        value = dot(lhs[0], rhs[: 2 * rows, part]) + dot(lhs[1], rhs[2 * rows :, part])
+    def wait(at):
+        pltpu.make_async_copy(x_refs[at], rhs.at[pl.ds(at * rows, rows)], sems.at[at]).wait()
+
+    parts = [pl.ds(start, min(256, cols - start)) for start in range(0, cols, 256)]
+    pltpu.make_async_copy(block_ref, lhs, sems.at[4]).wait()
+    wait(0)
+    wait(1)
+    for part in parts:
+        found_ref[:, part] = dot(lhs[0], rhs[: 2 * rows, part])
+    wait(2)
+    wait(3)
+    for part in parts:
+        value = found_ref[:, part] + dot(lhs[1], rhs[2 * rows :, part])
         if not mine:
             value = before_ref[:, part] + value
             sent_ref[:, part] = value.astype(bf16)
@@ -120,27 +128,44 @@
     )(block, *x_blocks, *([] if mine else [before]))
 
 
+def open_kernel(block_ref, got_ref, own_y, right, found_ref, own_ref, begun_ref, lhs, rhs, sems):
+    rows, cols = own_ref.shape
+    core = lax.rem(lax.axis_index("narrow"), 2)
+    copies = [
+        pltpu.make_async_copy(block_ref.at[0], lhs.at[core], sems.at[0]),
+        pltpu.make_async_copy(got_ref.at[0], lhs.at[1 - core], sems.at[1]),
+        pltpu.make_async_copy(own_y, rhs.at[pl.ds(0, rows)], sems.at[2]),
+        pltpu.make_async_copy(right, rhs.at[pl.ds(rows, rows)], sems.at[3]),
+    ]
+    for copy in copies:
+        copy.start()
+    for copy in copies:
+        copy.wait()
+    for start in range(0, cols, 256):
+        part = pl.ds(start, min(256, cols - start))
+        value = coef_a * own_ref[:, part].astype(f32) + coef_b * found_ref[:, part]
+        begun_ref[:, part] = value + coef_c * dot(lhs[0], rhs[:, part])
+
+
 def close_kernel(few, block_ref, got_ref, *refs):
-    own_y, right, left, across, via_y, via_right, via_left, across_far = refs[:8]
-    found_ref, own_ref, out_ref, lhs, rhs, total, sems = refs[8:]
-    rows, cols = own_ref.shape
+    left, across, via_y, via_right, via_left, across_far = refs[:6]
+    begun_ref, out_ref, lhs, rhs, total, sems = refs[6:]
+    rows, cols = out_ref.shape
     half, more = rows // 2, rows - few
     core = lax.rem(lax.axis_index("narrow"), 2)
 
     pieces = [
         (block_ref, lhs.at[core]),
         (got_ref, lhs.at[1 - core]),
-        (own_y, 0),
-        (right, rows),
-        (left, 2 * rows),
-        (via_right.at[pl.ds(0, half)], 3 * rows),
-        (via_left.at[pl.ds(0, half)], 3 * rows + half),
-        (across, 4 * rows),
-        (via_right.at[pl.ds(half, few)], 5 * rows),
-        (via_y.at[pl.ds(0, more)], 5 * rows + few),
-        (via_left.at[pl.ds(half, few)], 6 * rows),
-        (via_y.at[pl.ds(more, more)], 6 * rows + few),
-        (across_far, 7 * rows),
+        (left, 0),
+        (via_right.at[pl.ds(0, half)], rows),
+        (via_left.at[pl.ds(0, half)], rows + half),
+        (across, 2 * rows),
+        (via_right.at[pl.ds(half, few)], 3 * rows),
+        (via_y.at[pl.ds(0, more)], 3 * rows + few),
+        (via_left.at[pl.ds(half, few)], 4 * rows),
+        (via_y.at[pl.ds(more, more)], 4 * rows + few),
+        (across_far, 5 * rows),
     ]
     copies = []
     for at, (source, place) in enumerate(pieces):
@@ -150,36 +175,53 @@
         copy.start()
     parts = [pl.ds(start, min(256, cols - start)) for start in range(0, cols, 256)]
     width = 2 * rows
-    for copy in copies[:7]:
+    for copy in copies[:5]:
         copy.wait()
     for part in parts:
-        total[:, part] = dot(lhs[0, 0], rhs[:width, part]) + dot(lhs[1, 0], rhs[width : 2 * width, part])
-    for copy in copies[7:]:
+        total[:, part] = dot(lhs[1, 0], rhs[:width, part])
+    for copy in copies[5:]:
         copy.wait()
     scale = float(COLS) ** 0.5
     for part in parts:
-        value = dot(lhs[0, 1], rhs[2 * width : 3 * width, part]) + dot(lhs[1, 1], rhs[3 * width :, part])
-        value = coef_b * found_ref[:, part] + coef_c * (total[:, part] + value)
-        out_ref[:, part] = (scale * (coef_a * own_ref[:, part].astype(f32) + value)).astype(bf16)
-
-
-def close(few, block, got, blocks, found, own):
+        value = dot(lhs[0, 1], rhs[width : 2 * width, part]) + dot(lhs[1, 1], rhs[2 * width :, part])
+        out_ref[:, part] = (scale * (begun_ref[:, part] + coef_c * (total[:, part] + value))).astype(bf16)
+
+
+def open_product(block, got, own_y, right, found, own):
     rows, cols = own.shape
+    vmem = pl.BlockSpec(memory_space=pltpu.VMEM)
+    return pl.pallas_call(
+        open_kernel,
+        out_shape=jax.ShapeDtypeStruct((rows, cols), f32),
+        in_specs=[pl.BlockSpec(memory_space=pl.ANY)] * 4 + [vmem, vmem],
+        out_specs=vmem,
+        scratch_shapes=[
+            pltpu.VMEM(block.shape, bf16),
+            pltpu.VMEM((2 * rows, cols), bf16),
+            pltpu.SemaphoreType.DMA((4,)),
+        ],
+        compiler_params=pltpu.CompilerParams(vmem_limit_bytes=12 * 2**20),
+        cost_estimate=pl.CostEstimate(flops=4 * rows * rows * cols, bytes_accessed=5 * 2**20, transcendentals=0),
+    )(block, got, own_y, right, found, own)
+
+
+def close_product(few, block, got, blocks, begun):
+    rows, cols = begun.shape
     vmem = pl.BlockSpec(memory_space=pltpu.VMEM)
     return pl.pallas_call(
         functools.partial(close_kernel, few),
         out_shape=jax.ShapeDtypeStruct((rows, cols), bf16),
-        in_specs=[pl.BlockSpec(memory_space=pl.ANY)] * 10 + [vmem, vmem],
+        in_specs=[pl.BlockSpec(memory_space=pltpu.HBM)] * 8 + [vmem],
         out_specs=vmem,
         scratch_shapes=[
             pltpu.VMEM((2, *block.shape), bf16),
-            pltpu.VMEM((8 * rows, cols), bf16),
+            pltpu.VMEM((6 * rows, cols), bf16),
             pltpu.VMEM((rows, cols), f32),
-            pltpu.SemaphoreType.DMA((13,)),
+            pltpu.SemaphoreType.DMA((11,)),
         ],
         compiler_params=pltpu.CompilerParams(vmem_limit_bytes=16 * 2**20),
-        cost_estimate=pl.CostEstimate(flops=16 * rows * rows * cols, bytes_accessed=10 * 2**20, transcendentals=0),
-    )(block, got, *blocks, found, own)
+        cost_estimate=pl.CostEstimate(flops=12 * rows * rows * cols, bytes_accessed=9 * 2**20, transcendentals=0),
+    )(block, got, *blocks, begun)
 
 
 def local(own):
@@ -242,12 +284,13 @@
     x_blocks = (own, x_right, x_left, x_far, across, other_right, other_left, other_far)
     found, sent = found_part(got, x_blocks, found_part(block, x_blocks))
     right, left, across = gather_first(sent)
-    half, few = rows // 2, 80
+    half, few = rows // 2, rows // 4
     via_y = from_y(cat(right[few:], left[few:]))
     via_right = from_x(cat(right[:half], across[:few]), 1)
     via_left = from_x(cat(left[half:], across[:few]), -1)
     across_far = from_x(across, 2)
-    return close(few, block, got, (sent, right, left, across, via_y, via_right, via_left, across_far), found, own)
+    begun = open_product(block, got, sent, right, found, own)
+    return close_product(few, block, got, (left, across, via_y, via_right, via_left, across_far), begun)
 
 
 def solution(mesh):

time: 175 us -> 167 us (0.954)
  local copies, waits for them, and re-layouts: 19.6 us -> 9.56 us
  waiting for transfers between devices: 91.1 us -> 96 us
    ppermute x11, waiting for transfers between devices: 33 us -> 52.4 us  [from_x(): return lax.ppermute(value, 'wide', pairs)]
    ppermute x5, waiting for transfers between devices: 14.2 us -> 0.01 us  [from_y(): return lax.ppermute(value, 'wide', [(w, (w + 4) % 8) for w in range(8)])]
    unnamed x43 -> x25, local copies, waits for them, and re-layouts: 8.1 us -> 3.2 us
    concatenate x4 -> x3, local copies, waits for them, and re-layouts: 2.41 us -> 0.18 us  [cat(): return jnp.concatenate(parts, axis=axis)]
    concatenate x2, other arithmetic: 2.14 us -> 0.15 us  [cat(): return jnp.concatenate(parts, axis=axis)]
    ppermute x1 -> x0, local copies, waits for them, and re-layouts: 1.93 us -> none  [from_y(): return lax.ppermute(value, 'wide', [(w, (w + 4) % 8) for w in range(8)])]
    pallas_call x1 -> x2, Pallas kernels: 5.64 us -> 6.12 us  [the longest x1 4.88 us: close_product(): pl.pallas_call(functools.partial(close_kernel, few), out_shape=jax.ShapeD...]
  transfers between devices with their start and end apart: 33 -> 33, of which waited for: 18 -> 18; matrix products, arithmetic and copies ran while one was open for 10% -> 6% of each run, Pallas kernels for 1% -> 2%
where the time goes in v4:
time: 167 us; the launch traced here: 164 us
  waiting for transfers between devices  96 us (57%)
  starting transfers between devices  40.1 us (24%)
  Pallas kernels  11.4 us (7%)
  local copies, waits for them, and re-layouts  9.56 us (6%)
  other arithmetic  3.8 us (2%)
  matrix products  3 us (2%)
    ppermute x11, waiting for transfers between devices, from_x(): return lax.ppermute(value, 'wide', pairs)  52.4 us
    ppermute x4, waiting for transfers between devices, along_z(): return lax.ppermute(value, 'narrow', pairs)  23.3 us
    ppermute x11, starting transfers between devices, from_x(): return lax.ppermute(value, 'wide', pairs)  13.7 us
    ppermute x8, waiting for transfers between devices, from_z(): return lax.ppermute(value, 'narrow', pairs)  11.7 us
    ppermute x8, starting transfers between devices, from_z(): return lax.ppermute(value, 'narrow', pairs)  11.5 us
    ppermute x4, starting transfers between devices, along_z(): return lax.ppermute(value, 'narrow', pairs)  7.48 us
    pallas_call x2, Pallas kernels, found_part(): pl.pallas_call(functools.partial(found_kernel, mine), out_shape=found if...  5.24 us
    pallas_call x1, Pallas kernels, close_product(): pl.pallas_call(functools.partial(close_kernel, few), out_shape=jax.ShapeD...  4.88 us
  transfers between devices with their start and end apart: 33, of which 18 were waited for; matrix products, arithmetic and copies ran while one was open for 6% of the time, Pallas kernels for 2%

profile of v4, /device:TPU:24, one launch (start us, length us, event | category | flops | bytes accessed | tf_op | source)
XLA Modules:
  0.0 164.4 jit_solution(3953985293498912931)
XLA Ops:
  0.0 2.8 %collective-permute-start.1 = (bf16[448,576]{1,0:T(8,128)(2,1)}, bf16[448,576]{1,0:T(8,128)(2,1)S(1)}, u32[]{:S(2)}, u32[]{:S(2)}) collective-permute-start(bf16[448,576]{1,0:T(8,128)(2,1)} %own_ref.1), channel_id=1, source_target_pairs={{32,0},{64,32},{96,64},{0,96},{160,128},{192,160},{224,192},{128,2... | collective-permute-start | bytes 1548296 | tf_op jit(solution)/shard_map/ppermute | solution.py:22
  3.5 1.2 constant_dynamic-update-slice_fusion.6
  4.7 10.6 %collective-permute-done.1.refs_2_ = bf16[448,576]{1,0:T(8,128)(2,1)S(1)} collective-permute-done((bf16[448,576]{1,0:T(8,128)(2,1)}, bf16[448,576]{1,0:T(8,128)(2,1)S(1)}, u32[]{:S(2)}, u32[]{:S(2)}) %collective-permute-start.1) | collective-permute-done | bytes 516128 | tf_op jit(solution)/shard_map/ppermute | solution.py:22
  15.3 3.7 %collective-permute-start.3 = (bf16[224,576]{1,0:T(8,128)(2,1)S(1)}, bf16[224,576]{1,0:T(8,128)(2,1)S(1)}, u32[]{:S(2)}, u32[]{:S(2)}) collective-permute-start(bf16[224,576]{1,0:T(8,128)(2,1)S(1)} %slice.78), channel_id=1, source_target_pairs={{32,0},{64,32},{96,64},{0,96},{160,128},{192,160},{224,192},{128,2... | collective-permute-start | bytes 774152 | tf_op jit(solution)/shard_map/ppermute | solution.py:22
  19.7 4.5 %collective-permute-done.3 = bf16[224,576]{1,0:T(8,128)(2,1)S(1)} collective-permute-done((bf16[224,576]{1,0:T(8,128)(2,1)S(1)}, bf16[224,576]{1,0:T(8,128)(2,1)S(1)}, u32[]{:S(2)}, u32[]{:S(2)}) %collective-permute-start.3) | collective-permute-done | bytes 258080 | tf_op jit(solution)/shard_map/ppermute | solution.py:22
  24.3 3.5 %collective-permute-done.4 = bf16[224,576]{1,0:T(8,128)(2,1)S(1)} collective-permute-done((bf16[224,576]{1,0:T(8,128)(2,1)S(1)}, bf16[224,576]{1,0:T(8,128)(2,1)S(1)}, u32[]{:S(2)}, u32[]{:S(2)}) %collective-permute-start.4) | collective-permute-done | bytes 258080 | tf_op jit(solution)/shard_map/ppermute | solution.py:22
  27.8 1.5 convolution_convert_fusion
  29.4 1.5 fusion.6
  30.9 1.9 %collective-permute-done.5 = bf16[448,1792]{1,0:T(8,128)(2,1)S(1)} collective-permute-done((bf16[448,1792]{1,0:T(8,128)(2,1)S(1)}, bf16[448,1792]{1,0:T(8,128)(2,1)S(1)}, u32[]{:S(2)}, u32[]{:S(2)}) %collective-permute-start.5) | collective-permute-done | bytes 1605664 | tf_op jit(solution)/shard_map/ppermute | solution.py:44
  33.2 0.9 fusion.4
  34.1 1.9 %collective-permute-start.6 = (bf16[112,1792]{1,0:T(8,128)(2,1)S(1)}, bf16[112,1792]{1,0:T(8,128)(2,1)S(1)}, u32[]{:S(2)}, u32[]{:S(2)}) collective-permute-start(bf16[112,1792]{1,0:T(8,128)(2,1)S(1)} %get-tuple-element.28), channel_id=1, source_target_pairs={{0,4},{1,29},{2,6},{3,31},{4,8},{5,1},{6,10},{7,3},{8,12},{9,5},{1... | collective-permute-start | bytes 1204232 | tf_op jit(solution)/shard_map/ppermute | solution.py:65
  36.0 3.3 %collective-permute-start.7 = (bf16[56,1792]{1,0:T(8,128)(2,1)S(1)}, bf16[56,1792]{1,0:T(8,128)(2,1)S(1)}, u32[]{:S(2)}, u32[]{:S(2)}) collective-permute-start(bf16[56,1792]{1,0:T(8,128)(2,1)S(1)} %slice.82), channel_id=1, source_target_pairs={{0,8},{1,25},{2,10},{3,27},{4,12},{5,29},{6,14},{7,31},{8,16},{9,1... | collective-permute-start | bytes 602120 | tf_op jit(solution)/shard_map/ppermute | solution.py:65
  39.4 10.6 %collective-permute-done.7 = bf16[56,1792]{1,0:T(8,128)(2,1)S(1)} collective-permute-done((bf16[56,1792]{1,0:T(8,128)(2,1)S(1)}, bf16[56,1792]{1,0:T(8,128)(2,1)S(1)}, u32[]{:S(2)}, u32[]{:S(2)}) %collective-permute-start.7) | collective-permute-done | bytes 200736 | tf_op jit(solution)/shard_map/ppermute | solution.py:65
  50.2 2.1 %collective-permute-start.9 = (bf16[112,1792]{1,0:T(8,128)(2,1)}, bf16[112,1792]{1,0:T(8,128)(2,1)}, u32[]{:S(2)}, u32[]{:S(2)}) collective-permute-start(bf16[112,1792]{1,0:T(8,128)(2,1)} %get-tuple-element.16), channel_id=1, source_target_pairs={{0,4},{1,29},{2,6},{3,31},{4,8},{5,1},{6,10},{7,3},{8,12},{9,5},{1... | collective-permute-start | bytes 1204232 | tf_op jit(solution)/shard_map/ppermute | solution.py:65
  52.6 1.8 %collective-permute-start.11 = (bf16[448,576]{1,0:T(8,128)(2,1)S(1)}, bf16[448,576]{1,0:T(8,128)(2,1)}, u32[]{:S(2)}, u32[]{:S(2)}) collective-permute-start(bf16[448,576]{1,0:T(8,128)(2,1)S(1)} %collective-permute-done.refs_5_), channel_id=1, source_target_pairs={{96,0},{0,32},{32,64},{64,96},{224,128},{128,160},{160,192},{192,2... | collective-permute-start | bytes 1548296 | tf_op jit(solution)/shard_map/ppermute | solution.py:22
  55.1 1.0 slice.84
  56.1 8.5 %collective-permute-done.8 = bf16[112,1792]{1,0:T(8,128)(2,1)} collective-permute-done((bf16[112,1792]{1,0:T(8,128)(2,1)S(1)}, bf16[112,1792]{1,0:T(8,128)(2,1)}, u32[]{:S(2)}, u32[]{:S(2)}) %collective-permute-start.8) | collective-permute-done | bytes 401440 | tf_op jit(solution)/shard_map/ppermute | solution.py:65
  64.7 4.2 %collective-permute-done.9 = bf16[112,1792]{1,0:T(8,128)(2,1)} collective-permute-done((bf16[112,1792]{1,0:T(8,128)(2,1)}, bf16[112,1792]{1,0:T(8,128)(2,1)}, u32[]{:S(2)}, u32[]{:S(2)}) %collective-permute-start.9) | collective-permute-done | bytes 401440 | tf_op jit(solution)/shard_map/ppermute | solution.py:65
  68.9 1.2 pad_add_fusion
  70.9 0.9 copy-done.6
  72.0 1.4 collective-permute-done.13
  73.4 1.0 add_convert_fusion
  74.5 1.3 collective-permute-start.14
  75.8 2.9 %collective-permute-start.16 = (bf16[56,896]{1,0:T(8,128)(2,1)S(1)}, bf16[56,896]{1,0:T(8,128)(2,1)S(1)}, u32[]{:S(2)}, u32[]{:S(2)}) collective-permute-start(bf16[56,896]{1,0:T(8,128)(2,1)S(1)} %get-tuple-element.56), channel_id=1, source_target_pairs={{0,130},{1,131},{2,128},{3,129},{4,134},{5,135},{6,132},{7,133},{8... | collective-permute-start | bytes 301064 | tf_op jit(solution)/shard_map/ppermute | solution.py:40
  78.7 3.1 %collective-permute-done.14 = bf16[56,896]{1,0:T(8,128)(2,1)S(1)} collective-permute-done((bf16[56,896]{1,0:T(8,128)(2,1)S(1)}, bf16[56,896]{1,0:T(8,128)(2,1)S(1)}, u32[]{:S(2)}, u32[]{:S(2)}) %collective-permute-start.14) | collective-permute-done | bytes 100384 | tf_op jit(solution)/shard_map/ppermute | solution.py:35
  81.8 1.3 collective-permute-done.16
  84.0 2.9 %collective-permute-start.20 = (bf16[2,56,896]{2,1,0:T(8,128)(2,1)}, bf16[2,56,896]{2,1,0:T(8,128)(2,1)S(1)}, u32[]{:S(2)}, u32[]{:S(2)}) collective-permute-start(bf16[2,56,896]{2,1,0:T(8,128)(2,1)} %get-tuple-element.53), channel_id=1, source_target_pairs={{24,0},{25,1},{26,2},{27,3},{28,4},{29,5},{30,6},{31,7},{0,8},{1,9... | collective-permute-start | bytes 602120 | tf_op jit(solution)/shard_map/ppermute | solution.py:31
  86.9 1.8 %collective-permute-start.17 = (bf16[2,56,896]{2,1,0:T(8,128)(2,1)}, bf16[2,56,896]{2,1,0:T(8,128)(2,1)}, u32[]{:S(2)}, u32[]{:S(2)}) collective-permute-start(bf16[2,56,896]{2,1,0:T(8,128)(2,1)} %get-tuple-element.53), channel_id=1, source_target_pairs={{4,0},{5,1},{6,2},{7,3},{8,4},{9,5},{10,6},{11,7},{12,8},{13,9},{1... | collective-permute-start | bytes 602120 | tf_op jit(solution)/shard_map/ppermute | solution.py:31
  88.9 7.7 %collective-permute-done.19 = bf16[2,56,896]{2,1,0:T(8,128)(2,1)} collective-permute-done((bf16[2,56,896]{2,1,0:T(8,128)(2,1)}, bf16[2,56,896]{2,1,0:T(8,128)(2,1)}, u32[]{:S(2)}, u32[]{:S(2)}) %collective-permute-start.19) | collective-permute-done | bytes 200736 | tf_op jit(solution)/shard_map/ppermute | solution.py:31
  96.7 0.9 slice.87
  97.6 1.3 collective-permute-start.23
  98.9 1.7 %collective-permute-start.24 = (bf16[1,56,896]{2,1,0:T(8,128)(2,1)S(1)}, bf16[1,56,896]{2,1,0:T(8,128)(2,1)S(1)}, u32[]{:S(2)}, u32[]{:S(2)}) collective-permute-start(bf16[1,56,896]{2,1,0:T(8,128)(2,1)S(1)} %slice.88), channel_id=1, source_target_pairs={{24,0},{25,1},{26,2},{27,3},{28,4},{29,5},{30,6},{31,7},{0,8},{1,9... | collective-permute-start | bytes 301064 | tf_op jit(solution)/shard_map/ppermute | solution.py:31
  100.7 3.5 %collective-permute-start.21 = (bf16[2,56,896]{2,1,0:T(8,128)(2,1)}, bf16[2,56,896]{2,1,0:T(8,128)(2,1)S(1)}, u32[]{:S(2)}, u32[]{:S(2)}) collective-permute-start(bf16[2,56,896]{2,1,0:T(8,128)(2,1)} %collective-permute-done.19), channel_id=1, source_target_pairs={{4,0},{5,1},{6,2},{7,3},{8,4},{9,5},{10,6},{11,7},{12,8},{13,9},{1... | collective-permute-start | bytes 602120 | tf_op jit(solution)/shard_map/ppermute | solution.py:31
  104.2 1.0 constant_dynamic-update-slice_fusion.14
  105.1 1.0 constant_dynamic-update-slice_fusion.13
  106.1 1.0 constant_dynamic-update-slice_fusion.12
  107.1 1.5 collective-permute-done.21
  108.7 2.4 %collective-permute-done.22 = bf16[2,56,896]{2,1,0:T(8,128)(2,1)S(1)} collective-permute-done((bf16[2,56,896]{2,1,0:T(8,128)(2,1)S(1)}, bf16[2,56,896]{2,1,0:T(8,128)(2,1)S(1)}, u32[]{:S(2)}, u32[]{:S(2)}) %collective-permute-start.22) | collective-permute-done | bytes 200736 | tf_op jit(solution)/shard_map/ppermute | solution.py:31
  111.3 2.6 %shard_map.17.refs_9_ = f32[448,576]{1,0:T(8,128)S(1)} custom-call(bf16[2,448,896]{2,1,0:T(8,128)(2,1)S(1)} %maximum_dynamic-update-slice_fusion.refs_0_.block_ref, bf16[448,576]{1,0:T(8,128)(2,1)S(1)} %copy-done, bf16[448,576]{1,0:T(8,128)(2,1)S(1)} %collective-permute-done.1.refs_2_, bf16[448,576]{1,0:T(8,128)(2,1)S(1)} %collective-permute-done.2.refs_3_, ...), custom_call_target="tpu_custom_call" | custom-call | flops 924844032 | bytes 6291456 | tf_op jit(solution)/shard_map/pallas_call | solution.py:116
  114.7 2.6 %shard_map.18 = (f32[448,576]{1,0:T(8,128)S(1)}, bf16[448,576]{1,0:T(8,128)(2,1)S(1)}) custom-call(bf16[2,448,896]{2,1,0:T(8,128)(2,1)S(1)} %collective-permute-done.25.refs_0_.got_ref, bf16[448,576]{1,0:T(8,128)(2,1)S(1)} %copy-done, bf16[448,576]{1,0:T(8,128)(2,1)S(1)} %collective-permute-done.1.refs_2_, ...), custom_call_target="tpu_custom_call" | custom-call | flops 924844032 | bytes 6291456 | tf_op jit(solution)/shard_map/pallas_call | solution.py:116
  118.1 1.4 collective-permute-start.26
  120.2 12.3 %collective-permute-done.28.right = bf16[448,576]{1,0:T(8,128)(2,1)S(1)} collective-permute-done((bf16[448,576]{1,0:T(8,128)(2,1)S(1)}, bf16[448,576]{1,0:T(8,128)(2,1)S(1)}, u32[]{:S(2)}, u32[]{:S(2)}) %collective-permute-start.28) | collective-permute-done | bytes 516128 | tf_op jit(solution)/shard_map/ppermute | solution.py:22
  132.5 1.6 collective-permute-done.26.refs_0_
  135.7 2.4 %collective-permute-start.30 = (bf16[336,576]{1,0:T(8,128)(2,1)S(1)}, bf16[336,576]{1,0:T(8,128)(2,1)S(1)}, u32[]{:S(2)}, u32[]{:S(2)}) collective-permute-start(bf16[336,576]{1,0:T(8,128)(2,1)S(1)} %get-tuple-element.58), channel_id=1, source_target_pairs={{32,0},{64,32},{96,64},{0,96},{160,128},{192,160},{224,192},{128,2... | collective-permute-start | bytes 1161224 | tf_op jit(solution)/shard_map/ppermute | solution.py:22
  138.1 1.2 shard_map.19.refs_6_
  139.4 18.1 %collective-permute-done.30.refs_3_ = bf16[336,576]{1,0:T(8,128)(2,1)S(1)} collective-permute-done((bf16[336,576]{1,0:T(8,128)(2,1)S(1)}, bf16[336,576]{1,0:T(8,128)(2,1)S(1)}, u32[]{:S(2)}, u32[]{:S(2)}) %collective-permute-start.30) | collective-permute-done | bytes 387104 | tf_op jit(solution)/shard_map/ppermute | solution.py:22
  157.5 1.9 %collective-permute-done.31.refs_4_ = bf16[336,576]{1,0:T(8,128)(2,1)S(1)} collective-permute-done((bf16[336,576]{1,0:T(8,128)(2,1)S(1)}, bf16[336,576]{1,0:T(8,128)(2,1)S(1)}, u32[]{:S(2)}, u32[]{:S(2)}) %collective-permute-start.31) | collective-permute-done | bytes 387104 | tf_op jit(solution)/shard_map/ppermute | solution.py:22
  159.4 4.9 %shard_map.20 = bf16[448,576]{1,0:T(8,128)(2,1)} custom-call(bf16[2,448,896]{2,1,0:T(8,128)(2,1)S(1)} %maximum_dynamic-update-slice_fusion.refs_0_.block_ref, bf16[2,448,896]{2,1,0:T(8,128)(2,1)S(1)} %collective-permute-done.25.refs_0_.got_ref, bf16[448,576]{1,0:T(8,128)(2,1)S(1)} %collective-permute-done.26.refs_0_, ...), custom_call_target="tpu_custom_call" | custom-call | flops 1387266048 | bytes 9437184 | tf_op jit(solution)/shard_map/pallas_call | solution.py:211
  (85 shorter events, 9.4 us)
Async XLA Ops:
  0.0 15.3 %collective-permute-start.1 = (bf16[448,576]{1,0:T(8,128)(2,1)}, bf16[448,576]{1,0:T(8,128)(2,1)S(1)}, u32[]{:S(2)}, u32[]{:S(2)}) collective-permute-start(bf16[448,576]{1,0:T(8,128)(2,1)} %own_ref.1), channel_id=1, source_target_pairs={{32,0},{64,32},{96,64},{0,96},{160,128},{192,160},{224,192},{128,2... | collective-permute-start | bytes 1548296 | tf_op jit(solution)/shard_map/ppermute | solution.py:22
  2.8 16.2 %collective-permute-start.2 = (bf16[448,576]{1,0:T(8,128)(2,1)}, bf16[448,576]{1,0:T(8,128)(2,1)S(1)}, u32[]{:S(2)}, u32[]{:S(2)}) collective-permute-start(bf16[448,576]{1,0:T(8,128)(2,1)} %own_ref.1), channel_id=1, source_target_pairs={{96,0},{0,32},{32,64},{64,96},{224,128},{128,160},{160,192},{192,2... | collective-permute-start | bytes 1548296 | tf_op jit(solution)/shard_map/ppermute | solution.py:22
  2.8 16.4 %collective-permute-start = (bf16[448,576]{1,0:T(8,128)(2,1)}, bf16[448,576]{1,0:T(8,128)(2,1)S(1)}, u32[]{:S(2)}, u32[]{:S(2)}) collective-permute-start(bf16[448,576]{1,0:T(8,128)(2,1)} %own_ref.1), channel_id=1, source_target_pairs={{0,128},{32,160},{64,192},{96,224},{128,0},{160,32},{192,64},{224,... | collective-permute-start | bytes 1548296 | tf_op jit(solution)/shard_map/ppermute | solution.py:26
  15.3 8.9 %collective-permute-start.3 = (bf16[224,576]{1,0:T(8,128)(2,1)S(1)}, bf16[224,576]{1,0:T(8,128)(2,1)S(1)}, u32[]{:S(2)}, u32[]{:S(2)}) collective-permute-start(bf16[224,576]{1,0:T(8,128)(2,1)S(1)} %slice.78), channel_id=1, source_target_pairs={{32,0},{64,32},{96,64},{0,96},{160,128},{192,160},{224,192},{128,2... | collective-permute-start | bytes 774152 | tf_op jit(solution)/shard_map/ppermute | solution.py:22
  19.0 8.7 %collective-permute-start.4 = (bf16[224,576]{1,0:T(8,128)(2,1)S(1)}, bf16[224,576]{1,0:T(8,128)(2,1)S(1)}, u32[]{:S(2)}, u32[]{:S(2)}) collective-permute-start(bf16[224,576]{1,0:T(8,128)(2,1)S(1)} %slice.79), channel_id=1, source_target_pairs={{96,0},{0,32},{32,64},{64,96},{224,128},{128,160},{160,192},{192,2... | collective-permute-start | bytes 774152 | tf_op jit(solution)/shard_map/ppermute | solution.py:22
  27.8 26.5 %copy-start.1 = (bf16[448,576]{1,0:T(8,128)(2,1)}, bf16[448,576]{1,0:T(8,128)(2,1)S(1)}, u32[]{:S(2)}) copy-start(bf16[448,576]{1,0:T(8,128)(2,1)S(1)} %get-tuple-element.18.refs_4_) | copy-start | bytes 1548292
  29.3 3.5 %collective-permute-start.5 = (bf16[448,1792]{1,0:T(8,128)(2,1)S(1)}, bf16[448,1792]{1,0:T(8,128)(2,1)S(1)}, u32[]{:S(2)}, u32[]{:S(2)}) collective-permute-start(bf16[448,1792]{1,0:T(8,128)(2,1)S(1)} %convolution_convert_fusion), channel_id=1, source_target_pairs={{0,1},{1,0},{2,3},{3,2},{4,5},{5,4},{6,7},{7,6},{8,9},{9,8},{10,11... | collective-permute-start | bytes 4816904 | tf_op jit(solution)/shard_map/ppermute | solution.py:44
  33.2 16.9 %copy-start.5 = (f32[448,1792]{1,0:T(8,128)}, f32[448,1792]{1,0:T(8,128)S(1)}, u32[]{:S(2)}) copy-start(f32[448,1792]{1,0:T(8,128)S(1)} %get-tuple-element.26) | copy-start | bytes 9633796
  34.1 15.9 %collective-permute-start.6 = (bf16[112,1792]{1,0:T(8,128)(2,1)S(1)}, bf16[112,1792]{1,0:T(8,128)(2,1)S(1)}, u32[]{:S(2)}, u32[]{:S(2)}) collective-permute-start(bf16[112,1792]{1,0:T(8,128)(2,1)S(1)} %get-tuple-element.28), channel_id=1, source_target_pairs={{0,4},{1,29},{2,6},{3,31},{4,8},{5,1},{6,10},{7,3},{8,12},{9,5},{1... | collective-permute-start | bytes 1204232 | tf_op jit(solution)/shard_map/ppermute | solution.py:65
  36.0 13.9 %collective-permute-start.7 = (bf16[56,1792]{1,0:T(8,128)(2,1)S(1)}, bf16[56,1792]{1,0:T(8,128)(2,1)S(1)}, u32[]{:S(2)}, u32[]{:S(2)}) collective-permute-start(bf16[56,1792]{1,0:T(8,128)(2,1)S(1)} %slice.82), channel_id=1, source_target_pairs={{0,8},{1,25},{2,10},{3,27},{4,12},{5,29},{6,14},{7,31},{8,16},{9,1... | collective-permute-start | bytes 602120 | tf_op jit(solution)/shard_map/ppermute | solution.py:65
  50.1 14.6 %collective-permute-start.8 = (bf16[112,1792]{1,0:T(8,128)(2,1)S(1)}, bf16[112,1792]{1,0:T(8,128)(2,1)}, u32[]{:S(2)}, u32[]{:S(2)}) collective-permute-start(bf16[112,1792]{1,0:T(8,128)(2,1)S(1)} %fusion), channel_id=1, source_target_pairs={{0,8},{1,25},{2,10},{3,27},{4,12},{5,29},{6,14},{7,31},{8,16},{9,1... | collective-permute-start | bytes 1204232 | tf_op jit(solution)/shard_map/ppermute | solution.py:65
  50.2 18.7 %collective-permute-start.9 = (bf16[112,1792]{1,0:T(8,128)(2,1)}, bf16[112,1792]{1,0:T(8,128)(2,1)}, u32[]{:S(2)}, u32[]{:S(2)}) collective-permute-start(bf16[112,1792]{1,0:T(8,128)(2,1)} %get-tuple-element.16), channel_id=1, source_target_pairs={{0,4},{1,29},{2,6},{3,31},{4,8},{5,1},{6,10},{7,3},{8,12},{9,5},{1... | collective-permute-start | bytes 1204232 | tf_op jit(solution)/shard_map/ppermute | solution.py:65
  52.3 17.8 %collective-permute-start.10 = (bf16[448,576]{1,0:T(8,128)(2,1)S(1)}, bf16[448,576]{1,0:T(8,128)(2,1)S(1)}, u32[]{:S(2)}, u32[]{:S(2)}) collective-permute-start(bf16[448,576]{1,0:T(8,128)(2,1)S(1)} %collective-permute-done.refs_5_), channel_id=1, source_target_pairs={{32,0},{64,32},{96,64},{0,96},{160,128},{192,160},{224,192},{128,2... | collective-permute-start | bytes 1548296 | tf_op jit(solution)/shard_map/ppermute | solution.py:22
  52.6 17.5 %collective-permute-start.11 = (bf16[448,576]{1,0:T(8,128)(2,1)S(1)}, bf16[448,576]{1,0:T(8,128)(2,1)}, u32[]{:S(2)}, u32[]{:S(2)}) collective-permute-start(bf16[448,576]{1,0:T(8,128)(2,1)S(1)} %collective-permute-done.refs_5_), channel_id=1, source_target_pairs={{96,0},{0,32},{32,64},{64,96},{224,128},{128,160},{160,192},{192,2... | collective-permute-start | bytes 1548296 | tf_op jit(solution)/shard_map/ppermute | solution.py:22
  54.4 15.8 %collective-permute-start.12 = (bf16[448,576]{1,0:T(8,128)(2,1)S(1)}, bf16[448,576]{1,0:T(8,128)(2,1)}, u32[]{:S(2)}, u32[]{:S(2)}) collective-permute-start(bf16[448,576]{1,0:T(8,128)(2,1)S(1)} %get-tuple-element.18.refs_4_), channel_id=1, source_target_pairs={{0,128},{32,160},{64,192},{96,224},{128,0},{160,32},{192,64},{224,... | collective-permute-start | bytes 1548296 | tf_op jit(solution)/shard_map/ppermute | solution.py:26
  70.1 0.8 copy-start.3
  70.9 0.9 copy-start.6
  71.9 1.5 collective-permute-start.13
  74.5 7.3 %collective-permute-start.14 = (bf16[56,896]{1,0:T(8,128)(2,1)S(1)}, bf16[56,896]{1,0:T(8,128)(2,1)S(1)}, u32[]{:S(2)}, u32[]{:S(2)}) collective-permute-start(bf16[56,896]{1,0:T(8,128)(2,1)S(1)} %get-tuple-element.55), channel_id=1, source_target_pairs={{0,2},{1,3},{2,0},{3,1},{4,6},{5,7},{6,4},{7,5},{8,10},{9,11},{10,... | collective-permute-start | bytes 301064 | tf_op jit(solution)/shard_map/ppermute | solution.py:35
  75.8 6.0 %collective-permute-start.15 = (bf16[56,896]{1,0:T(8,128)(2,1)S(1)}, bf16[56,896]{1,0:T(8,128)(2,1)S(1)}, u32[]{:S(2)}, u32[]{:S(2)}) collective-permute-start(bf16[56,896]{1,0:T(8,128)(2,1)S(1)} %get-tuple-element.56), channel_id=1, source_target_pairs={{0,128},{32,160},{64,192},{96,224},{128,0},{160,32},{192,64},{224,... | collective-permute-start | bytes 301064 | tf_op jit(solution)/shard_map/ppermute | solution.py:26
  75.8 7.3 %collective-permute-start.16 = (bf16[56,896]{1,0:T(8,128)(2,1)S(1)}, bf16[56,896]{1,0:T(8,128)(2,1)S(1)}, u32[]{:S(2)}, u32[]{:S(2)}) collective-permute-start(bf16[56,896]{1,0:T(8,128)(2,1)S(1)} %get-tuple-element.56), channel_id=1, source_target_pairs={{0,130},{1,131},{2,128},{3,129},{4,134},{5,135},{6,132},{7,133},{8... | collective-permute-start | bytes 301064 | tf_op jit(solution)/shard_map/ppermute | solution.py:40
  84.0 12.7 %collective-permute-start.19 = (bf16[2,56,896]{2,1,0:T(8,128)(2,1)}, bf16[2,56,896]{2,1,0:T(8,128)(2,1)}, u32[]{:S(2)}, u32[]{:S(2)}) collective-permute-start(bf16[2,56,896]{2,1,0:T(8,128)(2,1)} %get-tuple-element.53), channel_id=1, source_target_pairs={{8,0},{9,1},{10,2},{11,3},{12,4},{13,5},{14,6},{15,7},{16,8},{17,9... | collective-permute-start | bytes 602120 | tf_op jit(solution)/shard_map/ppermute | solution.py:31
  84.0 15.0 %collective-permute-start.20 = (bf16[2,56,896]{2,1,0:T(8,128)(2,1)}, bf16[2,56,896]{2,1,0:T(8,128)(2,1)S(1)}, u32[]{:S(2)}, u32[]{:S(2)}) collective-permute-start(bf16[2,56,896]{2,1,0:T(8,128)(2,1)} %get-tuple-element.53), channel_id=1, source_target_pairs={{24,0},{25,1},{26,2},{27,3},{28,4},{29,5},{30,6},{31,7},{0,8},{1,9... | collective-permute-start | bytes 602120 | tf_op jit(solution)/shard_map/ppermute | solution.py:31
  86.9 17.3 %collective-permute-start.17 = (bf16[2,56,896]{2,1,0:T(8,128)(2,1)}, bf16[2,56,896]{2,1,0:T(8,128)(2,1)}, u32[]{:S(2)}, u32[]{:S(2)}) collective-permute-start(bf16[2,56,896]{2,1,0:T(8,128)(2,1)} %get-tuple-element.53), channel_id=1, source_target_pairs={{4,0},{5,1},{6,2},{7,3},{8,4},{9,5},{10,6},{11,7},{12,8},{13,9},{1... | collective-permute-start | bytes 602120 | tf_op jit(solution)/shard_map/ppermute | solution.py:31
  88.7 16.5 %collective-permute-start.18 = (bf16[2,56,896]{2,1,0:T(8,128)(2,1)}, bf16[2,56,896]{2,1,0:T(8,128)(2,1)}, u32[]{:S(2)}, u32[]{:S(2)}) collective-permute-start(bf16[2,56,896]{2,1,0:T(8,128)(2,1)} %get-tuple-element.53), channel_id=1, source_target_pairs={{28,0},{29,1},{30,2},{31,3},{0,4},{1,5},{2,6},{3,7},{4,8},{5,9},{6... | collective-permute-start | bytes 602120 | tf_op jit(solution)/shard_map/ppermute | solution.py:31
  88.9 22.4 %copy-start = (bf16[448,576]{1,0:T(8,128)(2,1)S(1)}, bf16[448,576]{1,0:T(8,128)(2,1)}, u32[]{:S(2)}) copy-start(bf16[448,576]{1,0:T(8,128)(2,1)} %own_ref.1) | copy-start | bytes 1548292
  88.9 22.4 %copy-start.2 = (bf16[448,576]{1,0:T(8,128)(2,1)S(1)}, bf16[448,576]{1,0:T(8,128)(2,1)}, u32[]{:S(2)}) copy-start(bf16[448,576]{1,0:T(8,128)(2,1)} %copy-done.1) | copy-start | bytes 1548292
  88.9 22.4 %copy-start.4 = (bf16[448,576]{1,0:T(8,128)(2,1)S(1)}, bf16[448,576]{1,0:T(8,128)(2,1)}, u32[]{:S(2)}) copy-start(bf16[448,576]{1,0:T(8,128)(2,1)} %copy-done.3) | copy-start | bytes 1548292
  97.6 13.5 %collective-permute-start.23 = (bf16[1,56,896]{2,1,0:T(8,128)(2,1)S(1)}, bf16[1,56,896]{2,1,0:T(8,128)(2,1)S(1)}, u32[]{:S(2)}, u32[]{:S(2)}) collective-permute-start(bf16[1,56,896]{2,1,0:T(8,128)(2,1)S(1)} %slice.87), channel_id=1, source_target_pairs={{8,0},{9,1},{10,2},{11,3},{12,4},{13,5},{14,6},{15,7},{16,8},{17,9... | collective-permute-start | bytes 301064 | tf_op jit(solution)/shard_map/ppermute | solution.py:31
  98.9 12.2 %collective-permute-start.24 = (bf16[1,56,896]{2,1,0:T(8,128)(2,1)S(1)}, bf16[1,56,896]{2,1,0:T(8,128)(2,1)S(1)}, u32[]{:S(2)}, u32[]{:S(2)}) collective-permute-start(bf16[1,56,896]{2,1,0:T(8,128)(2,1)S(1)} %slice.88), channel_id=1, source_target_pairs={{24,0},{25,1},{26,2},{27,3},{28,4},{29,5},{30,6},{31,7},{0,8},{1,9... | collective-permute-start | bytes 301064 | tf_op jit(solution)/shard_map/ppermute | solution.py:31
  100.7 8.0 %collective-permute-start.21 = (bf16[2,56,896]{2,1,0:T(8,128)(2,1)}, bf16[2,56,896]{2,1,0:T(8,128)(2,1)S(1)}, u32[]{:S(2)}, u32[]{:S(2)}) collective-permute-start(bf16[2,56,896]{2,1,0:T(8,128)(2,1)} %collective-permute-done.19), channel_id=1, source_target_pairs={{4,0},{5,1},{6,2},{7,3},{8,4},{9,5},{10,6},{11,7},{12,8},{13,9},{1... | collective-permute-start | bytes 602120 | tf_op jit(solution)/shard_map/ppermute | solution.py:31
  104.2 6.9 %collective-permute-start.22 = (bf16[2,56,896]{2,1,0:T(8,128)(2,1)S(1)}, bf16[2,56,896]{2,1,0:T(8,128)(2,1)S(1)}, u32[]{:S(2)}, u32[]{:S(2)}) collective-permute-start(bf16[2,56,896]{2,1,0:T(8,128)(2,1)S(1)} %collective-permute-done.20), channel_id=1, source_target_pairs={{28,0},{29,1},{30,2},{31,3},{0,4},{1,5},{2,6},{3,7},{4,8},{5,9},{6... | collective-permute-start | bytes 602120 | tf_op jit(solution)/shard_map/ppermute | solution.py:31
  111.2 3.5 %collective-permute-start.25 = (bf16[2,448,896]{2,1,0:T(8,128)(2,1)S(1)}, bf16[2,448,896]{2,1,0:T(8,128)(2,1)S(1)}, u32[]{:S(2)}, u32[]{:S(2)}) collective-permute-start(bf16[2,448,896]{2,1,0:T(8,128)(2,1)S(1)} %maximum_dynamic-update-slice_fusion.refs_0_.block_ref), channel_id=1, source_target_pairs={{0,1},{1,0},{2,3},{3,2},{4,5},{5,4},{6,7},{7,6},{8,9},{9,8},{10,11... | collective-permute-start | bytes 4816904 | tf_op jit(solution)/shard_map/ppermute | solution.py:44
  117.4 15.1 %collective-permute-start.28 = (bf16[448,576]{1,0:T(8,128)(2,1)S(1)}, bf16[448,576]{1,0:T(8,128)(2,1)S(1)}, u32[]{:S(2)}, u32[]{:S(2)}) collective-permute-start(bf16[448,576]{1,0:T(8,128)(2,1)S(1)} %get-tuple-element.23.own_y), channel_id=1, source_target_pairs={{32,0},{64,32},{96,64},{0,96},{160,128},{192,160},{224,192},{128,2... | collective-permute-start | bytes 1548296 | tf_op jit(solution)/shard_map/ppermute | solution.py:22
  118.1 15.9 %collective-permute-start.26 = (bf16[448,576]{1,0:T(8,128)(2,1)S(1)}, bf16[448,576]{1,0:T(8,128)(2,1)S(1)}, u32[]{:S(2)}, u32[]{:S(2)}) collective-permute-start(bf16[448,576]{1,0:T(8,128)(2,1)S(1)} %get-tuple-element.23.own_y), channel_id=1, source_target_pairs={{96,0},{0,32},{32,64},{64,96},{224,128},{128,160},{160,192},{192,2... | collective-permute-start | bytes 1548296 | tf_op jit(solution)/shard_map/ppermute | solution.py:22
  119.5 15.5 %collective-permute-start.27 = (bf16[448,576]{1,0:T(8,128)(2,1)S(1)}, bf16[448,576]{1,0:T(8,128)(2,1)S(1)}, u32[]{:S(2)}, u32[]{:S(2)}) collective-permute-start(bf16[448,576]{1,0:T(8,128)(2,1)S(1)} %get-tuple-element.23.own_y), channel_id=1, source_target_pairs={{0,128},{32,160},{64,192},{96,224},{128,0},{160,32},{192,64},{224,... | collective-permute-start | bytes 1548296 | tf_op jit(solution)/shard_map/ppermute | solution.py:26
  134.2 25.2 %collective-permute-start.29 = (bf16[672,576]{1,0:T(8,128)(2,1)S(1)}, bf16[672,576]{1,0:T(8,128)(2,1)S(1)}, u32[]{:S(2)}, u32[]{:S(2)}) collective-permute-start(bf16[672,576]{1,0:T(8,128)(2,1)S(1)} %pad_maximum_fusion), channel_id=1, source_target_pairs={{0,128},{32,160},{64,192},{96,224},{128,0},{160,32},{192,64},{224,... | collective-permute-start | bytes 2322440 | tf_op jit(solution)/shard_map/ppermute | solution.py:26
  135.0 24.4 %collective-permute-start.32 = (bf16[448,576]{1,0:T(8,128)(2,1)S(1)}, bf16[448,576]{1,0:T(8,128)(2,1)S(1)}, u32[]{:S(2)}, u32[]{:S(2)}) collective-permute-start(bf16[448,576]{1,0:T(8,128)(2,1)S(1)} %collective-permute-done.27.refs_1_), channel_id=1, source_target_pairs={{64,0},{96,32},{0,64},{32,96},{192,128},{224,160},{128,192},{160,2... | collective-permute-start | bytes 1548296 | tf_op jit(solution)/shard_map/ppermute | solution.py:22
  135.7 21.8 %collective-permute-start.30 = (bf16[336,576]{1,0:T(8,128)(2,1)S(1)}, bf16[336,576]{1,0:T(8,128)(2,1)S(1)}, u32[]{:S(2)}, u32[]{:S(2)}) collective-permute-start(bf16[336,576]{1,0:T(8,128)(2,1)S(1)} %get-tuple-element.58), channel_id=1, source_target_pairs={{32,0},{64,32},{96,64},{0,96},{160,128},{192,160},{224,192},{128,2... | collective-permute-start | bytes 1161224 | tf_op jit(solution)/shard_map/ppermute | solution.py:22
  138.1 21.2 %collective-permute-start.31 = (bf16[336,576]{1,0:T(8,128)(2,1)S(1)}, bf16[336,576]{1,0:T(8,128)(2,1)S(1)}, u32[]{:S(2)}, u32[]{:S(2)}) collective-permute-start(bf16[336,576]{1,0:T(8,128)(2,1)S(1)} %get-tuple-element.57), channel_id=1, source_target_pairs={{96,0},{0,32},{32,64},{64,96},{224,128},{128,160},{160,192},{192,2... | collective-permute-start | bytes 1161224 | tf_op jit(solution)/shard_map/ppermute | solution.py:22

commit v5 on v4

--- a/solution.py
+++ b/solution.py
@@ -128,15 +128,11 @@
     )(block, *x_blocks, *([] if mine else [before]))
 
 
-def open_kernel(block_ref, got_ref, own_y, right, found_ref, own_ref, begun_ref, lhs, rhs, sems):
+def open_kernel(lhs_ref, own_y, right, left, across, found_ref, own_ref, begun_ref, lhs, rhs, sems):
     rows, cols = own_ref.shape
-    core = lax.rem(lax.axis_index("narrow"), 2)
-    copies = [
-        pltpu.make_async_copy(block_ref.at[0], lhs.at[core], sems.at[0]),
-        pltpu.make_async_copy(got_ref.at[0], lhs.at[1 - core], sems.at[1]),
-        pltpu.make_async_copy(own_y, rhs.at[pl.ds(0, rows)], sems.at[2]),
-        pltpu.make_async_copy(right, rhs.at[pl.ds(rows, rows)], sems.at[3]),
-    ]
+    copies = [pltpu.make_async_copy(lhs_ref, lhs, sems.at[4])]
+    for at, block in enumerate((own_y, right, left, across)):
+        copies.append(pltpu.make_async_copy(block, rhs.at[pl.ds(at * rows, rows)], sems.at[at]))
     for copy in copies:
         copy.start()
     for copy in copies:
@@ -144,84 +140,70 @@
     for start in range(0, cols, 256):
         part = pl.ds(start, min(256, cols - start))
         value = coef_a * own_ref[:, part].astype(f32) + coef_b * found_ref[:, part]
-        begun_ref[:, part] = value + coef_c * dot(lhs[0], rhs[:, part])
-
-
-def close_kernel(few, block_ref, got_ref, *refs):
-    left, across, via_y, via_right, via_left, across_far = refs[:6]
-    begun_ref, out_ref, lhs, rhs, total, sems = refs[6:]
+        begun_ref[:, part] = value + coef_c * dot(lhs[...], rhs[:, part])
+
+
+def close_kernel(few, lhs_ref, via_y, via_right, via_left, across_far, begun_ref, out_ref, lhs, rhs, begun, sems):
     rows, cols = out_ref.shape
     half, more = rows // 2, rows - few
-    core = lax.rem(lax.axis_index("narrow"), 2)
-
     pieces = [
-        (block_ref, lhs.at[core]),
-        (got_ref, lhs.at[1 - core]),
-        (left, 0),
-        (via_right.at[pl.ds(0, half)], rows),
-        (via_left.at[pl.ds(0, half)], rows + half),
-        (across, 2 * rows),
-        (via_right.at[pl.ds(half, few)], 3 * rows),
-        (via_y.at[pl.ds(0, more)], 3 * rows + few),
-        (via_left.at[pl.ds(half, few)], 4 * rows),
-        (via_y.at[pl.ds(more, more)], 4 * rows + few),
-        (across_far, 5 * rows),
+        (via_right.at[pl.ds(0, half)], 0),
+        (via_left.at[pl.ds(0, half)], half),
+        (via_right.at[pl.ds(half, few)], rows),
+        (via_y.at[pl.ds(0, more)], rows + few),
+        (via_left.at[pl.ds(half, few)], 2 * rows),
+        (via_y.at[pl.ds(more, more)], 2 * rows + few),
+        (across_far, 3 * rows),
     ]
-    copies = []
+    copies = [pltpu.make_async_copy(lhs_ref, lhs, sems.at[7])]
     for at, (source, place) in enumerate(pieces):
-        target = rhs.at[pl.ds(place, source.shape[0])] if isinstance(place, int) else place
-        copies.append(pltpu.make_async_copy(source, target, sems.at[at]))
+        copies.append(pltpu.make_async_copy(source, rhs.at[pl.ds(place, source.shape[0])], sems.at[at]))
+    copies.append(pltpu.make_async_copy(begun_ref, begun, sems.at[8]))
     for copy in copies:
         copy.start()
     parts = [pl.ds(start, min(256, cols - start)) for start in range(0, cols, 256)]
-    width = 2 * rows
-    for copy in copies[:5]:
-        copy.wait()
-    for part in parts:
-        total[:, part] = dot(lhs[1, 0], rhs[:width, part])
-    for copy in copies[5:]:
+    for copy in copies:
         copy.wait()
     scale = float(COLS) ** 0.5
     for part in parts:
-        value = dot(lhs[0, 1], rhs[width : 2 * width, part]) + dot(lhs[1, 1], rhs[2 * width :, part])
-        out_ref[:, part] = (scale * (begun_ref[:, part] + coef_c * (total[:, part] + value))).astype(bf16)
-
-
-def open_product(block, got, own_y, right, found, own):
+        value = begun[:, part] + coef_c * dot(lhs[...], rhs[:, part])
+        out_ref[:, part] = (scale * value).astype(bf16)
+
+
+def open_product(lhs, blocks, found, own):
     rows, cols = own.shape
     vmem = pl.BlockSpec(memory_space=pltpu.VMEM)
     return pl.pallas_call(
         open_kernel,
         out_shape=jax.ShapeDtypeStruct((rows, cols), f32),
-        in_specs=[pl.BlockSpec(memory_space=pl.ANY)] * 4 + [vmem, vmem],
+        in_specs=[pl.BlockSpec(memory_space=pl.ANY)] * 5 + [vmem, vmem],
         out_specs=vmem,
         scratch_shapes=[
-            pltpu.VMEM(block.shape, bf16),
-            pltpu.VMEM((2 * rows, cols), bf16),
-            pltpu.SemaphoreType.DMA((4,)),
+            pltpu.VMEM(lhs.shape, bf16),
+            pltpu.VMEM((4 * rows, cols), bf16),
+            pltpu.SemaphoreType.DMA((5,)),
         ],
         compiler_params=pltpu.CompilerParams(vmem_limit_bytes=12 * 2**20),
-        cost_estimate=pl.CostEstimate(flops=4 * rows * rows * cols, bytes_accessed=5 * 2**20, transcendentals=0),
-    )(block, got, own_y, right, found, own)
-
-
-def close_product(few, block, got, blocks, begun):
+        cost_estimate=pl.CostEstimate(flops=8 * rows * rows * cols, bytes_accessed=6 * 2**20, transcendentals=0),
+    )(lhs, *blocks, found, own)
+
+
+def close_product(few, lhs, blocks, begun):
     rows, cols = begun.shape
-    vmem = pl.BlockSpec(memory_space=pltpu.VMEM)
     return pl.pallas_call(
         functools.partial(close_kernel, few),
         out_shape=jax.ShapeDtypeStruct((rows, cols), bf16),
-        in_specs=[pl.BlockSpec(memory_space=pltpu.HBM)] * 8 + [vmem],
-        out_specs=vmem,
+        in_specs=[pl.BlockSpec(memory_space=pltpu.HBM)] * 6,
+        out_specs=pl.BlockSpec(memory_space=pltpu.VMEM),
         scratch_shapes=[
-            pltpu.VMEM((2, *block.shape), bf16),
-            pltpu.VMEM((6 * rows, cols), bf16),
+            pltpu.VMEM(lhs.shape, bf16),
+            pltpu.VMEM((4 * rows, cols), bf16),
             pltpu.VMEM((rows, cols), f32),
-            pltpu.SemaphoreType.DMA((11,)),
+            pltpu.SemaphoreType.DMA((9,)),
         ],
-        compiler_params=pltpu.CompilerParams(vmem_limit_bytes=16 * 2**20),
-        cost_estimate=pl.CostEstimate(flops=12 * rows * rows * cols, bytes_accessed=9 * 2**20, transcendentals=0),
-    )(block, got, *blocks, begun)
+        compiler_params=pltpu.CompilerParams(vmem_limit_bytes=12 * 2**20),
+        cost_estimate=pl.CostEstimate(flops=8 * rows * rows * cols, bytes_accessed=6 * 2**20, transcendentals=0),
+    )(lhs, *blocks, begun)
 
 
 def local(own):
@@ -264,13 +246,14 @@
     total, other_right, other_left, other_far = lax.optimization_barrier((total, *others))
 
     width = 2 * rows
-    total = jnp.where(core == 0, total, cat(total[unit:], total[:unit])).reshape(2, unit, 2 * width)
-    given = lax.dynamic_slice_in_dim(total, (1 - core) * width, width, 2).astype(bf16)
-    total = (lax.dynamic_slice_in_dim(total, core * width, width, 2) + from_core(given).astype(f32)).astype(bf16)
-
-    gram_same = total[0].astype(f32) + from_y_hi(total[0]).astype(f32)
-    gram_other = from_y(total[1]).astype(f32) + from_y_both(total[1]).astype(f32)
-    gram = jnp.stack([gram_same, gram_other]).astype(bf16)
+    total = total.astype(bf16)
+    kept_part = jnp.where(core == 0, total[:unit], total[unit:])
+    given_part = jnp.where(core == 0, total[unit:], total[:unit])
+    gram_same = kept_part.astype(f32) + from_y_hi(kept_part).astype(f32)
+    gram_other = from_y(given_part).astype(f32) + from_y_both(given_part).astype(f32)
+    gram = jnp.stack([gram_same, gram_other])
+    given = lax.dynamic_slice_in_dim(gram, (1 - core) * width, width, 2).astype(bf16)
+    gram = (lax.dynamic_slice_in_dim(gram, core * width, width, 2) + from_core(given).astype(f32)).astype(bf16)
 
     up1, down1 = from_z(gram, 1), from_z(gram, -1)
     up2, down2 = from_z(gram, 2), from_z(gram, -2)
@@ -289,8 +272,13 @@
     via_right = from_x(cat(right[:half], across[:few]), 1)
     via_left = from_x(cat(left[half:], across[:few]), -1)
     across_far = from_x(across, 2)
-    begun = open_product(block, got, sent, right, found, own)
-    return close_product(few, block, got, (left, across, via_y, via_right, via_left, across_far), begun)
+    block, got, _ = lax.optimization_barrier((block, got, right))
+    low = jnp.where(core == 0, block, got)
+    high = jnp.where(core == 0, got, block)
+    early = cat(low[0], high[0, :, :rows], low[1, :, :rows], axis=1)
+    late = cat(high[0, :, rows:], low[1, :, rows:], high[1], axis=1)
+    begun = open_product(early, (sent, right, left, across), found, own)
+    return close_product(few, late, (via_y, via_right, via_left, across_far), begun)
 
 
 def solution(mesh):

time: 167 us -> 171 us (1.024)
  local copies, waits for them, and re-layouts: 9.56 us -> 25.4 us
  waiting for transfers between devices: 96 us -> 84.6 us
    ppermute x11, waiting for transfers between devices: 52.4 us -> 37.2 us  [from_x(): return lax.ppermute(value, 'wide', pairs)]
    unnamed x25 -> x51, local copies, waits for them, and re-layouts: 3.2 us -> 9.89 us
    concatenate x3 -> x5, local copies, waits for them, and re-layouts: 0.18 us -> 6.81 us  [cat(): return jnp.concatenate(parts, axis=axis)]
    squeeze x1 -> x3, local copies, waits for them, and re-layouts: 0.02 us -> 3.58 us  [the longest x2 2.6 us: local(): early = cat(low[0], high[0, :, :rows], low[1, :, :rows], axis=1)]
    ppermute x1, waiting for transfers between devices: 3.09 us -> 5.3 us  [from_y_hi(): return lax.ppermute(value, 'narrow', [(n, n ^ 2) for n in range(32)])]
    concatenate x2, other arithmetic: 0.15 us -> 2.01 us  [cat(): return jnp.concatenate(parts, axis=axis)]
    slice x3, local copies, waits for them, and re-layouts: 1.91 us -> 0.1 us  [units(): return summed[start * unit:stop * unit]]
    pallas_call x1, Pallas kernels: 1.25 us -> 2.97 us  [open_product(): pl.pallas_call(open_kernel, out_shape=jax.ShapeDtypeStruct((rows, cols),...]
  transfers between devices with their start and end apart: 33 -> 33, of which waited for: 18 -> 18; matrix products, arithmetic and copies ran while one was open for 6% -> 11% of each run, Pallas kernels for 2% -> 3%
where the time goes in v5:
time: 171 us; the launch traced here: 170 us
  waiting for transfers between devices  84.6 us (49%)
  starting transfers between devices  40 us (23%)
  local copies, waits for them, and re-layouts  25.4 us (15%)
  Pallas kernels  12.4 us (7%)
  other arithmetic  3.81 us (2%)
  matrix products  3 us (2%)
    ppermute x11, waiting for transfers between devices, from_x(): return lax.ppermute(value, 'wide', pairs)  37.2 us
    ppermute x4, waiting for transfers between devices, along_z(): return lax.ppermute(value, 'narrow', pairs)  24.2 us
    ppermute x11, starting transfers between devices, from_x(): return lax.ppermute(value, 'wide', pairs)  13.9 us
    ppermute x8, waiting for transfers between devices, from_z(): return lax.ppermute(value, 'narrow', pairs)  11.4 us
    ppermute x8, starting transfers between devices, from_z(): return lax.ppermute(value, 'narrow', pairs)  11 us
    unnamed x51, local copies, waits for them, and re-layouts  9.89 us
    ppermute x4, starting transfers between devices, along_z(): return lax.ppermute(value, 'narrow', pairs)  7.56 us
    concatenate x5, local copies, waits for them, and re-layouts, cat(): return jnp.concatenate(parts, axis=axis)  6.81 us
  transfers between devices with their start and end apart: 33, of which 18 were waited for; matrix products, arithmetic and copies ran while one was open for 11% of the time, Pallas kernels for 3%

profile of v5, /device:TPU:24, one launch (start us, length us, event | category | flops | bytes accessed | tf_op | source)
XLA Modules:
  0.0 170.0 jit_solution(14226953640240255158)
XLA Ops:
  0.0 2.8 %collective-permute-start.1 = (bf16[448,576]{1,0:T(8,128)(2,1)}, bf16[448,576]{1,0:T(8,128)(2,1)S(1)}, u32[]{:S(2)}, u32[]{:S(2)}) collective-permute-start(bf16[448,576]{1,0:T(8,128)(2,1)} %own_ref.1), channel_id=1, source_target_pairs={{32,0},{64,32},{96,64},{0,96},{160,128},{192,160},{224,192},{128,2... | collective-permute-start | bytes 1548296 | tf_op jit(solution)/shard_map/ppermute | solution.py:22
  3.5 1.2 constant_dynamic-update-slice_fusion.6
  4.7 10.6 %collective-permute-done.1.refs_2_ = bf16[448,576]{1,0:T(8,128)(2,1)S(1)} collective-permute-done((bf16[448,576]{1,0:T(8,128)(2,1)}, bf16[448,576]{1,0:T(8,128)(2,1)S(1)}, u32[]{:S(2)}, u32[]{:S(2)}) %collective-permute-start.1) | collective-permute-done | bytes 516128 | tf_op jit(solution)/shard_map/ppermute | solution.py:22
  15.3 3.7 %collective-permute-start.3 = (bf16[224,576]{1,0:T(8,128)(2,1)S(1)}, bf16[224,576]{1,0:T(8,128)(2,1)S(1)}, u32[]{:S(2)}, u32[]{:S(2)}) collective-permute-start(bf16[224,576]{1,0:T(8,128)(2,1)S(1)} %slice.94), channel_id=1, source_target_pairs={{32,0},{64,32},{96,64},{0,96},{160,128},{192,160},{224,192},{128,2... | collective-permute-start | bytes 774152 | tf_op jit(solution)/shard_map/ppermute | solution.py:22
  19.7 4.5 %collective-permute-done.3 = bf16[224,576]{1,0:T(8,128)(2,1)S(1)} collective-permute-done((bf16[224,576]{1,0:T(8,128)(2,1)S(1)}, bf16[224,576]{1,0:T(8,128)(2,1)S(1)}, u32[]{:S(2)}, u32[]{:S(2)}) %collective-permute-start.3) | collective-permute-done | bytes 258080 | tf_op jit(solution)/shard_map/ppermute | solution.py:22
  24.3 3.5 %collective-permute-done.4 = bf16[224,576]{1,0:T(8,128)(2,1)S(1)} collective-permute-done((bf16[224,576]{1,0:T(8,128)(2,1)S(1)}, bf16[224,576]{1,0:T(8,128)(2,1)S(1)}, u32[]{:S(2)}, u32[]{:S(2)}) %collective-permute-start.4) | collective-permute-done | bytes 258080 | tf_op jit(solution)/shard_map/ppermute | solution.py:22
  27.8 1.5 convolution_convert_fusion
  29.4 1.5 fusion.9
  30.9 1.9 %collective-permute-done.5 = bf16[448,1792]{1,0:T(8,128)(2,1)S(1)} collective-permute-done((bf16[448,1792]{1,0:T(8,128)(2,1)S(1)}, bf16[448,1792]{1,0:T(8,128)(2,1)S(1)}, u32[]{:S(2)}, u32[]{:S(2)}) %collective-permute-start.5) | collective-permute-done | bytes 1605664 | tf_op jit(solution)/shard_map/ppermute | solution.py:44
  33.3 2.0 %collective-permute-start.6 = (bf16[112,1792]{1,0:T(8,128)(2,1)S(1)}, bf16[112,1792]{1,0:T(8,128)(2,1)S(1)}, u32[]{:S(2)}, u32[]{:S(2)}) collective-permute-start(bf16[112,1792]{1,0:T(8,128)(2,1)S(1)} %get-tuple-element.40), channel_id=1, source_target_pairs={{0,4},{1,29},{2,6},{3,31},{4,8},{5,1},{6,10},{7,3},{8,12},{9,5},{1... | collective-permute-start | bytes 1204232 | tf_op jit(solution)/shard_map/ppermute | solution.py:65
  35.3 3.3 %collective-permute-start.7 = (bf16[56,1792]{1,0:T(8,128)(2,1)S(1)}, bf16[56,1792]{1,0:T(8,128)(2,1)S(1)}, u32[]{:S(2)}, u32[]{:S(2)}) collective-permute-start(bf16[56,1792]{1,0:T(8,128)(2,1)S(1)} %slice.98), channel_id=1, source_target_pairs={{0,8},{1,25},{2,10},{3,27},{4,12},{5,29},{6,14},{7,31},{8,16},{9,1... | collective-permute-start | bytes 602120 | tf_op jit(solution)/shard_map/ppermute | solution.py:65
  38.7 10.6 %collective-permute-done.7 = bf16[56,1792]{1,0:T(8,128)(2,1)S(1)} collective-permute-done((bf16[56,1792]{1,0:T(8,128)(2,1)S(1)}, bf16[56,1792]{1,0:T(8,128)(2,1)S(1)}, u32[]{:S(2)}, u32[]{:S(2)}) %collective-permute-start.7) | collective-permute-done | bytes 200736 | tf_op jit(solution)/shard_map/ppermute | solution.py:65
  49.4 2.1 %collective-permute-start.9 = (bf16[112,1792]{1,0:T(8,128)(2,1)S(1)}, bf16[112,1792]{1,0:T(8,128)(2,1)S(1)}, u32[]{:S(2)}, u32[]{:S(2)}) collective-permute-start(bf16[112,1792]{1,0:T(8,128)(2,1)S(1)} %get-tuple-element.18), channel_id=1, source_target_pairs={{0,4},{1,29},{2,6},{3,31},{4,8},{5,1},{6,10},{7,3},{8,12},{9,5},{1... | collective-permute-start | bytes 1204232 | tf_op jit(solution)/shard_map/ppermute | solution.py:65
  51.8 1.8 %collective-permute-start.11 = (bf16[448,576]{1,0:T(8,128)(2,1)S(1)}, bf16[448,576]{1,0:T(8,128)(2,1)S(1)}, u32[]{:S(2)}, u32[]{:S(2)}) collective-permute-start(bf16[448,576]{1,0:T(8,128)(2,1)S(1)} %collective-permute-done.refs_5_), channel_id=1, source_target_pairs={{96,0},{0,32},{32,64},{64,96},{224,128},{128,160},{160,192},{192,2... | collective-permute-start | bytes 1548296 | tf_op jit(solution)/shard_map/ppermute | solution.py:22
  54.4 9.4 %collective-permute-done.8 = bf16[112,1792]{1,0:T(8,128)(2,1)S(1)} collective-permute-done((bf16[112,1792]{1,0:T(8,128)(2,1)S(1)}, bf16[112,1792]{1,0:T(8,128)(2,1)S(1)}, u32[]{:S(2)}, u32[]{:S(2)}) %collective-permute-start.8) | collective-permute-done | bytes 401440 | tf_op jit(solution)/shard_map/ppermute | solution.py:65
  63.8 4.2 %collective-permute-done.9 = bf16[112,1792]{1,0:T(8,128)(2,1)S(1)} collective-permute-done((bf16[112,1792]{1,0:T(8,128)(2,1)S(1)}, bf16[112,1792]{1,0:T(8,128)(2,1)S(1)}, u32[]{:S(2)}, u32[]{:S(2)}) %collective-permute-start.9) | collective-permute-done | bytes 401440 | tf_op jit(solution)/shard_map/ppermute | solution.py:65
  70.5 1.3 collective-permute-start.13
  71.8 2.9 %collective-permute-start.15 = (bf16[56,1792]{1,0:T(8,128)(2,1)S(1)}, bf16[56,1792]{1,0:T(8,128)(2,1)S(1)}, u32[]{:S(2)}, u32[]{:S(2)}) collective-permute-start(bf16[56,1792]{1,0:T(8,128)(2,1)S(1)} %get-tuple-element.59), channel_id=1, source_target_pairs={{0,130},{1,131},{2,128},{3,129},{4,134},{5,135},{6,132},{7,133},{8... | collective-permute-start | bytes 602120 | tf_op jit(solution)/shard_map/ppermute | solution.py:40
  74.7 5.3 %collective-permute-done.13 = bf16[56,1792]{1,0:T(8,128)(2,1)S(1)} collective-permute-done((bf16[56,1792]{1,0:T(8,128)(2,1)S(1)}, bf16[56,1792]{1,0:T(8,128)(2,1)S(1)}, u32[]{:S(2)}, u32[]{:S(2)}) %collective-permute-start.13) | collective-permute-done | bytes 200736 | tf_op jit(solution)/shard_map/ppermute | solution.py:35
  80.8 2.4 %collective-permute-done.15 = bf16[56,1792]{1,0:T(8,128)(2,1)S(1)} collective-permute-done((bf16[56,1792]{1,0:T(8,128)(2,1)S(1)}, bf16[56,1792]{1,0:T(8,128)(2,1)S(1)}, u32[]{:S(2)}, u32[]{:S(2)}) %collective-permute-start.15) | collective-permute-done | bytes 200736 | tf_op jit(solution)/shard_map/ppermute | solution.py:40
  84.3 1.4 collective-permute-done.16
  86.6 2.9 %collective-permute-start.20 = (bf16[2,56,896]{2,1,0:T(8,128)(2,1)}, bf16[2,56,896]{2,1,0:T(8,128)(2,1)S(1)}, u32[]{:S(2)}, u32[]{:S(2)}) collective-permute-start(bf16[2,56,896]{2,1,0:T(8,128)(2,1)} %get-tuple-element.30), channel_id=1, source_target_pairs={{24,0},{25,1},{26,2},{27,3},{28,4},{29,5},{30,6},{31,7},{0,8},{1,9... | collective-permute-start | bytes 602120 | tf_op jit(solution)/shard_map/ppermute | solution.py:31
  90.1 1.4 collective-permute-start.18
  91.5 7.9 %collective-permute-done.19 = bf16[2,56,896]{2,1,0:T(8,128)(2,1)} collective-permute-done((bf16[2,56,896]{2,1,0:T(8,128)(2,1)}, bf16[2,56,896]{2,1,0:T(8,128)(2,1)}, u32[]{:S(2)}, u32[]{:S(2)}) %collective-permute-start.19) | collective-permute-done | bytes 200736 | tf_op jit(solution)/shard_map/ppermute | solution.py:31
  100.3 1.5 collective-permute-start.23
  101.9 1.5 collective-permute-start.24
  103.8 2.7 %collective-permute-start.22 = (bf16[2,56,896]{2,1,0:T(8,128)(2,1)S(1)}, bf16[2,56,896]{2,1,0:T(8,128)(2,1)S(1)}, u32[]{:S(2)}, u32[]{:S(2)}) collective-permute-start(bf16[2,56,896]{2,1,0:T(8,128)(2,1)S(1)} %collective-permute-done.20), channel_id=1, source_target_pairs={{28,0},{29,1},{30,2},{31,3},{0,4},{1,5},{2,6},{3,7},{4,8},{5,9},{6... | collective-permute-start | bytes 602120 | tf_op jit(solution)/shard_map/ppermute | solution.py:31
  109.4 2.2 %collective-permute-done.21 = bf16[2,56,896]{2,1,0:T(8,128)(2,1)S(1)} collective-permute-done((bf16[2,56,896]{2,1,0:T(8,128)(2,1)}, bf16[2,56,896]{2,1,0:T(8,128)(2,1)S(1)}, u32[]{:S(2)}, u32[]{:S(2)}) %collective-permute-start.21) | collective-permute-done | bytes 200736 | tf_op jit(solution)/shard_map/ppermute | solution.py:31
  111.6 1.2 collective-permute-done.22
  113.1 1.1 copy-done.11
  114.1 2.6 %shard_map.17.refs_9_ = f32[448,576]{1,0:T(8,128)S(1)} custom-call(bf16[2,448,896]{2,1,0:T(8,128)(2,1)S(1)} %maximum_dynamic-update-slice_fusion.refs_0_, bf16[448,576]{1,0:T(8,128)(2,1)S(1)} %copy-done, bf16[448,576]{1,0:T(8,128)(2,1)S(1)} %collective-permute-done.1.refs_2_, bf16[448,576]{1,0:T(8,128)(2,1)S(1)} %collective-permute-done.2.refs_3_, ...), custom_call_target="tpu_custom_call" | custom-call | flops 924844032 | bytes 6291456 | tf_op jit(solution)/shard_map/pallas_call | solution.py:116
  116.7 2.8 %shard_map.18 = (f32[448,576]{1,0:T(8,128)S(1)}, bf16[448,576]{1,0:T(8,128)(2,1)S(1)}) custom-call(bf16[2,448,896]{2,1,0:T(8,128)(2,1)S(1)} %collective-permute-done.25.refs_0_, bf16[448,576]{1,0:T(8,128)(2,1)S(1)} %copy-done, bf16[448,576]{1,0:T(8,128)(2,1)S(1)} %collective-permute-done.1.refs_2_, bf16[448,576]{1,0:T(8,128)(2,1)S(1)} %collective-permute-done.2.refs_3_, ...), custom_call_target="tpu_custom_call" | custom-call | flops 924844032 | bytes 6291456 | tf_op jit(solution)/shard_map/pallas_call | solution.py:116
  121.3 1.3 collective-permute-start.27
  123.4 12.6 %collective-permute-done.26.right = bf16[448,576]{1,0:T(8,128)(2,1)S(1)} collective-permute-done((bf16[448,576]{1,0:T(8,128)(2,1)S(1)}, bf16[448,576]{1,0:T(8,128)(2,1)S(1)}, u32[]{:S(2)}, u32[]{:S(2)}) %collective-permute-start.26) | collective-permute-done | bytes 516128 | tf_op jit(solution)/shard_map/ppermute | solution.py:22
  136.0 1.6 collective-permute-done.27.left
  138.6 1.0 pad_maximum_fusion.1
  139.6 1.8 %collective-permute-start.30 = (bf16[336,576]{1,0:T(8,128)(2,1)}, bf16[336,576]{1,0:T(8,128)(2,1)}, u32[]{:S(2)}, u32[]{:S(2)}) collective-permute-start(bf16[336,576]{1,0:T(8,128)(2,1)} %get-tuple-element.66), channel_id=1, source_target_pairs={{32,0},{64,32},{96,64},{0,96},{160,128},{192,160},{224,192},{128,2... | collective-permute-start | bytes 1161224 | tf_op jit(solution)/shard_map/ppermute | solution.py:22
  141.7 1.0 pad_maximum_fusion
  143.8 1.3 collective-permute-start.32
  145.1 1.6 slice_bitcast_fusion.2
  147.7 4.0 %concatenate.44.lhs_ref = bf16[448,1792]{1,0:T(8,128)(2,1)} concatenate(bf16[448,896]{1,0:T(8,128)(2,1)} %slice_bitcast_fusion, bf16[448,448]{1,0:T(8,128)(2,1)} %get-tuple-element.68, bf16[448,448]{1,0:T(8,128)(2,1)} %get-tuple-element.35), dimensions={1} | concatenate | bytes 3211264 | tf_op jit(solution)/shard_map/concatenate | solution.py:56
  152.7 2.6 %concatenate.40.lhs_ref = bf16[448,1792]{1,0:T(8,128)(2,1)S(1)} concatenate(bf16[448,448]{1,0:T(8,128)(2,1)} %get-tuple-element.67, bf16[448,448]{1,0:T(8,128)(2,1)} %get-tuple-element.36, bf16[448,896]{1,0:T(8,128)(2,1)} %slice_bitcast_fusion.1), dimensions={1} | concatenate | bytes 3211264 | tf_op jit(solution)/shard_map/concatenate | solution.py:56
  155.3 1.4 copy-done.1
  156.8 1.3 copy-done.13
  158.0 1.1 copy-done.15
  159.1 3.0 %shard_map.19.begun_ref = f32[448,576]{1,0:T(8,128)S(1)} custom-call(bf16[448,1792]{1,0:T(8,128)(2,1)S(1)} %copy-done.1, bf16[448,576]{1,0:T(8,128)(2,1)S(1)} %copy-done.15, bf16[448,576]{1,0:T(8,128)(2,1)S(1)} %collective-permute-done.26.right, bf16[448,576]{1,0:T(8,128)(2,1)S(1)} %collective-permute-done.27.left, ...), custom_call_target="tpu_custom_call" | custom-call | flops 924844032 | bytes 6291456 | tf_op jit(solution)/shard_map/pallas_call | solution.py:176
  162.1 3.7 %collective-permute-done.31.via_left = bf16[336,576]{1,0:T(8,128)(2,1)} collective-permute-done((bf16[336,576]{1,0:T(8,128)(2,1)}, bf16[336,576]{1,0:T(8,128)(2,1)}, u32[]{:S(2)}, u32[]{:S(2)}) %collective-permute-start.31) | collective-permute-done | bytes 387104 | tf_op jit(solution)/shard_map/ppermute | solution.py:22
  165.8 4.0 %shard_map.20 = bf16[448,576]{1,0:T(8,128)(2,1)} custom-call(bf16[448,1792]{1,0:T(8,128)(2,1)S(1)} %concatenate.40.lhs_ref, bf16[672,576]{1,0:T(8,128)(2,1)} %collective-permute-done.28.via_y, bf16[336,576]{1,0:T(8,128)(2,1)} %collective-permute-done.30.via_right, bf16[336,576]{1,0:T(8,128)(2,1)} %collective-permute-done.31.via_left, ...), custom_call_target="tpu_custom_call" | custom-call | flops 924844032 | bytes 6291456 | tf_op jit(solution)/shard_map/pallas_call | solution.py:193
  (114 shorter events, 20.1 us)
Async XLA Ops:
  0.0 15.3 %collective-permute-start.1 = (bf16[448,576]{1,0:T(8,128)(2,1)}, bf16[448,576]{1,0:T(8,128)(2,1)S(1)}, u32[]{:S(2)}, u32[]{:S(2)}) collective-permute-start(bf16[448,576]{1,0:T(8,128)(2,1)} %own_ref.1), channel_id=1, source_target_pairs={{32,0},{64,32},{96,64},{0,96},{160,128},{192,160},{224,192},{128,2... | collective-permute-start | bytes 1548296 | tf_op jit(solution)/shard_map/ppermute | solution.py:22
  2.8 16.2 %collective-permute-start.2 = (bf16[448,576]{1,0:T(8,128)(2,1)}, bf16[448,576]{1,0:T(8,128)(2,1)S(1)}, u32[]{:S(2)}, u32[]{:S(2)}) collective-permute-start(bf16[448,576]{1,0:T(8,128)(2,1)} %own_ref.1), channel_id=1, source_target_pairs={{96,0},{0,32},{32,64},{64,96},{224,128},{128,160},{160,192},{192,2... | collective-permute-start | bytes 1548296 | tf_op jit(solution)/shard_map/ppermute | solution.py:22
  2.8 16.4 %collective-permute-start = (bf16[448,576]{1,0:T(8,128)(2,1)}, bf16[448,576]{1,0:T(8,128)(2,1)S(1)}, u32[]{:S(2)}, u32[]{:S(2)}) collective-permute-start(bf16[448,576]{1,0:T(8,128)(2,1)} %own_ref.1), channel_id=1, source_target_pairs={{0,128},{32,160},{64,192},{96,224},{128,0},{160,32},{192,64},{224,... | collective-permute-start | bytes 1548296 | tf_op jit(solution)/shard_map/ppermute | solution.py:26
  15.3 8.9 %collective-permute-start.3 = (bf16[224,576]{1,0:T(8,128)(2,1)S(1)}, bf16[224,576]{1,0:T(8,128)(2,1)S(1)}, u32[]{:S(2)}, u32[]{:S(2)}) collective-permute-start(bf16[224,576]{1,0:T(8,128)(2,1)S(1)} %slice.94), channel_id=1, source_target_pairs={{32,0},{64,32},{96,64},{0,96},{160,128},{192,160},{224,192},{128,2... | collective-permute-start | bytes 774152 | tf_op jit(solution)/shard_map/ppermute | solution.py:22
  19.0 8.7 %collective-permute-start.4 = (bf16[224,576]{1,0:T(8,128)(2,1)S(1)}, bf16[224,576]{1,0:T(8,128)(2,1)S(1)}, u32[]{:S(2)}, u32[]{:S(2)}) collective-permute-start(bf16[224,576]{1,0:T(8,128)(2,1)S(1)} %slice.95), channel_id=1, source_target_pairs={{96,0},{0,32},{32,64},{64,96},{224,128},{128,160},{160,192},{192,2... | collective-permute-start | bytes 774152 | tf_op jit(solution)/shard_map/ppermute | solution.py:22
  19.1 32.7 %copy-start.2 = (bf16[448,576]{1,0:T(8,128)(2,1)}, bf16[448,576]{1,0:T(8,128)(2,1)S(1)}, u32[]{:S(2)}) copy-start(bf16[448,576]{1,0:T(8,128)(2,1)S(1)} %collective-permute-done.refs_5_) | copy-start | bytes 1548292
  27.8 25.8 %copy-start.4 = (bf16[448,576]{1,0:T(8,128)(2,1)}, bf16[448,576]{1,0:T(8,128)(2,1)S(1)}, u32[]{:S(2)}) copy-start(bf16[448,576]{1,0:T(8,128)(2,1)S(1)} %get-tuple-element.20.refs_4_) | copy-start | bytes 1548292
  29.3 3.5 %collective-permute-start.5 = (bf16[448,1792]{1,0:T(8,128)(2,1)S(1)}, bf16[448,1792]{1,0:T(8,128)(2,1)S(1)}, u32[]{:S(2)}, u32[]{:S(2)}) collective-permute-start(bf16[448,1792]{1,0:T(8,128)(2,1)S(1)} %convolution_convert_fusion), channel_id=1, source_target_pairs={{0,1},{1,0},{2,3},{3,2},{4,5},{5,4},{6,7},{7,6},{8,9},{9,8},{10,11... | collective-permute-start | bytes 4816904 | tf_op jit(solution)/shard_map/ppermute | solution.py:44
  33.3 15.9 %collective-permute-start.6 = (bf16[112,1792]{1,0:T(8,128)(2,1)S(1)}, bf16[112,1792]{1,0:T(8,128)(2,1)S(1)}, u32[]{:S(2)}, u32[]{:S(2)}) collective-permute-start(bf16[112,1792]{1,0:T(8,128)(2,1)S(1)} %get-tuple-element.40), channel_id=1, source_target_pairs={{0,4},{1,29},{2,6},{3,31},{4,8},{5,1},{6,10},{7,3},{8,12},{9,5},{1... | collective-permute-start | bytes 1204232 | tf_op jit(solution)/shard_map/ppermute | solution.py:65
  35.3 13.9 %collective-permute-start.7 = (bf16[56,1792]{1,0:T(8,128)(2,1)S(1)}, bf16[56,1792]{1,0:T(8,128)(2,1)S(1)}, u32[]{:S(2)}, u32[]{:S(2)}) collective-permute-start(bf16[56,1792]{1,0:T(8,128)(2,1)S(1)} %slice.98), channel_id=1, source_target_pairs={{0,8},{1,25},{2,10},{3,27},{4,12},{5,29},{6,14},{7,31},{8,16},{9,1... | collective-permute-start | bytes 602120 | tf_op jit(solution)/shard_map/ppermute | solution.py:65
  49.3 14.5 %collective-permute-start.8 = (bf16[112,1792]{1,0:T(8,128)(2,1)S(1)}, bf16[112,1792]{1,0:T(8,128)(2,1)S(1)}, u32[]{:S(2)}, u32[]{:S(2)}) collective-permute-start(bf16[112,1792]{1,0:T(8,128)(2,1)S(1)} %fusion), channel_id=1, source_target_pairs={{0,8},{1,25},{2,10},{3,27},{4,12},{5,29},{6,14},{7,31},{8,16},{9,1... | collective-permute-start | bytes 1204232 | tf_op jit(solution)/shard_map/ppermute | solution.py:65
  49.4 18.6 %collective-permute-start.9 = (bf16[112,1792]{1,0:T(8,128)(2,1)S(1)}, bf16[112,1792]{1,0:T(8,128)(2,1)S(1)}, u32[]{:S(2)}, u32[]{:S(2)}) collective-permute-start(bf16[112,1792]{1,0:T(8,128)(2,1)S(1)} %get-tuple-element.18), channel_id=1, source_target_pairs={{0,4},{1,29},{2,6},{3,31},{4,8},{5,1},{6,10},{7,3},{8,12},{9,5},{1... | collective-permute-start | bytes 1204232 | tf_op jit(solution)/shard_map/ppermute | solution.py:65
  51.6 16.5 %collective-permute-start.10 = (bf16[448,576]{1,0:T(8,128)(2,1)S(1)}, bf16[448,576]{1,0:T(8,128)(2,1)S(1)}, u32[]{:S(2)}, u32[]{:S(2)}) collective-permute-start(bf16[448,576]{1,0:T(8,128)(2,1)S(1)} %collective-permute-done.refs_5_), channel_id=1, source_target_pairs={{32,0},{64,32},{96,64},{0,96},{160,128},{192,160},{224,192},{128,2... | collective-permute-start | bytes 1548296 | tf_op jit(solution)/shard_map/ppermute | solution.py:22
  51.8 17.0 %collective-permute-start.11 = (bf16[448,576]{1,0:T(8,128)(2,1)S(1)}, bf16[448,576]{1,0:T(8,128)(2,1)S(1)}, u32[]{:S(2)}, u32[]{:S(2)}) collective-permute-start(bf16[448,576]{1,0:T(8,128)(2,1)S(1)} %collective-permute-done.refs_5_), channel_id=1, source_target_pairs={{96,0},{0,32},{32,64},{64,96},{224,128},{128,160},{160,192},{192,2... | collective-permute-start | bytes 1548296 | tf_op jit(solution)/shard_map/ppermute | solution.py:22
  53.6 16.0 %collective-permute-start.12 = (bf16[448,576]{1,0:T(8,128)(2,1)S(1)}, bf16[448,576]{1,0:T(8,128)(2,1)S(1)}, u32[]{:S(2)}, u32[]{:S(2)}) collective-permute-start(bf16[448,576]{1,0:T(8,128)(2,1)S(1)} %get-tuple-element.20.refs_4_), channel_id=1, source_target_pairs={{0,128},{32,160},{64,192},{96,224},{128,0},{160,32},{192,64},{224,... | collective-permute-start | bytes 1548296 | tf_op jit(solution)/shard_map/ppermute | solution.py:26
  68.1 16.0 %copy-start.6 = (bf16[448,576]{1,0:T(8,128)(2,1)}, bf16[448,576]{1,0:T(8,128)(2,1)S(1)}, u32[]{:S(2)}) copy-start(bf16[448,576]{1,0:T(8,128)(2,1)S(1)} %collective-permute-done.10.refs_6_) | copy-start | bytes 1548292
  70.5 9.5 %collective-permute-start.13 = (bf16[56,1792]{1,0:T(8,128)(2,1)S(1)}, bf16[56,1792]{1,0:T(8,128)(2,1)S(1)}, u32[]{:S(2)}, u32[]{:S(2)}) collective-permute-start(bf16[56,1792]{1,0:T(8,128)(2,1)S(1)} %get-tuple-element.60), channel_id=1, source_target_pairs={{0,2},{1,3},{2,0},{3,1},{4,6},{5,7},{6,4},{7,5},{8,10},{9,11},{10,... | collective-permute-start | bytes 602120 | tf_op jit(solution)/shard_map/ppermute | solution.py:35
  71.8 9.0 %collective-permute-start.14 = (bf16[56,1792]{1,0:T(8,128)(2,1)S(1)}, bf16[56,1792]{1,0:T(8,128)(2,1)S(1)}, u32[]{:S(2)}, u32[]{:S(2)}) collective-permute-start(bf16[56,1792]{1,0:T(8,128)(2,1)S(1)} %get-tuple-element.59), channel_id=1, source_target_pairs={{0,128},{32,160},{64,192},{96,224},{128,0},{160,32},{192,64},{224,... | collective-permute-start | bytes 602120 | tf_op jit(solution)/shard_map/ppermute | solution.py:26
  71.8 11.5 %collective-permute-start.15 = (bf16[56,1792]{1,0:T(8,128)(2,1)S(1)}, bf16[56,1792]{1,0:T(8,128)(2,1)S(1)}, u32[]{:S(2)}, u32[]{:S(2)}) collective-permute-start(bf16[56,1792]{1,0:T(8,128)(2,1)S(1)} %get-tuple-element.59), channel_id=1, source_target_pairs={{0,130},{1,131},{2,128},{3,129},{4,134},{5,135},{6,132},{7,133},{8... | collective-permute-start | bytes 602120 | tf_op jit(solution)/shard_map/ppermute | solution.py:40
  84.1 1.5 collective-permute-start.16
  84.3 1.5 copy-start.19
  86.5 12.9 %collective-permute-start.19 = (bf16[2,56,896]{2,1,0:T(8,128)(2,1)}, bf16[2,56,896]{2,1,0:T(8,128)(2,1)}, u32[]{:S(2)}, u32[]{:S(2)}) collective-permute-start(bf16[2,56,896]{2,1,0:T(8,128)(2,1)} %get-tuple-element.30), channel_id=1, source_target_pairs={{8,0},{9,1},{10,2},{11,3},{12,4},{13,5},{14,6},{15,7},{16,8},{17,9... | collective-permute-start | bytes 602120 | tf_op jit(solution)/shard_map/ppermute | solution.py:31
  86.6 15.3 %collective-permute-start.20 = (bf16[2,56,896]{2,1,0:T(8,128)(2,1)}, bf16[2,56,896]{2,1,0:T(8,128)(2,1)S(1)}, u32[]{:S(2)}, u32[]{:S(2)}) collective-permute-start(bf16[2,56,896]{2,1,0:T(8,128)(2,1)} %get-tuple-element.30), channel_id=1, source_target_pairs={{24,0},{25,1},{26,2},{27,3},{28,4},{29,5},{30,6},{31,7},{0,8},{1,9... | collective-permute-start | bytes 602120 | tf_op jit(solution)/shard_map/ppermute | solution.py:31
  89.5 14.3 %collective-permute-start.17 = (bf16[2,56,896]{2,1,0:T(8,128)(2,1)}, bf16[2,56,896]{2,1,0:T(8,128)(2,1)}, u32[]{:S(2)}, u32[]{:S(2)}) collective-permute-start(bf16[2,56,896]{2,1,0:T(8,128)(2,1)} %get-tuple-element.30), channel_id=1, source_target_pairs={{4,0},{5,1},{6,2},{7,3},{8,4},{9,5},{10,6},{11,7},{12,8},{13,9},{1... | collective-permute-start | bytes 602120 | tf_op jit(solution)/shard_map/ppermute | solution.py:31
  90.1 17.3 %collective-permute-start.18 = (bf16[2,56,896]{2,1,0:T(8,128)(2,1)}, bf16[2,56,896]{2,1,0:T(8,128)(2,1)}, u32[]{:S(2)}, u32[]{:S(2)}) collective-permute-start(bf16[2,56,896]{2,1,0:T(8,128)(2,1)} %get-tuple-element.30), channel_id=1, source_target_pairs={{28,0},{29,1},{30,2},{31,3},{0,4},{1,5},{2,6},{3,7},{4,8},{5,9},{6... | collective-permute-start | bytes 602120 | tf_op jit(solution)/shard_map/ppermute | solution.py:31
  91.5 21.5 %copy-start = (bf16[448,576]{1,0:T(8,128)(2,1)S(1)}, bf16[448,576]{1,0:T(8,128)(2,1)}, u32[]{:S(2)}) copy-start(bf16[448,576]{1,0:T(8,128)(2,1)} %own_ref.1) | copy-start | bytes 1548292
  91.5 21.5 %copy-start.3 = (bf16[448,576]{1,0:T(8,128)(2,1)S(1)}, bf16[448,576]{1,0:T(8,128)(2,1)}, u32[]{:S(2)}) copy-start(bf16[448,576]{1,0:T(8,128)(2,1)} %copy-done.2) | copy-start | bytes 1548292
  91.5 21.5 %copy-start.5 = (bf16[448,576]{1,0:T(8,128)(2,1)S(1)}, bf16[448,576]{1,0:T(8,128)(2,1)}, u32[]{:S(2)}) copy-start(bf16[448,576]{1,0:T(8,128)(2,1)} %copy-done.4) | copy-start | bytes 1548292
  91.5 21.5 %copy-start.7 = (bf16[448,576]{1,0:T(8,128)(2,1)S(1)}, bf16[448,576]{1,0:T(8,128)(2,1)}, u32[]{:S(2)}) copy-start(bf16[448,576]{1,0:T(8,128)(2,1)} %copy-done.6) | copy-start | bytes 1548292
  91.5 21.5 %copy-start.9 = (bf16[448,576]{1,0:T(8,128)(2,1)S(1)}, bf16[448,576]{1,0:T(8,128)(2,1)}, u32[]{:S(2)}) copy-start(bf16[448,576]{1,0:T(8,128)(2,1)} %copy-done.8) | copy-start | bytes 1548292
  100.3 12.5 %collective-permute-start.23 = (bf16[1,56,896]{2,1,0:T(8,128)(2,1)S(1)}, bf16[1,56,896]{2,1,0:T(8,128)(2,1)S(1)}, u32[]{:S(2)}, u32[]{:S(2)}) collective-permute-start(bf16[1,56,896]{2,1,0:T(8,128)(2,1)S(1)} %slice.103), channel_id=1, source_target_pairs={{8,0},{9,1},{10,2},{11,3},{12,4},{13,5},{14,6},{15,7},{16,8},{17,9... | collective-permute-start | bytes 301064 | tf_op jit(solution)/shard_map/ppermute | solution.py:31
  101.9 11.0 %collective-permute-start.24 = (bf16[1,56,896]{2,1,0:T(8,128)(2,1)S(1)}, bf16[1,56,896]{2,1,0:T(8,128)(2,1)S(1)}, u32[]{:S(2)}, u32[]{:S(2)}) collective-permute-start(bf16[1,56,896]{2,1,0:T(8,128)(2,1)S(1)} %slice.104), channel_id=1, source_target_pairs={{24,0},{25,1},{26,2},{27,3},{28,4},{29,5},{30,6},{31,7},{0,8},{1,9... | collective-permute-start | bytes 301064 | tf_op jit(solution)/shard_map/ppermute | solution.py:31
  103.4 8.1 %collective-permute-start.21 = (bf16[2,56,896]{2,1,0:T(8,128)(2,1)}, bf16[2,56,896]{2,1,0:T(8,128)(2,1)S(1)}, u32[]{:S(2)}, u32[]{:S(2)}) collective-permute-start(bf16[2,56,896]{2,1,0:T(8,128)(2,1)} %collective-permute-done.19), channel_id=1, source_target_pairs={{4,0},{5,1},{6,2},{7,3},{8,4},{9,5},{10,6},{11,7},{12,8},{13,9},{1... | collective-permute-start | bytes 602120 | tf_op jit(solution)/shard_map/ppermute | solution.py:31
  103.8 9.1 %collective-permute-start.22 = (bf16[2,56,896]{2,1,0:T(8,128)(2,1)S(1)}, bf16[2,56,896]{2,1,0:T(8,128)(2,1)S(1)}, u32[]{:S(2)}, u32[]{:S(2)}) collective-permute-start(bf16[2,56,896]{2,1,0:T(8,128)(2,1)S(1)} %collective-permute-done.20), channel_id=1, source_target_pairs={{28,0},{29,1},{30,2},{31,3},{0,4},{1,5},{2,6},{3,7},{4,8},{5,9},{6... | collective-permute-start | bytes 602120 | tf_op jit(solution)/shard_map/ppermute | solution.py:31
  112.9 3.8 %collective-permute-start.25 = (bf16[2,448,896]{2,1,0:T(8,128)(2,1)S(1)}, bf16[2,448,896]{2,1,0:T(8,128)(2,1)S(1)}, u32[]{:S(2)}, u32[]{:S(2)}) collective-permute-start(bf16[2,448,896]{2,1,0:T(8,128)(2,1)S(1)} %maximum_dynamic-update-slice_fusion.refs_0_), channel_id=1, source_target_pairs={{0,1},{1,0},{2,3},{3,2},{4,5},{5,4},{6,7},{7,6},{8,9},{9,8},{10,11... | collective-permute-start | bytes 4816904 | tf_op jit(solution)/shard_map/ppermute | solution.py:44
  113.1 1.1 copy-start.11
  120.6 21.0 %copy-start.14 = (bf16[448,576]{1,0:T(8,128)(2,1)}, bf16[448,576]{1,0:T(8,128)(2,1)S(1)}, u32[]{:S(2)}) copy-start(bf16[448,576]{1,0:T(8,128)(2,1)S(1)} %get-tuple-element.25.own_y) | copy-start | bytes 1548292
  120.6 15.3 %collective-permute-start.26 = (bf16[448,576]{1,0:T(8,128)(2,1)S(1)}, bf16[448,576]{1,0:T(8,128)(2,1)S(1)}, u32[]{:S(2)}, u32[]{:S(2)}) collective-permute-start(bf16[448,576]{1,0:T(8,128)(2,1)S(1)} %get-tuple-element.25.own_y), channel_id=1, source_target_pairs={{32,0},{64,32},{96,64},{0,96},{160,128},{192,160},{224,192},{128,2... | collective-permute-start | bytes 1548296 | tf_op jit(solution)/shard_map/ppermute | solution.py:22
  121.3 16.3 %collective-permute-start.27 = (bf16[448,576]{1,0:T(8,128)(2,1)S(1)}, bf16[448,576]{1,0:T(8,128)(2,1)S(1)}, u32[]{:S(2)}, u32[]{:S(2)}) collective-permute-start(bf16[448,576]{1,0:T(8,128)(2,1)S(1)} %get-tuple-element.25.own_y), channel_id=1, source_target_pairs={{96,0},{0,32},{32,64},{64,96},{224,128},{128,160},{160,192},{192,2... | collective-permute-start | bytes 1548296 | tf_op jit(solution)/shard_map/ppermute | solution.py:22
  122.6 15.0 %collective-permute-start.29 = (bf16[448,576]{1,0:T(8,128)(2,1)S(1)}, bf16[448,576]{1,0:T(8,128)(2,1)}, u32[]{:S(2)}, u32[]{:S(2)}) collective-permute-start(bf16[448,576]{1,0:T(8,128)(2,1)S(1)} %get-tuple-element.25.own_y), channel_id=1, source_target_pairs={{0,128},{32,160},{64,192},{96,224},{128,0},{160,32},{192,64},{224,... | collective-permute-start | bytes 1548296 | tf_op jit(solution)/shard_map/ppermute | solution.py:26
  139.6 22.5 %collective-permute-start.30 = (bf16[336,576]{1,0:T(8,128)(2,1)}, bf16[336,576]{1,0:T(8,128)(2,1)}, u32[]{:S(2)}, u32[]{:S(2)}) collective-permute-start(bf16[336,576]{1,0:T(8,128)(2,1)} %get-tuple-element.66), channel_id=1, source_target_pairs={{32,0},{64,32},{96,64},{0,96},{160,128},{192,160},{224,192},{128,2... | collective-permute-start | bytes 1161224 | tf_op jit(solution)/shard_map/ppermute | solution.py:22
  141.4 24.4 %collective-permute-start.31 = (bf16[336,576]{1,0:T(8,128)(2,1)}, bf16[336,576]{1,0:T(8,128)(2,1)}, u32[]{:S(2)}, u32[]{:S(2)}) collective-permute-start(bf16[336,576]{1,0:T(8,128)(2,1)} %get-tuple-element.65), channel_id=1, source_target_pairs={{96,0},{0,32},{32,64},{64,96},{224,128},{128,160},{160,192},{192,2... | collective-permute-start | bytes 1161224 | tf_op jit(solution)/shard_map/ppermute | solution.py:22
  142.7 23.1 %collective-permute-start.28 = (bf16[672,576]{1,0:T(8,128)(2,1)}, bf16[672,576]{1,0:T(8,128)(2,1)}, u32[]{:S(2)}, u32[]{:S(2)}) collective-permute-start(bf16[672,576]{1,0:T(8,128)(2,1)} %pad_maximum_fusion), channel_id=1, source_target_pairs={{0,128},{32,160},{64,192},{96,224},{128,0},{160,32},{192,64},{224,... | collective-permute-start | bytes 2322440 | tf_op jit(solution)/shard_map/ppermute | solution.py:26
  143.8 3.0 %copy-start.16 = (bf16[2,448,896]{2,1,0:T(8,128)(2,1)}, bf16[2,448,896]{2,1,0:T(8,128)(2,1)S(1)}, u32[]{:S(2)}) copy-start(bf16[2,448,896]{2,1,0:T(8,128)(2,1)S(1)} %get-tuple-element.34) | copy-start | bytes 4816900
  143.8 22.0 %collective-permute-start.32 = (bf16[448,576]{1,0:T(8,128)(2,1)}, bf16[448,576]{1,0:T(8,128)(2,1)}, u32[]{:S(2)}, u32[]{:S(2)}) collective-permute-start(bf16[448,576]{1,0:T(8,128)(2,1)} %collective-permute-done.29.across), channel_id=1, source_target_pairs={{64,0},{96,32},{0,64},{32,96},{192,128},{224,160},{128,192},{160,2... | collective-permute-start | bytes 1548296 | tf_op jit(solution)/shard_map/ppermute | solution.py:22
  147.7 4.0 %copy-start.17 = (bf16[2,448,896]{2,1,0:T(8,128)(2,1)S(1)}, bf16[2,448,896]{2,1,0:T(8,128)(2,1)}, u32[]{:S(2)}) copy-start(bf16[2,448,896]{2,1,0:T(8,128)(2,1)} %copy-done.16) | copy-start | bytes 4816900
  155.3 1.4 copy-start.1
  156.8 1.3 copy-start.13
  (5 other events, 4.5 us)

commit v6 on v4

--- a/solution.py
+++ b/solution.py
@@ -31,12 +31,13 @@
     return lax.ppermute(value, "narrow", pairs)
 
 
-def from_y_hi(value):
-    return lax.ppermute(value, "narrow", [(n, n ^ 2) for n in range(32)])
-
-
-def from_y_both(value):
-    pairs = [((w, n), ((w + 4) % 8, n ^ 2)) for w in range(8) for n in range(32)]
+def from_y_first(value):
+    pairs = [((w, n ^ 2) if n % 2 == 0 else ((w + 4) % 8, n), (w, n)) for w in range(8) for n in range(32)]
+    return lax.ppermute(value, ("wide", "narrow"), [(a * 32 + b, c * 32 + d) for (a, b), (c, d) in pairs])
+
+
+def from_y_second(value):
+    pairs = [(((w + 4) % 8, n ^ 2), (w, n)) for w in range(8) for n in range(1, 32, 2)]
     return lax.ppermute(value, ("wide", "narrow"), [(a * 32 + b, c * 32 + d) for (a, b), (c, d) in pairs])
 
 
@@ -83,11 +84,11 @@
 
     @pl.when(core == (0 if mine else 1))
     def _():
-        run((0, 1, 4, 5))
+        run((0, 1, 2, 3))
 
     @pl.when(core == (1 if mine else 0))
     def _():
-        run((2, 3, 6, 7))
+        run((4, 5, 6, 7))
 
     def wait(at):
         pltpu.make_async_copy(x_refs[at], rhs.at[pl.ds(at * rows, rows)], sems.at[at]).wait()
@@ -97,11 +98,11 @@
     wait(0)
     wait(1)
     for part in parts:
-        found_ref[:, part] = dot(lhs[0], rhs[: 2 * rows, part])
+        found_ref[:, part] = dot(lhs[:, : 2 * rows], rhs[: 2 * rows, part])
     wait(2)
     wait(3)
     for part in parts:
-        value = found_ref[:, part] + dot(lhs[1], rhs[2 * rows :, part])
+        value = found_ref[:, part] + dot(lhs[:, 2 * rows :], rhs[2 * rows :, part])
         if not mine:
             value = before_ref[:, part] + value
             sent_ref[:, part] = value.astype(bf16)
@@ -132,8 +133,8 @@
     rows, cols = own_ref.shape
     core = lax.rem(lax.axis_index("narrow"), 2)
     copies = [
-        pltpu.make_async_copy(block_ref.at[0], lhs.at[core], sems.at[0]),
-        pltpu.make_async_copy(got_ref.at[0], lhs.at[1 - core], sems.at[1]),
+        pltpu.make_async_copy(block_ref, lhs.at[core], sems.at[0]),
+        pltpu.make_async_copy(got_ref, lhs.at[1 - core], sems.at[1]),
         pltpu.make_async_copy(own_y, rhs.at[pl.ds(0, rows)], sems.at[2]),
         pltpu.make_async_copy(right, rhs.at[pl.ds(rows, rows)], sems.at[3]),
     ]
@@ -144,7 +145,7 @@
     for start in range(0, cols, 256):
         part = pl.ds(start, min(256, cols - start))
         value = coef_a * own_ref[:, part].astype(f32) + coef_b * found_ref[:, part]
-        begun_ref[:, part] = value + coef_c * dot(lhs[0], rhs[:, part])
+        begun_ref[:, part] = value + coef_c * dot(lhs[0, :, : 2 * rows], rhs[:, part])
 
 
 def close_kernel(few, block_ref, got_ref, *refs):
@@ -178,12 +179,12 @@
     for copy in copies[:5]:
         copy.wait()
     for part in parts:
-        total[:, part] = dot(lhs[1, 0], rhs[:width, part])
+        total[:, part] = dot(lhs[0, :, width:], rhs[:width, part])
     for copy in copies[5:]:
         copy.wait()
     scale = float(COLS) ** 0.5
     for part in parts:
-        value = dot(lhs[0, 1], rhs[width : 2 * width, part]) + dot(lhs[1, 1], rhs[2 * width :, part])
+        value = dot(lhs[1], rhs[width:, part])
         out_ref[:, part] = (scale * (begun_ref[:, part] + coef_c * (total[:, part] + value))).astype(bf16)
 
 
@@ -196,7 +197,7 @@
         in_specs=[pl.BlockSpec(memory_space=pl.ANY)] * 4 + [vmem, vmem],
         out_specs=vmem,
         scratch_shapes=[
-            pltpu.VMEM(block.shape, bf16),
+            pltpu.VMEM((2, *block.shape), bf16),
             pltpu.VMEM((2 * rows, cols), bf16),
             pltpu.SemaphoreType.DMA((4,)),
         ],
@@ -263,24 +264,22 @@
     others = (from_x(late_across, 1), from_x(late_across, -1), from_y(late_far))
     total, other_right, other_left, other_far = lax.optimization_barrier((total, *others))
 
-    width = 2 * rows
-    total = jnp.where(core == 0, total, cat(total[unit:], total[:unit])).reshape(2, unit, 2 * width)
-    given = lax.dynamic_slice_in_dim(total, (1 - core) * width, width, 2).astype(bf16)
-    total = (lax.dynamic_slice_in_dim(total, core * width, width, 2) + from_core(given).astype(f32)).astype(bf16)
-
-    gram_same = total[0].astype(f32) + from_y_hi(total[0]).astype(f32)
-    gram_other = from_y(total[1]).astype(f32) + from_y_both(total[1]).astype(f32)
-    gram = jnp.stack([gram_same, gram_other]).astype(bf16)
+    total = total[:unit] + from_core(total[unit:].astype(bf16)).astype(f32)
+    total = total.astype(bf16)
+
+    first, second = from_y_first(total).astype(f32), from_y_second(total).astype(f32)
+    gram = (jnp.where(core == 0, total.astype(f32), second) + first).astype(bf16)
 
     up1, down1 = from_z(gram, 1), from_z(gram, -1)
     up2, down2 = from_z(gram, 2), from_z(gram, -2)
     up3, down3 = from_z(up2, 1), from_z(down2, -1)
-    up4, down4 = from_z(up2[:1], 2), from_z(down2[1:], -2)
-    block = jnp.zeros((2, rows, width), bf16)
-    pieces = ((0, gram), (1, up1), (-1, down1), (2, up2), (-2, down2), (3, up3), (-3, down3), (4, cat(up4, down4)))
+    four = along_z(jnp.where(core == 0, up2, down2), -2)
+    block = jnp.zeros((rows, 4 * rows), bf16)
+    pieces = ((0, gram), (1, up1), (-1, down1), (2, up2), (-2, down2), (3, up3), (-3, down3), (4, four))
     for step, piece in pieces:
-        block = lax.dynamic_update_slice_in_dim(block, piece, ((z_pos + step) % 8) * unit, 1)
+        block = lax.dynamic_update_slice_in_dim(block, piece, ((z_pos + step) % 8) * unit, 0)
     got = from_core(block)
+
     x_blocks = (own, x_right, x_left, x_far, across, other_right, other_left, other_far)
     found, sent = found_part(got, x_blocks, found_part(block, x_blocks))
     right, left, across = gather_first(sent)

time: 167 us -> 172 us (1.030)
  waiting for transfers between devices: 96 us -> 110 us
  starting transfers between devices: 40.1 us -> 35.9 us
  local copies, waits for them, and re-layouts: 9.56 us -> 7.42 us
    ppermute x8 -> x6, waiting for transfers between devices: 11.7 us -> 21 us  [from_z(): return lax.ppermute(value, 'narrow', pairs)]
    unnamed x25 -> x33, local copies, waits for them, and re-layouts: 3.2 us -> 5.62 us
    ppermute x2, starting transfers between devices: 4.18 us -> 2 us  [the longest x1 1.33 us: from_y_first(): lax.ppermute(value, ('wide', 'narrow'), [(a * 32 + b, c * 32 + d) for (a,...]
    ppermute x2, waiting for transfers between devices: 4.4 us -> 6.32 us  [the longest x1 6.32 us: from_y_first(): lax.ppermute(value, ('wide', 'narrow'), [(a * 32 + b, c * 32 + d) for (a,...]
    ppermute x11, waiting for transfers between devices: 52.4 us -> 54.3 us  [from_x(): return lax.ppermute(value, 'wide', pairs)]
    ppermute x8 -> x6, starting transfers between devices: 11.5 us -> 9.71 us  [from_z(): return lax.ppermute(value, 'narrow', pairs)]
    slice x3, local copies, waits for them, and re-layouts: 1.91 us -> 0.1 us  [units(): return summed[start * unit:stop * unit]]
    dynamic_update_slice x6, local copies, waits for them, and re-layouts: 2.95 us -> 1.2 us  [local(): lax.dynamic_update_slice_in_dim(block, piece, (z_pos + step) % 8 * unit, 0)]
  transfers between devices with their start and end apart: 33 -> 31, of which waited for: 18 -> 18; matrix products, arithmetic and copies ran while one was open for 6% -> 3% of each run, Pallas kernels for 2% -> 2%
where the time goes in v6:
time: 172 us; the launch traced here: 171 us
  waiting for transfers between devices  110 us (64%)
  starting transfers between devices  35.9 us (21%)
  Pallas kernels  11.7 us (7%)
  local copies, waits for them, and re-layouts  7.42 us (4%)
  matrix products  3 us (2%)
  other arithmetic  2.53 us (1%)
    ppermute x11, waiting for transfers between devices, from_x(): return lax.ppermute(value, 'wide', pairs)  54.3 us
    ppermute x5, waiting for transfers between devices, along_z(): return lax.ppermute(value, 'narrow', pairs)  24.2 us
    ppermute x6, waiting for transfers between devices, from_z(): return lax.ppermute(value, 'narrow', pairs)  21 us
    ppermute x11, starting transfers between devices, from_x(): return lax.ppermute(value, 'wide', pairs)  13.6 us
    ppermute x6, starting transfers between devices, from_z(): return lax.ppermute(value, 'narrow', pairs)  9.71 us
    ppermute x5, starting transfers between devices, along_z(): return lax.ppermute(value, 'narrow', pairs)  7.65 us
    ppermute x1, waiting for transfers between devices, from_y_first(): lax.ppermute(value, ('wide', 'narrow'), [(a * 32 + b, c * 32 + d) for (a,...  6.32 us
    unnamed x33, local copies, waits for them, and re-layouts  5.62 us
  transfers between devices with their start and end apart: 31, of which 18 were waited for; matrix products, arithmetic and copies ran while one was open for 3% of the time, Pallas kernels for 2%

profile of v6, /device:TPU:24, one launch (start us, length us, event | category | flops | bytes accessed | tf_op | source)
XLA Modules:
  0.0 170.6 jit_solution(6679790295486902557)
XLA Ops:
  0.0 2.8 %collective-permute-start.1 = (bf16[448,576]{1,0:T(8,128)(2,1)}, bf16[448,576]{1,0:T(8,128)(2,1)S(1)}, u32[]{:S(2)}, u32[]{:S(2)}) collective-permute-start(bf16[448,576]{1,0:T(8,128)(2,1)} %own_ref.1), channel_id=1, source_target_pairs={{32,0},{64,32},{96,64},{0,96},{160,128},{192,160},{224,192},{128,2... | collective-permute-start | bytes 1548296 | tf_op jit(solution)/shard_map/ppermute | solution.py:22
  2.8 0.7 collective-permute-start
  3.5 1.2 constant_dynamic-update-slice_fusion.6
  4.7 10.6 %collective-permute-done.1.refs_2_ = bf16[448,576]{1,0:T(8,128)(2,1)S(1)} collective-permute-done((bf16[448,576]{1,0:T(8,128)(2,1)}, bf16[448,576]{1,0:T(8,128)(2,1)S(1)}, u32[]{:S(2)}, u32[]{:S(2)}) %collective-permute-start.1) | collective-permute-done | bytes 516128 | tf_op jit(solution)/shard_map/ppermute | solution.py:22
  15.3 3.7 %collective-permute-start.3 = (bf16[224,576]{1,0:T(8,128)(2,1)S(1)}, bf16[224,576]{1,0:T(8,128)(2,1)S(1)}, u32[]{:S(2)}, u32[]{:S(2)}) collective-permute-start(bf16[224,576]{1,0:T(8,128)(2,1)S(1)} %slice.61), channel_id=1, source_target_pairs={{32,0},{64,32},{96,64},{0,96},{160,128},{192,160},{224,192},{128,2... | collective-permute-start | bytes 774152 | tf_op jit(solution)/shard_map/ppermute | solution.py:22
  19.7 4.5 %collective-permute-done.3 = bf16[224,576]{1,0:T(8,128)(2,1)S(1)} collective-permute-done((bf16[224,576]{1,0:T(8,128)(2,1)S(1)}, bf16[224,576]{1,0:T(8,128)(2,1)S(1)}, u32[]{:S(2)}, u32[]{:S(2)}) %collective-permute-start.3) | collective-permute-done | bytes 258080 | tf_op jit(solution)/shard_map/ppermute | solution.py:22
  24.3 3.5 %collective-permute-done.4 = bf16[224,576]{1,0:T(8,128)(2,1)S(1)} collective-permute-done((bf16[224,576]{1,0:T(8,128)(2,1)S(1)}, bf16[224,576]{1,0:T(8,128)(2,1)S(1)}, u32[]{:S(2)}, u32[]{:S(2)}) %collective-permute-start.4) | collective-permute-done | bytes 258080 | tf_op jit(solution)/shard_map/ppermute | solution.py:22
  27.8 1.5 convolution_convert_fusion
  29.4 1.5 fusion.3
  30.9 1.9 %collective-permute-done.5 = bf16[448,1792]{1,0:T(8,128)(2,1)S(1)} collective-permute-done((bf16[448,1792]{1,0:T(8,128)(2,1)S(1)}, bf16[448,1792]{1,0:T(8,128)(2,1)S(1)}, u32[]{:S(2)}, u32[]{:S(2)}) %collective-permute-start.5) | collective-permute-done | bytes 1605664 | tf_op jit(solution)/shard_map/ppermute | solution.py:45
  33.3 2.0 %collective-permute-start.6 = (bf16[112,1792]{1,0:T(8,128)(2,1)S(1)}, bf16[112,1792]{1,0:T(8,128)(2,1)S(1)}, u32[]{:S(2)}, u32[]{:S(2)}) collective-permute-start(bf16[112,1792]{1,0:T(8,128)(2,1)S(1)} %get-tuple-element.30), channel_id=1, source_target_pairs={{0,4},{1,29},{2,6},{3,31},{4,8},{5,1},{6,10},{7,3},{8,12},{9,5},{1... | collective-permute-start | bytes 1204232 | tf_op jit(solution)/shard_map/ppermute | solution.py:66
  35.3 3.3 %collective-permute-start.7 = (bf16[56,1792]{1,0:T(8,128)(2,1)S(1)}, bf16[56,1792]{1,0:T(8,128)(2,1)S(1)}, u32[]{:S(2)}, u32[]{:S(2)}) collective-permute-start(bf16[56,1792]{1,0:T(8,128)(2,1)S(1)} %slice.65), channel_id=1, source_target_pairs={{0,8},{1,25},{2,10},{3,27},{4,12},{5,29},{6,14},{7,31},{8,16},{9,1... | collective-permute-start | bytes 602120 | tf_op jit(solution)/shard_map/ppermute | solution.py:66
  38.7 10.6 %collective-permute-done.7 = bf16[56,1792]{1,0:T(8,128)(2,1)S(1)} collective-permute-done((bf16[56,1792]{1,0:T(8,128)(2,1)S(1)}, bf16[56,1792]{1,0:T(8,128)(2,1)S(1)}, u32[]{:S(2)}, u32[]{:S(2)}) %collective-permute-start.7) | collective-permute-done | bytes 200736 | tf_op jit(solution)/shard_map/ppermute | solution.py:66
  49.4 2.1 %collective-permute-start.9 = (bf16[112,1792]{1,0:T(8,128)(2,1)S(1)}, bf16[112,1792]{1,0:T(8,128)(2,1)S(1)}, u32[]{:S(2)}, u32[]{:S(2)}) collective-permute-start(bf16[112,1792]{1,0:T(8,128)(2,1)S(1)} %get-tuple-element.16), channel_id=1, source_target_pairs={{0,4},{1,29},{2,6},{3,31},{4,8},{5,1},{6,10},{7,3},{8,12},{9,5},{1... | collective-permute-start | bytes 1204232 | tf_op jit(solution)/shard_map/ppermute | solution.py:66
  51.8 1.8 %collective-permute-start.11 = (bf16[448,576]{1,0:T(8,128)(2,1)S(1)}, bf16[448,576]{1,0:T(8,128)(2,1)S(1)}, u32[]{:S(2)}, u32[]{:S(2)}) collective-permute-start(bf16[448,576]{1,0:T(8,128)(2,1)S(1)} %collective-permute-done.refs_5_), channel_id=1, source_target_pairs={{96,0},{0,32},{32,64},{64,96},{224,128},{128,160},{160,192},{192,2... | collective-permute-start | bytes 1548296 | tf_op jit(solution)/shard_map/ppermute | solution.py:22
  53.6 0.7 collective-permute-start.12
  54.4 9.4 %collective-permute-done.8 = bf16[112,1792]{1,0:T(8,128)(2,1)S(1)} collective-permute-done((bf16[112,1792]{1,0:T(8,128)(2,1)S(1)}, bf16[112,1792]{1,0:T(8,128)(2,1)S(1)}, u32[]{:S(2)}, u32[]{:S(2)}) %collective-permute-start.8) | collective-permute-done | bytes 401440 | tf_op jit(solution)/shard_map/ppermute | solution.py:66
  63.8 4.2 %collective-permute-done.9 = bf16[112,1792]{1,0:T(8,128)(2,1)S(1)} collective-permute-done((bf16[112,1792]{1,0:T(8,128)(2,1)S(1)}, bf16[112,1792]{1,0:T(8,128)(2,1)S(1)}, u32[]{:S(2)}, u32[]{:S(2)}) %collective-permute-start.9) | collective-permute-done | bytes 401440 | tf_op jit(solution)/shard_map/ppermute | solution.py:66
  68.1 0.8 copy-done.3
  69.0 0.8 copy-done.5
  69.8 0.8 copy-done.7
  70.7 1.4 collective-permute-done.13
  72.2 0.7 collective-permute-start.14
  72.9 1.3 collective-permute-start.15
  74.9 6.3 %collective-permute-done.15 = bf16[56,1792]{1,0:T(8,128)(2,1)} collective-permute-done((bf16[56,1792]{1,0:T(8,128)(2,1)S(1)}, bf16[56,1792]{1,0:T(8,128)(2,1)}, u32[]{:S(2)}, u32[]{:S(2)}) %collective-permute-start.15) | collective-permute-done | bytes 200736 | tf_op jit(solution)/shard_map/ppermute | solution.py:36
  81.3 0.8 copy-done.10
  82.1 1.7 constant_dynamic-update-slice_fusion.16
  84.1 1.7 %collective-permute-start.16 = (bf16[56,1792]{1,0:T(8,128)(2,1)}, bf16[56,1792]{1,0:T(8,128)(2,1)}, u32[]{:S(2)}, u32[]{:S(2)}) collective-permute-start(bf16[56,1792]{1,0:T(8,128)(2,1)} %get-tuple-element.26), channel_id=1, source_target_pairs={{4,0},{5,1},{6,2},{7,3},{8,4},{9,5},{10,6},{11,7},{12,8},{13,9},{1... | collective-permute-start | bytes 602120 | tf_op jit(solution)/shard_map/ppermute | solution.py:31
  86.2 2.6 %collective-permute-start.19 = (bf16[56,1792]{1,0:T(8,128)(2,1)}, bf16[56,1792]{1,0:T(8,128)(2,1)S(1)}, u32[]{:S(2)}, u32[]{:S(2)}) collective-permute-start(bf16[56,1792]{1,0:T(8,128)(2,1)} %get-tuple-element.26), channel_id=1, source_target_pairs={{24,0},{25,1},{26,2},{27,3},{28,4},{29,5},{30,6},{31,7},{0,8},{1,9... | collective-permute-start | bytes 602120 | tf_op jit(solution)/shard_map/ppermute | solution.py:31
  88.8 5.9 %collective-permute-done.18 = bf16[56,1792]{1,0:T(8,128)(2,1)S(1)} collective-permute-done((bf16[56,1792]{1,0:T(8,128)(2,1)}, bf16[56,1792]{1,0:T(8,128)(2,1)S(1)}, u32[]{:S(2)}, u32[]{:S(2)}) %collective-permute-start.18) | collective-permute-done | bytes 200736 | tf_op jit(solution)/shard_map/ppermute | solution.py:31
  94.7 3.0 %collective-permute-start.20 = (bf16[56,1792]{1,0:T(8,128)(2,1)S(1)}, bf16[56,1792]{1,0:T(8,128)(2,1)S(1)}, u32[]{:S(2)}, u32[]{:S(2)}) collective-permute-start(bf16[56,1792]{1,0:T(8,128)(2,1)S(1)} %collective-permute-done.18), channel_id=1, source_target_pairs={{4,0},{5,1},{6,2},{7,3},{8,4},{9,5},{10,6},{11,7},{12,8},{13,9},{1... | collective-permute-start | bytes 602120 | tf_op jit(solution)/shard_map/ppermute | solution.py:31
  97.6 2.2 %collective-permute-done.16 = bf16[56,1792]{1,0:T(8,128)(2,1)} collective-permute-done((bf16[56,1792]{1,0:T(8,128)(2,1)}, bf16[56,1792]{1,0:T(8,128)(2,1)}, u32[]{:S(2)}, u32[]{:S(2)}) %collective-permute-start.16) | collective-permute-done | bytes 200736 | tf_op jit(solution)/shard_map/ppermute | solution.py:31
  99.9 1.1 constant_dynamic-update-slice_fusion.15
  101.1 3.2 %collective-permute-done.19 = bf16[56,1792]{1,0:T(8,128)(2,1)S(1)} collective-permute-done((bf16[56,1792]{1,0:T(8,128)(2,1)}, bf16[56,1792]{1,0:T(8,128)(2,1)S(1)}, u32[]{:S(2)}, u32[]{:S(2)}) %collective-permute-start.19) | collective-permute-done | bytes 200736 | tf_op jit(solution)/shard_map/ppermute | solution.py:31
  104.4 1.8 %collective-permute-start.21 = (bf16[56,1792]{1,0:T(8,128)(2,1)S(1)}, bf16[56,1792]{1,0:T(8,128)(2,1)S(1)}, u32[]{:S(2)}, u32[]{:S(2)}) collective-permute-start(bf16[56,1792]{1,0:T(8,128)(2,1)S(1)} %collective-permute-done.19), channel_id=1, source_target_pairs={{28,0},{29,1},{30,2},{31,3},{0,4},{1,5},{2,6},{3,7},{4,8},{5,9},{6... | collective-permute-start | bytes 602120 | tf_op jit(solution)/shard_map/ppermute | solution.py:31
  106.2 9.6 %collective-permute-done.21 = bf16[56,1792]{1,0:T(8,128)(2,1)S(1)} collective-permute-done((bf16[56,1792]{1,0:T(8,128)(2,1)S(1)}, bf16[56,1792]{1,0:T(8,128)(2,1)S(1)}, u32[]{:S(2)}, u32[]{:S(2)}) %collective-permute-start.21) | collective-permute-done | bytes 200736 | tf_op jit(solution)/shard_map/ppermute | solution.py:31
  115.9 1.1 collective-permute-start.23
  117.0 2.6 %shard_map.17.refs_9_ = f32[448,576]{1,0:T(8,128)S(1)} custom-call(bf16[448,1792]{1,0:T(8,128)(2,1)S(1)} %constant_dynamic-update-slice_fusion.9.refs_0_.block_ref, bf16[448,576]{1,0:T(8,128)(2,1)S(1)} %copy-done, bf16[448,576]{1,0:T(8,128)(2,1)S(1)} %collective-permute-done.1.refs_2_, bf16[448,576]{1,0:T(8,128)(2,1)S(1)} %collective-permute-done.2.refs_3_, ...), custom_call_target="tpu_custom_call" | custom-call | flops 924844032 | bytes 6291456 | tf_op jit(solution)/shard_map/pallas_call | solution.py:117
  120.1 2.6 %shard_map.18 = (f32[448,576]{1,0:T(8,128)S(1)}, bf16[448,576]{1,0:T(8,128)(2,1)S(1)}) custom-call(bf16[448,1792]{1,0:T(8,128)(2,1)S(1)} %collective-permute-done.23.refs_0_.got_ref, bf16[448,576]{1,0:T(8,128)(2,1)S(1)} %copy-done, bf16[448,576]{1,0:T(8,128)(2,1)S(1)} %collective-permute-done.1.refs_2_, bf16[448,576]{1,0:T(8,128)(2,1)S(1)} %collective-permute-done.2.refs_3_, ...), custom_call_target="tpu_custom_call" | custom-call | flops 924844032 | bytes 6291456 | tf_op jit(solution)/shard_map/pallas_call | solution.py:117
  122.7 1.2 collective-permute-start.26
  123.9 1.1 collective-permute-start.24
  125.1 13.2 %collective-permute-done.26.right = bf16[448,576]{1,0:T(8,128)(2,1)S(1)} collective-permute-done((bf16[448,576]{1,0:T(8,128)(2,1)S(1)}, bf16[448,576]{1,0:T(8,128)(2,1)S(1)}, u32[]{:S(2)}, u32[]{:S(2)}) %collective-permute-start.26) | collective-permute-done | bytes 516128 | tf_op jit(solution)/shard_map/ppermute | solution.py:22
  138.3 1.8 %collective-permute-done.24.refs_0_ = bf16[448,576]{1,0:T(8,128)(2,1)S(1)} collective-permute-done((bf16[448,576]{1,0:T(8,128)(2,1)S(1)}, bf16[448,576]{1,0:T(8,128)(2,1)S(1)}, u32[]{:S(2)}, u32[]{:S(2)}) %collective-permute-start.24) | collective-permute-done | bytes 516128 | tf_op jit(solution)/shard_map/ppermute | solution.py:22
  140.9 2.4 %collective-permute-start.28 = (bf16[336,576]{1,0:T(8,128)(2,1)S(1)}, bf16[336,576]{1,0:T(8,128)(2,1)S(1)}, u32[]{:S(2)}, u32[]{:S(2)}) collective-permute-start(bf16[336,576]{1,0:T(8,128)(2,1)S(1)} %get-tuple-element.56), channel_id=1, source_target_pairs={{32,0},{64,32},{96,64},{0,96},{160,128},{192,160},{224,192},{128,2... | collective-permute-start | bytes 1161224 | tf_op jit(solution)/shard_map/ppermute | solution.py:22
  143.3 1.4 shard_map.19.refs_6_
  144.7 19.2 %collective-permute-done.28.refs_3_ = bf16[336,576]{1,0:T(8,128)(2,1)S(1)} collective-permute-done((bf16[336,576]{1,0:T(8,128)(2,1)S(1)}, bf16[336,576]{1,0:T(8,128)(2,1)S(1)}, u32[]{:S(2)}, u32[]{:S(2)}) %collective-permute-start.28) | collective-permute-done | bytes 387104 | tf_op jit(solution)/shard_map/ppermute | solution.py:22
  163.8 1.5 collective-permute-done.29.refs_4_
  165.4 5.0 %shard_map.20 = bf16[448,576]{1,0:T(8,128)(2,1)} custom-call(bf16[448,1792]{1,0:T(8,128)(2,1)S(1)} %constant_dynamic-update-slice_fusion.9.refs_0_.block_ref, bf16[448,1792]{1,0:T(8,128)(2,1)S(1)} %collective-permute-done.23.refs_0_.got_ref, bf16[448,576]{1,0:T(8,128)(2,1)S(1)} %collective-permute-done.24.refs_0_, ...), custom_call_target="tpu_custom_call" | custom-call | flops 1387266048 | bytes 9437184 | tf_op jit(solution)/shard_map/pallas_call | solution.py:212
  (82 shorter events, 4.9 us)
Async XLA Ops:
  0.0 15.3 %collective-permute-start.1 = (bf16[448,576]{1,0:T(8,128)(2,1)}, bf16[448,576]{1,0:T(8,128)(2,1)S(1)}, u32[]{:S(2)}, u32[]{:S(2)}) collective-permute-start(bf16[448,576]{1,0:T(8,128)(2,1)} %own_ref.1), channel_id=1, source_target_pairs={{32,0},{64,32},{96,64},{0,96},{160,128},{192,160},{224,192},{128,2... | collective-permute-start | bytes 1548296 | tf_op jit(solution)/shard_map/ppermute | solution.py:22
  2.8 16.2 %collective-permute-start.2 = (bf16[448,576]{1,0:T(8,128)(2,1)}, bf16[448,576]{1,0:T(8,128)(2,1)S(1)}, u32[]{:S(2)}, u32[]{:S(2)}) collective-permute-start(bf16[448,576]{1,0:T(8,128)(2,1)} %own_ref.1), channel_id=1, source_target_pairs={{96,0},{0,32},{32,64},{64,96},{224,128},{128,160},{160,192},{192,2... | collective-permute-start | bytes 1548296 | tf_op jit(solution)/shard_map/ppermute | solution.py:22
  2.8 16.4 %collective-permute-start = (bf16[448,576]{1,0:T(8,128)(2,1)}, bf16[448,576]{1,0:T(8,128)(2,1)S(1)}, u32[]{:S(2)}, u32[]{:S(2)}) collective-permute-start(bf16[448,576]{1,0:T(8,128)(2,1)} %own_ref.1), channel_id=1, source_target_pairs={{0,128},{32,160},{64,192},{96,224},{128,0},{160,32},{192,64},{224,... | collective-permute-start | bytes 1548296 | tf_op jit(solution)/shard_map/ppermute | solution.py:26
  15.3 8.9 %collective-permute-start.3 = (bf16[224,576]{1,0:T(8,128)(2,1)S(1)}, bf16[224,576]{1,0:T(8,128)(2,1)S(1)}, u32[]{:S(2)}, u32[]{:S(2)}) collective-permute-start(bf16[224,576]{1,0:T(8,128)(2,1)S(1)} %slice.61), channel_id=1, source_target_pairs={{32,0},{64,32},{96,64},{0,96},{160,128},{192,160},{224,192},{128,2... | collective-permute-start | bytes 774152 | tf_op jit(solution)/shard_map/ppermute | solution.py:22
  19.0 8.7 %collective-permute-start.4 = (bf16[224,576]{1,0:T(8,128)(2,1)S(1)}, bf16[224,576]{1,0:T(8,128)(2,1)S(1)}, u32[]{:S(2)}, u32[]{:S(2)}) collective-permute-start(bf16[224,576]{1,0:T(8,128)(2,1)S(1)} %slice.62), channel_id=1, source_target_pairs={{96,0},{0,32},{32,64},{64,96},{224,128},{128,160},{160,192},{192,2... | collective-permute-start | bytes 774152 | tf_op jit(solution)/shard_map/ppermute | solution.py:22
  27.8 25.8 %copy-start.1 = (bf16[448,576]{1,0:T(8,128)(2,1)}, bf16[448,576]{1,0:T(8,128)(2,1)S(1)}, u32[]{:S(2)}) copy-start(bf16[448,576]{1,0:T(8,128)(2,1)S(1)} %get-tuple-element.18.refs_4_) | copy-start | bytes 1548292
  29.3 3.5 %collective-permute-start.5 = (bf16[448,1792]{1,0:T(8,128)(2,1)S(1)}, bf16[448,1792]{1,0:T(8,128)(2,1)S(1)}, u32[]{:S(2)}, u32[]{:S(2)}) collective-permute-start(bf16[448,1792]{1,0:T(8,128)(2,1)S(1)} %convolution_convert_fusion), channel_id=1, source_target_pairs={{0,1},{1,0},{2,3},{3,2},{4,5},{5,4},{6,7},{7,6},{8,9},{9,8},{10,11... | collective-permute-start | bytes 4816904 | tf_op jit(solution)/shard_map/ppermute | solution.py:45
  33.3 15.9 %collective-permute-start.6 = (bf16[112,1792]{1,0:T(8,128)(2,1)S(1)}, bf16[112,1792]{1,0:T(8,128)(2,1)S(1)}, u32[]{:S(2)}, u32[]{:S(2)}) collective-permute-start(bf16[112,1792]{1,0:T(8,128)(2,1)S(1)} %get-tuple-element.30), channel_id=1, source_target_pairs={{0,4},{1,29},{2,6},{3,31},{4,8},{5,1},{6,10},{7,3},{8,12},{9,5},{1... | collective-permute-start | bytes 1204232 | tf_op jit(solution)/shard_map/ppermute | solution.py:66
  35.3 13.9 %collective-permute-start.7 = (bf16[56,1792]{1,0:T(8,128)(2,1)S(1)}, bf16[56,1792]{1,0:T(8,128)(2,1)S(1)}, u32[]{:S(2)}, u32[]{:S(2)}) collective-permute-start(bf16[56,1792]{1,0:T(8,128)(2,1)S(1)} %slice.65), channel_id=1, source_target_pairs={{0,8},{1,25},{2,10},{3,27},{4,12},{5,29},{6,14},{7,31},{8,16},{9,1... | collective-permute-start | bytes 602120 | tf_op jit(solution)/shard_map/ppermute | solution.py:66
  49.3 14.5 %collective-permute-start.8 = (bf16[112,1792]{1,0:T(8,128)(2,1)S(1)}, bf16[112,1792]{1,0:T(8,128)(2,1)S(1)}, u32[]{:S(2)}, u32[]{:S(2)}) collective-permute-start(bf16[112,1792]{1,0:T(8,128)(2,1)S(1)} %fusion), channel_id=1, source_target_pairs={{0,8},{1,25},{2,10},{3,27},{4,12},{5,29},{6,14},{7,31},{8,16},{9,1... | collective-permute-start | bytes 1204232 | tf_op jit(solution)/shard_map/ppermute | solution.py:66
  49.4 18.6 %collective-permute-start.9 = (bf16[112,1792]{1,0:T(8,128)(2,1)S(1)}, bf16[112,1792]{1,0:T(8,128)(2,1)S(1)}, u32[]{:S(2)}, u32[]{:S(2)}) collective-permute-start(bf16[112,1792]{1,0:T(8,128)(2,1)S(1)} %get-tuple-element.16), channel_id=1, source_target_pairs={{0,4},{1,29},{2,6},{3,31},{4,8},{5,1},{6,10},{7,3},{8,12},{9,5},{1... | collective-permute-start | bytes 1204232 | tf_op jit(solution)/shard_map/ppermute | solution.py:66
  51.6 16.5 %collective-permute-start.10 = (bf16[448,576]{1,0:T(8,128)(2,1)S(1)}, bf16[448,576]{1,0:T(8,128)(2,1)S(1)}, u32[]{:S(2)}, u32[]{:S(2)}) collective-permute-start(bf16[448,576]{1,0:T(8,128)(2,1)S(1)} %collective-permute-done.refs_5_), channel_id=1, source_target_pairs={{32,0},{64,32},{96,64},{0,96},{160,128},{192,160},{224,192},{128,2... | collective-permute-start | bytes 1548296 | tf_op jit(solution)/shard_map/ppermute | solution.py:22
  51.8 17.1 %collective-permute-start.11 = (bf16[448,576]{1,0:T(8,128)(2,1)S(1)}, bf16[448,576]{1,0:T(8,128)(2,1)S(1)}, u32[]{:S(2)}, u32[]{:S(2)}) collective-permute-start(bf16[448,576]{1,0:T(8,128)(2,1)S(1)} %collective-permute-done.refs_5_), channel_id=1, source_target_pairs={{96,0},{0,32},{32,64},{64,96},{224,128},{128,160},{160,192},{192,2... | collective-permute-start | bytes 1548296 | tf_op jit(solution)/shard_map/ppermute | solution.py:22
  53.6 16.2 %collective-permute-start.12 = (bf16[448,576]{1,0:T(8,128)(2,1)S(1)}, bf16[448,576]{1,0:T(8,128)(2,1)S(1)}, u32[]{:S(2)}, u32[]{:S(2)}) collective-permute-start(bf16[448,576]{1,0:T(8,128)(2,1)S(1)} %get-tuple-element.18.refs_4_), channel_id=1, source_target_pairs={{0,128},{32,160},{64,192},{96,224},{128,0},{160,32},{192,64},{224,... | collective-permute-start | bytes 1548296 | tf_op jit(solution)/shard_map/ppermute | solution.py:26
  68.1 0.8 copy-start.3
  69.0 0.8 copy-start.5
  69.8 0.8 copy-start.7
  70.6 1.5 collective-permute-start.13
  72.2 2.0 %collective-permute-start.14 = (bf16[56,1792]{1,0:T(8,128)(2,1)S(1)}, bf16[56,1792]{1,0:T(8,128)(2,1)S(1)}, u32[]{:S(2)}, u32[]{:S(2)}) collective-permute-start(bf16[56,1792]{1,0:T(8,128)(2,1)S(1)} %add_convert_fusion.1), channel_id=1, source_target_pairs={{131,1},{129,3},{135,5},{133,7},{139,9},{137,11},{143,13},{141,15}... | collective-permute-start | bytes 602120 | tf_op jit(solution)/shard_map/ppermute | solution.py:41
  72.9 8.3 %collective-permute-start.15 = (bf16[56,1792]{1,0:T(8,128)(2,1)S(1)}, bf16[56,1792]{1,0:T(8,128)(2,1)}, u32[]{:S(2)}, u32[]{:S(2)}) collective-permute-start(bf16[56,1792]{1,0:T(8,128)(2,1)S(1)} %add_convert_fusion.1), channel_id=1, source_target_pairs={{2,0},{129,1},{0,2},{131,3},{6,4},{133,5},{4,6},{135,7},{10,8},{13... | collective-permute-start | bytes 602120 | tf_op jit(solution)/shard_map/ppermute | solution.py:36
  74.2 0.7 copy-start.9
  81.2 0.9 copy-start.10
  83.8 10.8 %collective-permute-start.18 = (bf16[56,1792]{1,0:T(8,128)(2,1)}, bf16[56,1792]{1,0:T(8,128)(2,1)S(1)}, u32[]{:S(2)}, u32[]{:S(2)}) collective-permute-start(bf16[56,1792]{1,0:T(8,128)(2,1)} %get-tuple-element.26), channel_id=1, source_target_pairs={{8,0},{9,1},{10,2},{11,3},{12,4},{13,5},{14,6},{15,7},{16,8},{17,9... | collective-permute-start | bytes 602120 | tf_op jit(solution)/shard_map/ppermute | solution.py:31
  84.1 15.7 %collective-permute-start.16 = (bf16[56,1792]{1,0:T(8,128)(2,1)}, bf16[56,1792]{1,0:T(8,128)(2,1)}, u32[]{:S(2)}, u32[]{:S(2)}) collective-permute-start(bf16[56,1792]{1,0:T(8,128)(2,1)} %get-tuple-element.26), channel_id=1, source_target_pairs={{4,0},{5,1},{6,2},{7,3},{8,4},{9,5},{10,6},{11,7},{12,8},{13,9},{1... | collective-permute-start | bytes 602120 | tf_op jit(solution)/shard_map/ppermute | solution.py:31
  85.8 15.1 %collective-permute-start.17 = (bf16[56,1792]{1,0:T(8,128)(2,1)}, bf16[56,1792]{1,0:T(8,128)(2,1)S(1)}, u32[]{:S(2)}, u32[]{:S(2)}) collective-permute-start(bf16[56,1792]{1,0:T(8,128)(2,1)} %get-tuple-element.26), channel_id=1, source_target_pairs={{28,0},{29,1},{30,2},{31,3},{0,4},{1,5},{2,6},{3,7},{4,8},{5,9},{6... | collective-permute-start | bytes 602120 | tf_op jit(solution)/shard_map/ppermute | solution.py:31
  86.2 18.1 %collective-permute-start.19 = (bf16[56,1792]{1,0:T(8,128)(2,1)}, bf16[56,1792]{1,0:T(8,128)(2,1)S(1)}, u32[]{:S(2)}, u32[]{:S(2)}) collective-permute-start(bf16[56,1792]{1,0:T(8,128)(2,1)} %get-tuple-element.26), channel_id=1, source_target_pairs={{24,0},{25,1},{26,2},{27,3},{28,4},{29,5},{30,6},{31,7},{0,8},{1,9... | collective-permute-start | bytes 602120 | tf_op jit(solution)/shard_map/ppermute | solution.py:31
  94.7 11.5 %collective-permute-start.20 = (bf16[56,1792]{1,0:T(8,128)(2,1)S(1)}, bf16[56,1792]{1,0:T(8,128)(2,1)S(1)}, u32[]{:S(2)}, u32[]{:S(2)}) collective-permute-start(bf16[56,1792]{1,0:T(8,128)(2,1)S(1)} %collective-permute-done.18), channel_id=1, source_target_pairs={{4,0},{5,1},{6,2},{7,3},{8,4},{9,5},{10,6},{11,7},{12,8},{13,9},{1... | collective-permute-start | bytes 602120 | tf_op jit(solution)/shard_map/ppermute | solution.py:31
  99.9 17.2 %copy-start = (bf16[448,576]{1,0:T(8,128)(2,1)S(1)}, bf16[448,576]{1,0:T(8,128)(2,1)}, u32[]{:S(2)}) copy-start(bf16[448,576]{1,0:T(8,128)(2,1)} %own_ref.1) | copy-start | bytes 1548292
  99.9 17.2 %copy-start.2 = (bf16[448,576]{1,0:T(8,128)(2,1)S(1)}, bf16[448,576]{1,0:T(8,128)(2,1)}, u32[]{:S(2)}) copy-start(bf16[448,576]{1,0:T(8,128)(2,1)} %copy-done.1) | copy-start | bytes 1548292
  99.9 17.2 %copy-start.4 = (bf16[448,576]{1,0:T(8,128)(2,1)S(1)}, bf16[448,576]{1,0:T(8,128)(2,1)}, u32[]{:S(2)}) copy-start(bf16[448,576]{1,0:T(8,128)(2,1)} %copy-done.3) | copy-start | bytes 1548292
  99.9 17.2 %copy-start.6 = (bf16[448,576]{1,0:T(8,128)(2,1)S(1)}, bf16[448,576]{1,0:T(8,128)(2,1)}, u32[]{:S(2)}) copy-start(bf16[448,576]{1,0:T(8,128)(2,1)} %copy-done.5) | copy-start | bytes 1548292
  99.9 17.2 %copy-start.8 = (bf16[448,576]{1,0:T(8,128)(2,1)S(1)}, bf16[448,576]{1,0:T(8,128)(2,1)}, u32[]{:S(2)}) copy-start(bf16[448,576]{1,0:T(8,128)(2,1)} %copy-done.7) | copy-start | bytes 1548292
  104.3 11.5 %collective-permute-start.22 = (bf16[56,1792]{1,0:T(8,128)(2,1)S(1)}, bf16[56,1792]{1,0:T(8,128)(2,1)S(1)}, u32[]{:S(2)}, u32[]{:S(2)}) collective-permute-start(bf16[56,1792]{1,0:T(8,128)(2,1)S(1)} %get-tuple-element.53), channel_id=1, source_target_pairs={{0,24},{1,9},{2,26},{3,11},{4,28},{5,13},{6,30},{7,15},{8,0},{9,17... | collective-permute-start | bytes 602120 | tf_op jit(solution)/shard_map/ppermute | solution.py:66
  104.4 11.4 %collective-permute-start.21 = (bf16[56,1792]{1,0:T(8,128)(2,1)S(1)}, bf16[56,1792]{1,0:T(8,128)(2,1)S(1)}, u32[]{:S(2)}, u32[]{:S(2)}) collective-permute-start(bf16[56,1792]{1,0:T(8,128)(2,1)S(1)} %collective-permute-done.19), channel_id=1, source_target_pairs={{28,0},{29,1},{30,2},{31,3},{0,4},{1,5},{2,6},{3,7},{4,8},{5,9},{6... | collective-permute-start | bytes 602120 | tf_op jit(solution)/shard_map/ppermute | solution.py:31
  115.9 4.2 %collective-permute-start.23 = (bf16[448,1792]{1,0:T(8,128)(2,1)S(1)}, bf16[448,1792]{1,0:T(8,128)(2,1)S(1)}, u32[]{:S(2)}, u32[]{:S(2)}) collective-permute-start(bf16[448,1792]{1,0:T(8,128)(2,1)S(1)} %constant_dynamic-update-slice_fusion.9.refs_0_.block_ref), channel_id=1, source_target_pairs={{0,1},{1,0},{2,3},{3,2},{4,5},{5,4},{6,7},{7,6},{8,9},{9,8},{10,11... | collective-permute-start | bytes 4816904 | tf_op jit(solution)/shard_map/ppermute | solution.py:45
  122.7 15.6 %collective-permute-start.26 = (bf16[448,576]{1,0:T(8,128)(2,1)S(1)}, bf16[448,576]{1,0:T(8,128)(2,1)S(1)}, u32[]{:S(2)}, u32[]{:S(2)}) collective-permute-start(bf16[448,576]{1,0:T(8,128)(2,1)S(1)} %get-tuple-element.23.own_y), channel_id=1, source_target_pairs={{32,0},{64,32},{96,64},{0,96},{160,128},{192,160},{224,192},{128,2... | collective-permute-start | bytes 1548296 | tf_op jit(solution)/shard_map/ppermute | solution.py:22
  123.9 16.2 %collective-permute-start.24 = (bf16[448,576]{1,0:T(8,128)(2,1)S(1)}, bf16[448,576]{1,0:T(8,128)(2,1)S(1)}, u32[]{:S(2)}, u32[]{:S(2)}) collective-permute-start(bf16[448,576]{1,0:T(8,128)(2,1)S(1)} %get-tuple-element.23.own_y), channel_id=1, source_target_pairs={{96,0},{0,32},{32,64},{64,96},{224,128},{128,160},{160,192},{192,2... | collective-permute-start | bytes 1548296 | tf_op jit(solution)/shard_map/ppermute | solution.py:22
  125.0 15.3 %collective-permute-start.25 = (bf16[448,576]{1,0:T(8,128)(2,1)S(1)}, bf16[448,576]{1,0:T(8,128)(2,1)S(1)}, u32[]{:S(2)}, u32[]{:S(2)}) collective-permute-start(bf16[448,576]{1,0:T(8,128)(2,1)S(1)} %get-tuple-element.23.own_y), channel_id=1, source_target_pairs={{0,128},{32,160},{64,192},{96,224},{128,0},{160,32},{192,64},{224,... | collective-permute-start | bytes 1548296 | tf_op jit(solution)/shard_map/ppermute | solution.py:26
  140.2 25.1 %collective-permute-start.27 = (bf16[672,576]{1,0:T(8,128)(2,1)S(1)}, bf16[672,576]{1,0:T(8,128)(2,1)S(1)}, u32[]{:S(2)}, u32[]{:S(2)}) collective-permute-start(bf16[672,576]{1,0:T(8,128)(2,1)S(1)} %pad_maximum_fusion), channel_id=1, source_target_pairs={{0,128},{32,160},{64,192},{96,224},{128,0},{160,32},{192,64},{224,... | collective-permute-start | bytes 2322440 | tf_op jit(solution)/shard_map/ppermute | solution.py:26
  140.4 24.9 %collective-permute-start.30 = (bf16[448,576]{1,0:T(8,128)(2,1)S(1)}, bf16[448,576]{1,0:T(8,128)(2,1)S(1)}, u32[]{:S(2)}, u32[]{:S(2)}) collective-permute-start(bf16[448,576]{1,0:T(8,128)(2,1)S(1)} %collective-permute-done.25.refs_1_), channel_id=1, source_target_pairs={{64,0},{96,32},{0,64},{32,96},{192,128},{224,160},{128,192},{160,2... | collective-permute-start | bytes 1548296 | tf_op jit(solution)/shard_map/ppermute | solution.py:22
  140.9 23.0 %collective-permute-start.28 = (bf16[336,576]{1,0:T(8,128)(2,1)S(1)}, bf16[336,576]{1,0:T(8,128)(2,1)S(1)}, u32[]{:S(2)}, u32[]{:S(2)}) collective-permute-start(bf16[336,576]{1,0:T(8,128)(2,1)S(1)} %get-tuple-element.56), channel_id=1, source_target_pairs={{32,0},{64,32},{96,64},{0,96},{160,128},{192,160},{224,192},{128,2... | collective-permute-start | bytes 1161224 | tf_op jit(solution)/shard_map/ppermute | solution.py:22
  143.3 22.1 %collective-permute-start.29 = (bf16[336,576]{1,0:T(8,128)(2,1)S(1)}, bf16[336,576]{1,0:T(8,128)(2,1)S(1)}, u32[]{:S(2)}, u32[]{:S(2)}) collective-permute-start(bf16[336,576]{1,0:T(8,128)(2,1)S(1)} %get-tuple-element.55), channel_id=1, source_target_pairs={{96,0},{0,32},{32,64},{64,96},{224,128},{128,160},{160,192},{192,2... | collective-permute-start | bytes 1161224 | tf_op jit(solution)/shard_map/ppermute | solution.py:22

commit v7 on v4

--- a/solution.py
+++ b/solution.py
@@ -149,7 +149,7 @@
 
 def close_kernel(few, block_ref, got_ref, *refs):
     left, across, via_y, via_right, via_left, across_far = refs[:6]
-    begun_ref, out_ref, lhs, rhs, total, sems = refs[6:]
+    begun_ref, out_ref, lhs, rhs, total, begun, sems = refs[6:]
     rows, cols = out_ref.shape
     half, more = rows // 2, rows - few
     core = lax.rem(lax.axis_index("narrow"), 2)
@@ -171,6 +171,7 @@
     for at, (source, place) in enumerate(pieces):
         target = rhs.at[pl.ds(place, source.shape[0])] if isinstance(place, int) else place
         copies.append(pltpu.make_async_copy(source, target, sems.at[at]))
+    copies.append(pltpu.make_async_copy(begun_ref, begun, sems.at[11]))
     for copy in copies:
         copy.start()
     parts = [pl.ds(start, min(256, cols - start)) for start in range(0, cols, 256)]
@@ -184,7 +185,7 @@
     scale = float(COLS) ** 0.5
     for part in parts:
         value = dot(lhs[0, 1], rhs[width : 2 * width, part]) + dot(lhs[1, 1], rhs[2 * width :, part])
-        out_ref[:, part] = (scale * (begun_ref[:, part] + coef_c * (total[:, part] + value))).astype(bf16)
+        out_ref[:, part] = (scale * (begun[:, part] + coef_c * (total[:, part] + value))).astype(bf16)
 
 
 def open_product(block, got, own_y, right, found, own):
@@ -211,13 +212,14 @@
     return pl.pallas_call(
         functools.partial(close_kernel, few),
         out_shape=jax.ShapeDtypeStruct((rows, cols), bf16),
-        in_specs=[pl.BlockSpec(memory_space=pltpu.HBM)] * 8 + [vmem],
+        in_specs=[pl.BlockSpec(memory_space=pltpu.HBM)] * 9,
         out_specs=vmem,
         scratch_shapes=[
             pltpu.VMEM((2, *block.shape), bf16),
             pltpu.VMEM((6 * rows, cols), bf16),
             pltpu.VMEM((rows, cols), f32),
-            pltpu.SemaphoreType.DMA((11,)),
+            pltpu.VMEM((rows, cols), f32),
+            pltpu.SemaphoreType.DMA((12,)),
         ],
         compiler_params=pltpu.CompilerParams(vmem_limit_bytes=16 * 2**20),
         cost_estimate=pl.CostEstimate(flops=12 * rows * rows * cols, bytes_accessed=9 * 2**20, transcendentals=0),
@@ -264,20 +266,23 @@
     total, other_right, other_left, other_far = lax.optimization_barrier((total, *others))
 
     width = 2 * rows
-    total = jnp.where(core == 0, total, cat(total[unit:], total[:unit])).reshape(2, unit, 2 * width)
-    given = lax.dynamic_slice_in_dim(total, (1 - core) * width, width, 2).astype(bf16)
-    total = (lax.dynamic_slice_in_dim(total, core * width, width, 2) + from_core(given).astype(f32)).astype(bf16)
-
-    gram_same = total[0].astype(f32) + from_y_hi(total[0]).astype(f32)
-    gram_other = from_y(total[1]).astype(f32) + from_y_both(total[1]).astype(f32)
+    total = total.reshape(2, unit, 2 * width)
+    given = from_core(lax.dynamic_slice_in_dim(total, (1 - core) * width, width, 2).astype(bf16))
+    total = lax.dynamic_slice_in_dim(total, core * width, width, 2) + cat(given[1:], given[:1]).astype(f32)
+    total = total.astype(bf16)
+    kept = jnp.where(core == 0, total[0], total[1])
+    given = jnp.where(core == 0, total[1], total[0])
+
+    gram_same = kept.astype(f32) + from_y_hi(kept).astype(f32)
+    gram_other = from_y(given).astype(f32) + from_y_both(given).astype(f32)
     gram = jnp.stack([gram_same, gram_other]).astype(bf16)
 
     up1, down1 = from_z(gram, 1), from_z(gram, -1)
     up2, down2 = from_z(gram, 2), from_z(gram, -2)
     up3, down3 = from_z(up2, 1), from_z(down2, -1)
-    up4, down4 = from_z(up2[:1], 2), from_z(down2[1:], -2)
+    four = along_z(jnp.where(core == 0, up2, down2), -2)
     block = jnp.zeros((2, rows, width), bf16)
-    pieces = ((0, gram), (1, up1), (-1, down1), (2, up2), (-2, down2), (3, up3), (-3, down3), (4, cat(up4, down4)))
+    pieces = ((0, gram), (1, up1), (-1, down1), (2, up2), (-2, down2), (3, up3), (-3, down3), (4, four))
     for step, piece in pieces:
         block = lax.dynamic_update_slice_in_dim(block, piece, ((z_pos + step) % 8) * unit, 1)
     got = from_core(block)

time: 167 us -> 169 us (1.012)
  waiting for transfers between devices: 96 us -> 102 us
  local copies, waits for them, and re-layouts: 9.56 us -> 7.12 us
  starting transfers between devices: 40.1 us -> 38.1 us
    ppermute x4 -> x5, waiting for transfers between devices: 23.3 us -> 30.3 us  [along_z(): return lax.ppermute(value, 'narrow', pairs)]
    ppermute x8 -> x6, waiting for transfers between devices: 11.7 us -> 9.37 us  [from_z(): return lax.ppermute(value, 'narrow', pairs)]
    ppermute x8 -> x6, starting transfers between devices: 11.5 us -> 9.38 us  [from_z(): return lax.ppermute(value, 'narrow', pairs)]
    ppermute x4 -> x5, starting transfers between devices: 7.48 us -> 7.9 us  [along_z(): return lax.ppermute(value, 'narrow', pairs)]
  transfers between devices with their start and end apart: 33 -> 32, of which waited for: 18 -> 20; matrix products, arithmetic and copies ran while one was open for 6% -> 5% of each run, Pallas kernels for 2% -> 2%
where the time goes in v7:
time: 169 us; the launch traced here: 167 us
  waiting for transfers between devices  102 us (60%)
  starting transfers between devices  38.1 us (23%)
  Pallas kernels  11.6 us (7%)
  local copies, waits for them, and re-layouts  7.12 us (4%)
  other arithmetic  4.67 us (3%)
  matrix products  3 us (2%)
    ppermute x11, waiting for transfers between devices, from_x(): return lax.ppermute(value, 'wide', pairs)  53.5 us
    ppermute x5, waiting for transfers between devices, along_z(): return lax.ppermute(value, 'narrow', pairs)  30.3 us
    ppermute x11, starting transfers between devices, from_x(): return lax.ppermute(value, 'wide', pairs)  13.4 us
    ppermute x6, starting transfers between devices, from_z(): return lax.ppermute(value, 'narrow', pairs)  9.38 us
    ppermute x6, waiting for transfers between devices, from_z(): return lax.ppermute(value, 'narrow', pairs)  9.37 us
    ppermute x5, starting transfers between devices, along_z(): return lax.ppermute(value, 'narrow', pairs)  7.9 us
    pallas_call x2, Pallas kernels, found_part(): pl.pallas_call(functools.partial(found_kernel, mine), out_shape=found if...  5.28 us
    pallas_call x1, Pallas kernels, close_product(): pl.pallas_call(functools.partial(close_kernel, few), out_shape=jax.ShapeD...  5.08 us
  transfers between devices with their start and end apart: 32, of which 20 were waited for; matrix products, arithmetic and copies ran while one was open for 5% of the time, Pallas kernels for 2%

profile of v7, /device:TPU:24, one launch (start us, length us, event | category | flops | bytes accessed | tf_op | source)
XLA Modules:
  0.0 166.8 jit_solution(14651988086471555988)
XLA Ops:
  0.0 2.8 %collective-permute-start.1 = (bf16[448,576]{1,0:T(8,128)(2,1)}, bf16[448,576]{1,0:T(8,128)(2,1)S(1)}, u32[]{:S(2)}, u32[]{:S(2)}) collective-permute-start(bf16[448,576]{1,0:T(8,128)(2,1)} %own_ref.1), channel_id=1, source_target_pairs={{32,0},{64,32},{96,64},{0,96},{160,128},{192,160},{224,192},{128,2... | collective-permute-start | bytes 1548296 | tf_op jit(solution)/shard_map/ppermute | solution.py:22
  3.5 1.2 constant_dynamic-update-slice_fusion.6
  4.7 10.6 %collective-permute-done.1.refs_2_ = bf16[448,576]{1,0:T(8,128)(2,1)S(1)} collective-permute-done((bf16[448,576]{1,0:T(8,128)(2,1)}, bf16[448,576]{1,0:T(8,128)(2,1)S(1)}, u32[]{:S(2)}, u32[]{:S(2)}) %collective-permute-start.1) | collective-permute-done | bytes 516128 | tf_op jit(solution)/shard_map/ppermute | solution.py:22
  15.3 3.7 %collective-permute-start.3 = (bf16[224,576]{1,0:T(8,128)(2,1)S(1)}, bf16[224,576]{1,0:T(8,128)(2,1)S(1)}, u32[]{:S(2)}, u32[]{:S(2)}) collective-permute-start(bf16[224,576]{1,0:T(8,128)(2,1)S(1)} %slice.70), channel_id=1, source_target_pairs={{32,0},{64,32},{96,64},{0,96},{160,128},{192,160},{224,192},{128,2... | collective-permute-start | bytes 774152 | tf_op jit(solution)/shard_map/ppermute | solution.py:22
  19.7 4.5 %collective-permute-done.3 = bf16[224,576]{1,0:T(8,128)(2,1)S(1)} collective-permute-done((bf16[224,576]{1,0:T(8,128)(2,1)S(1)}, bf16[224,576]{1,0:T(8,128)(2,1)S(1)}, u32[]{:S(2)}, u32[]{:S(2)}) %collective-permute-start.3) | collective-permute-done | bytes 258080 | tf_op jit(solution)/shard_map/ppermute | solution.py:22
  24.3 3.5 %collective-permute-done.4 = bf16[224,576]{1,0:T(8,128)(2,1)S(1)} collective-permute-done((bf16[224,576]{1,0:T(8,128)(2,1)S(1)}, bf16[224,576]{1,0:T(8,128)(2,1)S(1)}, u32[]{:S(2)}, u32[]{:S(2)}) %collective-permute-start.4) | collective-permute-done | bytes 258080 | tf_op jit(solution)/shard_map/ppermute | solution.py:22
  27.8 1.5 convolution_convert_fusion
  29.4 1.5 fusion.6
  30.9 1.9 %collective-permute-done.5 = bf16[448,1792]{1,0:T(8,128)(2,1)S(1)} collective-permute-done((bf16[448,1792]{1,0:T(8,128)(2,1)S(1)}, bf16[448,1792]{1,0:T(8,128)(2,1)S(1)}, u32[]{:S(2)}, u32[]{:S(2)}) %collective-permute-start.5) | collective-permute-done | bytes 1605664 | tf_op jit(solution)/shard_map/ppermute | solution.py:44
  33.2 0.9 fusion.4
  34.1 1.9 %collective-permute-start.6 = (bf16[112,1792]{1,0:T(8,128)(2,1)S(1)}, bf16[112,1792]{1,0:T(8,128)(2,1)S(1)}, u32[]{:S(2)}, u32[]{:S(2)}) collective-permute-start(bf16[112,1792]{1,0:T(8,128)(2,1)S(1)} %get-tuple-element.28), channel_id=1, source_target_pairs={{0,4},{1,29},{2,6},{3,31},{4,8},{5,1},{6,10},{7,3},{8,12},{9,5},{1... | collective-permute-start | bytes 1204232 | tf_op jit(solution)/shard_map/ppermute | solution.py:65
  36.0 3.3 %collective-permute-start.7 = (bf16[56,1792]{1,0:T(8,128)(2,1)S(1)}, bf16[56,1792]{1,0:T(8,128)(2,1)S(1)}, u32[]{:S(2)}, u32[]{:S(2)}) collective-permute-start(bf16[56,1792]{1,0:T(8,128)(2,1)S(1)} %slice.74), channel_id=1, source_target_pairs={{0,8},{1,25},{2,10},{3,27},{4,12},{5,29},{6,14},{7,31},{8,16},{9,1... | collective-permute-start | bytes 602120 | tf_op jit(solution)/shard_map/ppermute | solution.py:65
  39.4 10.6 %collective-permute-done.7 = bf16[56,1792]{1,0:T(8,128)(2,1)S(1)} collective-permute-done((bf16[56,1792]{1,0:T(8,128)(2,1)S(1)}, bf16[56,1792]{1,0:T(8,128)(2,1)S(1)}, u32[]{:S(2)}, u32[]{:S(2)}) %collective-permute-start.7) | collective-permute-done | bytes 200736 | tf_op jit(solution)/shard_map/ppermute | solution.py:65
  50.2 2.1 %collective-permute-start.9 = (bf16[112,1792]{1,0:T(8,128)(2,1)}, bf16[112,1792]{1,0:T(8,128)(2,1)}, u32[]{:S(2)}, u32[]{:S(2)}) collective-permute-start(bf16[112,1792]{1,0:T(8,128)(2,1)} %get-tuple-element.16), channel_id=1, source_target_pairs={{0,4},{1,29},{2,6},{3,31},{4,8},{5,1},{6,10},{7,3},{8,12},{9,5},{1... | collective-permute-start | bytes 1204232 | tf_op jit(solution)/shard_map/ppermute | solution.py:65
  52.6 1.8 %collective-permute-start.11 = (bf16[448,576]{1,0:T(8,128)(2,1)S(1)}, bf16[448,576]{1,0:T(8,128)(2,1)}, u32[]{:S(2)}, u32[]{:S(2)}) collective-permute-start(bf16[448,576]{1,0:T(8,128)(2,1)S(1)} %collective-permute-done.refs_5_), channel_id=1, source_target_pairs={{96,0},{0,32},{32,64},{64,96},{224,128},{128,160},{160,192},{192,2... | collective-permute-start | bytes 1548296 | tf_op jit(solution)/shard_map/ppermute | solution.py:22
  55.1 1.0 slice.76
  56.1 8.5 %collective-permute-done.8 = bf16[112,1792]{1,0:T(8,128)(2,1)} collective-permute-done((bf16[112,1792]{1,0:T(8,128)(2,1)S(1)}, bf16[112,1792]{1,0:T(8,128)(2,1)}, u32[]{:S(2)}, u32[]{:S(2)}) %collective-permute-start.8) | collective-permute-done | bytes 401440 | tf_op jit(solution)/shard_map/ppermute | solution.py:65
  64.7 4.2 %collective-permute-done.9 = bf16[112,1792]{1,0:T(8,128)(2,1)} collective-permute-done((bf16[112,1792]{1,0:T(8,128)(2,1)}, bf16[112,1792]{1,0:T(8,128)(2,1)}, u32[]{:S(2)}, u32[]{:S(2)}) %collective-permute-start.9) | collective-permute-done | bytes 401440 | tf_op jit(solution)/shard_map/ppermute | solution.py:65
  68.9 1.2 pad_add_fusion
  70.1 0.9 copy-done.6
  71.1 1.4 collective-permute-done.13
  72.6 1.1 add_convert_fusion
  73.7 1.3 collective-permute-start.14
  75.0 2.9 %collective-permute-start.16 = (bf16[56,896]{1,0:T(8,128)(2,1)S(1)}, bf16[56,896]{1,0:T(8,128)(2,1)S(1)}, u32[]{:S(2)}, u32[]{:S(2)}) collective-permute-start(bf16[56,896]{1,0:T(8,128)(2,1)S(1)} %get-tuple-element.56), channel_id=1, source_target_pairs={{0,130},{1,131},{2,128},{3,129},{4,134},{5,135},{6,132},{7,133},{8... | collective-permute-start | bytes 301064 | tf_op jit(solution)/shard_map/ppermute | solution.py:40
  77.9 3.1 %collective-permute-done.14 = bf16[56,896]{1,0:T(8,128)(2,1)S(1)} collective-permute-done((bf16[56,896]{1,0:T(8,128)(2,1)S(1)}, bf16[56,896]{1,0:T(8,128)(2,1)S(1)}, u32[]{:S(2)}, u32[]{:S(2)}) %collective-permute-start.14) | collective-permute-done | bytes 100384 | tf_op jit(solution)/shard_map/ppermute | solution.py:35
  81.0 1.3 collective-permute-done.16
  83.2 2.9 %collective-permute-start.20 = (bf16[2,56,896]{2,1,0:T(8,128)(2,1)}, bf16[2,56,896]{2,1,0:T(8,128)(2,1)}, u32[]{:S(2)}, u32[]{:S(2)}) collective-permute-start(bf16[2,56,896]{2,1,0:T(8,128)(2,1)} %get-tuple-element.53), channel_id=1, source_target_pairs={{24,0},{25,1},{26,2},{27,3},{28,4},{29,5},{30,6},{31,7},{0,8},{1,9... | collective-permute-start | bytes 602120 | tf_op jit(solution)/shard_map/ppermute | solution.py:31
  86.1 1.8 %collective-permute-start.17 = (bf16[2,56,896]{2,1,0:T(8,128)(2,1)}, bf16[2,56,896]{2,1,0:T(8,128)(2,1)}, u32[]{:S(2)}, u32[]{:S(2)}) collective-permute-start(bf16[2,56,896]{2,1,0:T(8,128)(2,1)} %get-tuple-element.53), channel_id=1, source_target_pairs={{4,0},{5,1},{6,2},{7,3},{8,4},{9,5},{10,6},{11,7},{12,8},{13,9},{1... | collective-permute-start | bytes 602120 | tf_op jit(solution)/shard_map/ppermute | solution.py:31
  88.1 7.2 %collective-permute-done.19 = bf16[2,56,896]{2,1,0:T(8,128)(2,1)S(1)} collective-permute-done((bf16[2,56,896]{2,1,0:T(8,128)(2,1)}, bf16[2,56,896]{2,1,0:T(8,128)(2,1)S(1)}, u32[]{:S(2)}, u32[]{:S(2)}) %collective-permute-start.19) | collective-permute-done | bytes 200736 | tf_op jit(solution)/shard_map/ppermute | solution.py:31
  95.3 2.9 %collective-permute-start.21 = (bf16[2,56,896]{2,1,0:T(8,128)(2,1)S(1)}, bf16[2,56,896]{2,1,0:T(8,128)(2,1)S(1)}, u32[]{:S(2)}, u32[]{:S(2)}) collective-permute-start(bf16[2,56,896]{2,1,0:T(8,128)(2,1)S(1)} %collective-permute-done.19), channel_id=1, source_target_pairs={{4,0},{5,1},{6,2},{7,3},{8,4},{9,5},{10,6},{11,7},{12,8},{13,9},{1... | collective-permute-start | bytes 602120 | tf_op jit(solution)/shard_map/ppermute | solution.py:31
  98.2 1.5 collective-permute-start.22
  100.0 1.1 constant_dynamic-update-slice_fusion.15
  101.0 1.0 collective-permute-done.18
  102.0 1.0 constant_dynamic-update-slice_fusion.14
  103.0 1.0 broadcast_select_fusion
  104.4 1.0 collective-permute-done.22
  105.5 7.0 %collective-permute-done.23 = bf16[2,56,896]{2,1,0:T(8,128)(2,1)S(1)} collective-permute-done((bf16[2,56,896]{2,1,0:T(8,128)(2,1)S(1)}, bf16[2,56,896]{2,1,0:T(8,128)(2,1)S(1)}, u32[]{:S(2)}, u32[]{:S(2)}) %collective-permute-start.23) | collective-permute-done | bytes 200736 | tf_op jit(solution)/shard_map/ppermute | solution.py:65
  112.6 2.6 %shard_map.17.refs_9_ = f32[448,576]{1,0:T(8,128)S(1)} custom-call(bf16[2,448,896]{2,1,0:T(8,128)(2,1)S(1)} %constant_dynamic-update-slice_fusion.9.refs_0_.block_ref, bf16[448,576]{1,0:T(8,128)(2,1)S(1)} %copy-done, bf16[448,576]{1,0:T(8,128)(2,1)S(1)} %collective-permute-done.1.refs_2_, bf16[448,576]{1,0:T(8,128)(2,1)S(1)} %collective-permute-done.2.refs_3_, ...), custom_call_target="tpu_custom_call" | custom-call | flops 924844032 | bytes 6291456 | tf_op jit(solution)/shard_map/pallas_call | solution.py:116
  116.0 2.7 %shard_map.18 = (f32[448,576]{1,0:T(8,128)S(1)}, bf16[448,576]{1,0:T(8,128)(2,1)S(1)}) custom-call(bf16[2,448,896]{2,1,0:T(8,128)(2,1)S(1)} %collective-permute-done.24.refs_0_.got_ref, bf16[448,576]{1,0:T(8,128)(2,1)S(1)} %copy-done, bf16[448,576]{1,0:T(8,128)(2,1)S(1)} %collective-permute-done.1.refs_2_, ...), custom_call_target="tpu_custom_call" | custom-call | flops 924844032 | bytes 6291456 | tf_op jit(solution)/shard_map/pallas_call | solution.py:116
  118.7 1.0 collective-permute-start.27
  119.7 1.1 collective-permute-start.25
  121.5 12.5 %collective-permute-done.27.right = bf16[448,576]{1,0:T(8,128)(2,1)S(1)} collective-permute-done((bf16[448,576]{1,0:T(8,128)(2,1)S(1)}, bf16[448,576]{1,0:T(8,128)(2,1)S(1)}, u32[]{:S(2)}, u32[]{:S(2)}) %collective-permute-start.27) | collective-permute-done | bytes 516128 | tf_op jit(solution)/shard_map/ppermute | solution.py:22
  134.0 1.8 %collective-permute-done.25.refs_0_ = bf16[448,576]{1,0:T(8,128)(2,1)S(1)} collective-permute-done((bf16[448,576]{1,0:T(8,128)(2,1)S(1)}, bf16[448,576]{1,0:T(8,128)(2,1)S(1)}, u32[]{:S(2)}, u32[]{:S(2)}) %collective-permute-start.25) | collective-permute-done | bytes 516128 | tf_op jit(solution)/shard_map/ppermute | solution.py:22
  137.3 2.4 %collective-permute-start.29 = (bf16[336,576]{1,0:T(8,128)(2,1)S(1)}, bf16[336,576]{1,0:T(8,128)(2,1)S(1)}, u32[]{:S(2)}, u32[]{:S(2)}) collective-permute-start(bf16[336,576]{1,0:T(8,128)(2,1)S(1)} %get-tuple-element.60), channel_id=1, source_target_pairs={{32,0},{64,32},{96,64},{0,96},{160,128},{192,160},{224,192},{128,2... | collective-permute-start | bytes 1161224 | tf_op jit(solution)/shard_map/ppermute | solution.py:22
  139.7 1.2 shard_map.19.refs_6_
  140.9 18.6 %collective-permute-done.29.refs_3_ = bf16[336,576]{1,0:T(8,128)(2,1)S(1)} collective-permute-done((bf16[336,576]{1,0:T(8,128)(2,1)S(1)}, bf16[336,576]{1,0:T(8,128)(2,1)S(1)}, u32[]{:S(2)}, u32[]{:S(2)}) %collective-permute-start.29) | collective-permute-done | bytes 387104 | tf_op jit(solution)/shard_map/ppermute | solution.py:22
  159.6 1.9 %collective-permute-done.30.refs_4_ = bf16[336,576]{1,0:T(8,128)(2,1)S(1)} collective-permute-done((bf16[336,576]{1,0:T(8,128)(2,1)S(1)}, bf16[336,576]{1,0:T(8,128)(2,1)S(1)}, u32[]{:S(2)}, u32[]{:S(2)}) %collective-permute-start.30) | collective-permute-done | bytes 387104 | tf_op jit(solution)/shard_map/ppermute | solution.py:22
  161.5 5.1 %shard_map.20 = bf16[448,576]{1,0:T(8,128)(2,1)} custom-call(bf16[2,448,896]{2,1,0:T(8,128)(2,1)S(1)} %constant_dynamic-update-slice_fusion.9.refs_0_.block_ref, bf16[2,448,896]{2,1,0:T(8,128)(2,1)S(1)} %collective-permute-done.24.refs_0_.got_ref, bf16[448,576]{1,0:T(8,128)(2,1)S(1)} %collective-permute-done.25.refs_0_, ...), custom_call_target="tpu_custom_call" | custom-call | flops 1387266048 | bytes 9437184 | tf_op jit(solution)/shard_map/pallas_call | solution.py:212
  (80 shorter events, 8.2 us)
Async XLA Ops:
  0.0 15.3 %collective-permute-start.1 = (bf16[448,576]{1,0:T(8,128)(2,1)}, bf16[448,576]{1,0:T(8,128)(2,1)S(1)}, u32[]{:S(2)}, u32[]{:S(2)}) collective-permute-start(bf16[448,576]{1,0:T(8,128)(2,1)} %own_ref.1), channel_id=1, source_target_pairs={{32,0},{64,32},{96,64},{0,96},{160,128},{192,160},{224,192},{128,2... | collective-permute-start | bytes 1548296 | tf_op jit(solution)/shard_map/ppermute | solution.py:22
  2.8 16.2 %collective-permute-start.2 = (bf16[448,576]{1,0:T(8,128)(2,1)}, bf16[448,576]{1,0:T(8,128)(2,1)S(1)}, u32[]{:S(2)}, u32[]{:S(2)}) collective-permute-start(bf16[448,576]{1,0:T(8,128)(2,1)} %own_ref.1), channel_id=1, source_target_pairs={{96,0},{0,32},{32,64},{64,96},{224,128},{128,160},{160,192},{192,2... | collective-permute-start | bytes 1548296 | tf_op jit(solution)/shard_map/ppermute | solution.py:22
  2.8 16.4 %collective-permute-start = (bf16[448,576]{1,0:T(8,128)(2,1)}, bf16[448,576]{1,0:T(8,128)(2,1)S(1)}, u32[]{:S(2)}, u32[]{:S(2)}) collective-permute-start(bf16[448,576]{1,0:T(8,128)(2,1)} %own_ref.1), channel_id=1, source_target_pairs={{0,128},{32,160},{64,192},{96,224},{128,0},{160,32},{192,64},{224,... | collective-permute-start | bytes 1548296 | tf_op jit(solution)/shard_map/ppermute | solution.py:26
  15.3 8.9 %collective-permute-start.3 = (bf16[224,576]{1,0:T(8,128)(2,1)S(1)}, bf16[224,576]{1,0:T(8,128)(2,1)S(1)}, u32[]{:S(2)}, u32[]{:S(2)}) collective-permute-start(bf16[224,576]{1,0:T(8,128)(2,1)S(1)} %slice.70), channel_id=1, source_target_pairs={{32,0},{64,32},{96,64},{0,96},{160,128},{192,160},{224,192},{128,2... | collective-permute-start | bytes 774152 | tf_op jit(solution)/shard_map/ppermute | solution.py:22
  19.0 8.7 %collective-permute-start.4 = (bf16[224,576]{1,0:T(8,128)(2,1)S(1)}, bf16[224,576]{1,0:T(8,128)(2,1)S(1)}, u32[]{:S(2)}, u32[]{:S(2)}) collective-permute-start(bf16[224,576]{1,0:T(8,128)(2,1)S(1)} %slice.71), channel_id=1, source_target_pairs={{96,0},{0,32},{32,64},{64,96},{224,128},{128,160},{160,192},{192,2... | collective-permute-start | bytes 774152 | tf_op jit(solution)/shard_map/ppermute | solution.py:22
  27.8 26.5 %copy-start.1 = (bf16[448,576]{1,0:T(8,128)(2,1)}, bf16[448,576]{1,0:T(8,128)(2,1)S(1)}, u32[]{:S(2)}) copy-start(bf16[448,576]{1,0:T(8,128)(2,1)S(1)} %get-tuple-element.18.refs_4_) | copy-start | bytes 1548292
  29.3 3.5 %collective-permute-start.5 = (bf16[448,1792]{1,0:T(8,128)(2,1)S(1)}, bf16[448,1792]{1,0:T(8,128)(2,1)S(1)}, u32[]{:S(2)}, u32[]{:S(2)}) collective-permute-start(bf16[448,1792]{1,0:T(8,128)(2,1)S(1)} %convolution_convert_fusion), channel_id=1, source_target_pairs={{0,1},{1,0},{2,3},{3,2},{4,5},{5,4},{6,7},{7,6},{8,9},{9,8},{10,11... | collective-permute-start | bytes 4816904 | tf_op jit(solution)/shard_map/ppermute | solution.py:44
  33.2 16.9 %copy-start.5 = (f32[448,1792]{1,0:T(8,128)}, f32[448,1792]{1,0:T(8,128)S(1)}, u32[]{:S(2)}) copy-start(f32[448,1792]{1,0:T(8,128)S(1)} %get-tuple-element.26) | copy-start | bytes 9633796
  34.1 15.9 %collective-permute-start.6 = (bf16[112,1792]{1,0:T(8,128)(2,1)S(1)}, bf16[112,1792]{1,0:T(8,128)(2,1)S(1)}, u32[]{:S(2)}, u32[]{:S(2)}) collective-permute-start(bf16[112,1792]{1,0:T(8,128)(2,1)S(1)} %get-tuple-element.28), channel_id=1, source_target_pairs={{0,4},{1,29},{2,6},{3,31},{4,8},{5,1},{6,10},{7,3},{8,12},{9,5},{1... | collective-permute-start | bytes 1204232 | tf_op jit(solution)/shard_map/ppermute | solution.py:65
  36.0 13.9 %collective-permute-start.7 = (bf16[56,1792]{1,0:T(8,128)(2,1)S(1)}, bf16[56,1792]{1,0:T(8,128)(2,1)S(1)}, u32[]{:S(2)}, u32[]{:S(2)}) collective-permute-start(bf16[56,1792]{1,0:T(8,128)(2,1)S(1)} %slice.74), channel_id=1, source_target_pairs={{0,8},{1,25},{2,10},{3,27},{4,12},{5,29},{6,14},{7,31},{8,16},{9,1... | collective-permute-start | bytes 602120 | tf_op jit(solution)/shard_map/ppermute | solution.py:65
  50.1 14.6 %collective-permute-start.8 = (bf16[112,1792]{1,0:T(8,128)(2,1)S(1)}, bf16[112,1792]{1,0:T(8,128)(2,1)}, u32[]{:S(2)}, u32[]{:S(2)}) collective-permute-start(bf16[112,1792]{1,0:T(8,128)(2,1)S(1)} %fusion), channel_id=1, source_target_pairs={{0,8},{1,25},{2,10},{3,27},{4,12},{5,29},{6,14},{7,31},{8,16},{9,1... | collective-permute-start | bytes 1204232 | tf_op jit(solution)/shard_map/ppermute | solution.py:65
  50.2 18.7 %collective-permute-start.9 = (bf16[112,1792]{1,0:T(8,128)(2,1)}, bf16[112,1792]{1,0:T(8,128)(2,1)}, u32[]{:S(2)}, u32[]{:S(2)}) collective-permute-start(bf16[112,1792]{1,0:T(8,128)(2,1)} %get-tuple-element.16), channel_id=1, source_target_pairs={{0,4},{1,29},{2,6},{3,31},{4,8},{5,1},{6,10},{7,3},{8,12},{9,5},{1... | collective-permute-start | bytes 1204232 | tf_op jit(solution)/shard_map/ppermute | solution.py:65
  52.3 17.8 %collective-permute-start.10 = (bf16[448,576]{1,0:T(8,128)(2,1)S(1)}, bf16[448,576]{1,0:T(8,128)(2,1)S(1)}, u32[]{:S(2)}, u32[]{:S(2)}) collective-permute-start(bf16[448,576]{1,0:T(8,128)(2,1)S(1)} %collective-permute-done.refs_5_), channel_id=1, source_target_pairs={{32,0},{64,32},{96,64},{0,96},{160,128},{192,160},{224,192},{128,2... | collective-permute-start | bytes 1548296 | tf_op jit(solution)/shard_map/ppermute | solution.py:22
  52.6 17.5 %collective-permute-start.11 = (bf16[448,576]{1,0:T(8,128)(2,1)S(1)}, bf16[448,576]{1,0:T(8,128)(2,1)}, u32[]{:S(2)}, u32[]{:S(2)}) collective-permute-start(bf16[448,576]{1,0:T(8,128)(2,1)S(1)} %collective-permute-done.refs_5_), channel_id=1, source_target_pairs={{96,0},{0,32},{32,64},{64,96},{224,128},{128,160},{160,192},{192,2... | collective-permute-start | bytes 1548296 | tf_op jit(solution)/shard_map/ppermute | solution.py:22
  54.4 15.8 %collective-permute-start.12 = (bf16[448,576]{1,0:T(8,128)(2,1)S(1)}, bf16[448,576]{1,0:T(8,128)(2,1)}, u32[]{:S(2)}, u32[]{:S(2)}) collective-permute-start(bf16[448,576]{1,0:T(8,128)(2,1)S(1)} %get-tuple-element.18.refs_4_), channel_id=1, source_target_pairs={{0,128},{32,160},{64,192},{96,224},{128,0},{160,32},{192,64},{224,... | collective-permute-start | bytes 1548296 | tf_op jit(solution)/shard_map/ppermute | solution.py:26
  70.1 0.9 copy-start.6
  70.1 12.2 %copy-start.3 = (bf16[448,576]{1,0:T(8,128)(2,1)}, bf16[448,576]{1,0:T(8,128)(2,1)S(1)}, u32[]{:S(2)}) copy-start(bf16[448,576]{1,0:T(8,128)(2,1)S(1)} %collective-permute-done.10.refs_6_) | copy-start | bytes 1548292
  71.0 1.5 collective-permute-start.13
  73.7 7.3 %collective-permute-start.14 = (bf16[56,896]{1,0:T(8,128)(2,1)S(1)}, bf16[56,896]{1,0:T(8,128)(2,1)S(1)}, u32[]{:S(2)}, u32[]{:S(2)}) collective-permute-start(bf16[56,896]{1,0:T(8,128)(2,1)S(1)} %get-tuple-element.55), channel_id=1, source_target_pairs={{0,2},{1,3},{2,0},{3,1},{4,6},{5,7},{6,4},{7,5},{8,10},{9,11},{10,... | collective-permute-start | bytes 301064 | tf_op jit(solution)/shard_map/ppermute | solution.py:35
  75.0 6.0 %collective-permute-start.15 = (bf16[56,896]{1,0:T(8,128)(2,1)S(1)}, bf16[56,896]{1,0:T(8,128)(2,1)S(1)}, u32[]{:S(2)}, u32[]{:S(2)}) collective-permute-start(bf16[56,896]{1,0:T(8,128)(2,1)S(1)} %get-tuple-element.56), channel_id=1, source_target_pairs={{0,128},{32,160},{64,192},{96,224},{128,0},{160,32},{192,64},{224,... | collective-permute-start | bytes 301064 | tf_op jit(solution)/shard_map/ppermute | solution.py:26
  75.0 7.3 %collective-permute-start.16 = (bf16[56,896]{1,0:T(8,128)(2,1)S(1)}, bf16[56,896]{1,0:T(8,128)(2,1)S(1)}, u32[]{:S(2)}, u32[]{:S(2)}) collective-permute-start(bf16[56,896]{1,0:T(8,128)(2,1)S(1)} %get-tuple-element.56), channel_id=1, source_target_pairs={{0,130},{1,131},{2,128},{3,129},{4,134},{5,135},{6,132},{7,133},{8... | collective-permute-start | bytes 301064 | tf_op jit(solution)/shard_map/ppermute | solution.py:40
  83.2 12.1 %collective-permute-start.19 = (bf16[2,56,896]{2,1,0:T(8,128)(2,1)}, bf16[2,56,896]{2,1,0:T(8,128)(2,1)S(1)}, u32[]{:S(2)}, u32[]{:S(2)}) collective-permute-start(bf16[2,56,896]{2,1,0:T(8,128)(2,1)} %get-tuple-element.53), channel_id=1, source_target_pairs={{8,0},{9,1},{10,2},{11,3},{12,4},{13,5},{14,6},{15,7},{16,8},{17,9... | collective-permute-start | bytes 602120 | tf_op jit(solution)/shard_map/ppermute | solution.py:31
  83.2 15.0 %collective-permute-start.20 = (bf16[2,56,896]{2,1,0:T(8,128)(2,1)}, bf16[2,56,896]{2,1,0:T(8,128)(2,1)}, u32[]{:S(2)}, u32[]{:S(2)}) collective-permute-start(bf16[2,56,896]{2,1,0:T(8,128)(2,1)} %get-tuple-element.53), channel_id=1, source_target_pairs={{24,0},{25,1},{26,2},{27,3},{28,4},{29,5},{30,6},{31,7},{0,8},{1,9... | collective-permute-start | bytes 602120 | tf_op jit(solution)/shard_map/ppermute | solution.py:31
  86.1 13.8 %collective-permute-start.17 = (bf16[2,56,896]{2,1,0:T(8,128)(2,1)}, bf16[2,56,896]{2,1,0:T(8,128)(2,1)}, u32[]{:S(2)}, u32[]{:S(2)}) collective-permute-start(bf16[2,56,896]{2,1,0:T(8,128)(2,1)} %get-tuple-element.53), channel_id=1, source_target_pairs={{4,0},{5,1},{6,2},{7,3},{8,4},{9,5},{10,6},{11,7},{12,8},{13,9},{1... | collective-permute-start | bytes 602120 | tf_op jit(solution)/shard_map/ppermute | solution.py:31
  87.9 14.1 %collective-permute-start.18 = (bf16[2,56,896]{2,1,0:T(8,128)(2,1)}, bf16[2,56,896]{2,1,0:T(8,128)(2,1)}, u32[]{:S(2)}, u32[]{:S(2)}) collective-permute-start(bf16[2,56,896]{2,1,0:T(8,128)(2,1)} %get-tuple-element.53), channel_id=1, source_target_pairs={{28,0},{29,1},{30,2},{31,3},{0,4},{1,5},{2,6},{3,7},{4,8},{5,9},{6... | collective-permute-start | bytes 602120 | tf_op jit(solution)/shard_map/ppermute | solution.py:31
  95.3 9.1 %collective-permute-start.21 = (bf16[2,56,896]{2,1,0:T(8,128)(2,1)S(1)}, bf16[2,56,896]{2,1,0:T(8,128)(2,1)S(1)}, u32[]{:S(2)}, u32[]{:S(2)}) collective-permute-start(bf16[2,56,896]{2,1,0:T(8,128)(2,1)S(1)} %collective-permute-done.19), channel_id=1, source_target_pairs={{4,0},{5,1},{6,2},{7,3},{8,4},{9,5},{10,6},{11,7},{12,8},{13,9},{1... | collective-permute-start | bytes 602120 | tf_op jit(solution)/shard_map/ppermute | solution.py:31
  98.2 7.2 %collective-permute-start.22 = (bf16[2,56,896]{2,1,0:T(8,128)(2,1)}, bf16[2,56,896]{2,1,0:T(8,128)(2,1)S(1)}, u32[]{:S(2)}, u32[]{:S(2)}) collective-permute-start(bf16[2,56,896]{2,1,0:T(8,128)(2,1)} %collective-permute-done.20), channel_id=1, source_target_pairs={{28,0},{29,1},{30,2},{31,3},{0,4},{1,5},{2,6},{3,7},{4,8},{5,9},{6... | collective-permute-start | bytes 602120 | tf_op jit(solution)/shard_map/ppermute | solution.py:31
  100.0 12.6 %copy-start = (bf16[448,576]{1,0:T(8,128)(2,1)S(1)}, bf16[448,576]{1,0:T(8,128)(2,1)}, u32[]{:S(2)}) copy-start(bf16[448,576]{1,0:T(8,128)(2,1)} %own_ref.1) | copy-start | bytes 1548292
  100.0 12.7 %copy-start.2 = (bf16[448,576]{1,0:T(8,128)(2,1)S(1)}, bf16[448,576]{1,0:T(8,128)(2,1)}, u32[]{:S(2)}) copy-start(bf16[448,576]{1,0:T(8,128)(2,1)} %copy-done.1) | copy-start | bytes 1548292
  100.0 12.7 %copy-start.4 = (bf16[448,576]{1,0:T(8,128)(2,1)S(1)}, bf16[448,576]{1,0:T(8,128)(2,1)}, u32[]{:S(2)}) copy-start(bf16[448,576]{1,0:T(8,128)(2,1)} %copy-done.3) | copy-start | bytes 1548292
  104.0 8.5 %collective-permute-start.23 = (bf16[2,56,896]{2,1,0:T(8,128)(2,1)S(1)}, bf16[2,56,896]{2,1,0:T(8,128)(2,1)S(1)}, u32[]{:S(2)}, u32[]{:S(2)}) collective-permute-start(bf16[2,56,896]{2,1,0:T(8,128)(2,1)S(1)} %get-tuple-element.51), channel_id=1, source_target_pairs={{0,24},{1,9},{2,26},{3,11},{4,28},{5,13},{6,30},{7,15},{8,0},{9,17... | collective-permute-start | bytes 602120 | tf_op jit(solution)/shard_map/ppermute | solution.py:65
  112.5 3.5 %collective-permute-start.24 = (bf16[2,448,896]{2,1,0:T(8,128)(2,1)S(1)}, bf16[2,448,896]{2,1,0:T(8,128)(2,1)S(1)}, u32[]{:S(2)}, u32[]{:S(2)}) collective-permute-start(bf16[2,448,896]{2,1,0:T(8,128)(2,1)S(1)} %constant_dynamic-update-slice_fusion.9.refs_0_.block_ref), channel_id=1, source_target_pairs={{0,1},{1,0},{2,3},{3,2},{4,5},{5,4},{6,7},{7,6},{8,9},{9,8},{10,11... | collective-permute-start | bytes 4816904 | tf_op jit(solution)/shard_map/ppermute | solution.py:44
  118.7 15.3 %collective-permute-start.27 = (bf16[448,576]{1,0:T(8,128)(2,1)S(1)}, bf16[448,576]{1,0:T(8,128)(2,1)S(1)}, u32[]{:S(2)}, u32[]{:S(2)}) collective-permute-start(bf16[448,576]{1,0:T(8,128)(2,1)S(1)} %get-tuple-element.23.own_y), channel_id=1, source_target_pairs={{32,0},{64,32},{96,64},{0,96},{160,128},{192,160},{224,192},{128,2... | collective-permute-start | bytes 1548296 | tf_op jit(solution)/shard_map/ppermute | solution.py:22
  119.7 16.2 %collective-permute-start.25 = (bf16[448,576]{1,0:T(8,128)(2,1)S(1)}, bf16[448,576]{1,0:T(8,128)(2,1)S(1)}, u32[]{:S(2)}, u32[]{:S(2)}) collective-permute-start(bf16[448,576]{1,0:T(8,128)(2,1)S(1)} %get-tuple-element.23.own_y), channel_id=1, source_target_pairs={{96,0},{0,32},{32,64},{64,96},{224,128},{128,160},{160,192},{192,2... | collective-permute-start | bytes 1548296 | tf_op jit(solution)/shard_map/ppermute | solution.py:22
  120.8 16.0 %collective-permute-start.26 = (bf16[448,576]{1,0:T(8,128)(2,1)S(1)}, bf16[448,576]{1,0:T(8,128)(2,1)S(1)}, u32[]{:S(2)}, u32[]{:S(2)}) collective-permute-start(bf16[448,576]{1,0:T(8,128)(2,1)S(1)} %get-tuple-element.23.own_y), channel_id=1, source_target_pairs={{0,128},{32,160},{64,192},{96,224},{128,0},{160,32},{192,64},{224,... | collective-permute-start | bytes 1548296 | tf_op jit(solution)/shard_map/ppermute | solution.py:26
  136.0 25.5 %collective-permute-start.28 = (bf16[672,576]{1,0:T(8,128)(2,1)S(1)}, bf16[672,576]{1,0:T(8,128)(2,1)S(1)}, u32[]{:S(2)}, u32[]{:S(2)}) collective-permute-start(bf16[672,576]{1,0:T(8,128)(2,1)S(1)} %pad_maximum_fusion), channel_id=1, source_target_pairs={{0,128},{32,160},{64,192},{96,224},{128,0},{160,32},{192,64},{224,... | collective-permute-start | bytes 2322440 | tf_op jit(solution)/shard_map/ppermute | solution.py:26
  136.9 24.6 %collective-permute-start.31 = (bf16[448,576]{1,0:T(8,128)(2,1)S(1)}, bf16[448,576]{1,0:T(8,128)(2,1)S(1)}, u32[]{:S(2)}, u32[]{:S(2)}) collective-permute-start(bf16[448,576]{1,0:T(8,128)(2,1)S(1)} %collective-permute-done.26.refs_1_), channel_id=1, source_target_pairs={{64,0},{96,32},{0,64},{32,96},{192,128},{224,160},{128,192},{160,2... | collective-permute-start | bytes 1548296 | tf_op jit(solution)/shard_map/ppermute | solution.py:22
  137.3 22.3 %collective-permute-start.29 = (bf16[336,576]{1,0:T(8,128)(2,1)S(1)}, bf16[336,576]{1,0:T(8,128)(2,1)S(1)}, u32[]{:S(2)}, u32[]{:S(2)}) collective-permute-start(bf16[336,576]{1,0:T(8,128)(2,1)S(1)} %get-tuple-element.60), channel_id=1, source_target_pairs={{32,0},{64,32},{96,64},{0,96},{160,128},{192,160},{224,192},{128,2... | collective-permute-start | bytes 1161224 | tf_op jit(solution)/shard_map/ppermute | solution.py:22
  139.7 21.8 %collective-permute-start.30 = (bf16[336,576]{1,0:T(8,128)(2,1)S(1)}, bf16[336,576]{1,0:T(8,128)(2,1)S(1)}, u32[]{:S(2)}, u32[]{:S(2)}) collective-permute-start(bf16[336,576]{1,0:T(8,128)(2,1)S(1)} %get-tuple-element.59), channel_id=1, source_target_pairs={{96,0},{0,32},{32,64},{64,96},{224,128},{128,160},{160,192},{192,2... | collective-permute-start | bytes 1161224 | tf_op jit(solution)/shard_map/ppermute | solution.py:22

commit v8 on v7

--- a/solution.py
+++ b/solution.py
@@ -149,17 +149,25 @@
 
 def close_kernel(few, block_ref, got_ref, *refs):
     left, across, via_y, via_right, via_left, across_far = refs[:6]
-    begun_ref, out_ref, lhs, rhs, total, begun, sems = refs[6:]
+    begun_ref, out_ref, lhs, rhs, total, sems = refs[6:]
     rows, cols = out_ref.shape
     half, more = rows // 2, rows - few
     core = lax.rem(lax.axis_index("narrow"), 2)
 
+    @pl.when(core == 0)
+    def _():
+        pltpu.make_async_copy(got_ref.at[0], lhs.at[0], sems.at[0]).start()
+
+    @pl.when(core == 1)
+    def _():
+        pltpu.make_async_copy(block_ref.at[0], lhs.at[0], sems.at[0]).start()
+
     pieces = [
-        (block_ref, lhs.at[core]),
-        (got_ref, lhs.at[1 - core]),
         (left, 0),
         (via_right.at[pl.ds(0, half)], rows),
         (via_left.at[pl.ds(0, half)], rows + half),
+        (block_ref.at[1], lhs.at[1 + core]),
+        (got_ref.at[1], lhs.at[2 - core]),
         (across, 2 * rows),
         (via_right.at[pl.ds(half, few)], 3 * rows),
         (via_y.at[pl.ds(0, more)], 3 * rows + few),
@@ -170,22 +178,26 @@
     copies = []
     for at, (source, place) in enumerate(pieces):
         target = rhs.at[pl.ds(place, source.shape[0])] if isinstance(place, int) else place
-        copies.append(pltpu.make_async_copy(source, target, sems.at[at]))
-    copies.append(pltpu.make_async_copy(begun_ref, begun, sems.at[11]))
+        copies.append(pltpu.make_async_copy(source, target, sems.at[1 + at]))
     for copy in copies:
         copy.start()
     parts = [pl.ds(start, min(256, cols - start)) for start in range(0, cols, 256)]
     width = 2 * rows
-    for copy in copies[:5]:
+    pltpu.make_async_copy(block_ref.at[0], lhs.at[0], sems.at[0]).wait()
+    for copy in copies[:3]:
         copy.wait()
     for part in parts:
-        total[:, part] = dot(lhs[1, 0], rhs[:width, part])
-    for copy in copies[5:]:
+        total[:, part] = dot(lhs[0], rhs[:width, part])
+    for copy in copies[3:8]:
+        copy.wait()
+    for part in parts:
+        total[:, part] += dot(lhs[1], rhs[width : 2 * width, part])
+    for copy in copies[8:]:
         copy.wait()
     scale = float(COLS) ** 0.5
     for part in parts:
-        value = dot(lhs[0, 1], rhs[width : 2 * width, part]) + dot(lhs[1, 1], rhs[2 * width :, part])
-        out_ref[:, part] = (scale * (begun[:, part] + coef_c * (total[:, part] + value))).astype(bf16)
+        value = total[:, part] + dot(lhs[2], rhs[2 * width :, part])
+        out_ref[:, part] = (scale * (begun_ref[:, part] + coef_c * value)).astype(bf16)
 
 
 def open_product(block, got, own_y, right, found, own):
@@ -212,12 +224,11 @@
     return pl.pallas_call(
         functools.partial(close_kernel, few),
         out_shape=jax.ShapeDtypeStruct((rows, cols), bf16),
-        in_specs=[pl.BlockSpec(memory_space=pltpu.HBM)] * 9,
+        in_specs=[pl.BlockSpec(memory_space=pltpu.HBM)] * 8 + [vmem],
         out_specs=vmem,
         scratch_shapes=[
-            pltpu.VMEM((2, *block.shape), bf16),
+            pltpu.VMEM((3, *block.shape[1:]), bf16),
             pltpu.VMEM((6 * rows, cols), bf16),
-            pltpu.VMEM((rows, cols), f32),
             pltpu.VMEM((rows, cols), f32),
             pltpu.SemaphoreType.DMA((12,)),
         ],
@@ -280,9 +291,9 @@
     up1, down1 = from_z(gram, 1), from_z(gram, -1)
     up2, down2 = from_z(gram, 2), from_z(gram, -2)
     up3, down3 = from_z(up2, 1), from_z(down2, -1)
-    four = along_z(jnp.where(core == 0, up2, down2), -2)
+    up4, down4 = from_z(up2[:1], 2), from_z(down2[1:], -2)
     block = jnp.zeros((2, rows, width), bf16)
-    pieces = ((0, gram), (1, up1), (-1, down1), (2, up2), (-2, down2), (3, up3), (-3, down3), (4, four))
+    pieces = ((0, gram), (1, up1), (-1, down1), (2, up2), (-2, down2), (3, up3), (-3, down3), (4, cat(up4, down4)))
     for step, piece in pieces:
         block = lax.dynamic_update_slice_in_dim(block, piece, ((z_pos + step) % 8) * unit, 1)
     got = from_core(block)

time: 169 us -> 167 us (0.988)
  waiting for transfers between devices: 102 us -> 95.8 us
  starting transfers between devices: 38.1 us -> 41.1 us
  local copies, waits for them, and re-layouts: 7.12 us -> 8.84 us
    ppermute x5 -> x4, waiting for transfers between devices: 30.3 us -> 23.3 us  [along_z(): return lax.ppermute(value, 'narrow', pairs)]
    ppermute x6 -> x8, starting transfers between devices: 9.38 us -> 12.2 us  [from_z(): return lax.ppermute(value, 'narrow', pairs)]
    ppermute x6 -> x8, waiting for transfers between devices: 9.37 us -> 11.3 us  [from_z(): return lax.ppermute(value, 'narrow', pairs)]
    ppermute x5 -> x4, starting transfers between devices: 7.9 us -> 7.48 us  [along_z(): return lax.ppermute(value, 'narrow', pairs)]
  transfers between devices with their start and end apart: 32 -> 33, of which waited for: 20 -> 18; matrix products, arithmetic and copies ran while one was open for 5% -> 6% of each run, Pallas kernels for 2% -> 2%
where the time goes in v8:
time: 167 us; the launch traced here: 165 us
  waiting for transfers between devices  95.8 us (57%)
  starting transfers between devices  41.1 us (25%)
  Pallas kernels  11.8 us (7%)
  local copies, waits for them, and re-layouts  8.84 us (5%)
  other arithmetic  3.72 us (2%)
  matrix products  3 us (2%)
    ppermute x11, waiting for transfers between devices, from_x(): return lax.ppermute(value, 'wide', pairs)  52.6 us
    ppermute x4, waiting for transfers between devices, along_z(): return lax.ppermute(value, 'narrow', pairs)  23.3 us
    ppermute x11, starting transfers between devices, from_x(): return lax.ppermute(value, 'wide', pairs)  13.9 us
    ppermute x8, starting transfers between devices, from_z(): return lax.ppermute(value, 'narrow', pairs)  12.2 us
    ppermute x8, waiting for transfers between devices, from_z(): return lax.ppermute(value, 'narrow', pairs)  11.3 us
    ppermute x4, starting transfers between devices, along_z(): return lax.ppermute(value, 'narrow', pairs)  7.48 us
    pallas_call x1, Pallas kernels, close_product(): pl.pallas_call(functools.partial(close_kernel, few), out_shape=jax.ShapeD...  5.28 us
    pallas_call x2, Pallas kernels, found_part(): pl.pallas_call(functools.partial(found_kernel, mine), out_shape=found if...  5.24 us
  transfers between devices with their start and end apart: 33, of which 18 were waited for; matrix products, arithmetic and copies ran while one was open for 6% of the time, Pallas kernels for 2%

profile of v8, /device:TPU:24, one launch (start us, length us, event | category | flops | bytes accessed | tf_op | source)
XLA Modules:
  0.0 164.8 jit_solution(2617170966311095715)
XLA Ops:
  0.0 2.8 %collective-permute-start.1 = (bf16[448,576]{1,0:T(8,128)(2,1)}, bf16[448,576]{1,0:T(8,128)(2,1)S(1)}, u32[]{:S(2)}, u32[]{:S(2)}) collective-permute-start(bf16[448,576]{1,0:T(8,128)(2,1)} %own_ref.1), channel_id=1, source_target_pairs={{32,0},{64,32},{96,64},{0,96},{160,128},{192,160},{224,192},{128,2... | collective-permute-start | bytes 1548296 | tf_op jit(solution)/shard_map/ppermute | solution.py:22
  3.5 1.2 constant_dynamic-update-slice_fusion.6
  4.7 10.6 %collective-permute-done.1.refs_2_ = bf16[448,576]{1,0:T(8,128)(2,1)S(1)} collective-permute-done((bf16[448,576]{1,0:T(8,128)(2,1)}, bf16[448,576]{1,0:T(8,128)(2,1)S(1)}, u32[]{:S(2)}, u32[]{:S(2)}) %collective-permute-start.1) | collective-permute-done | bytes 516128 | tf_op jit(solution)/shard_map/ppermute | solution.py:22
  15.3 3.7 %collective-permute-start.3 = (bf16[224,576]{1,0:T(8,128)(2,1)S(1)}, bf16[224,576]{1,0:T(8,128)(2,1)S(1)}, u32[]{:S(2)}, u32[]{:S(2)}) collective-permute-start(bf16[224,576]{1,0:T(8,128)(2,1)S(1)} %slice.78), channel_id=1, source_target_pairs={{32,0},{64,32},{96,64},{0,96},{160,128},{192,160},{224,192},{128,2... | collective-permute-start | bytes 774152 | tf_op jit(solution)/shard_map/ppermute | solution.py:22
  19.7 4.5 %collective-permute-done.3 = bf16[224,576]{1,0:T(8,128)(2,1)S(1)} collective-permute-done((bf16[224,576]{1,0:T(8,128)(2,1)S(1)}, bf16[224,576]{1,0:T(8,128)(2,1)S(1)}, u32[]{:S(2)}, u32[]{:S(2)}) %collective-permute-start.3) | collective-permute-done | bytes 258080 | tf_op jit(solution)/shard_map/ppermute | solution.py:22
  24.3 3.5 %collective-permute-done.4 = bf16[224,576]{1,0:T(8,128)(2,1)S(1)} collective-permute-done((bf16[224,576]{1,0:T(8,128)(2,1)S(1)}, bf16[224,576]{1,0:T(8,128)(2,1)S(1)}, u32[]{:S(2)}, u32[]{:S(2)}) %collective-permute-start.4) | collective-permute-done | bytes 258080 | tf_op jit(solution)/shard_map/ppermute | solution.py:22
  27.8 1.5 convolution_convert_fusion
  29.4 1.5 fusion.6
  30.9 1.9 %collective-permute-done.5 = bf16[448,1792]{1,0:T(8,128)(2,1)S(1)} collective-permute-done((bf16[448,1792]{1,0:T(8,128)(2,1)S(1)}, bf16[448,1792]{1,0:T(8,128)(2,1)S(1)}, u32[]{:S(2)}, u32[]{:S(2)}) %collective-permute-start.5) | collective-permute-done | bytes 1605664 | tf_op jit(solution)/shard_map/ppermute | solution.py:44
  33.2 0.9 fusion.4
  34.1 1.9 %collective-permute-start.6 = (bf16[112,1792]{1,0:T(8,128)(2,1)S(1)}, bf16[112,1792]{1,0:T(8,128)(2,1)S(1)}, u32[]{:S(2)}, u32[]{:S(2)}) collective-permute-start(bf16[112,1792]{1,0:T(8,128)(2,1)S(1)} %get-tuple-element.28), channel_id=1, source_target_pairs={{0,4},{1,29},{2,6},{3,31},{4,8},{5,1},{6,10},{7,3},{8,12},{9,5},{1... | collective-permute-start | bytes 1204232 | tf_op jit(solution)/shard_map/ppermute | solution.py:65
  36.0 3.3 %collective-permute-start.7 = (bf16[56,1792]{1,0:T(8,128)(2,1)S(1)}, bf16[56,1792]{1,0:T(8,128)(2,1)S(1)}, u32[]{:S(2)}, u32[]{:S(2)}) collective-permute-start(bf16[56,1792]{1,0:T(8,128)(2,1)S(1)} %slice.82), channel_id=1, source_target_pairs={{0,8},{1,25},{2,10},{3,27},{4,12},{5,29},{6,14},{7,31},{8,16},{9,1... | collective-permute-start | bytes 602120 | tf_op jit(solution)/shard_map/ppermute | solution.py:65
  39.4 10.6 %collective-permute-done.7 = bf16[56,1792]{1,0:T(8,128)(2,1)S(1)} collective-permute-done((bf16[56,1792]{1,0:T(8,128)(2,1)S(1)}, bf16[56,1792]{1,0:T(8,128)(2,1)S(1)}, u32[]{:S(2)}, u32[]{:S(2)}) %collective-permute-start.7) | collective-permute-done | bytes 200736 | tf_op jit(solution)/shard_map/ppermute | solution.py:65
  50.2 2.1 %collective-permute-start.9 = (bf16[112,1792]{1,0:T(8,128)(2,1)}, bf16[112,1792]{1,0:T(8,128)(2,1)}, u32[]{:S(2)}, u32[]{:S(2)}) collective-permute-start(bf16[112,1792]{1,0:T(8,128)(2,1)} %get-tuple-element.16), channel_id=1, source_target_pairs={{0,4},{1,29},{2,6},{3,31},{4,8},{5,1},{6,10},{7,3},{8,12},{9,5},{1... | collective-permute-start | bytes 1204232 | tf_op jit(solution)/shard_map/ppermute | solution.py:65
  52.6 1.8 %collective-permute-start.11 = (bf16[448,576]{1,0:T(8,128)(2,1)S(1)}, bf16[448,576]{1,0:T(8,128)(2,1)}, u32[]{:S(2)}, u32[]{:S(2)}) collective-permute-start(bf16[448,576]{1,0:T(8,128)(2,1)S(1)} %collective-permute-done.refs_5_), channel_id=1, source_target_pairs={{96,0},{0,32},{32,64},{64,96},{224,128},{128,160},{160,192},{192,2... | collective-permute-start | bytes 1548296 | tf_op jit(solution)/shard_map/ppermute | solution.py:22
  55.1 1.0 slice.84
  56.1 8.5 %collective-permute-done.8 = bf16[112,1792]{1,0:T(8,128)(2,1)} collective-permute-done((bf16[112,1792]{1,0:T(8,128)(2,1)S(1)}, bf16[112,1792]{1,0:T(8,128)(2,1)}, u32[]{:S(2)}, u32[]{:S(2)}) %collective-permute-start.8) | collective-permute-done | bytes 401440 | tf_op jit(solution)/shard_map/ppermute | solution.py:65
  64.7 4.2 %collective-permute-done.9 = bf16[112,1792]{1,0:T(8,128)(2,1)} collective-permute-done((bf16[112,1792]{1,0:T(8,128)(2,1)}, bf16[112,1792]{1,0:T(8,128)(2,1)}, u32[]{:S(2)}, u32[]{:S(2)}) %collective-permute-start.9) | collective-permute-done | bytes 401440 | tf_op jit(solution)/shard_map/ppermute | solution.py:65
  68.9 1.2 pad_add_fusion
  70.1 0.9 copy-done.6
  71.1 1.4 collective-permute-done.13
  72.6 1.1 add_convert_fusion
  73.7 1.3 collective-permute-start.14
  75.0 2.9 %collective-permute-start.16 = (bf16[56,896]{1,0:T(8,128)(2,1)S(1)}, bf16[56,896]{1,0:T(8,128)(2,1)S(1)}, u32[]{:S(2)}, u32[]{:S(2)}) collective-permute-start(bf16[56,896]{1,0:T(8,128)(2,1)S(1)} %get-tuple-element.54), channel_id=1, source_target_pairs={{0,130},{1,131},{2,128},{3,129},{4,134},{5,135},{6,132},{7,133},{8... | collective-permute-start | bytes 301064 | tf_op jit(solution)/shard_map/ppermute | solution.py:40
  77.9 3.1 %collective-permute-done.14 = bf16[56,896]{1,0:T(8,128)(2,1)S(1)} collective-permute-done((bf16[56,896]{1,0:T(8,128)(2,1)S(1)}, bf16[56,896]{1,0:T(8,128)(2,1)S(1)}, u32[]{:S(2)}, u32[]{:S(2)}) %collective-permute-start.14) | collective-permute-done | bytes 100384 | tf_op jit(solution)/shard_map/ppermute | solution.py:35
  81.0 1.3 collective-permute-done.16
  83.2 2.9 %collective-permute-start.20 = (bf16[2,56,896]{2,1,0:T(8,128)(2,1)}, bf16[2,56,896]{2,1,0:T(8,128)(2,1)S(1)}, u32[]{:S(2)}, u32[]{:S(2)}) collective-permute-start(bf16[2,56,896]{2,1,0:T(8,128)(2,1)} %get-tuple-element.51), channel_id=1, source_target_pairs={{24,0},{25,1},{26,2},{27,3},{28,4},{29,5},{30,6},{31,7},{0,8},{1,9... | collective-permute-start | bytes 602120 | tf_op jit(solution)/shard_map/ppermute | solution.py:31
  86.1 1.8 %collective-permute-start.17 = (bf16[2,56,896]{2,1,0:T(8,128)(2,1)}, bf16[2,56,896]{2,1,0:T(8,128)(2,1)}, u32[]{:S(2)}, u32[]{:S(2)}) collective-permute-start(bf16[2,56,896]{2,1,0:T(8,128)(2,1)} %get-tuple-element.51), channel_id=1, source_target_pairs={{4,0},{5,1},{6,2},{7,3},{8,4},{9,5},{10,6},{11,7},{12,8},{13,9},{1... | collective-permute-start | bytes 602120 | tf_op jit(solution)/shard_map/ppermute | solution.py:31
  88.1 7.3 %collective-permute-done.19 = bf16[2,56,896]{2,1,0:T(8,128)(2,1)} collective-permute-done((bf16[2,56,896]{2,1,0:T(8,128)(2,1)}, bf16[2,56,896]{2,1,0:T(8,128)(2,1)}, u32[]{:S(2)}, u32[]{:S(2)}) %collective-permute-start.19) | collective-permute-done | bytes 200736 | tf_op jit(solution)/shard_map/ppermute | solution.py:31
  95.4 0.9 slice.89
  96.3 1.8 %collective-permute-start.23 = (bf16[1,56,896]{2,1,0:T(8,128)(2,1)S(1)}, bf16[1,56,896]{2,1,0:T(8,128)(2,1)S(1)}, u32[]{:S(2)}, u32[]{:S(2)}) collective-permute-start(bf16[1,56,896]{2,1,0:T(8,128)(2,1)S(1)} %slice.89), channel_id=1, source_target_pairs={{8,0},{9,1},{10,2},{11,3},{12,4},{13,5},{14,6},{15,7},{16,8},{17,9... | collective-permute-start | bytes 301064 | tf_op jit(solution)/shard_map/ppermute | solution.py:31
  98.1 1.3 collective-permute-start.24
  99.4 4.1 %collective-permute-start.21 = (bf16[2,56,896]{2,1,0:T(8,128)(2,1)}, bf16[2,56,896]{2,1,0:T(8,128)(2,1)S(1)}, u32[]{:S(2)}, u32[]{:S(2)}) collective-permute-start(bf16[2,56,896]{2,1,0:T(8,128)(2,1)} %collective-permute-done.19), channel_id=1, source_target_pairs={{4,0},{5,1},{6,2},{7,3},{8,4},{9,5},{10,6},{11,7},{12,8},{13,9},{1... | collective-permute-start | bytes 602120 | tf_op jit(solution)/shard_map/ppermute | solution.py:31
  103.5 1.0 constant_dynamic-update-slice_fusion.14
  104.5 1.0 constant_dynamic-update-slice_fusion.13
  105.5 1.0 constant_dynamic-update-slice_fusion.12
  106.5 1.4 collective-permute-done.21
  107.9 2.6 %collective-permute-done.22 = bf16[2,56,896]{2,1,0:T(8,128)(2,1)S(1)} collective-permute-done((bf16[2,56,896]{2,1,0:T(8,128)(2,1)S(1)}, bf16[2,56,896]{2,1,0:T(8,128)(2,1)S(1)}, u32[]{:S(2)}, u32[]{:S(2)}) %collective-permute-start.22) | collective-permute-done | bytes 200736 | tf_op jit(solution)/shard_map/ppermute | solution.py:31
  110.7 2.6 %shard_map.17.refs_9_ = f32[448,576]{1,0:T(8,128)S(1)} custom-call(bf16[2,448,896]{2,1,0:T(8,128)(2,1)S(1)} %maximum_dynamic-update-slice_fusion.refs_0_.block_ref, bf16[448,576]{1,0:T(8,128)(2,1)S(1)} %copy-done, bf16[448,576]{1,0:T(8,128)(2,1)S(1)} %collective-permute-done.1.refs_2_, bf16[448,576]{1,0:T(8,128)(2,1)S(1)} %collective-permute-done.2.refs_3_, ...), custom_call_target="tpu_custom_call" | custom-call | flops 924844032 | bytes 6291456 | tf_op jit(solution)/shard_map/pallas_call | solution.py:116
  114.1 2.6 %shard_map.18 = (f32[448,576]{1,0:T(8,128)S(1)}, bf16[448,576]{1,0:T(8,128)(2,1)S(1)}) custom-call(bf16[2,448,896]{2,1,0:T(8,128)(2,1)S(1)} %collective-permute-done.25.refs_0_.got_ref, bf16[448,576]{1,0:T(8,128)(2,1)S(1)} %copy-done, bf16[448,576]{1,0:T(8,128)(2,1)S(1)} %collective-permute-done.1.refs_2_, ...), custom_call_target="tpu_custom_call" | custom-call | flops 924844032 | bytes 6291456 | tf_op jit(solution)/shard_map/pallas_call | solution.py:116
  116.8 2.0 %collective-permute-start.26 = (bf16[448,576]{1,0:T(8,128)(2,1)S(1)}, bf16[448,576]{1,0:T(8,128)(2,1)S(1)}, u32[]{:S(2)}, u32[]{:S(2)}) collective-permute-start(bf16[448,576]{1,0:T(8,128)(2,1)S(1)} %get-tuple-element.23.own_y), channel_id=1, source_target_pairs={{96,0},{0,32},{32,64},{64,96},{224,128},{128,160},{160,192},{192,2... | collective-permute-start | bytes 1548296 | tf_op jit(solution)/shard_map/ppermute | solution.py:22
  119.6 12.4 %collective-permute-done.28.right = bf16[448,576]{1,0:T(8,128)(2,1)S(1)} collective-permute-done((bf16[448,576]{1,0:T(8,128)(2,1)S(1)}, bf16[448,576]{1,0:T(8,128)(2,1)S(1)}, u32[]{:S(2)}, u32[]{:S(2)}) %collective-permute-start.28) | collective-permute-done | bytes 516128 | tf_op jit(solution)/shard_map/ppermute | solution.py:22
  132.1 1.3 collective-permute-done.26.refs_0_
  135.3 2.4 %collective-permute-start.30 = (bf16[336,576]{1,0:T(8,128)(2,1)S(1)}, bf16[336,576]{1,0:T(8,128)(2,1)S(1)}, u32[]{:S(2)}, u32[]{:S(2)}) collective-permute-start(bf16[336,576]{1,0:T(8,128)(2,1)S(1)} %get-tuple-element.58), channel_id=1, source_target_pairs={{32,0},{64,32},{96,64},{0,96},{160,128},{192,160},{224,192},{128,2... | collective-permute-start | bytes 1161224 | tf_op jit(solution)/shard_map/ppermute | solution.py:22
  137.7 1.2 shard_map.19.refs_6_
  139.0 18.4 %collective-permute-done.30.refs_3_ = bf16[336,576]{1,0:T(8,128)(2,1)S(1)} collective-permute-done((bf16[336,576]{1,0:T(8,128)(2,1)S(1)}, bf16[336,576]{1,0:T(8,128)(2,1)S(1)}, u32[]{:S(2)}, u32[]{:S(2)}) %collective-permute-start.30) | collective-permute-done | bytes 387104 | tf_op jit(solution)/shard_map/ppermute | solution.py:22
  157.4 2.0 %collective-permute-done.31.refs_4_ = bf16[336,576]{1,0:T(8,128)(2,1)S(1)} collective-permute-done((bf16[336,576]{1,0:T(8,128)(2,1)S(1)}, bf16[336,576]{1,0:T(8,128)(2,1)S(1)}, u32[]{:S(2)}, u32[]{:S(2)}) %collective-permute-start.31) | collective-permute-done | bytes 387104 | tf_op jit(solution)/shard_map/ppermute | solution.py:22
  159.3 5.3 %shard_map.20 = bf16[448,576]{1,0:T(8,128)(2,1)} custom-call(bf16[2,448,896]{2,1,0:T(8,128)(2,1)S(1)} %maximum_dynamic-update-slice_fusion.refs_0_.block_ref, bf16[2,448,896]{2,1,0:T(8,128)(2,1)S(1)} %collective-permute-done.25.refs_0_.got_ref, bf16[448,576]{1,0:T(8,128)(2,1)S(1)} %collective-permute-done.26.refs_0_, ...), custom_call_target="tpu_custom_call" | custom-call | flops 1387266048 | bytes 9437184 | tf_op jit(solution)/shard_map/pallas_call | solution.py:224
  (84 shorter events, 8.4 us)
Async XLA Ops:
  0.0 15.3 %collective-permute-start.1 = (bf16[448,576]{1,0:T(8,128)(2,1)}, bf16[448,576]{1,0:T(8,128)(2,1)S(1)}, u32[]{:S(2)}, u32[]{:S(2)}) collective-permute-start(bf16[448,576]{1,0:T(8,128)(2,1)} %own_ref.1), channel_id=1, source_target_pairs={{32,0},{64,32},{96,64},{0,96},{160,128},{192,160},{224,192},{128,2... | collective-permute-start | bytes 1548296 | tf_op jit(solution)/shard_map/ppermute | solution.py:22
  2.8 16.2 %collective-permute-start.2 = (bf16[448,576]{1,0:T(8,128)(2,1)}, bf16[448,576]{1,0:T(8,128)(2,1)S(1)}, u32[]{:S(2)}, u32[]{:S(2)}) collective-permute-start(bf16[448,576]{1,0:T(8,128)(2,1)} %own_ref.1), channel_id=1, source_target_pairs={{96,0},{0,32},{32,64},{64,96},{224,128},{128,160},{160,192},{192,2... | collective-permute-start | bytes 1548296 | tf_op jit(solution)/shard_map/ppermute | solution.py:22
  2.8 16.4 %collective-permute-start = (bf16[448,576]{1,0:T(8,128)(2,1)}, bf16[448,576]{1,0:T(8,128)(2,1)S(1)}, u32[]{:S(2)}, u32[]{:S(2)}) collective-permute-start(bf16[448,576]{1,0:T(8,128)(2,1)} %own_ref.1), channel_id=1, source_target_pairs={{0,128},{32,160},{64,192},{96,224},{128,0},{160,32},{192,64},{224,... | collective-permute-start | bytes 1548296 | tf_op jit(solution)/shard_map/ppermute | solution.py:26
  15.3 8.9 %collective-permute-start.3 = (bf16[224,576]{1,0:T(8,128)(2,1)S(1)}, bf16[224,576]{1,0:T(8,128)(2,1)S(1)}, u32[]{:S(2)}, u32[]{:S(2)}) collective-permute-start(bf16[224,576]{1,0:T(8,128)(2,1)S(1)} %slice.78), channel_id=1, source_target_pairs={{32,0},{64,32},{96,64},{0,96},{160,128},{192,160},{224,192},{128,2... | collective-permute-start | bytes 774152 | tf_op jit(solution)/shard_map/ppermute | solution.py:22
  19.0 8.7 %collective-permute-start.4 = (bf16[224,576]{1,0:T(8,128)(2,1)S(1)}, bf16[224,576]{1,0:T(8,128)(2,1)S(1)}, u32[]{:S(2)}, u32[]{:S(2)}) collective-permute-start(bf16[224,576]{1,0:T(8,128)(2,1)S(1)} %slice.79), channel_id=1, source_target_pairs={{96,0},{0,32},{32,64},{64,96},{224,128},{128,160},{160,192},{192,2... | collective-permute-start | bytes 774152 | tf_op jit(solution)/shard_map/ppermute | solution.py:22
  27.8 26.5 %copy-start.1 = (bf16[448,576]{1,0:T(8,128)(2,1)}, bf16[448,576]{1,0:T(8,128)(2,1)S(1)}, u32[]{:S(2)}) copy-start(bf16[448,576]{1,0:T(8,128)(2,1)S(1)} %get-tuple-element.18.refs_4_) | copy-start | bytes 1548292
  29.3 3.5 %collective-permute-start.5 = (bf16[448,1792]{1,0:T(8,128)(2,1)S(1)}, bf16[448,1792]{1,0:T(8,128)(2,1)S(1)}, u32[]{:S(2)}, u32[]{:S(2)}) collective-permute-start(bf16[448,1792]{1,0:T(8,128)(2,1)S(1)} %convolution_convert_fusion), channel_id=1, source_target_pairs={{0,1},{1,0},{2,3},{3,2},{4,5},{5,4},{6,7},{7,6},{8,9},{9,8},{10,11... | collective-permute-start | bytes 4816904 | tf_op jit(solution)/shard_map/ppermute | solution.py:44
  33.2 16.9 %copy-start.5 = (f32[448,1792]{1,0:T(8,128)}, f32[448,1792]{1,0:T(8,128)S(1)}, u32[]{:S(2)}) copy-start(f32[448,1792]{1,0:T(8,128)S(1)} %get-tuple-element.26) | copy-start | bytes 9633796
  34.1 15.9 %collective-permute-start.6 = (bf16[112,1792]{1,0:T(8,128)(2,1)S(1)}, bf16[112,1792]{1,0:T(8,128)(2,1)S(1)}, u32[]{:S(2)}, u32[]{:S(2)}) collective-permute-start(bf16[112,1792]{1,0:T(8,128)(2,1)S(1)} %get-tuple-element.28), channel_id=1, source_target_pairs={{0,4},{1,29},{2,6},{3,31},{4,8},{5,1},{6,10},{7,3},{8,12},{9,5},{1... | collective-permute-start | bytes 1204232 | tf_op jit(solution)/shard_map/ppermute | solution.py:65
  36.0 13.9 %collective-permute-start.7 = (bf16[56,1792]{1,0:T(8,128)(2,1)S(1)}, bf16[56,1792]{1,0:T(8,128)(2,1)S(1)}, u32[]{:S(2)}, u32[]{:S(2)}) collective-permute-start(bf16[56,1792]{1,0:T(8,128)(2,1)S(1)} %slice.82), channel_id=1, source_target_pairs={{0,8},{1,25},{2,10},{3,27},{4,12},{5,29},{6,14},{7,31},{8,16},{9,1... | collective-permute-start | bytes 602120 | tf_op jit(solution)/shard_map/ppermute | solution.py:65
  50.1 14.6 %collective-permute-start.8 = (bf16[112,1792]{1,0:T(8,128)(2,1)S(1)}, bf16[112,1792]{1,0:T(8,128)(2,1)}, u32[]{:S(2)}, u32[]{:S(2)}) collective-permute-start(bf16[112,1792]{1,0:T(8,128)(2,1)S(1)} %fusion), channel_id=1, source_target_pairs={{0,8},{1,25},{2,10},{3,27},{4,12},{5,29},{6,14},{7,31},{8,16},{9,1... | collective-permute-start | bytes 1204232 | tf_op jit(solution)/shard_map/ppermute | solution.py:65
  50.2 18.7 %collective-permute-start.9 = (bf16[112,1792]{1,0:T(8,128)(2,1)}, bf16[112,1792]{1,0:T(8,128)(2,1)}, u32[]{:S(2)}, u32[]{:S(2)}) collective-permute-start(bf16[112,1792]{1,0:T(8,128)(2,1)} %get-tuple-element.16), channel_id=1, source_target_pairs={{0,4},{1,29},{2,6},{3,31},{4,8},{5,1},{6,10},{7,3},{8,12},{9,5},{1... | collective-permute-start | bytes 1204232 | tf_op jit(solution)/shard_map/ppermute | solution.py:65
  52.3 17.8 %collective-permute-start.10 = (bf16[448,576]{1,0:T(8,128)(2,1)S(1)}, bf16[448,576]{1,0:T(8,128)(2,1)S(1)}, u32[]{:S(2)}, u32[]{:S(2)}) collective-permute-start(bf16[448,576]{1,0:T(8,128)(2,1)S(1)} %collective-permute-done.refs_5_), channel_id=1, source_target_pairs={{32,0},{64,32},{96,64},{0,96},{160,128},{192,160},{224,192},{128,2... | collective-permute-start | bytes 1548296 | tf_op jit(solution)/shard_map/ppermute | solution.py:22
  52.6 17.5 %collective-permute-start.11 = (bf16[448,576]{1,0:T(8,128)(2,1)S(1)}, bf16[448,576]{1,0:T(8,128)(2,1)}, u32[]{:S(2)}, u32[]{:S(2)}) collective-permute-start(bf16[448,576]{1,0:T(8,128)(2,1)S(1)} %collective-permute-done.refs_5_), channel_id=1, source_target_pairs={{96,0},{0,32},{32,64},{64,96},{224,128},{128,160},{160,192},{192,2... | collective-permute-start | bytes 1548296 | tf_op jit(solution)/shard_map/ppermute | solution.py:22
  54.4 15.8 %collective-permute-start.12 = (bf16[448,576]{1,0:T(8,128)(2,1)S(1)}, bf16[448,576]{1,0:T(8,128)(2,1)}, u32[]{:S(2)}, u32[]{:S(2)}) collective-permute-start(bf16[448,576]{1,0:T(8,128)(2,1)S(1)} %get-tuple-element.18.refs_4_), channel_id=1, source_target_pairs={{0,128},{32,160},{64,192},{96,224},{128,0},{160,32},{192,64},{224,... | collective-permute-start | bytes 1548296 | tf_op jit(solution)/shard_map/ppermute | solution.py:26
  70.1 0.9 copy-start.6
  70.1 12.2 %copy-start.3 = (bf16[448,576]{1,0:T(8,128)(2,1)}, bf16[448,576]{1,0:T(8,128)(2,1)S(1)}, u32[]{:S(2)}) copy-start(bf16[448,576]{1,0:T(8,128)(2,1)S(1)} %collective-permute-done.10.refs_6_) | copy-start | bytes 1548292
  71.0 1.5 collective-permute-start.13
  73.7 7.3 %collective-permute-start.14 = (bf16[56,896]{1,0:T(8,128)(2,1)S(1)}, bf16[56,896]{1,0:T(8,128)(2,1)S(1)}, u32[]{:S(2)}, u32[]{:S(2)}) collective-permute-start(bf16[56,896]{1,0:T(8,128)(2,1)S(1)} %get-tuple-element.53), channel_id=1, source_target_pairs={{0,2},{1,3},{2,0},{3,1},{4,6},{5,7},{6,4},{7,5},{8,10},{9,11},{10,... | collective-permute-start | bytes 301064 | tf_op jit(solution)/shard_map/ppermute | solution.py:35
  75.0 6.0 %collective-permute-start.15 = (bf16[56,896]{1,0:T(8,128)(2,1)S(1)}, bf16[56,896]{1,0:T(8,128)(2,1)S(1)}, u32[]{:S(2)}, u32[]{:S(2)}) collective-permute-start(bf16[56,896]{1,0:T(8,128)(2,1)S(1)} %get-tuple-element.54), channel_id=1, source_target_pairs={{0,128},{32,160},{64,192},{96,224},{128,0},{160,32},{192,64},{224,... | collective-permute-start | bytes 301064 | tf_op jit(solution)/shard_map/ppermute | solution.py:26
  75.0 7.3 %collective-permute-start.16 = (bf16[56,896]{1,0:T(8,128)(2,1)S(1)}, bf16[56,896]{1,0:T(8,128)(2,1)S(1)}, u32[]{:S(2)}, u32[]{:S(2)}) collective-permute-start(bf16[56,896]{1,0:T(8,128)(2,1)S(1)} %get-tuple-element.54), channel_id=1, source_target_pairs={{0,130},{1,131},{2,128},{3,129},{4,134},{5,135},{6,132},{7,133},{8... | collective-permute-start | bytes 301064 | tf_op jit(solution)/shard_map/ppermute | solution.py:40
  83.2 12.2 %collective-permute-start.19 = (bf16[2,56,896]{2,1,0:T(8,128)(2,1)}, bf16[2,56,896]{2,1,0:T(8,128)(2,1)}, u32[]{:S(2)}, u32[]{:S(2)}) collective-permute-start(bf16[2,56,896]{2,1,0:T(8,128)(2,1)} %get-tuple-element.51), channel_id=1, source_target_pairs={{8,0},{9,1},{10,2},{11,3},{12,4},{13,5},{14,6},{15,7},{16,8},{17,9... | collective-permute-start | bytes 602120 | tf_op jit(solution)/shard_map/ppermute | solution.py:31
  83.2 14.9 %collective-permute-start.20 = (bf16[2,56,896]{2,1,0:T(8,128)(2,1)}, bf16[2,56,896]{2,1,0:T(8,128)(2,1)S(1)}, u32[]{:S(2)}, u32[]{:S(2)}) collective-permute-start(bf16[2,56,896]{2,1,0:T(8,128)(2,1)} %get-tuple-element.51), channel_id=1, source_target_pairs={{24,0},{25,1},{26,2},{27,3},{28,4},{29,5},{30,6},{31,7},{0,8},{1,9... | collective-permute-start | bytes 602120 | tf_op jit(solution)/shard_map/ppermute | solution.py:31
  86.1 17.4 %collective-permute-start.17 = (bf16[2,56,896]{2,1,0:T(8,128)(2,1)}, bf16[2,56,896]{2,1,0:T(8,128)(2,1)}, u32[]{:S(2)}, u32[]{:S(2)}) collective-permute-start(bf16[2,56,896]{2,1,0:T(8,128)(2,1)} %get-tuple-element.51), channel_id=1, source_target_pairs={{4,0},{5,1},{6,2},{7,3},{8,4},{9,5},{10,6},{11,7},{12,8},{13,9},{1... | collective-permute-start | bytes 602120 | tf_op jit(solution)/shard_map/ppermute | solution.py:31
  87.9 16.6 %collective-permute-start.18 = (bf16[2,56,896]{2,1,0:T(8,128)(2,1)}, bf16[2,56,896]{2,1,0:T(8,128)(2,1)}, u32[]{:S(2)}, u32[]{:S(2)}) collective-permute-start(bf16[2,56,896]{2,1,0:T(8,128)(2,1)} %get-tuple-element.51), channel_id=1, source_target_pairs={{28,0},{29,1},{30,2},{31,3},{0,4},{1,5},{2,6},{3,7},{4,8},{5,9},{6... | collective-permute-start | bytes 602120 | tf_op jit(solution)/shard_map/ppermute | solution.py:31
  88.1 22.5 %copy-start = (bf16[448,576]{1,0:T(8,128)(2,1)S(1)}, bf16[448,576]{1,0:T(8,128)(2,1)}, u32[]{:S(2)}) copy-start(bf16[448,576]{1,0:T(8,128)(2,1)} %own_ref.1) | copy-start | bytes 1548292
  88.1 22.5 %copy-start.2 = (bf16[448,576]{1,0:T(8,128)(2,1)S(1)}, bf16[448,576]{1,0:T(8,128)(2,1)}, u32[]{:S(2)}) copy-start(bf16[448,576]{1,0:T(8,128)(2,1)} %copy-done.1) | copy-start | bytes 1548292
  88.1 22.5 %copy-start.4 = (bf16[448,576]{1,0:T(8,128)(2,1)S(1)}, bf16[448,576]{1,0:T(8,128)(2,1)}, u32[]{:S(2)}) copy-start(bf16[448,576]{1,0:T(8,128)(2,1)} %copy-done.3) | copy-start | bytes 1548292
  96.3 14.2 %collective-permute-start.23 = (bf16[1,56,896]{2,1,0:T(8,128)(2,1)S(1)}, bf16[1,56,896]{2,1,0:T(8,128)(2,1)S(1)}, u32[]{:S(2)}, u32[]{:S(2)}) collective-permute-start(bf16[1,56,896]{2,1,0:T(8,128)(2,1)S(1)} %slice.89), channel_id=1, source_target_pairs={{8,0},{9,1},{10,2},{11,3},{12,4},{13,5},{14,6},{15,7},{16,8},{17,9... | collective-permute-start | bytes 301064 | tf_op jit(solution)/shard_map/ppermute | solution.py:31
  98.1 12.4 %collective-permute-start.24 = (bf16[1,56,896]{2,1,0:T(8,128)(2,1)S(1)}, bf16[1,56,896]{2,1,0:T(8,128)(2,1)S(1)}, u32[]{:S(2)}, u32[]{:S(2)}) collective-permute-start(bf16[1,56,896]{2,1,0:T(8,128)(2,1)S(1)} %slice.90), channel_id=1, source_target_pairs={{24,0},{25,1},{26,2},{27,3},{28,4},{29,5},{30,6},{31,7},{0,8},{1,9... | collective-permute-start | bytes 301064 | tf_op jit(solution)/shard_map/ppermute | solution.py:31
  99.4 8.4 %collective-permute-start.21 = (bf16[2,56,896]{2,1,0:T(8,128)(2,1)}, bf16[2,56,896]{2,1,0:T(8,128)(2,1)S(1)}, u32[]{:S(2)}, u32[]{:S(2)}) collective-permute-start(bf16[2,56,896]{2,1,0:T(8,128)(2,1)} %collective-permute-done.19), channel_id=1, source_target_pairs={{4,0},{5,1},{6,2},{7,3},{8,4},{9,5},{10,6},{11,7},{12,8},{13,9},{1... | collective-permute-start | bytes 602120 | tf_op jit(solution)/shard_map/ppermute | solution.py:31
  103.5 6.9 %collective-permute-start.22 = (bf16[2,56,896]{2,1,0:T(8,128)(2,1)S(1)}, bf16[2,56,896]{2,1,0:T(8,128)(2,1)S(1)}, u32[]{:S(2)}, u32[]{:S(2)}) collective-permute-start(bf16[2,56,896]{2,1,0:T(8,128)(2,1)S(1)} %collective-permute-done.20), channel_id=1, source_target_pairs={{28,0},{29,1},{30,2},{31,3},{0,4},{1,5},{2,6},{3,7},{4,8},{5,9},{6... | collective-permute-start | bytes 602120 | tf_op jit(solution)/shard_map/ppermute | solution.py:31
  110.5 3.5 %collective-permute-start.25 = (bf16[2,448,896]{2,1,0:T(8,128)(2,1)S(1)}, bf16[2,448,896]{2,1,0:T(8,128)(2,1)S(1)}, u32[]{:S(2)}, u32[]{:S(2)}) collective-permute-start(bf16[2,448,896]{2,1,0:T(8,128)(2,1)S(1)} %maximum_dynamic-update-slice_fusion.refs_0_.block_ref), channel_id=1, source_target_pairs={{0,1},{1,0},{2,3},{3,2},{4,5},{5,4},{6,7},{7,6},{8,9},{9,8},{10,11... | collective-permute-start | bytes 4816904 | tf_op jit(solution)/shard_map/ppermute | solution.py:44
  116.7 15.3 %collective-permute-start.28 = (bf16[448,576]{1,0:T(8,128)(2,1)S(1)}, bf16[448,576]{1,0:T(8,128)(2,1)S(1)}, u32[]{:S(2)}, u32[]{:S(2)}) collective-permute-start(bf16[448,576]{1,0:T(8,128)(2,1)S(1)} %get-tuple-element.23.own_y), channel_id=1, source_target_pairs={{32,0},{64,32},{96,64},{0,96},{160,128},{192,160},{224,192},{128,2... | collective-permute-start | bytes 1548296 | tf_op jit(solution)/shard_map/ppermute | solution.py:22
  116.8 16.5 %collective-permute-start.26 = (bf16[448,576]{1,0:T(8,128)(2,1)S(1)}, bf16[448,576]{1,0:T(8,128)(2,1)S(1)}, u32[]{:S(2)}, u32[]{:S(2)}) collective-permute-start(bf16[448,576]{1,0:T(8,128)(2,1)S(1)} %get-tuple-element.23.own_y), channel_id=1, source_target_pairs={{96,0},{0,32},{32,64},{64,96},{224,128},{128,160},{160,192},{192,2... | collective-permute-start | bytes 1548296 | tf_op jit(solution)/shard_map/ppermute | solution.py:22
  118.8 15.5 %collective-permute-start.27 = (bf16[448,576]{1,0:T(8,128)(2,1)S(1)}, bf16[448,576]{1,0:T(8,128)(2,1)S(1)}, u32[]{:S(2)}, u32[]{:S(2)}) collective-permute-start(bf16[448,576]{1,0:T(8,128)(2,1)S(1)} %get-tuple-element.23.own_y), channel_id=1, source_target_pairs={{0,128},{32,160},{64,192},{96,224},{128,0},{160,32},{192,64},{224,... | collective-permute-start | bytes 1548296 | tf_op jit(solution)/shard_map/ppermute | solution.py:26
  133.4 25.9 %collective-permute-start.29 = (bf16[672,576]{1,0:T(8,128)(2,1)S(1)}, bf16[672,576]{1,0:T(8,128)(2,1)S(1)}, u32[]{:S(2)}, u32[]{:S(2)}) collective-permute-start(bf16[672,576]{1,0:T(8,128)(2,1)S(1)} %pad_maximum_fusion), channel_id=1, source_target_pairs={{0,128},{32,160},{64,192},{96,224},{128,0},{160,32},{192,64},{224,... | collective-permute-start | bytes 2322440 | tf_op jit(solution)/shard_map/ppermute | solution.py:26
  134.4 25.0 %collective-permute-start.32 = (bf16[448,576]{1,0:T(8,128)(2,1)S(1)}, bf16[448,576]{1,0:T(8,128)(2,1)S(1)}, u32[]{:S(2)}, u32[]{:S(2)}) collective-permute-start(bf16[448,576]{1,0:T(8,128)(2,1)S(1)} %collective-permute-done.27.refs_1_), channel_id=1, source_target_pairs={{64,0},{96,32},{0,64},{32,96},{192,128},{224,160},{128,192},{160,2... | collective-permute-start | bytes 1548296 | tf_op jit(solution)/shard_map/ppermute | solution.py:22
  135.3 22.0 %collective-permute-start.30 = (bf16[336,576]{1,0:T(8,128)(2,1)S(1)}, bf16[336,576]{1,0:T(8,128)(2,1)S(1)}, u32[]{:S(2)}, u32[]{:S(2)}) collective-permute-start(bf16[336,576]{1,0:T(8,128)(2,1)S(1)} %get-tuple-element.58), channel_id=1, source_target_pairs={{32,0},{64,32},{96,64},{0,96},{160,128},{192,160},{224,192},{128,2... | collective-permute-start | bytes 1161224 | tf_op jit(solution)/shard_map/ppermute | solution.py:22
  137.7 21.6 %collective-permute-start.31 = (bf16[336,576]{1,0:T(8,128)(2,1)S(1)}, bf16[336,576]{1,0:T(8,128)(2,1)S(1)}, u32[]{:S(2)}, u32[]{:S(2)}) collective-permute-start(bf16[336,576]{1,0:T(8,128)(2,1)S(1)} %get-tuple-element.57), channel_id=1, source_target_pairs={{96,0},{0,32},{32,64},{64,96},{224,128},{128,160},{160,192},{192,2... | collective-permute-start | bytes 1161224 | tf_op jit(solution)/shard_map/ppermute | solution.py:22

commit v9 on v8

--- a/solution.py
+++ b/solution.py
@@ -274,7 +274,6 @@
     passed = along_z(two, 2).astype(f32) + along_z(one, 1).astype(f32)
     total = passed + jnp.pad(units(7, 8), ((unit, 0), (0, 0)))
     others = (from_x(late_across, 1), from_x(late_across, -1), from_y(late_far))
-    total, other_right, other_left, other_far = lax.optimization_barrier((total, *others))
 
     width = 2 * rows
     total = total.reshape(2, unit, 2 * width)
@@ -287,6 +286,8 @@
     gram_same = kept.astype(f32) + from_y_hi(kept).astype(f32)
     gram_other = from_y(given).astype(f32) + from_y_both(given).astype(f32)
     gram = jnp.stack([gram_same, gram_other]).astype(bf16)
+
+    gram, other_right, other_left, other_far = lax.optimization_barrier((gram, *others))
 
     up1, down1 = from_z(gram, 1), from_z(gram, -1)
     up2, down2 = from_z(gram, 2), from_z(gram, -2)

time: 167 us -> 178 us (1.066)
  waiting for transfers between devices: 95.8 us -> 104 us
    ppermute x5, waiting for transfers between devices: 0.01 us -> 12.1 us  [from_y(): return lax.ppermute(value, 'wide', [(w, (w + 4) % 8) for w in range(8)])]
    ppermute x4, waiting for transfers between devices: 23.3 us -> 26.1 us  [along_z(): return lax.ppermute(value, 'narrow', pairs)]
    ppermute x5, starting transfers between devices: 3.07 us -> 5.56 us  [from_y(): return lax.ppermute(value, 'wide', [(w, (w + 4) % 8) for w in range(8)])]
    ppermute x8, waiting for transfers between devices: 11.3 us -> 8.9 us  [from_z(): return lax.ppermute(value, 'narrow', pairs)]
    ppermute x1, waiting for transfers between devices: 3.09 us -> 1.09 us  [from_y_hi(): return lax.ppermute(value, 'narrow', [(n, n ^ 2) for n in range(32)])]
    dynamic_update_slice x6 -> x7, local copies, waits for them, and re-layouts: 2.95 us -> 3.91 us  [local(): lax.dynamic_update_slice_in_dim(block, piece, (z_pos + step) % 8 * unit, 1)]
where the time goes in v9:
time: 178 us; the launch traced here: 175 us
  waiting for transfers between devices  104 us (58%)
  starting transfers between devices  42.6 us (24%)
  Pallas kernels  12.1 us (7%)
  local copies, waits for them, and re-layouts  9.81 us (6%)
  matrix products  3 us (2%)
  other arithmetic  2.57 us (1%)
    ppermute x11, waiting for transfers between devices, from_x(): return lax.ppermute(value, 'wide', pairs)  52 us
    ppermute x4, waiting for transfers between devices, along_z(): return lax.ppermute(value, 'narrow', pairs)  26.1 us
    ppermute x11, starting transfers between devices, from_x(): return lax.ppermute(value, 'wide', pairs)  13.9 us
    ppermute x8, starting transfers between devices, from_z(): return lax.ppermute(value, 'narrow', pairs)  12.7 us
    ppermute x5, waiting for transfers between devices, from_y(): return lax.ppermute(value, 'wide', [(w, (w + 4) % 8) for w in range(8)])  12.1 us
    ppermute x8, waiting for transfers between devices, from_z(): return lax.ppermute(value, 'narrow', pairs)  8.9 us
    ppermute x4, starting transfers between devices, along_z(): return lax.ppermute(value, 'narrow', pairs)  7.56 us
    ppermute x5, starting transfers between devices, from_y(): return lax.ppermute(value, 'wide', [(w, (w + 4) % 8) for w in range(8)])  5.56 us
  transfers between devices with their start and end apart: 33, of which 18 were waited for; matrix products, arithmetic and copies ran while one was open for 6% of the time, Pallas kernels for 2%

profile of v9, /device:TPU:24, one launch (start us, length us, event | category | flops | bytes accessed | tf_op | source)
XLA Modules:
  0.0 174.7 jit_solution(7134412478716719044)
XLA Ops:
  0.0 2.8 %collective-permute-start.1 = (bf16[448,576]{1,0:T(8,128)(2,1)}, bf16[448,576]{1,0:T(8,128)(2,1)S(1)}, u32[]{:S(2)}, u32[]{:S(2)}) collective-permute-start(bf16[448,576]{1,0:T(8,128)(2,1)} %own_ref.1), channel_id=1, source_target_pairs={{32,0},{64,32},{96,64},{0,96},{160,128},{192,160},{224,192},{128,2... | collective-permute-start | bytes 1548296 | tf_op jit(solution)/shard_map/ppermute | solution.py:22
  3.5 1.2 constant_dynamic-update-slice_fusion.6
  4.7 10.6 %collective-permute-done.1.refs_2_ = bf16[448,576]{1,0:T(8,128)(2,1)S(1)} collective-permute-done((bf16[448,576]{1,0:T(8,128)(2,1)}, bf16[448,576]{1,0:T(8,128)(2,1)S(1)}, u32[]{:S(2)}, u32[]{:S(2)}) %collective-permute-start.1) | collective-permute-done | bytes 516128 | tf_op jit(solution)/shard_map/ppermute | solution.py:22
  15.3 3.7 %collective-permute-start.3 = (bf16[224,576]{1,0:T(8,128)(2,1)S(1)}, bf16[224,576]{1,0:T(8,128)(2,1)S(1)}, u32[]{:S(2)}, u32[]{:S(2)}) collective-permute-start(bf16[224,576]{1,0:T(8,128)(2,1)S(1)} %slice.78), channel_id=1, source_target_pairs={{32,0},{64,32},{96,64},{0,96},{160,128},{192,160},{224,192},{128,2... | collective-permute-start | bytes 774152 | tf_op jit(solution)/shard_map/ppermute | solution.py:22
  19.7 4.5 %collective-permute-done.3 = bf16[224,576]{1,0:T(8,128)(2,1)S(1)} collective-permute-done((bf16[224,576]{1,0:T(8,128)(2,1)S(1)}, bf16[224,576]{1,0:T(8,128)(2,1)S(1)}, u32[]{:S(2)}, u32[]{:S(2)}) %collective-permute-start.3) | collective-permute-done | bytes 258080 | tf_op jit(solution)/shard_map/ppermute | solution.py:22
  24.3 3.5 %collective-permute-done.4 = bf16[224,576]{1,0:T(8,128)(2,1)S(1)} collective-permute-done((bf16[224,576]{1,0:T(8,128)(2,1)S(1)}, bf16[224,576]{1,0:T(8,128)(2,1)S(1)}, u32[]{:S(2)}, u32[]{:S(2)}) %collective-permute-start.4) | collective-permute-done | bytes 258080 | tf_op jit(solution)/shard_map/ppermute | solution.py:22
  27.8 1.5 convolution_convert_fusion
  29.4 1.5 fusion.6
  30.9 1.9 %collective-permute-done.5 = bf16[448,1792]{1,0:T(8,128)(2,1)S(1)} collective-permute-done((bf16[448,1792]{1,0:T(8,128)(2,1)S(1)}, bf16[448,1792]{1,0:T(8,128)(2,1)S(1)}, u32[]{:S(2)}, u32[]{:S(2)}) %collective-permute-start.5) | collective-permute-done | bytes 1605664 | tf_op jit(solution)/shard_map/ppermute | solution.py:44
  33.3 2.0 %collective-permute-start.6 = (bf16[112,1792]{1,0:T(8,128)(2,1)S(1)}, bf16[112,1792]{1,0:T(8,128)(2,1)S(1)}, u32[]{:S(2)}, u32[]{:S(2)}) collective-permute-start(bf16[112,1792]{1,0:T(8,128)(2,1)S(1)} %get-tuple-element.28), channel_id=1, source_target_pairs={{0,4},{1,29},{2,6},{3,31},{4,8},{5,1},{6,10},{7,3},{8,12},{9,5},{1... | collective-permute-start | bytes 1204232 | tf_op jit(solution)/shard_map/ppermute | solution.py:65
  35.3 3.3 %collective-permute-start.7 = (bf16[56,1792]{1,0:T(8,128)(2,1)S(1)}, bf16[56,1792]{1,0:T(8,128)(2,1)S(1)}, u32[]{:S(2)}, u32[]{:S(2)}) collective-permute-start(bf16[56,1792]{1,0:T(8,128)(2,1)S(1)} %slice.82), channel_id=1, source_target_pairs={{0,8},{1,25},{2,10},{3,27},{4,12},{5,29},{6,14},{7,31},{8,16},{9,1... | collective-permute-start | bytes 602120 | tf_op jit(solution)/shard_map/ppermute | solution.py:65
  38.6 10.6 %collective-permute-done.7 = bf16[56,1792]{1,0:T(8,128)(2,1)S(1)} collective-permute-done((bf16[56,1792]{1,0:T(8,128)(2,1)S(1)}, bf16[56,1792]{1,0:T(8,128)(2,1)S(1)}, u32[]{:S(2)}, u32[]{:S(2)}) %collective-permute-start.7) | collective-permute-done | bytes 200736 | tf_op jit(solution)/shard_map/ppermute | solution.py:65
  49.4 2.1 %collective-permute-start.9 = (bf16[112,1792]{1,0:T(8,128)(2,1)S(1)}, bf16[112,1792]{1,0:T(8,128)(2,1)}, u32[]{:S(2)}, u32[]{:S(2)}) collective-permute-start(bf16[112,1792]{1,0:T(8,128)(2,1)S(1)} %get-tuple-element.16), channel_id=1, source_target_pairs={{0,4},{1,29},{2,6},{3,31},{4,8},{5,1},{6,10},{7,3},{8,12},{9,5},{1... | collective-permute-start | bytes 1204232 | tf_op jit(solution)/shard_map/ppermute | solution.py:65
  51.6 1.0 slice.84
  52.6 11.2 %collective-permute-done.8 = bf16[112,1792]{1,0:T(8,128)(2,1)S(1)} collective-permute-done((bf16[112,1792]{1,0:T(8,128)(2,1)S(1)}, bf16[112,1792]{1,0:T(8,128)(2,1)S(1)}, u32[]{:S(2)}, u32[]{:S(2)}) %collective-permute-start.8) | collective-permute-done | bytes 401440 | tf_op jit(solution)/shard_map/ppermute | solution.py:65
  63.8 4.3 %collective-permute-done.9 = bf16[112,1792]{1,0:T(8,128)(2,1)} collective-permute-done((bf16[112,1792]{1,0:T(8,128)(2,1)S(1)}, bf16[112,1792]{1,0:T(8,128)(2,1)}, u32[]{:S(2)}, u32[]{:S(2)}) %collective-permute-start.9) | collective-permute-done | bytes 401440 | tf_op jit(solution)/shard_map/ppermute | solution.py:65
  68.1 1.1 pad_add_fusion
  69.5 1.4 collective-permute-done.10
  71.1 1.3 collective-permute-start.11
  72.6 1.8 %collective-permute-start.15 = (bf16[448,576]{1,0:T(8,128)(2,1)S(1)}, bf16[448,576]{1,0:T(8,128)(2,1)S(1)}, u32[]{:S(2)}, u32[]{:S(2)}) collective-permute-start(bf16[448,576]{1,0:T(8,128)(2,1)S(1)} %collective-permute-done.refs_5_), channel_id=1, source_target_pairs={{96,0},{0,32},{32,64},{64,96},{224,128},{128,160},{160,192},{192,2... | collective-permute-start | bytes 1548296 | tf_op jit(solution)/shard_map/ppermute | solution.py:22
  74.4 2.0 %collective-permute-start.12 = (bf16[56,896]{1,0:T(8,128)(2,1)S(1)}, bf16[56,896]{1,0:T(8,128)(2,1)S(1)}, u32[]{:S(2)}, u32[]{:S(2)}) collective-permute-start(bf16[56,896]{1,0:T(8,128)(2,1)S(1)} %get-tuple-element.52), channel_id=1, source_target_pairs={{0,128},{32,160},{64,192},{96,224},{128,0},{160,32},{192,64},{224,... | collective-permute-start | bytes 301064 | tf_op jit(solution)/shard_map/ppermute | solution.py:26
  76.5 1.1 collective-permute-done.11
  77.5 1.1 collective-permute-start.13
  78.7 12.1 %collective-permute-done.12 = bf16[56,896]{1,0:T(8,128)(2,1)S(1)} collective-permute-done((bf16[56,896]{1,0:T(8,128)(2,1)S(1)}, bf16[56,896]{1,0:T(8,128)(2,1)S(1)}, u32[]{:S(2)}, u32[]{:S(2)}) %collective-permute-start.12) | collective-permute-done | bytes 100384 | tf_op jit(solution)/shard_map/ppermute | solution.py:26
  92.3 2.9 %collective-permute-start.20 = (bf16[2,56,896]{2,1,0:T(8,128)(2,1)}, bf16[2,56,896]{2,1,0:T(8,128)(2,1)}, u32[]{:S(2)}, u32[]{:S(2)}) collective-permute-start(bf16[2,56,896]{2,1,0:T(8,128)(2,1)} %pad_maximum_fusion.3), channel_id=1, source_target_pairs={{24,0},{25,1},{26,2},{27,3},{28,4},{29,5},{30,6},{31,7},{0,8},{1,9... | collective-permute-start | bytes 602120 | tf_op jit(solution)/shard_map/ppermute | solution.py:31
  95.2 1.8 %collective-permute-start.17 = (bf16[2,56,896]{2,1,0:T(8,128)(2,1)}, bf16[2,56,896]{2,1,0:T(8,128)(2,1)}, u32[]{:S(2)}, u32[]{:S(2)}) collective-permute-start(bf16[2,56,896]{2,1,0:T(8,128)(2,1)} %pad_maximum_fusion.3), channel_id=1, source_target_pairs={{4,0},{5,1},{6,2},{7,3},{8,4},{9,5},{10,6},{11,7},{12,8},{13,9},{1... | collective-permute-start | bytes 602120 | tf_op jit(solution)/shard_map/ppermute | solution.py:31
  97.4 1.0 constant_dynamic-update-slice_fusion.15
  98.4 4.7 %collective-permute-done.19 = bf16[2,56,896]{2,1,0:T(8,128)(2,1)} collective-permute-done((bf16[2,56,896]{2,1,0:T(8,128)(2,1)}, bf16[2,56,896]{2,1,0:T(8,128)(2,1)}, u32[]{:S(2)}, u32[]{:S(2)}) %collective-permute-start.19) | collective-permute-done | bytes 200736 | tf_op jit(solution)/shard_map/ppermute | solution.py:31
  103.1 0.9 slice.89
  104.0 2.0 %collective-permute-start.23 = (bf16[1,56,896]{2,1,0:T(8,128)(2,1)S(1)}, bf16[1,56,896]{2,1,0:T(8,128)(2,1)S(1)}, u32[]{:S(2)}, u32[]{:S(2)}) collective-permute-start(bf16[1,56,896]{2,1,0:T(8,128)(2,1)S(1)} %slice.89), channel_id=1, source_target_pairs={{8,0},{9,1},{10,2},{11,3},{12,4},{13,5},{14,6},{15,7},{16,8},{17,9... | collective-permute-start | bytes 301064 | tf_op jit(solution)/shard_map/ppermute | solution.py:31
  106.0 0.9 slice.90
  106.9 1.1 collective-permute-start.24
  108.0 4.6 %collective-permute-start.21 = (bf16[2,56,896]{2,1,0:T(8,128)(2,1)}, bf16[2,56,896]{2,1,0:T(8,128)(2,1)S(1)}, u32[]{:S(2)}, u32[]{:S(2)}) collective-permute-start(bf16[2,56,896]{2,1,0:T(8,128)(2,1)} %collective-permute-done.19), channel_id=1, source_target_pairs={{4,0},{5,1},{6,2},{7,3},{8,4},{9,5},{10,6},{11,7},{12,8},{13,9},{1... | collective-permute-start | bytes 602120 | tf_op jit(solution)/shard_map/ppermute | solution.py:31
  112.6 1.0 constant_dynamic-update-slice_fusion.14
  113.6 1.0 constant_dynamic-update-slice_fusion.12
  114.5 1.0 constant_dynamic-update-slice_fusion.11
  116.2 3.6 %collective-permute-done.22 = bf16[2,56,896]{2,1,0:T(8,128)(2,1)S(1)} collective-permute-done((bf16[2,56,896]{2,1,0:T(8,128)(2,1)}, bf16[2,56,896]{2,1,0:T(8,128)(2,1)S(1)}, u32[]{:S(2)}, u32[]{:S(2)}) %collective-permute-start.22) | collective-permute-done | bytes 200736 | tf_op jit(solution)/shard_map/ppermute | solution.py:31
  119.9 2.8 %shard_map.17.refs_9_ = f32[448,576]{1,0:T(8,128)S(1)} custom-call(bf16[2,448,896]{2,1,0:T(8,128)(2,1)S(1)} %maximum_dynamic-update-slice_fusion.refs_0_.block_ref, bf16[448,576]{1,0:T(8,128)(2,1)S(1)} %copy-done, bf16[448,576]{1,0:T(8,128)(2,1)S(1)} %collective-permute-done.1.refs_2_, bf16[448,576]{1,0:T(8,128)(2,1)S(1)} %collective-permute-done.2.refs_3_, ...), custom_call_target="tpu_custom_call" | custom-call | flops 924844032 | bytes 6291456 | tf_op jit(solution)/shard_map/pallas_call | solution.py:116
  123.3 2.6 %shard_map.18 = (f32[448,576]{1,0:T(8,128)S(1)}, bf16[448,576]{1,0:T(8,128)(2,1)S(1)}) custom-call(bf16[2,448,896]{2,1,0:T(8,128)(2,1)S(1)} %collective-permute-done.25.refs_0_.got_ref, bf16[448,576]{1,0:T(8,128)(2,1)S(1)} %copy-done, bf16[448,576]{1,0:T(8,128)(2,1)S(1)} %collective-permute-done.1.refs_2_, ...), custom_call_target="tpu_custom_call" | custom-call | flops 924844032 | bytes 6291456 | tf_op jit(solution)/shard_map/pallas_call | solution.py:116
  126.0 1.6 collective-permute-start.28
  128.1 1.9 %collective-permute-start.27 = (bf16[448,576]{1,0:T(8,128)(2,1)S(1)}, bf16[448,576]{1,0:T(8,128)(2,1)S(1)}, u32[]{:S(2)}, u32[]{:S(2)}) collective-permute-start(bf16[448,576]{1,0:T(8,128)(2,1)S(1)} %get-tuple-element.23.own_y), channel_id=1, source_target_pairs={{0,128},{32,160},{64,192},{96,224},{128,0},{160,32},{192,64},{224,... | collective-permute-start | bytes 1548296 | tf_op jit(solution)/shard_map/ppermute | solution.py:26
  130.0 11.1 %collective-permute-done.28.right = bf16[448,576]{1,0:T(8,128)(2,1)S(1)} collective-permute-done((bf16[448,576]{1,0:T(8,128)(2,1)S(1)}, bf16[448,576]{1,0:T(8,128)(2,1)S(1)}, u32[]{:S(2)}, u32[]{:S(2)}) %collective-permute-start.28) | collective-permute-done | bytes 516128 | tf_op jit(solution)/shard_map/ppermute | solution.py:22
  141.1 2.4 %collective-permute-done.26.refs_0_ = bf16[448,576]{1,0:T(8,128)(2,1)S(1)} collective-permute-done((bf16[448,576]{1,0:T(8,128)(2,1)S(1)}, bf16[448,576]{1,0:T(8,128)(2,1)S(1)}, u32[]{:S(2)}, u32[]{:S(2)}) %collective-permute-start.26) | collective-permute-done | bytes 516128 | tf_op jit(solution)/shard_map/ppermute | solution.py:22
  145.6 2.4 %collective-permute-start.30 = (bf16[336,576]{1,0:T(8,128)(2,1)S(1)}, bf16[336,576]{1,0:T(8,128)(2,1)S(1)}, u32[]{:S(2)}, u32[]{:S(2)}) collective-permute-start(bf16[336,576]{1,0:T(8,128)(2,1)S(1)} %get-tuple-element.56), channel_id=1, source_target_pairs={{32,0},{64,32},{96,64},{0,96},{160,128},{192,160},{224,192},{128,2... | collective-permute-start | bytes 1161224 | tf_op jit(solution)/shard_map/ppermute | solution.py:22
  148.0 1.3 shard_map.19.refs_6_
  149.3 17.8 %collective-permute-done.30.refs_3_ = bf16[336,576]{1,0:T(8,128)(2,1)S(1)} collective-permute-done((bf16[336,576]{1,0:T(8,128)(2,1)S(1)}, bf16[336,576]{1,0:T(8,128)(2,1)S(1)}, u32[]{:S(2)}, u32[]{:S(2)}) %collective-permute-start.30) | collective-permute-done | bytes 387104 | tf_op jit(solution)/shard_map/ppermute | solution.py:22
  167.1 2.1 %collective-permute-done.31.refs_4_ = bf16[336,576]{1,0:T(8,128)(2,1)S(1)} collective-permute-done((bf16[336,576]{1,0:T(8,128)(2,1)S(1)}, bf16[336,576]{1,0:T(8,128)(2,1)S(1)}, u32[]{:S(2)}, u32[]{:S(2)}) %collective-permute-start.31) | collective-permute-done | bytes 387104 | tf_op jit(solution)/shard_map/ppermute | solution.py:22
  169.2 5.3 %shard_map.20 = bf16[448,576]{1,0:T(8,128)(2,1)} custom-call(bf16[2,448,896]{2,1,0:T(8,128)(2,1)S(1)} %maximum_dynamic-update-slice_fusion.refs_0_.block_ref, bf16[2,448,896]{2,1,0:T(8,128)(2,1)S(1)} %collective-permute-done.25.refs_0_.got_ref, bf16[448,576]{1,0:T(8,128)(2,1)S(1)} %collective-permute-done.26.refs_0_, ...), custom_call_target="tpu_custom_call" | custom-call | flops 1387266048 | bytes 9437184 | tf_op jit(solution)/shard_map/pallas_call | solution.py:224
  (79 shorter events, 8.8 us)
Async XLA Ops:
  0.0 15.3 %collective-permute-start.1 = (bf16[448,576]{1,0:T(8,128)(2,1)}, bf16[448,576]{1,0:T(8,128)(2,1)S(1)}, u32[]{:S(2)}, u32[]{:S(2)}) collective-permute-start(bf16[448,576]{1,0:T(8,128)(2,1)} %own_ref.1), channel_id=1, source_target_pairs={{32,0},{64,32},{96,64},{0,96},{160,128},{192,160},{224,192},{128,2... | collective-permute-start | bytes 1548296 | tf_op jit(solution)/shard_map/ppermute | solution.py:22
  2.8 16.2 %collective-permute-start.2 = (bf16[448,576]{1,0:T(8,128)(2,1)}, bf16[448,576]{1,0:T(8,128)(2,1)S(1)}, u32[]{:S(2)}, u32[]{:S(2)}) collective-permute-start(bf16[448,576]{1,0:T(8,128)(2,1)} %own_ref.1), channel_id=1, source_target_pairs={{96,0},{0,32},{32,64},{64,96},{224,128},{128,160},{160,192},{192,2... | collective-permute-start | bytes 1548296 | tf_op jit(solution)/shard_map/ppermute | solution.py:22
  2.8 16.4 %collective-permute-start = (bf16[448,576]{1,0:T(8,128)(2,1)}, bf16[448,576]{1,0:T(8,128)(2,1)S(1)}, u32[]{:S(2)}, u32[]{:S(2)}) collective-permute-start(bf16[448,576]{1,0:T(8,128)(2,1)} %own_ref.1), channel_id=1, source_target_pairs={{0,128},{32,160},{64,192},{96,224},{128,0},{160,32},{192,64},{224,... | collective-permute-start | bytes 1548296 | tf_op jit(solution)/shard_map/ppermute | solution.py:26
  15.3 8.9 %collective-permute-start.3 = (bf16[224,576]{1,0:T(8,128)(2,1)S(1)}, bf16[224,576]{1,0:T(8,128)(2,1)S(1)}, u32[]{:S(2)}, u32[]{:S(2)}) collective-permute-start(bf16[224,576]{1,0:T(8,128)(2,1)S(1)} %slice.78), channel_id=1, source_target_pairs={{32,0},{64,32},{96,64},{0,96},{160,128},{192,160},{224,192},{128,2... | collective-permute-start | bytes 774152 | tf_op jit(solution)/shard_map/ppermute | solution.py:22
  19.0 8.7 %collective-permute-start.4 = (bf16[224,576]{1,0:T(8,128)(2,1)S(1)}, bf16[224,576]{1,0:T(8,128)(2,1)S(1)}, u32[]{:S(2)}, u32[]{:S(2)}) collective-permute-start(bf16[224,576]{1,0:T(8,128)(2,1)S(1)} %slice.79), channel_id=1, source_target_pairs={{96,0},{0,32},{32,64},{64,96},{224,128},{128,160},{160,192},{192,2... | collective-permute-start | bytes 774152 | tf_op jit(solution)/shard_map/ppermute | solution.py:22
  29.3 3.5 %collective-permute-start.5 = (bf16[448,1792]{1,0:T(8,128)(2,1)S(1)}, bf16[448,1792]{1,0:T(8,128)(2,1)S(1)}, u32[]{:S(2)}, u32[]{:S(2)}) collective-permute-start(bf16[448,1792]{1,0:T(8,128)(2,1)S(1)} %convolution_convert_fusion), channel_id=1, source_target_pairs={{0,1},{1,0},{2,3},{3,2},{4,5},{5,4},{6,7},{7,6},{8,9},{9,8},{10,11... | collective-permute-start | bytes 4816904 | tf_op jit(solution)/shard_map/ppermute | solution.py:44
  33.2 16.1 %copy-start.3 = (f32[448,1792]{1,0:T(8,128)}, f32[448,1792]{1,0:T(8,128)S(1)}, u32[]{:S(2)}) copy-start(f32[448,1792]{1,0:T(8,128)S(1)} %get-tuple-element.26) | copy-start | bytes 9633796
  33.3 15.9 %collective-permute-start.6 = (bf16[112,1792]{1,0:T(8,128)(2,1)S(1)}, bf16[112,1792]{1,0:T(8,128)(2,1)S(1)}, u32[]{:S(2)}, u32[]{:S(2)}) collective-permute-start(bf16[112,1792]{1,0:T(8,128)(2,1)S(1)} %get-tuple-element.28), channel_id=1, source_target_pairs={{0,4},{1,29},{2,6},{3,31},{4,8},{5,1},{6,10},{7,3},{8,12},{9,5},{1... | collective-permute-start | bytes 1204232 | tf_op jit(solution)/shard_map/ppermute | solution.py:65
  35.3 13.9 %collective-permute-start.7 = (bf16[56,1792]{1,0:T(8,128)(2,1)S(1)}, bf16[56,1792]{1,0:T(8,128)(2,1)S(1)}, u32[]{:S(2)}, u32[]{:S(2)}) collective-permute-start(bf16[56,1792]{1,0:T(8,128)(2,1)S(1)} %slice.82), channel_id=1, source_target_pairs={{0,8},{1,25},{2,10},{3,27},{4,12},{5,29},{6,14},{7,31},{8,16},{9,1... | collective-permute-start | bytes 602120 | tf_op jit(solution)/shard_map/ppermute | solution.py:65
  49.4 14.5 %collective-permute-start.8 = (bf16[112,1792]{1,0:T(8,128)(2,1)S(1)}, bf16[112,1792]{1,0:T(8,128)(2,1)S(1)}, u32[]{:S(2)}, u32[]{:S(2)}) collective-permute-start(bf16[112,1792]{1,0:T(8,128)(2,1)S(1)} %fusion), channel_id=1, source_target_pairs={{0,8},{1,25},{2,10},{3,27},{4,12},{5,29},{6,14},{7,31},{8,16},{9,1... | collective-permute-start | bytes 1204232 | tf_op jit(solution)/shard_map/ppermute | solution.py:65
  49.4 18.7 %collective-permute-start.9 = (bf16[112,1792]{1,0:T(8,128)(2,1)S(1)}, bf16[112,1792]{1,0:T(8,128)(2,1)}, u32[]{:S(2)}, u32[]{:S(2)}) collective-permute-start(bf16[112,1792]{1,0:T(8,128)(2,1)S(1)} %get-tuple-element.16), channel_id=1, source_target_pairs={{0,4},{1,29},{2,6},{3,31},{4,8},{5,1},{6,10},{7,3},{8,12},{9,5},{1... | collective-permute-start | bytes 1204232 | tf_op jit(solution)/shard_map/ppermute | solution.py:65
  69.3 1.7 collective-permute-start.10
  71.1 6.5 %collective-permute-start.11 = (bf16[56,896]{1,0:T(8,128)(2,1)S(1)}, bf16[56,896]{1,0:T(8,128)(2,1)S(1)}, u32[]{:S(2)}, u32[]{:S(2)}) collective-permute-start(bf16[56,896]{1,0:T(8,128)(2,1)S(1)} %get-tuple-element.51), channel_id=1, source_target_pairs={{0,2},{1,3},{2,0},{3,1},{4,6},{5,7},{6,4},{7,5},{8,10},{9,11},{10,... | collective-permute-start | bytes 301064 | tf_op jit(solution)/shard_map/ppermute | solution.py:35
  72.4 19.1 %collective-permute-start.14 = (bf16[448,576]{1,0:T(8,128)(2,1)S(1)}, bf16[448,576]{1,0:T(8,128)(2,1)S(1)}, u32[]{:S(2)}, u32[]{:S(2)}) collective-permute-start(bf16[448,576]{1,0:T(8,128)(2,1)S(1)} %collective-permute-done.refs_5_), channel_id=1, source_target_pairs={{32,0},{64,32},{96,64},{0,96},{160,128},{192,160},{224,192},{128,2... | collective-permute-start | bytes 1548296 | tf_op jit(solution)/shard_map/ppermute | solution.py:22
  72.6 18.9 %collective-permute-start.15 = (bf16[448,576]{1,0:T(8,128)(2,1)S(1)}, bf16[448,576]{1,0:T(8,128)(2,1)S(1)}, u32[]{:S(2)}, u32[]{:S(2)}) collective-permute-start(bf16[448,576]{1,0:T(8,128)(2,1)S(1)} %collective-permute-done.refs_5_), channel_id=1, source_target_pairs={{96,0},{0,32},{32,64},{64,96},{224,128},{128,160},{160,192},{192,2... | collective-permute-start | bytes 1548296 | tf_op jit(solution)/shard_map/ppermute | solution.py:22
  74.4 17.1 %collective-permute-start.16 = (bf16[448,576]{1,0:T(8,128)(2,1)S(1)}, bf16[448,576]{1,0:T(8,128)(2,1)S(1)}, u32[]{:S(2)}, u32[]{:S(2)}) collective-permute-start(bf16[448,576]{1,0:T(8,128)(2,1)S(1)} %get-tuple-element.18.refs_4_), channel_id=1, source_target_pairs={{0,128},{32,160},{64,192},{96,224},{128,0},{160,32},{192,64},{224,... | collective-permute-start | bytes 1548296 | tf_op jit(solution)/shard_map/ppermute | solution.py:26
  74.4 16.3 %collective-permute-start.12 = (bf16[56,896]{1,0:T(8,128)(2,1)S(1)}, bf16[56,896]{1,0:T(8,128)(2,1)S(1)}, u32[]{:S(2)}, u32[]{:S(2)}) collective-permute-start(bf16[56,896]{1,0:T(8,128)(2,1)S(1)} %get-tuple-element.52), channel_id=1, source_target_pairs={{0,128},{32,160},{64,192},{96,224},{128,0},{160,32},{192,64},{224,... | collective-permute-start | bytes 301064 | tf_op jit(solution)/shard_map/ppermute | solution.py:26
  77.5 13.2 %collective-permute-start.13 = (bf16[56,896]{1,0:T(8,128)(2,1)S(1)}, bf16[56,896]{1,0:T(8,128)(2,1)S(1)}, u32[]{:S(2)}, u32[]{:S(2)}) collective-permute-start(bf16[56,896]{1,0:T(8,128)(2,1)S(1)} %get-tuple-element.52), channel_id=1, source_target_pairs={{0,130},{1,131},{2,128},{3,129},{4,134},{5,135},{6,132},{7,133},{8... | collective-permute-start | bytes 301064 | tf_op jit(solution)/shard_map/ppermute | solution.py:40
  91.5 0.8 copy-start.1
  92.3 10.8 %collective-permute-start.19 = (bf16[2,56,896]{2,1,0:T(8,128)(2,1)}, bf16[2,56,896]{2,1,0:T(8,128)(2,1)}, u32[]{:S(2)}, u32[]{:S(2)}) collective-permute-start(bf16[2,56,896]{2,1,0:T(8,128)(2,1)} %pad_maximum_fusion.3), channel_id=1, source_target_pairs={{8,0},{9,1},{10,2},{11,3},{12,4},{13,5},{14,6},{15,7},{16,8},{17,9... | collective-permute-start | bytes 602120 | tf_op jit(solution)/shard_map/ppermute | solution.py:31
  92.3 13.7 %collective-permute-start.20 = (bf16[2,56,896]{2,1,0:T(8,128)(2,1)}, bf16[2,56,896]{2,1,0:T(8,128)(2,1)}, u32[]{:S(2)}, u32[]{:S(2)}) collective-permute-start(bf16[2,56,896]{2,1,0:T(8,128)(2,1)} %pad_maximum_fusion.3), channel_id=1, source_target_pairs={{24,0},{25,1},{26,2},{27,3},{28,4},{29,5},{30,6},{31,7},{0,8},{1,9... | collective-permute-start | bytes 602120 | tf_op jit(solution)/shard_map/ppermute | solution.py:31
  95.2 17.3 %collective-permute-start.17 = (bf16[2,56,896]{2,1,0:T(8,128)(2,1)}, bf16[2,56,896]{2,1,0:T(8,128)(2,1)}, u32[]{:S(2)}, u32[]{:S(2)}) collective-permute-start(bf16[2,56,896]{2,1,0:T(8,128)(2,1)} %pad_maximum_fusion.3), channel_id=1, source_target_pairs={{4,0},{5,1},{6,2},{7,3},{8,4},{9,5},{10,6},{11,7},{12,8},{13,9},{1... | collective-permute-start | bytes 602120 | tf_op jit(solution)/shard_map/ppermute | solution.py:31
  97.0 16.5 %collective-permute-start.18 = (bf16[2,56,896]{2,1,0:T(8,128)(2,1)}, bf16[2,56,896]{2,1,0:T(8,128)(2,1)S(1)}, u32[]{:S(2)}, u32[]{:S(2)}) collective-permute-start(bf16[2,56,896]{2,1,0:T(8,128)(2,1)} %pad_maximum_fusion.3), channel_id=1, source_target_pairs={{28,0},{29,1},{30,2},{31,3},{0,4},{1,5},{2,6},{3,7},{4,8},{5,9},{6... | collective-permute-start | bytes 602120 | tf_op jit(solution)/shard_map/ppermute | solution.py:31
  98.3 21.6 %copy-start = (bf16[448,576]{1,0:T(8,128)(2,1)S(1)}, bf16[448,576]{1,0:T(8,128)(2,1)}, u32[]{:S(2)}) copy-start(bf16[448,576]{1,0:T(8,128)(2,1)} %own_ref.1) | copy-start | bytes 1548292
  98.4 21.6 %copy-start.2 = (bf16[448,576]{1,0:T(8,128)(2,1)S(1)}, bf16[448,576]{1,0:T(8,128)(2,1)}, u32[]{:S(2)}) copy-start(bf16[448,576]{1,0:T(8,128)(2,1)} %copy-done.1) | copy-start | bytes 1548292
  104.0 15.8 %collective-permute-start.23 = (bf16[1,56,896]{2,1,0:T(8,128)(2,1)S(1)}, bf16[1,56,896]{2,1,0:T(8,128)(2,1)S(1)}, u32[]{:S(2)}, u32[]{:S(2)}) collective-permute-start(bf16[1,56,896]{2,1,0:T(8,128)(2,1)S(1)} %slice.89), channel_id=1, source_target_pairs={{8,0},{9,1},{10,2},{11,3},{12,4},{13,5},{14,6},{15,7},{16,8},{17,9... | collective-permute-start | bytes 301064 | tf_op jit(solution)/shard_map/ppermute | solution.py:31
  106.9 12.9 %collective-permute-start.24 = (bf16[1,56,896]{2,1,0:T(8,128)(2,1)S(1)}, bf16[1,56,896]{2,1,0:T(8,128)(2,1)S(1)}, u32[]{:S(2)}, u32[]{:S(2)}) collective-permute-start(bf16[1,56,896]{2,1,0:T(8,128)(2,1)S(1)} %slice.90), channel_id=1, source_target_pairs={{24,0},{25,1},{26,2},{27,3},{28,4},{29,5},{30,6},{31,7},{0,8},{1,9... | collective-permute-start | bytes 301064 | tf_op jit(solution)/shard_map/ppermute | solution.py:31
  108.0 8.2 %collective-permute-start.21 = (bf16[2,56,896]{2,1,0:T(8,128)(2,1)}, bf16[2,56,896]{2,1,0:T(8,128)(2,1)S(1)}, u32[]{:S(2)}, u32[]{:S(2)}) collective-permute-start(bf16[2,56,896]{2,1,0:T(8,128)(2,1)} %collective-permute-done.19), channel_id=1, source_target_pairs={{4,0},{5,1},{6,2},{7,3},{8,4},{9,5},{10,6},{11,7},{12,8},{13,9},{1... | collective-permute-start | bytes 602120 | tf_op jit(solution)/shard_map/ppermute | solution.py:31
  112.6 7.1 %collective-permute-start.22 = (bf16[2,56,896]{2,1,0:T(8,128)(2,1)}, bf16[2,56,896]{2,1,0:T(8,128)(2,1)S(1)}, u32[]{:S(2)}, u32[]{:S(2)}) collective-permute-start(bf16[2,56,896]{2,1,0:T(8,128)(2,1)} %collective-permute-done.20), channel_id=1, source_target_pairs={{28,0},{29,1},{30,2},{31,3},{0,4},{1,5},{2,6},{3,7},{4,8},{5,9},{6... | collective-permute-start | bytes 602120 | tf_op jit(solution)/shard_map/ppermute | solution.py:31
  119.8 3.5 %collective-permute-start.25 = (bf16[2,448,896]{2,1,0:T(8,128)(2,1)S(1)}, bf16[2,448,896]{2,1,0:T(8,128)(2,1)S(1)}, u32[]{:S(2)}, u32[]{:S(2)}) collective-permute-start(bf16[2,448,896]{2,1,0:T(8,128)(2,1)S(1)} %maximum_dynamic-update-slice_fusion.refs_0_.block_ref), channel_id=1, source_target_pairs={{0,1},{1,0},{2,3},{3,2},{4,5},{5,4},{6,7},{7,6},{8,9},{9,8},{10,11... | collective-permute-start | bytes 4816904 | tf_op jit(solution)/shard_map/ppermute | solution.py:44
  126.0 15.1 %collective-permute-start.28 = (bf16[448,576]{1,0:T(8,128)(2,1)S(1)}, bf16[448,576]{1,0:T(8,128)(2,1)S(1)}, u32[]{:S(2)}, u32[]{:S(2)}) collective-permute-start(bf16[448,576]{1,0:T(8,128)(2,1)S(1)} %get-tuple-element.23.own_y), channel_id=1, source_target_pairs={{32,0},{64,32},{96,64},{0,96},{160,128},{192,160},{224,192},{128,2... | collective-permute-start | bytes 1548296 | tf_op jit(solution)/shard_map/ppermute | solution.py:22
  127.6 16.0 %collective-permute-start.26 = (bf16[448,576]{1,0:T(8,128)(2,1)S(1)}, bf16[448,576]{1,0:T(8,128)(2,1)S(1)}, u32[]{:S(2)}, u32[]{:S(2)}) collective-permute-start(bf16[448,576]{1,0:T(8,128)(2,1)S(1)} %get-tuple-element.23.own_y), channel_id=1, source_target_pairs={{96,0},{0,32},{32,64},{64,96},{224,128},{128,160},{160,192},{192,2... | collective-permute-start | bytes 1548296 | tf_op jit(solution)/shard_map/ppermute | solution.py:22
  128.1 16.5 %collective-permute-start.27 = (bf16[448,576]{1,0:T(8,128)(2,1)S(1)}, bf16[448,576]{1,0:T(8,128)(2,1)S(1)}, u32[]{:S(2)}, u32[]{:S(2)}) collective-permute-start(bf16[448,576]{1,0:T(8,128)(2,1)S(1)} %get-tuple-element.23.own_y), channel_id=1, source_target_pairs={{0,128},{32,160},{64,192},{96,224},{128,0},{160,32},{192,64},{224,... | collective-permute-start | bytes 1548296 | tf_op jit(solution)/shard_map/ppermute | solution.py:26
  143.7 25.5 %collective-permute-start.29 = (bf16[672,576]{1,0:T(8,128)(2,1)S(1)}, bf16[672,576]{1,0:T(8,128)(2,1)S(1)}, u32[]{:S(2)}, u32[]{:S(2)}) collective-permute-start(bf16[672,576]{1,0:T(8,128)(2,1)S(1)} %pad_maximum_fusion), channel_id=1, source_target_pairs={{0,128},{32,160},{64,192},{96,224},{128,0},{160,32},{192,64},{224,... | collective-permute-start | bytes 2322440 | tf_op jit(solution)/shard_map/ppermute | solution.py:26
  144.6 24.6 %collective-permute-start.32 = (bf16[448,576]{1,0:T(8,128)(2,1)S(1)}, bf16[448,576]{1,0:T(8,128)(2,1)S(1)}, u32[]{:S(2)}, u32[]{:S(2)}) collective-permute-start(bf16[448,576]{1,0:T(8,128)(2,1)S(1)} %collective-permute-done.27.refs_1_), channel_id=1, source_target_pairs={{64,0},{96,32},{0,64},{32,96},{192,128},{224,160},{128,192},{160,2... | collective-permute-start | bytes 1548296 | tf_op jit(solution)/shard_map/ppermute | solution.py:22
  145.6 21.5 %collective-permute-start.30 = (bf16[336,576]{1,0:T(8,128)(2,1)S(1)}, bf16[336,576]{1,0:T(8,128)(2,1)S(1)}, u32[]{:S(2)}, u32[]{:S(2)}) collective-permute-start(bf16[336,576]{1,0:T(8,128)(2,1)S(1)} %get-tuple-element.56), channel_id=1, source_target_pairs={{32,0},{64,32},{96,64},{0,96},{160,128},{192,160},{224,192},{128,2... | collective-permute-start | bytes 1161224 | tf_op jit(solution)/shard_map/ppermute | solution.py:22
  148.0 21.2 %collective-permute-start.31 = (bf16[336,576]{1,0:T(8,128)(2,1)S(1)}, bf16[336,576]{1,0:T(8,128)(2,1)S(1)}, u32[]{:S(2)}, u32[]{:S(2)}) collective-permute-start(bf16[336,576]{1,0:T(8,128)(2,1)S(1)} %get-tuple-element.55), channel_id=1, source_target_pairs={{96,0},{0,32},{32,64},{64,96},{224,128},{128,160},{160,192},{192,2... | collective-permute-start | bytes 1161224 | tf_op jit(solution)/shard_map/ppermute | solution.py:22
